TPU v7x, 32 devices: a whole 2x2x4 slice. The times are simulated.
32 devices in a mesh: grp: 2 (over x), tile: 16 (over z, y, core).
Axes of the slice: x: 2, y: 2, z: 4, core: 2. Of those that a mesh axis runs over, the one named last changes fastest.
Arguments:
- cotangent: bfloat16 [512, 48, 128], P(('grp', 'tile')), parts along dimension 0, may hold values from -6 to 6
- remap_weight: bfloat16 [2048, 128, 128], P('tile'), may hold values from -0.5 to 0.5
- target_block: int32 [16, 128], P('tile'), may hold values from 0 to 17, as said below
- dest_device: int32 [16, 128], P('tile'), may hold values from 0 to 15, as said below
- source_block: int32 [16, 128], P('tile'), may hold values from 0 to 15
- send_count: int32 [16], P('tile'), may hold values from 32 to 128, as said below
- lev_index: int32 [8], replicated, may hold values from 0 to 18
- lev_frac: float32 [8], replicated, may hold values from 0 to 1
Outputs:
- source_grad: float32 [512, 120, 128], P(('grp', 'tile')), parts along dimension 0
There are 2 independent parts, one for each index of `grp`. A program takes and returns all parts, laid end to end along the dimension named above; an argument that names none is the same for every part. Nothing has to cross between parts.
Inputs may be any that keep to these rules, and one draw needn't show every extreme that they name: `target_block`: 0 names the previous device's last block (cyclic), 1 to 16 the device's own blocks, 17 the next device's first block; entry 0 of every device names 0 and entry 1 names 17. `dest_device`: among the first send_count entries of a device each destination appears at most 16 times, and some device names some destination exactly 16 times; later entries are ignored. `send_count`: some device has 128 live entries.
All inputs are finite; a program needn't handle non-finite values.
Results may differ from a plain program's by a relative error of at most 0.0003.
Values may be sent and summed in bfloat16 or wider, within the bound.
No kernel may reach another device: no remote copies, remote signals or barrier semaphores. Data moves between devices by JAX's collectives and lax.ppermute only.
A program may use at most 128 MiB of HBM per device.

v0:
```python
import jax
import jax.numpy as jnp
from jax import lax
from jax.sharding import PartitionSpec as P

VARS = 6
LEV = 20
LEVT = 8
SB = 16


def padded(value, sides, width):
    for axis, dim in sides:
        peers, length = (lax.axis_size(axis), value.shape[dim])
        up = [(i, (i + 1) % peers) for i in range(peers)]
        down = [(j, i) for i, j in up]
        last = lax.slice_in_dim(value, length - width, length, axis=dim)
        initial = lax.slice_in_dim(value, 0, width, axis=dim)
        before = lax.ppermute(last, axis, up)
        after = lax.ppermute(initial, axis, down)
        value = jnp.concatenate([before, value, after], axis=dim)
    return value


def vertical_matrix(lev_index, lev_frac, levels):
    columns = jnp.arange(levels)[None, :]
    lower = (columns == lev_index[:, None]).astype(jnp.float32)
    upper = (columns == lev_index[:, None] + 1).astype(jnp.float32)
    return (1.0 - lev_frac)[:, None] * lower + lev_frac[:, None] * upper


def raise_levels(blocks, lift_matrix):
    count = blocks.shape[0]
    cells = blocks.shape[2]
    shaped = blocks.reshape(count, VARS, LEVT, cells)
    lifted = jnp.einsum("jl,nvjs->nvls", lift_matrix, shaped, precision=lax.Precision.HIGHEST)
    return lifted.reshape(count, VARS * LEV, cells)


def on_device(
    cotangent,
    remap_weight,
    target_block,
    dest_device,
    source_block,
    send_count,
    lev_index,
    lev_frac,
):
    tile_count = lax.axis_size("tile")
    intersection_count = remap_weight.shape[0]
    capacity = max(2, 2 * intersection_count // tile_count)
    slot_total = tile_count * capacity
    lift_matrix = vertical_matrix(lev_index, lev_frac, LEV)
    window = padded(cotangent, (("tile", 0),), 1)
    picked = window[target_block[0]]
    contrib = jnp.einsum("ofp,ops->ofs", picked, remap_weight, preferred_element_type=jnp.float32)
    usable = jnp.arange(intersection_count) < send_count[0]
    destination = dest_device[0]
    matches = ((destination[:, None] == jnp.arange(tile_count)[None, :]) & usable[:, None]).astype(
        jnp.int32
    )
    running = jnp.cumsum(matches, axis=0)
    rank_index = jnp.sum(matches * running, axis=1) - 1
    slot_index = jnp.where(usable, destination * capacity + rank_index, slot_total)
    labels = jnp.full((slot_total,), SB, jnp.int32).at[slot_index].set(source_block[0], mode="drop")
    contrib = raise_levels(contrib, lift_matrix)
    outgoing = (
        jnp.zeros((slot_total, contrib.shape[1], contrib.shape[2]), jnp.float32)
        .at[slot_index]
        .set(contrib, mode="drop")
    )
    arrived, arrived_labels = (
        lax.all_to_all(outgoing, "tile", split_axis=0, concat_axis=0, tiled=True),
        lax.all_to_all(labels, "tile", split_axis=0, concat_axis=0, tiled=True),
    )
    chooser = (jnp.arange(SB)[:, None] == arrived_labels[None, :]).astype(jnp.float32)
    summed = jnp.einsum("br,rfs->bfs", chooser, arrived, precision=lax.Precision.HIGHEST)
    return summed


def solution(mesh):
    placed = (
        P(("grp", "tile"), None, None),
        P("tile", None, None),
        P("tile", None),
        P("tile", None),
        P("tile", None),
        P("tile"),
        P(),
        P(),
    )
    return jax.shard_map(
        on_device,
        mesh=mesh,
        in_specs=placed,
        out_specs=P(("grp", "tile"), None, None),
        check_vma=False,
    )
```

profile of v0, /device:TPU:15, one launch (start us, length us, event | category | flops | bytes accessed | tf_op | source)
XLA Modules:
  0.0 427.2 jit_solution(12834339754888870417)
XLA Ops:
  0.0 0.8 fusion.22
  0.8 1.8 collective-permute-start
  2.6 0.0 collective-permute-start.1
  3.2 0.8 fusion.4
  4.0 0.2 reduce_window_sum.11
  4.2 0.8 select_reduce_fusion
  5.0 0.7 fusion.20
  5.7 1.1 scatter_custom_fusion
  6.8 0.7 all_to_all.9
  7.5 6.6 %all-to-all-start = ((s32[16,16,1]{1,2,0:T(1,128)}), s32[16,16,1]{1,2,0:T(1,128)S(1)}, u32[]{:S(2)}, u32[]{:S(2)}) async-start(s32[16,16,1]{1,2,0:T(1,128)} %bitcast.6), calls=%async_computation | async-start | bytes 16384 | tf_op jit(solution)/shard_map/all_to_all | solution.py:75
  14.1 0.7 fusion.17
  14.8 0.7 broadcast_add_fusion
  15.4 0.7 broadcast_subtract_fusion
  16.1 0.0 collective-permute-done
  16.1 0.0 collective-permute-done.1
  16.1 1.0 pad_maximum_fusion
  17.1 0.9 gather_fusion
  17.9 3.4 fusion.23
  21.3 0.0 copy-done.1
  21.4 8.0 %convolution_bitcast_fusion = f32[128,6,20,128]{3,2,1,0:T(8,128)S(1)} fusion(f32[128,48,128]{2,1,0:T(8,128)S(1)} %fusion.23, f32[8]{0:T(128)S(1)} %copy-done, s32[8]{0:T(128)S(1)} %broadcast_add_fusion, f32[8]{0:T(128)S(1)} %broadcast_subtract_fusion, s32[8]{0:T(128)S(1)} %copy-done.1), kind=kOutput, calls=%fused_computation.5 | convolution fusion | flops 188744480 | bytes 11010176 | tf_op jit(solution)/shard_map/jl,nvjs->nvls/dot_general | solution.py:36
  29.3 2.5 copy.16
  31.9 7.8 %copy.17 = f32[128,120,128]{2,1,0:T(8,128)} copy(f32[128,120,128]{2,0,1:T(8,128)S(1)} %bitcast.39) | data formatting | bytes 15728640 | tf_op jit(solution)/shard_map/reshape | solution.py:37
  39.7 6.5 %broadcast_in_dim.9 = f32[256,120,128]{2,1,0:T(8,128)} broadcast(f32[]{:T(128)} %constant.6.clone.1), dimensions={} | broadcast | bytes 15728644 | tf_op jit(solution)/shard_map/broadcast_in_dim | solution.py:69
  46.2 21.6 %scatter_fusion = f32[256,120,128]{2,1,0:T(8,128)} fusion(f32[256,120,128]{2,1,0:T(8,128)} %broadcast_in_dim.9, s32[128]{0:T(128)S(1)} %fusion.20, f32[128,120,128]{2,1,0:T(8,128)} %copy.17), kind=kCustom, calls=%fused_computation.2 | custom fusion | bytes 23593472 | tf_op jit(solution)/shard_map/scatter | solution.py:71
  67.8 0.0 all-to-all-done
  67.9 7.2 %all-to-all-start.1 = ((f32[256,120,128]{2,1,0:T(8,128)}), f32[256,120,128]{2,1,0:T(8,128)}, u32[]{:S(2)}, u32[]{:S(2)}) async-start(f32[256,120,128]{2,1,0:T(8,128)} %scatter_fusion), calls=%async_computation.1 | async-start | bytes 31457280 | tf_op jit(solution)/shard_map/all_to_all | solution.py:74
  75.0 0.5 broadcast.111
  75.5 0.7 reduce.3
  76.2 0.1 eq.61
  76.3 338.4 %all-to-all-done.1 = f32[256,120,128]{2,1,0:T(8,128)} async-done(((f32[256,120,128]{2,1,0:T(8,128)}), f32[256,120,128]{2,1,0:T(8,128)}, u32[]{:S(2)}, u32[]{:S(2)}) %all-to-all-start.1) | async-done | bytes 15728672 | tf_op jit(solution)/shard_map/all_to_all | solution.py:74
  414.7 11.3 %fusion = f32[16,120,128]{2,0,1:T(8,128)S(1)} fusion(f32[256,120,128]{2,1,0:T(8,128)} %all-to-all-done.1, s32[256]{0:T(256)S(1)} %eq.61), kind=kOutput, calls=%fused_computation.3 | convolution fusion | flops 754978816 | bytes 16712704 | tf_op jit(solution)/shard_map/br,rfs->bfs/dot_general | solution.py:78
  426.0 1.2 copy.19
  (5 shorter events, 0.0 us)
Async XLA Ops:
  0.0 21.3 %copy-start.1 = (s32[8]{0:T(128)S(1)}, s32[8]{0:T(128)}, u32[]{:S(2)}) copy-start(s32[8]{0:T(128)} %param.14) | copy-start | bytes 100
  0.0 21.3 %copy-start = (f32[8]{0:T(128)S(1)}, f32[8]{0:T(128)}, u32[]{:S(2)}) copy-start(f32[8]{0:T(128)} %param.15) | copy-start | bytes 100
  0.8 15.3 %collective-permute-start = (bf16[1,48,128]{2,1,0:T(8,128)(2,1)S(1)}, bf16[1,48,128]{2,1,0:T(8,128)(2,1)S(1)}, u32[]{:S(2)}, u32[]{:S(2)}) collective-permute-start(bf16[1,48,128]{2,1,0:T(8,128)(2,1)S(1)} %get-tuple-element.5), channel_id=1, source_target_pairs={{0,1},{1,2},{2,3},{3,4},{4,5},{5,6},{6,7},{7,8},{8,9},{9,10},{10,1... | collective-permute-start | bytes 36872 | tf_op jit(solution)/shard_map/ppermute | solution.py:19
  2.6 13.5 %collective-permute-start.1 = (bf16[1,48,128]{2,1,0:T(8,128)(2,1)S(1)}, bf16[1,48,128]{2,1,0:T(8,128)(2,1)S(1)}, u32[]{:S(2)}, u32[]{:S(2)}) collective-permute-start(bf16[1,48,128]{2,1,0:T(8,128)(2,1)S(1)} %get-tuple-element.6), channel_id=1, source_target_pairs={{1,0},{2,1},{3,2},{4,3},{5,4},{6,5},{7,6},{8,7},{9,8},{10,9},{11,1... | collective-permute-start | bytes 36872 | tf_op jit(solution)/shard_map/ppermute | solution.py:20
  7.5 60.4 %all-to-all-start = ((s32[16,16,1]{1,2,0:T(1,128)}), s32[16,16,1]{1,2,0:T(1,128)S(1)}, u32[]{:S(2)}, u32[]{:S(2)}) async-start(s32[16,16,1]{1,2,0:T(1,128)} %bitcast.6), calls=%async_computation | async-start | bytes 16384 | tf_op jit(solution)/shard_map/all_to_all | solution.py:75
  67.9 346.8 %all-to-all-start.1 = ((f32[256,120,128]{2,1,0:T(8,128)}), f32[256,120,128]{2,1,0:T(8,128)}, u32[]{:S(2)}, u32[]{:S(2)}) async-start(f32[256,120,128]{2,1,0:T(8,128)} %scatter_fusion), calls=%async_computation.1 | async-start | bytes 31457280 | tf_op jit(solution)/shard_map/all_to_all | solution.py:74
where the time goes:
time: 428 us; the launch traced here: 427 us
  waiting for transfers between devices  338 us (79%)
  local copies, waits for them, and re-layouts  43.7 us (10%)
  matrix products  22.7 us (5%)
  starting transfers between devices  15.6 us (4%)
  other arithmetic  6.04 us (1%)
    all_to_all x1, waiting for transfers between devices, on_device(): lax.all_to_all(outgoing, 'tile', split_axis=0, concat_axis=0, tiled=True)  338 us
    scatter x1, local copies, waits for them, and re-layouts, on_device(): outgoing = jnp.zeros((slot_total, contrib.shape[1], contrib.shape[2]), jn...  21.6 us
    dot_general x1, matrix products, on_device(): jnp.einsum('br,rfs->bfs', chooser, arrived, precision=lax.Precision.HIGHEST)  11.3 us
  transfers between devices with their start and end apart: 4, of which 1 were waited for; matrix products, arithmetic and copies ran while one was open for 14% of the time, Pallas kernels for 0%

commit v1 on v0

v1 whole, which is shorter than its diff:
```python
import functools

import jax
import jax.numpy as jnp
from jax import lax
from jax.experimental import pallas as pl
from jax.experimental.pallas import tpu as pltpu
from jax.sharding import PartitionSpec as P

VARS = 6
LEV = 20
LEVT = 8
SB = 16
ROWS = VARS * LEVT
BODY = SB * ROWS
CODED = BODY + SB
GROUP = 16
MIB = 1 << 20


def encode(read, write, exps):
    for b in range(SB):
        x = read(b)
        top = jnp.max(jnp.abs(x), axis=0, keepdims=True)
        e = jnp.ceil(jnp.log2(jnp.maximum(top, 1e-30)) + 0.001) - 15.0
        exps[b : b + 1, :] = e
        q = jnp.round(x * jnp.exp2(-e))
        write(b * ROWS, ROWS, q.astype(jnp.int32).astype(jnp.int16))
    write(BODY, SB, exps[...].astype(jnp.int32).astype(jnp.int16))


def scales(ref):
    return jnp.exp2(ref[0, BODY:CODED, :].astype(jnp.int32).astype(jnp.float32))


def decode(ref, scale, b):
    q = ref[0, b * ROWS : (b + 1) * ROWS, :].astype(jnp.int32).astype(jnp.float32)
    return q * scale[b : b + 1, :]


def products_kernel(
    tb_ref,
    dest_ref,
    src_ref,
    count_ref,
    me_ref,
    cot_ref,
    before_ref,
    after_ref,
    w_hbm,
    far_hbm,
    near_hbm,
    keep_hbm,
    window,
    w,
    acc,
    coded,
    exps,
    bins,
    w_sems,
    keep_sem,
    out_sems,
):
    entries = w.shape[0]
    groups = entries // GROUP
    count = count_ref[0]
    me = me_ref[0]
    used = (count + GROUP - 1) // GROUP

    def w_copy(g):
        return pltpu.make_async_copy(
            w_hbm.at[pl.ds(g * GROUP, GROUP)], w.at[pl.ds(g * GROUP, GROUP)], w_sems.at[g]
        )

    for g in range(groups):

        @pl.when(g < used)
        def _():
            w_copy(g).start()

    window[0] = before_ref[0]
    window[1:-1] = cot_ref[...]
    window[window.shape[0] - 1] = after_ref[0]

    trash = 2 * 8 * SB

    @pl.loop(0, entries, unroll=4)
    def _(k):
        rel = dest_ref[0, k] ^ me
        slot = (rel & 1) * 8 + ((rel >> 1) & 1) * 4 + (rel >> 2)
        bins[k] = jnp.where(k < count, slot * SB + src_ref[0, k], trash)

    @pl.loop(0, 2 * 8 * SB, unroll=8)
    def _(b):
        acc[b] = jnp.zeros((ROWS, acc.shape[2]), jnp.float32)

    for g in range(groups):

        @pl.when(g < used)
        def _():
            w_copy(g).wait()

            @pl.loop(0, GROUP // 4)
            def _(part):
                first = g * GROUP + part * 4
                found = [
                    jnp.dot(
                        window[tb_ref[0, first + i]],
                        w[first + i],
                        preferred_element_type=jnp.float32,
                    )
                    for i in range(4)
                ]
                for i in range(4):
                    at = bins[first + i]
                    acc[at] = acc[at] + found[i]

    keep = pltpu.make_async_copy(acc.at[pl.ds(0, 8 * SB)], keep_hbm, keep_sem)
    keep.start()

    @pl.loop(0, 8)
    def _(i):
        slot = (i + 4) & 7

        def read(b):
            return acc[(8 + slot) * SB + b]

        def write(row, rows, value):
            coded[slot, row : row + rows, :] = value

        encode(read, write, exps)

        @pl.when(i < 4)
        def _():
            pltpu.make_async_copy(coded.at[slot], far_hbm.at[slot - 4], out_sems.at[i]).start()

        @pl.when(i >= 4)
        def _():
            pltpu.make_async_copy(coded.at[slot], near_hbm.at[slot], out_sems.at[i]).start()

    keep.wait()
    for i in range(8):
        slot = (i + 4) & 7
        target = far_hbm.at[slot - 4] if i < 4 else near_hbm.at[slot]
        pltpu.make_async_copy(coded.at[slot], target, out_sems.at[i]).wait()


def products(tables, me, cotangent, before, after, weight):
    entries, cells_in, cells = weight.shape
    smem = pl.BlockSpec(memory_space=pltpu.SMEM)
    vmem = pl.BlockSpec(memory_space=pltpu.VMEM)
    hbm = pl.BlockSpec(memory_space=pl.ANY)
    coded = jax.ShapeDtypeStruct((4, CODED, cells), jnp.int16)
    return pl.pallas_call(
        products_kernel,
        out_shape=(coded, coded, jax.ShapeDtypeStruct((8 * SB, ROWS, cells), jnp.float32)),
        in_specs=[smem] * 5 + [vmem] * 3 + [hbm],
        out_specs=(hbm, hbm, hbm),
        scratch_shapes=[
            pltpu.VMEM((cotangent.shape[0] + 2, ROWS, cells_in), jnp.bfloat16),
            pltpu.VMEM(weight.shape, jnp.bfloat16),
            pltpu.VMEM((16 * SB + 1, ROWS, cells), jnp.float32),
            pltpu.VMEM((8, CODED, cells), jnp.int16),
            pltpu.VMEM((SB, cells), jnp.float32),
            pltpu.SMEM((entries,), jnp.int32),
            pltpu.SemaphoreType.DMA((entries // GROUP,)),
            pltpu.SemaphoreType.DMA,
            pltpu.SemaphoreType.DMA((8,)),
        ],
        compiler_params=pltpu.CompilerParams(vmem_limit_bytes=32 * MIB),
        cost_estimate=pl.CostEstimate(
            flops=2 * entries * ROWS * cells_in * cells,
            bytes_accessed=12 * MIB,
            transcendentals=0,
        ),
    )(*tables, me, cotangent, before, after, weight)


def sum_and_code_kernel(n_coded, *refs):
    coded_refs, keep_ref, out_ref, exps = refs[:n_coded], refs[n_coded], refs[-2], refs[-1]
    each = [scales(r) for r in coded_refs]

    def read(b):
        total = keep_ref[b]
        for r, s in zip(coded_refs, each):
            total = total + decode(r, s, b)
        return total

    def write(row, rows, value):
        out_ref[0, row : row + rows, :] = value

    encode(read, write, exps)


def sum_and_code(coded, keep, keep_slot):
    cells = keep.shape[2]
    return pl.pallas_call(
        functools.partial(sum_and_code_kernel, len(coded)),
        grid=(1,),
        out_shape=jax.ShapeDtypeStruct((1, CODED, cells), jnp.int16),
        in_specs=[
            pl.BlockSpec((1, CODED, cells), functools.partial(lambda i, g: (i, 0, 0), i))
            for _, i in coded
        ]
        + [pl.BlockSpec((SB, ROWS, cells), lambda g: (keep_slot, 0, 0))],
        out_specs=pl.BlockSpec((1, CODED, cells), lambda g: (0, 0, 0)),
        scratch_shapes=[pltpu.VMEM((SB, cells), jnp.float32)],
        cost_estimate=pl.CostEstimate(
            flops=10 * BODY * cells, bytes_accessed=8 * BODY * cells, transcendentals=0
        ),
    )(*[a for a, _ in coded], keep)


def finish_kernel(n_coded, index_ref, frac_ref, *refs):
    coded_refs, keep_ref, out_ref = refs[:n_coded], refs[n_coded], refs[n_coded + 1]
    high = VARS * LEV
    row = lax.broadcasted_iota(jnp.int32, (high, ROWS), 0)
    col = lax.broadcasted_iota(jnp.int32, (high, ROWS), 1)
    level = row % LEV
    lift = jnp.zeros((high, ROWS), jnp.float32)
    for j in range(LEVT):
        at, frac = index_ref[j], frac_ref[j]
        here = jnp.where(level == at, 1.0 - frac, jnp.where(level == at + 1, frac, 0.0))
        lift = jnp.where(col % LEVT == j, here, lift)
    lift = jnp.where(row // LEV == col // LEVT, lift, 0.0)
    each = [scales(r) for r in coded_refs]
    for b in range(SB):
        total = keep_ref[b]
        for r, s in zip(coded_refs, each):
            total = total + decode(r, s, b)
        out_ref[b] = jnp.dot(
            lift, total, preferred_element_type=jnp.float32, precision=lax.Precision.HIGHEST
        )


def finish(lev_index, lev_frac, coded, keep):
    cells = keep.shape[2]
    smem = pl.BlockSpec(memory_space=pltpu.SMEM)
    return pl.pallas_call(
        functools.partial(finish_kernel, len(coded)),
        grid=(1,),
        out_shape=jax.ShapeDtypeStruct((SB, VARS * LEV, cells), jnp.float32),
        in_specs=[smem, smem]
        + [pl.BlockSpec((1, CODED, cells), lambda g: (0, 0, 0)) for _ in coded]
        + [pl.BlockSpec((SB, ROWS, cells), lambda g: (0, 0, 0))],
        out_specs=pl.BlockSpec((SB, VARS * LEV, cells), lambda g: (0, 0, 0)),
        cost_estimate=pl.CostEstimate(
            flops=10 * BODY * cells, bytes_accessed=16 * BODY * cells, transcendentals=0
        ),
    )(lev_index, lev_frac, *coded, keep)


def ring_ends(cotangent, peers):
    up = [(i, (i + 1) % peers) for i in range(peers)]
    down = [(j, i) for i, j in up]
    return (
        lax.ppermute(cotangent[-1:], "tile", up),
        lax.ppermute(cotangent[:1], "tile", down),
    )


def swap(value, bits, peers):
    return lax.ppermute(value, "tile", [(i, i ^ bits) for i in range(peers)])


def staged(cotangent, weight, target_block, dest, source, count, lev_index, lev_frac):
    peers = 16
    me = lax.axis_index("tile").astype(jnp.int32).reshape(1)
    before, after = ring_ends(cotangent, peers)
    far, near, keep = products(
        (target_block, dest, source, count), me, cotangent, before, after, weight
    )
    far = swap(far, 1, peers)
    near = swap(near, 1, peers)
    over_y = {r: swap(sum_and_code([(far, r)], keep, 4 + r), 2, peers) for r in (3, 2, 1, 0)}
    over_z = [
        swap(sum_and_code([(near, r), (over_y[r], 0)], keep, r), 4 * r, peers) for r in (3, 2, 1)
    ]
    return finish(lev_index, lev_frac, [near, over_y[0]] + over_z, keep)


def vertical_matrix(lev_index, lev_frac, levels):
    columns = jnp.arange(levels)[None, :]
    lower = (columns == lev_index[:, None]).astype(jnp.float32)
    upper = (columns == lev_index[:, None] + 1).astype(jnp.float32)
    return (1.0 - lev_frac)[:, None] * lower + lev_frac[:, None] * upper


def slotted(cotangent, weight, target_block, dest, source, count, lev_index, lev_frac):
    peers = lax.axis_size("tile")
    entries, _, cells = weight.shape
    capacity = max(2, 2 * entries // peers)
    slots = peers * capacity
    before, after = ring_ends(cotangent, peers)
    window = jnp.concatenate([before, cotangent, after], axis=0)
    contrib = jnp.einsum(
        "ofp,ops->ofs", window[target_block[0]], weight, preferred_element_type=jnp.float32
    )
    live = jnp.arange(entries) < count[0]
    matches = ((dest[0][:, None] == jnp.arange(peers)[None, :]) & live[:, None]).astype(jnp.int32)
    rank = jnp.sum(matches * jnp.cumsum(matches, axis=0), axis=1) - 1
    slot = jnp.where(live, dest[0] * capacity + rank, slots)
    labels = jnp.full((slots,), SB, jnp.int32).at[slot].set(source[0], mode="drop")
    outgoing = jnp.zeros((slots, ROWS, cells), jnp.float32).at[slot].set(contrib, mode="drop")
    arrived = lax.all_to_all(outgoing, "tile", split_axis=0, concat_axis=0, tiled=True)
    arrived_labels = lax.all_to_all(labels, "tile", split_axis=0, concat_axis=0, tiled=True)
    chooser = (jnp.arange(SB)[:, None] == arrived_labels[None, :]).astype(jnp.float32)
    summed = jnp.einsum("br,rfs->bfs", chooser, arrived, precision=lax.Precision.HIGHEST)
    lifted = jnp.einsum(
        "jl,bvjs->bvls",
        vertical_matrix(lev_index, lev_frac, LEV),
        summed.reshape(SB, VARS, LEVT, cells),
        precision=lax.Precision.HIGHEST,
    )
    return lifted.reshape(SB, VARS * LEV, cells)


def solution(mesh):
    placed = (
        P(("grp", "tile"), None, None),
        P("tile", None, None),
        P("tile", None),
        P("tile", None),
        P("tile", None),
        P("tile"),
        P(),
        P(),
    )
    return jax.shard_map(
        staged if mesh.shape["tile"] == 16 else slotted,
        mesh=mesh,
        in_specs=placed,
        out_specs=P(("grp", "tile"), None, None),
        check_vma=False,
    )
```

time: 428 us -> 71.7 us (0.17)
  the two profiles are of different devices: /device:TPU:15 before, /device:TPU:0 now
where the time goes in v1:
time: 71.7 us; the launch traced here: 71.2 us
  Pallas kernels  29.1 us (41%)
  waiting for transfers between devices  15.4 us (21%)
  starting transfers between devices  14.1 us (20%)
  local copies, waits for them, and re-layouts  11.9 us (17%)
  between operations  0.73 us (1%)
    pallas_call x7, Pallas kernels, sum_and_code(): pl.pallas_call(functools.partial(sum_and_code_kernel, len(coded)), grid=(...  14 us
    unnamed x30, local copies, waits for them, and re-layouts  11.2 us
    pallas_call x1, Pallas kernels, products(): pl.pallas_call(products_kernel, out_shape=(coded, coded, jax.ShapeDtypeSt...  10.9 us
    ppermute x9, waiting for transfers between devices, swap(): return lax.ppermute(value, 'tile', [(i, i ^ bits) for i in range(peers)])  10.2 us
    ppermute x9, starting transfers between devices, swap(): return lax.ppermute(value, 'tile', [(i, i ^ bits) for i in range(peers)])  8.61 us
    ppermute x1, starting transfers between devices, ring_ends(): lax.ppermute(cotangent[:1], 'tile', down)  5.44 us
    ppermute x1, waiting for transfers between devices, ring_ends(): lax.ppermute(cotangent[-1:], 'tile', up)  4.41 us
    pallas_call x1, Pallas kernels, finish(): pl.pallas_call(functools.partial(finish_kernel, len(coded)), grid=(1,), o...  4.18 us
  transfers between devices with their start and end apart: 11, of which 6 were waited for; matrix products, arithmetic and copies ran while one was open for 0% of the time, Pallas kernels for 20%

profile of v1, /device:TPU:0, one launch (start us, length us, event | category | flops | bytes accessed | tf_op | source)
XLA Modules:
  0.0 71.2 jit_solution(4341047452952983845)
XLA Ops:
  0.0 0.7 %fusion = (bf16[1,48,128]{2,1,0:T(8,128)(2,1)S(1)}, bf16[1,48,128]{2,1,0:T(8,128)(2,1)S(1)}) fusion(bf16[16,48,128]{2,1,0:T(8,128)(2,1)} %cot_ref.1), kind=kLoop, calls=%fused_computation | loop fusion | bytes 49152 | tf_op jit(solution)/shard_map/slice | solution.py:258
  0.7 5.4 %collective-permute-start.1 = (bf16[1,48,128]{2,1,0:T(8,128)(2,1)S(1)}, bf16[1,48,128]{2,1,0:T(8,128)(2,1)S(1)}, u32[]{:S(2)}, u32[]{:S(2)}) collective-permute-start(bf16[1,48,128]{2,1,0:T(8,128)(2,1)S(1)} %get-tuple-element.11), channel_id=1, source_target_pairs={{1,0},{2,1},{3,2},{4,3},{5,4},{6,5},{7,6},{8,7},{9,8},{10,9},{11,1... | collective-permute-start | bytes 36872 | tf_op jit(solution)/shard_map/ppermute | solution.py:258
  6.8 0.8 %collective-permute-done.1.after_ref = bf16[1,48,128]{2,1,0:T(8,128)(2,1)S(1)} collective-permute-done((bf16[1,48,128]{2,1,0:T(8,128)(2,1)S(1)}, bf16[1,48,128]{2,1,0:T(8,128)(2,1)S(1)}, u32[]{:S(2)}, u32[]{:S(2)}) %collective-permute-start.1) | collective-permute-done | bytes 12320 | tf_op jit(solution)/shard_map/ppermute | solution.py:258
  7.6 4.4 %collective-permute-done.before_ref = bf16[1,48,128]{2,1,0:T(8,128)(2,1)S(1)} collective-permute-done((bf16[1,48,128]{2,1,0:T(8,128)(2,1)S(1)}, bf16[1,48,128]{2,1,0:T(8,128)(2,1)S(1)}, u32[]{:S(2)}, u32[]{:S(2)}) %collective-permute-start) | collective-permute-done | bytes 12320 | tf_op jit(solution)/shard_map/ppermute | solution.py:257
  12.0 2.2 %copy-done.1 = bf16[128,128,128]{2,1,0:T(8,128)(2,1)S(1)} copy-done((bf16[128,128,128]{2,1,0:T(8,128)(2,1)S(1)}, bf16[128,128,128]{2,1,0:T(8,128)(2,1)}, u32[]{:S(2)}) %copy-start.1) | copy-done | bytes 4194328
  14.2 0.9 %copy-done.2 = bf16[16,48,128]{2,1,0:T(8,128)(2,1)S(1)} copy-done((bf16[16,48,128]{2,1,0:T(8,128)(2,1)S(1)}, bf16[16,48,128]{2,1,0:T(8,128)(2,1)}, u32[]{:S(2)}) %copy-start.2) | copy-done | bytes 196632
  15.1 0.7 copy-done.3
  15.8 0.7 copy-done.4
  16.4 0.7 copy-done.5
  17.1 10.9 %shard_map.82 = (s16[4,784,128]{2,1,0:T(8,128)(2,1)S(1)}, s16[4,784,128]{2,1,0:T(8,128)(2,1)S(1)}, f32[128,48,128]{2,1,0:T(8,128)S(1)}) custom-call(s32[1,128]{1,0:T(1,128)S(1)} %copy-done.3, s32[1,128]{1,0:T(1,128)S(1)} %copy-done.4, s32[1,128]{1,0:T(1,128)S(1)} %copy-done.5, s32[1]{0:T(128)S(6)} %copy.9.count_ref, s32[1]{0:T(128)} %bitcast.me_ref, ...), custom_call_target="tpu_custom_call" | custom-call | flops 201326592 | bytes 12582912 | tf_op jit(solution)/shard_map/pallas_call | solution.py:154
  28.0 1.6 %copy-done = f32[128,48,128]{2,1,0:T(8,128)} copy-done((f32[128,48,128]{2,1,0:T(8,128)}, f32[128,48,128]{2,1,0:T(8,128)S(1)}, u32[]{:S(2)}) %copy-start) | copy-done | bytes 3145752
  29.7 0.5 collective-permute-start.2
  30.2 1.8 %collective-permute-done.3.refs_0_ = s16[4,784,128]{2,1,0:T(8,128)(2,1)S(1)} collective-permute-done((s16[4,784,128]{2,1,0:T(8,128)(2,1)S(1)}, s16[4,784,128]{2,1,0:T(8,128)(2,1)S(1)}, u32[]{:S(2)}, u32[]{:S(2)}) %collective-permute-start.3) | collective-permute-done | bytes 802848 | tf_op jit(solution)/shard_map/ppermute | solution.py:263
  32.0 0.9 %copy-done.6 = s16[4,784,128]{2,1,0:T(8,128)(2,1)} copy-done((s16[4,784,128]{2,1,0:T(8,128)(2,1)}, s16[4,784,128]{2,1,0:T(8,128)(2,1)S(1)}, u32[]{:S(2)}) %copy-start.6) | copy-done | bytes 802840
  32.9 1.9 %shard_map.84 = s16[1,784,128]{2,1,0:T(8,128)(2,1)} custom-call(s16[4,784,128]{2,1,0:T(8,128)(2,1)} %copy-done.6, f32[128,48,128]{2,1,0:T(8,128)} %copy-done), custom_call_target="tpu_custom_call" | custom-call | flops 983040 | bytes 786432 | tf_op jit(solution)/shard_map/pallas_call | solution.py:197
  34.8 1.9 %shard_map.86 = s16[1,784,128]{2,1,0:T(8,128)(2,1)} custom-call(s16[4,784,128]{2,1,0:T(8,128)(2,1)} %copy-done.6, f32[128,48,128]{2,1,0:T(8,128)} %copy-done), custom_call_target="tpu_custom_call" | custom-call | flops 983040 | bytes 786432 | tf_op jit(solution)/shard_map/pallas_call | solution.py:197
  36.7 2.0 %collective-permute-start.7 = (s16[1,784,128]{2,1,0:T(8,128)(2,1)}, s16[1,784,128]{2,1,0:T(8,128)(2,1)S(1)}, u32[]{:S(2)}, u32[]{:S(2)}) collective-permute-start(s16[1,784,128]{2,1,0:T(8,128)(2,1)} %shard_map.86), channel_id=1, source_target_pairs={{0,2},{1,3},{2,0},{3,1},{4,6},{5,7},{6,4},{7,5},{8,10},{9,11},{10,... | collective-permute-start | bytes 602120 | tf_op jit(solution)/shard_map/ppermute | solution.py:263
  38.8 1.9 %shard_map.88 = s16[1,784,128]{2,1,0:T(8,128)(2,1)} custom-call(s16[4,784,128]{2,1,0:T(8,128)(2,1)} %copy-done.6, f32[128,48,128]{2,1,0:T(8,128)} %copy-done), custom_call_target="tpu_custom_call" | custom-call | flops 983040 | bytes 786432 | tf_op jit(solution)/shard_map/pallas_call | solution.py:197
  40.7 1.9 %shard_map.83 = s16[1,784,128]{2,1,0:T(8,128)(2,1)} custom-call(s16[4,784,128]{2,1,0:T(8,128)(2,1)} %copy-done.6, f32[128,48,128]{2,1,0:T(8,128)} %copy-done), custom_call_target="tpu_custom_call" | custom-call | flops 983040 | bytes 786432 | tf_op jit(solution)/shard_map/pallas_call | solution.py:197
  42.6 2.0 %collective-permute-start.4 = (s16[1,784,128]{2,1,0:T(8,128)(2,1)}, s16[1,784,128]{2,1,0:T(8,128)(2,1)S(1)}, u32[]{:S(2)}, u32[]{:S(2)}) collective-permute-start(s16[1,784,128]{2,1,0:T(8,128)(2,1)} %shard_map.83), channel_id=1, source_target_pairs={{0,2},{1,3},{2,0},{3,1},{4,6},{5,7},{6,4},{7,5},{8,10},{9,11},{10,... | collective-permute-start | bytes 602120 | tf_op jit(solution)/shard_map/ppermute | solution.py:263
  44.7 0.9 %copy-done.7 = s16[4,784,128]{2,1,0:T(8,128)(2,1)} copy-done((s16[4,784,128]{2,1,0:T(8,128)(2,1)}, s16[4,784,128]{2,1,0:T(8,128)(2,1)S(1)}, u32[]{:S(2)}) %copy-start.7) | copy-done | bytes 802840
  45.6 0.7 copy-done.14
  46.2 2.1 %shard_map.85 = s16[1,784,128]{2,1,0:T(8,128)(2,1)} custom-call(s16[4,784,128]{2,1,0:T(8,128)(2,1)} %copy-done.7, s16[1,784,128]{2,1,0:T(8,128)(2,1)} %copy-done.14, f32[128,48,128]{2,1,0:T(8,128)} %copy-done), custom_call_target="tpu_custom_call" | custom-call | flops 983040 | bytes 786432 | tf_op jit(solution)/shard_map/pallas_call | solution.py:197
  48.4 0.7 copy-done.13
  49.0 2.1 %shard_map.87 = s16[1,784,128]{2,1,0:T(8,128)(2,1)} custom-call(s16[4,784,128]{2,1,0:T(8,128)(2,1)} %copy-done.7, s16[1,784,128]{2,1,0:T(8,128)(2,1)} %copy-done.13, f32[128,48,128]{2,1,0:T(8,128)} %copy-done), custom_call_target="tpu_custom_call" | custom-call | flops 983040 | bytes 786432 | tf_op jit(solution)/shard_map/pallas_call | solution.py:197
  51.4 0.7 copy-done.12
  52.1 2.1 %shard_map.89 = s16[1,784,128]{2,1,0:T(8,128)(2,1)} custom-call(s16[4,784,128]{2,1,0:T(8,128)(2,1)} %copy-done.7, s16[1,784,128]{2,1,0:T(8,128)(2,1)} %copy-done.12, f32[128,48,128]{2,1,0:T(8,128)} %copy-done), custom_call_target="tpu_custom_call" | custom-call | flops 983040 | bytes 786432 | tf_op jit(solution)/shard_map/pallas_call | solution.py:197
  54.2 4.0 %collective-permute-start.10 = (s16[1,784,128]{2,1,0:T(8,128)(2,1)}, s16[1,784,128]{2,1,0:T(8,128)(2,1)S(1)}, u32[]{:S(2)}, u32[]{:S(2)}) collective-permute-start(s16[1,784,128]{2,1,0:T(8,128)(2,1)} %shard_map.89), channel_id=1, source_target_pairs={{0,4},{1,5},{2,6},{3,7},{4,0},{5,1},{6,2},{7,3},{8,12},{9,13},{10,... | collective-permute-start | bytes 602120 | tf_op jit(solution)/shard_map/ppermute | solution.py:263
  58.3 6.7 %collective-permute-done.8.refs_3_ = s16[1,784,128]{2,1,0:T(8,128)(2,1)S(1)} collective-permute-done((s16[1,784,128]{2,1,0:T(8,128)(2,1)}, s16[1,784,128]{2,1,0:T(8,128)(2,1)S(1)}, u32[]{:S(2)}, u32[]{:S(2)}) %collective-permute-start.8) | collective-permute-done | bytes 200736 | tf_op jit(solution)/shard_map/ppermute | solution.py:263
  65.0 1.4 %collective-permute-done.10.refs_4_ = s16[1,784,128]{2,1,0:T(8,128)(2,1)S(1)} collective-permute-done((s16[1,784,128]{2,1,0:T(8,128)(2,1)}, s16[1,784,128]{2,1,0:T(8,128)(2,1)S(1)}, u32[]{:S(2)}, u32[]{:S(2)}) %collective-permute-start.10) | collective-permute-done | bytes 200736 | tf_op jit(solution)/shard_map/ppermute | solution.py:263
  66.4 0.7 copy-done.11
  67.1 4.2 %shard_map.90 = f32[16,120,128]{2,1,0:T(8,128)} custom-call(s32[8]{0:T(128)} %index_ref.1, f32[8]{0:T(128)} %frac_ref.1, s16[4,784,128]{2,1,0:T(8,128)(2,1)} %copy-done.7, s16[1,784,128]{2,1,0:T(8,128)(2,1)} %copy-done.8, s16[1,784,128]{2,1,0:T(8,128)(2,1)} %copy-done.9, s16[1,784,128]{2,1,0:T(8,128)(2,1)} %copy-done.10, s16[1,784,128]{2,1,0:T(8,128)(2,1)} %copy-done.11, ...), custom_call_target="tpu_custom_call" | custom-call | flops 983040 | bytes 1572864 | tf_op jit(solution)/shard_map/pallas_call | solution.py:239
  (30 shorter events, 0.4 us)
Async XLA Ops:
  0.7 6.8 %collective-permute-start.1 = (bf16[1,48,128]{2,1,0:T(8,128)(2,1)S(1)}, bf16[1,48,128]{2,1,0:T(8,128)(2,1)S(1)}, u32[]{:S(2)}, u32[]{:S(2)}) collective-permute-start(bf16[1,48,128]{2,1,0:T(8,128)(2,1)S(1)} %get-tuple-element.11), channel_id=1, source_target_pairs={{1,0},{2,1},{3,2},{4,3},{5,4},{6,5},{7,6},{8,7},{9,8},{10,9},{11,1... | collective-permute-start | bytes 36872 | tf_op jit(solution)/shard_map/ppermute | solution.py:258
  6.2 5.8 %collective-permute-start = (bf16[1,48,128]{2,1,0:T(8,128)(2,1)S(1)}, bf16[1,48,128]{2,1,0:T(8,128)(2,1)S(1)}, u32[]{:S(2)}, u32[]{:S(2)}) collective-permute-start(bf16[1,48,128]{2,1,0:T(8,128)(2,1)S(1)} %get-tuple-element.12), channel_id=1, source_target_pairs={{0,1},{1,2},{2,3},{3,4},{4,5},{5,6},{6,7},{7,8},{8,9},{9,10},{10,1... | collective-permute-start | bytes 36872 | tf_op jit(solution)/shard_map/ppermute | solution.py:257
  12.0 2.2 %copy-start.1 = (bf16[128,128,128]{2,1,0:T(8,128)(2,1)S(1)}, bf16[128,128,128]{2,1,0:T(8,128)(2,1)}, u32[]{:S(2)}) copy-start(bf16[128,128,128]{2,1,0:T(8,128)(2,1)} %w_hbm.1) | copy-start | bytes 12582916
  14.2 0.9 %copy-start.2 = (bf16[16,48,128]{2,1,0:T(8,128)(2,1)S(1)}, bf16[16,48,128]{2,1,0:T(8,128)(2,1)}, u32[]{:S(2)}) copy-start(bf16[16,48,128]{2,1,0:T(8,128)(2,1)} %cot_ref.1) | copy-start | bytes 589828
  15.1 0.7 copy-start.3
  15.8 0.7 copy-start.4
  16.4 0.7 copy-start.5
  28.0 1.6 %copy-start = (f32[128,48,128]{2,1,0:T(8,128)}, f32[128,48,128]{2,1,0:T(8,128)S(1)}, u32[]{:S(2)}) copy-start(f32[128,48,128]{2,1,0:T(8,128)S(1)} %get-tuple-element.10.refs_1_.refs_2_.refs_5_) | copy-start | bytes 9437188
  29.7 2.3 %collective-permute-start.3 = (s16[4,784,128]{2,1,0:T(8,128)(2,1)S(1)}, s16[4,784,128]{2,1,0:T(8,128)(2,1)S(1)}, u32[]{:S(2)}, u32[]{:S(2)}) collective-permute-start(s16[4,784,128]{2,1,0:T(8,128)(2,1)S(1)} %get-tuple-element.9), channel_id=1, source_target_pairs={{0,1},{1,0},{2,3},{3,2},{4,5},{5,4},{6,7},{7,6},{8,9},{9,8},{10,11... | collective-permute-start | bytes 2408456 | tf_op jit(solution)/shard_map/ppermute | solution.py:263
  29.7 15.0 %collective-permute-start.2 = (s16[4,784,128]{2,1,0:T(8,128)(2,1)S(1)}, s16[4,784,128]{2,1,0:T(8,128)(2,1)S(1)}, u32[]{:S(2)}, u32[]{:S(2)}) collective-permute-start(s16[4,784,128]{2,1,0:T(8,128)(2,1)S(1)} %get-tuple-element.8), channel_id=1, source_target_pairs={{0,1},{1,0},{2,3},{3,2},{4,5},{5,4},{6,7},{7,6},{8,9},{9,8},{10,11... | collective-permute-start | bytes 2408456 | tf_op jit(solution)/shard_map/ppermute | solution.py:263
  32.0 0.9 %copy-start.6 = (s16[4,784,128]{2,1,0:T(8,128)(2,1)}, s16[4,784,128]{2,1,0:T(8,128)(2,1)S(1)}, u32[]{:S(2)}) copy-start(s16[4,784,128]{2,1,0:T(8,128)(2,1)S(1)} %collective-permute-done.3.refs_0_) | copy-start | bytes 2408452
  34.8 9.9 %collective-permute-start.5 = (s16[1,784,128]{2,1,0:T(8,128)(2,1)}, s16[1,784,128]{2,1,0:T(8,128)(2,1)S(1)}, u32[]{:S(2)}, u32[]{:S(2)}) collective-permute-start(s16[1,784,128]{2,1,0:T(8,128)(2,1)} %shard_map.84), channel_id=1, source_target_pairs={{0,2},{1,3},{2,0},{3,1},{4,6},{5,7},{6,4},{7,5},{8,10},{9,11},{10,... | collective-permute-start | bytes 602120 | tf_op jit(solution)/shard_map/ppermute | solution.py:263
  36.7 11.6 %collective-permute-start.7 = (s16[1,784,128]{2,1,0:T(8,128)(2,1)}, s16[1,784,128]{2,1,0:T(8,128)(2,1)S(1)}, u32[]{:S(2)}, u32[]{:S(2)}) collective-permute-start(s16[1,784,128]{2,1,0:T(8,128)(2,1)} %shard_map.86), channel_id=1, source_target_pairs={{0,2},{1,3},{2,0},{3,1},{4,6},{5,7},{6,4},{7,5},{8,10},{9,11},{10,... | collective-permute-start | bytes 602120 | tf_op jit(solution)/shard_map/ppermute | solution.py:263
  40.7 10.7 %collective-permute-start.9 = (s16[1,784,128]{2,1,0:T(8,128)(2,1)}, s16[1,784,128]{2,1,0:T(8,128)(2,1)S(1)}, u32[]{:S(2)}, u32[]{:S(2)}) collective-permute-start(s16[1,784,128]{2,1,0:T(8,128)(2,1)} %shard_map.88), channel_id=1, source_target_pairs={{0,2},{1,3},{2,0},{3,1},{4,6},{5,7},{6,4},{7,5},{8,10},{9,11},{10,... | collective-permute-start | bytes 602120 | tf_op jit(solution)/shard_map/ppermute | solution.py:263
  42.6 15.6 %collective-permute-start.4 = (s16[1,784,128]{2,1,0:T(8,128)(2,1)}, s16[1,784,128]{2,1,0:T(8,128)(2,1)S(1)}, u32[]{:S(2)}, u32[]{:S(2)}) collective-permute-start(s16[1,784,128]{2,1,0:T(8,128)(2,1)} %shard_map.83), channel_id=1, source_target_pairs={{0,2},{1,3},{2,0},{3,1},{4,6},{5,7},{6,4},{7,5},{8,10},{9,11},{10,... | collective-permute-start | bytes 602120 | tf_op jit(solution)/shard_map/ppermute | solution.py:263
  44.7 0.9 %copy-start.7 = (s16[4,784,128]{2,1,0:T(8,128)(2,1)}, s16[4,784,128]{2,1,0:T(8,128)(2,1)S(1)}, u32[]{:S(2)}) copy-start(s16[4,784,128]{2,1,0:T(8,128)(2,1)S(1)} %collective-permute-done.2.refs_0_) | copy-start | bytes 2408452
  45.6 0.7 copy-start.14
  48.3 9.9 %collective-permute-start.6 = (s16[1,784,128]{2,1,0:T(8,128)(2,1)}, s16[1,784,128]{2,1,0:T(8,128)(2,1)S(1)}, u32[]{:S(2)}, u32[]{:S(2)}) collective-permute-start(s16[1,784,128]{2,1,0:T(8,128)(2,1)} %shard_map.85), channel_id=1, source_target_pairs={{0,12},{1,13},{2,14},{3,15},{4,8},{5,9},{6,10},{7,11},{8,4},{9,5},... | collective-permute-start | bytes 602120 | tf_op jit(solution)/shard_map/ppermute | solution.py:263
  48.3 0.7 copy-start.13
  51.1 13.9 %collective-permute-start.8 = (s16[1,784,128]{2,1,0:T(8,128)(2,1)}, s16[1,784,128]{2,1,0:T(8,128)(2,1)S(1)}, u32[]{:S(2)}, u32[]{:S(2)}) collective-permute-start(s16[1,784,128]{2,1,0:T(8,128)(2,1)} %shard_map.87), channel_id=1, source_target_pairs={{0,8},{1,9},{2,10},{3,11},{4,12},{5,13},{6,14},{7,15},{8,0},{9,1},... | collective-permute-start | bytes 602120 | tf_op jit(solution)/shard_map/ppermute | solution.py:263
  51.4 0.7 copy-start.12
  54.2 12.1 %collective-permute-start.10 = (s16[1,784,128]{2,1,0:T(8,128)(2,1)}, s16[1,784,128]{2,1,0:T(8,128)(2,1)S(1)}, u32[]{:S(2)}, u32[]{:S(2)}) collective-permute-start(s16[1,784,128]{2,1,0:T(8,128)(2,1)} %shard_map.89), channel_id=1, source_target_pairs={{0,4},{1,5},{2,6},{3,7},{4,0},{5,1},{6,2},{7,3},{8,12},{9,13},{10,... | collective-permute-start | bytes 602120 | tf_op jit(solution)/shard_map/ppermute | solution.py:263
  58.3 8.1 %copy-start.8 = (s16[1,784,128]{2,1,0:T(8,128)(2,1)}, s16[1,784,128]{2,1,0:T(8,128)(2,1)S(1)}, u32[]{:S(2)}) copy-start(s16[1,784,128]{2,1,0:T(8,128)(2,1)S(1)} %collective-permute-done.4.refs_1_) | copy-start | bytes 602116
  58.3 8.1 %copy-start.9 = (s16[1,784,128]{2,1,0:T(8,128)(2,1)}, s16[1,784,128]{2,1,0:T(8,128)(2,1)S(1)}, u32[]{:S(2)}) copy-start(s16[1,784,128]{2,1,0:T(8,128)(2,1)S(1)} %collective-permute-done.6.refs_2_) | copy-start | bytes 602116
  65.0 1.4 %copy-start.10 = (s16[1,784,128]{2,1,0:T(8,128)(2,1)}, s16[1,784,128]{2,1,0:T(8,128)(2,1)S(1)}, u32[]{:S(2)}) copy-start(s16[1,784,128]{2,1,0:T(8,128)(2,1)S(1)} %collective-permute-done.8.refs_3_) | copy-start | bytes 602116
  66.4 0.7 copy-start.11

commit v2 on v1

v2 whole, which is shorter than its diff:
```python
import functools

import jax
import jax.numpy as jnp
from jax import lax
from jax.experimental import pallas as pl
from jax.experimental.pallas import tpu as pltpu
from jax.sharding import PartitionSpec as P

VARS = 6
LEV = 20
LEVT = 8
SB = 16
ROWS = VARS * LEVT
BODY = SB * ROWS
CODED = BODY + SB
GROUP = 16
MIB = 1 << 20


def encode(read, write, exps):
    for b in range(SB):
        x = read(b)
        top = jnp.max(jnp.abs(x), axis=0, keepdims=True)
        e = jnp.ceil(jnp.log2(jnp.maximum(top, 1e-30)) + 0.001) - 15.0
        exps[b : b + 1, :] = e
        q = jnp.round(x * jnp.exp2(-e))
        write(b * ROWS, ROWS, q.astype(jnp.int32).astype(jnp.int16))
    write(BODY, SB, exps[...].astype(jnp.int32).astype(jnp.int16))


def scales(ref, i):
    return jnp.exp2(ref[i, BODY:CODED, :].astype(jnp.int32).astype(jnp.float32))


def decode(ref, i, scale, b):
    q = ref[i, b * ROWS : (b + 1) * ROWS, :].astype(jnp.int32).astype(jnp.float32)
    return q * scale[b : b + 1, :]


TRASH = 16 * SB


def add_products(first, entry_of, bin_of, left_of, w, acc, wide):
    found = []
    for i in range(wide):
        e = entry_of(first + i)
        found.append(jnp.dot(left_of(first + i), w[e], preferred_element_type=jnp.float32))
    for i in range(wide):
        at = bin_of(first + i)
        acc[at] = acc[at] + found[i]


def products_kernel(
    count_ref,
    me_ref,
    tb_hbm,
    dest_hbm,
    src_hbm,
    cot_hbm,
    w_hbm,
    acc,
    w,
    ends,
    cot,
    tb,
    dest,
    src,
    bins,
    sems,
    w_sems,
):
    entries, blocks = w.shape[0], cot.shape[0]
    groups = entries // GROUP
    count = count_ref[0]
    me = me_ref[0]
    used = (count + GROUP - 1) // GROUP

    def w_copy(g):
        return pltpu.make_async_copy(
            w_hbm.at[pl.ds(g * GROUP, GROUP)], w.at[pl.ds(g * GROUP, GROUP)], w_sems.at[g]
        )

    small = [
        pltpu.make_async_copy(a, b, sems.at[i])
        for i, (a, b) in enumerate(
            ((tb_hbm, tb), (dest_hbm, dest), (src_hbm, src), (cot_hbm, cot))
        )
    ]
    for copy in small:
        copy.start()
    for g in range(groups):

        @pl.when(g < used)
        def _():
            w_copy(g).start()

    @pl.loop(0, TRASH, unroll=8)
    def _(b):
        acc[b] = jnp.zeros(acc.shape[1:], jnp.float32)

    acc[TRASH] = jnp.zeros(acc.shape[1:], jnp.float32)

    for copy in small:
        copy.wait()

    @pl.loop(0, entries, init_carry=jnp.int32(0), unroll=4)
    def listed(k, n):
        rel = dest[0, k] ^ me
        slot = (rel & 1) * 8 + ((rel >> 1) & 1) * 4 + (rel >> 2)
        live = k < count
        at = jnp.where(live, slot * SB + src[0, k], TRASH)
        block = tb[0, k]
        outer = (block == 0) | (block == blocks + 1)
        bins[k] = jnp.where(outer, TRASH, at)
        tb[0, k] = jnp.clip(block - 1, 0, blocks - 1)
        ends[0, n] = k
        ends[1, n] = at
        ends[2, n] = jnp.where(block == 0, 0, 1)
        return n + (outer & live).astype(jnp.int32)

    for i in range(4):
        ends[0, listed + i] = 0
        ends[1, listed + i] = TRASH
        ends[2, listed + i] = 0
    ends[3, 0] = listed

    for g in range(groups):

        @pl.when(g < used)
        def _():
            w_copy(g).wait()

            @pl.loop(0, GROUP // 8)
            def _(part):
                add_products(
                    g * GROUP + part * 8,
                    lambda k: k,
                    lambda k: bins[k],
                    lambda k: cot[tb[0, k]],
                    w,
                    acc,
                    8,
                )


def products(tables, count, me, cotangent, weight):
    entries, cells_in, cells = weight.shape
    smem = pl.BlockSpec(memory_space=pltpu.SMEM)
    vmem = pl.BlockSpec(memory_space=pltpu.VMEM)
    hbm = pl.BlockSpec(memory_space=pltpu.HBM)
    return pl.pallas_call(
        products_kernel,
        out_shape=(
            jax.ShapeDtypeStruct((TRASH + 1, ROWS, cells), jnp.float32),
            jax.ShapeDtypeStruct(weight.shape, jnp.bfloat16),
            jax.ShapeDtypeStruct((4, entries + 4), jnp.int32),
        ),
        in_specs=[smem, smem] + [hbm] * 5,
        out_specs=(vmem, vmem, smem),
        scratch_shapes=[
            pltpu.VMEM(cotangent.shape, jnp.bfloat16),
            pltpu.SMEM((1, entries), jnp.int32),
            pltpu.SMEM((1, entries), jnp.int32),
            pltpu.SMEM((1, entries), jnp.int32),
            pltpu.SMEM((entries,), jnp.int32),
            pltpu.SemaphoreType.DMA((4,)),
            pltpu.SemaphoreType.DMA((entries // GROUP,)),
        ],
        compiler_params=pltpu.CompilerParams(vmem_limit_bytes=24 * MIB),
        cost_estimate=pl.CostEstimate(
            flops=2 * entries * ROWS * cells_in * cells,
            bytes_accessed=12 * MIB,
            transcendentals=0,
        ),
    )(count, me, *tables, cotangent, weight)


def code_slot(acc, slot, coded, exps, out_ref, out_slot):
    def read(b):
        total = acc[slot * SB + b]
        for r, i, s in coded:
            total = total + decode(r, i, s, b)
        return total

    def write(row, rows, value):
        out_ref[out_slot, row : row + rows, :] = value

    encode(read, write, exps)


def ends_kernel(ends, before, after, w, acc_in, acc, far_ref, sides, exps):
    sides[0] = before[0]
    sides[1] = after[0]

    @pl.loop(0, (ends[3, 0] + 3) // 4)
    def _(part):
        add_products(
            part * 4,
            lambda k: ends[0, k],
            lambda k: ends[1, k],
            lambda k: sides[ends[2, k]],
            w,
            acc,
            4,
        )

    @pl.loop(0, 4)
    def _(i):
        code_slot(acc, 12 + i, [], exps, far_ref, i)


def add_ends(ends, before, after, w, acc):
    cells = acc.shape[2]
    smem = pl.BlockSpec(memory_space=pltpu.SMEM)
    vmem = pl.BlockSpec(memory_space=pltpu.VMEM)
    return pl.pallas_call(
        ends_kernel,
        out_shape=(
            jax.ShapeDtypeStruct(acc.shape, jnp.float32),
            jax.ShapeDtypeStruct((4, CODED, cells), jnp.int16),
        ),
        in_specs=[smem] + [vmem] * 4,
        out_specs=(vmem, vmem),
        scratch_shapes=[
            pltpu.VMEM((2,) + before.shape[1:], jnp.bfloat16),
            pltpu.VMEM((SB, cells), jnp.float32),
        ],
        input_output_aliases={4: 0},
        compiler_params=pltpu.CompilerParams(vmem_limit_bytes=32 * MIB),
        cost_estimate=pl.CostEstimate(
            flops=10 * BODY * cells, bytes_accessed=8 * BODY * cells, transcendentals=0
        ),
    )(ends, before, after, w, acc)


def code_kernel(slots, takes, acc, *refs):
    arrays = refs[: len(refs) - len(slots) - 1]
    outs, exps = refs[len(arrays) : -1], refs[-1]
    for slot, pairs, out in zip(slots, takes, outs):
        coded = [(arrays[a], i, scales(arrays[a], i)) for a, i in pairs]
        code_slot(acc, slot, coded, exps, out, 0)


def code(acc, slots, takes, arrays):
    cells = acc.shape[2]
    vmem = pl.BlockSpec(memory_space=pltpu.VMEM)
    return pl.pallas_call(
        functools.partial(code_kernel, slots, takes),
        out_shape=tuple(jax.ShapeDtypeStruct((1, CODED, cells), jnp.int16) for _ in slots),
        in_specs=[vmem] * (1 + len(arrays)),
        out_specs=(vmem,) * len(slots),
        scratch_shapes=[pltpu.VMEM((SB, cells), jnp.float32)],
        compiler_params=pltpu.CompilerParams(vmem_limit_bytes=32 * MIB),
        cost_estimate=pl.CostEstimate(
            flops=10 * BODY * cells, bytes_accessed=8 * BODY * cells, transcendentals=0
        ),
    )(acc, *arrays)


def code_near_kernel(acc, near_ref, exps):
    @pl.loop(0, 4)
    def _(i):
        code_slot(acc, 8 + i, [], exps, near_ref, i)


def code_near(acc):
    cells = acc.shape[2]
    vmem = pl.BlockSpec(memory_space=pltpu.VMEM)
    return pl.pallas_call(
        code_near_kernel,
        out_shape=jax.ShapeDtypeStruct((4, CODED, cells), jnp.int16),
        in_specs=[vmem],
        out_specs=vmem,
        scratch_shapes=[pltpu.VMEM((SB, cells), jnp.float32)],
        compiler_params=pltpu.CompilerParams(vmem_limit_bytes=32 * MIB),
        cost_estimate=pl.CostEstimate(
            flops=10 * BODY * cells, bytes_accessed=8 * BODY * cells, transcendentals=0
        ),
    )(acc)


def finish_kernel(takes, index_ref, frac_ref, acc, *refs):
    arrays, out_hbm, out, sems = refs[:-3], refs[-3], refs[-2], refs[-1]
    high = VARS * LEV
    row = lax.broadcasted_iota(jnp.int32, (high, ROWS), 0)
    col = lax.broadcasted_iota(jnp.int32, (high, ROWS), 1)
    level = row % LEV
    lift = jnp.zeros((high, ROWS), jnp.float32)
    for j in range(LEVT):
        at, frac = index_ref[j], frac_ref[j]
        here = jnp.where(level == at, 1.0 - frac, jnp.where(level == at + 1, frac, 0.0))
        lift = jnp.where(col % LEVT == j, here, lift)
    lift = jnp.where(row // LEV == col // LEVT, lift, 0.0)
    high_part = lift.astype(jnp.bfloat16)
    low_part = (lift - high_part.astype(jnp.float32)).astype(jnp.bfloat16)
    left = jnp.concatenate([high_part, high_part, low_part, low_part], axis=1)
    coded = [(arrays[a], i, scales(arrays[a], i)) for a, i in takes]
    copies = []
    for b in range(SB):
        total = acc[b]
        for r, i, s in coded:
            total = total + decode(r, i, s, b)
        first = total.astype(jnp.bfloat16)
        second = (total - first.astype(jnp.float32)).astype(jnp.bfloat16)
        right = jnp.concatenate([first, second, first, second], axis=0)
        out[b] = jnp.dot(left, right, preferred_element_type=jnp.float32)
        if b % 4 == 3:
            part = pl.ds(b - 3, 4)
            copy = pltpu.make_async_copy(out.at[part], out_hbm.at[part], sems.at[b // 4])
            copy.start()
            copies.append(copy)
    for copy in copies:
        copy.wait()


def finish(lev_index, lev_frac, acc, takes, arrays):
    cells = acc.shape[2]
    smem = pl.BlockSpec(memory_space=pltpu.SMEM)
    vmem = pl.BlockSpec(memory_space=pltpu.VMEM)
    result = jax.ShapeDtypeStruct((SB, VARS * LEV, cells), jnp.float32)
    return pl.pallas_call(
        functools.partial(finish_kernel, takes),
        out_shape=result,
        in_specs=[smem, smem] + [vmem] * (1 + len(arrays)),
        out_specs=pl.BlockSpec(memory_space=pltpu.HBM),
        scratch_shapes=[
            pltpu.VMEM(result.shape, jnp.float32),
            pltpu.SemaphoreType.DMA((SB // 4,)),
        ],
        compiler_params=pltpu.CompilerParams(vmem_limit_bytes=32 * MIB),
        cost_estimate=pl.CostEstimate(
            flops=10 * BODY * cells, bytes_accessed=16 * BODY * cells, transcendentals=0
        ),
    )(lev_index, lev_frac, acc, *arrays)


def ring_ends(cotangent, peers):
    up = [(i, (i + 1) % peers) for i in range(peers)]
    down = [(j, i) for i, j in up]
    return (
        lax.ppermute(cotangent[-1:], "tile", up),
        lax.ppermute(cotangent[:1], "tile", down),
    )


def swap(value, bits, peers):
    return lax.ppermute(value, "tile", [(i, i ^ bits) for i in range(peers)])


def staged(cotangent, weight, target_block, dest, source, count, lev_index, lev_frac):
    peers = 16
    me = lax.axis_index("tile").astype(jnp.int32).reshape(1)
    before, after = ring_ends(cotangent, peers)
    acc, w, ends = products((target_block, dest, source), count, me, cotangent, weight)
    acc, far = add_ends(ends, before, after, w, acc)
    far = swap(far, 1, peers)
    near = swap(code_near(acc), 1, peers)
    (y3,) = code(acc, (7,), (((0, 3),),), (far,))
    y3 = swap(y3, 2, peers)
    y2, y1, y0 = code(acc, (6, 5, 4), (((0, 2),), ((0, 1),), ((0, 0),)), (far,))
    y2, y1, y0 = (swap(v, 2, peers) for v in (y2, y1, y0))
    (a3,) = code(acc, (3,), (((0, 3), (1, 0)),), (near, y3))
    a3 = swap(a3, 4, peers)
    (b2,) = code(acc, (2,), (((0, 2), (1, 0), (2, 0)),), (near, y2, a3))
    b2 = swap(b2, 8, peers)
    (a1,) = code(acc, (1,), (((0, 1), (1, 0)),), (near, y1))
    a1 = swap(a1, 4, peers)
    return finish(
        lev_index, lev_frac, acc, ((0, 0), (1, 0), (2, 0), (3, 0)), (near, y0, a1, b2)
    )


def vertical_matrix(lev_index, lev_frac, levels):
    columns = jnp.arange(levels)[None, :]
    lower = (columns == lev_index[:, None]).astype(jnp.float32)
    upper = (columns == lev_index[:, None] + 1).astype(jnp.float32)
    return (1.0 - lev_frac)[:, None] * lower + lev_frac[:, None] * upper


def slotted(cotangent, weight, target_block, dest, source, count, lev_index, lev_frac):
    peers = lax.axis_size("tile")
    entries, _, cells = weight.shape
    capacity = max(2, 2 * entries // peers)
    slots = peers * capacity
    before, after = ring_ends(cotangent, peers)
    window = jnp.concatenate([before, cotangent, after], axis=0)
    contrib = jnp.einsum(
        "ofp,ops->ofs", window[target_block[0]], weight, preferred_element_type=jnp.float32
    )
    live = jnp.arange(entries) < count[0]
    matches = ((dest[0][:, None] == jnp.arange(peers)[None, :]) & live[:, None]).astype(jnp.int32)
    rank = jnp.sum(matches * jnp.cumsum(matches, axis=0), axis=1) - 1
    slot = jnp.where(live, dest[0] * capacity + rank, slots)
    labels = jnp.full((slots,), SB, jnp.int32).at[slot].set(source[0], mode="drop")
    outgoing = jnp.zeros((slots, ROWS, cells), jnp.float32).at[slot].set(contrib, mode="drop")
    arrived = lax.all_to_all(outgoing, "tile", split_axis=0, concat_axis=0, tiled=True)
    arrived_labels = lax.all_to_all(labels, "tile", split_axis=0, concat_axis=0, tiled=True)
    chooser = (jnp.arange(SB)[:, None] == arrived_labels[None, :]).astype(jnp.float32)
    summed = jnp.einsum("br,rfs->bfs", chooser, arrived, precision=lax.Precision.HIGHEST)
    lifted = jnp.einsum(
        "jl,bvjs->bvls",
        vertical_matrix(lev_index, lev_frac, LEV),
        summed.reshape(SB, VARS, LEVT, cells),
        precision=lax.Precision.HIGHEST,
    )
    return lifted.reshape(SB, VARS * LEV, cells)


def solution(mesh):
    placed = (
        P(("grp", "tile"), None, None),
        P("tile", None, None),
        P("tile", None),
        P("tile", None),
        P("tile", None),
        P("tile"),
        P(),
        P(),
    )
    return jax.shard_map(
        staged if mesh.shape["tile"] == 16 else slotted,
        mesh=mesh,
        in_specs=placed,
        out_specs=P(("grp", "tile"), None, None),
        check_vma=False,
    )
```

time: 71.7 us -> 53.3 us (0.74)
  Pallas kernels: 29.1 us -> 12.7 us
  waiting for transfers between devices: 15.4 us -> 25.1 us
  local copies, waits for them, and re-layouts: 11.9 us -> 5.81 us
  starting transfers between devices: 14.1 us -> 8.59 us
    pallas_call x9, Pallas kernels: 29.1 us -> 12.7 us  [the longest x1 7.1 us: products(): pl.pallas_call(products_kernel, out_shape=(jax.ShapeDtypeStruct((TRASH +...]
    ppermute x9, waiting for transfers between devices: 10.2 us -> 25.1 us  [swap(): return lax.ppermute(value, 'tile', [(i, i ^ bits) for i in range(peers)])]
    unnamed x30 -> x14, local copies, waits for them, and re-layouts: 11.2 us -> 5.09 us
    ppermute x9, starting transfers between devices: 8.61 us -> 3.14 us  [swap(): return lax.ppermute(value, 'tile', [(i, i ^ bits) for i in range(peers)])]
    ppermute x1, waiting for transfers between devices: 4.41 us -> 0.01 us  [ring_ends(): lax.ppermute(cotangent[-1:], 'tile', up)]
    ppermute x1, waiting for transfers between devices: 0.75 us -> 0.01 us  [ring_ends(): lax.ppermute(cotangent[:1], 'tile', down)]
  transfers between devices with their start and end apart: 11 -> 11, of which waited for: 6 -> 6; matrix products, arithmetic and copies ran while one was open for 0% -> 0% of each run, Pallas kernels for 20% -> 16%
where the time goes in v2:
time: 53.3 us; the launch traced here: 53 us
  waiting for transfers between devices  25.1 us (47%)
  Pallas kernels  12.7 us (24%)
  starting transfers between devices  8.59 us (16%)
  local copies, waits for them, and re-layouts  5.81 us (11%)
  between operations  0.78 us (1%)
    ppermute x9, waiting for transfers between devices, swap(): return lax.ppermute(value, 'tile', [(i, i ^ bits) for i in range(peers)])  25.1 us
    pallas_call x1, Pallas kernels, products(): pl.pallas_call(products_kernel, out_shape=(jax.ShapeDtypeStruct((TRASH +...  7.1 us
    ppermute x1, starting transfers between devices, ring_ends(): lax.ppermute(cotangent[:1], 'tile', down)  5.44 us
    unnamed x14, local copies, waits for them, and re-layouts  5.09 us
    ppermute x9, starting transfers between devices, swap(): return lax.ppermute(value, 'tile', [(i, i ^ bits) for i in range(peers)])  3.14 us
    pallas_call x1, Pallas kernels, add_ends(): pl.pallas_call(ends_kernel, out_shape=(jax.ShapeDtypeStruct(acc.shape, jn...  2.04 us
    pallas_call x1, Pallas kernels, finish(): pl.pallas_call(functools.partial(finish_kernel, takes), out_shape=result,...  1.91 us
    pallas_call x5, Pallas kernels, code(): pl.pallas_call(functools.partial(code_kernel, slots, takes), out_shape=tu...  1.26 us
  transfers between devices with their start and end apart: 11, of which 6 were waited for; matrix products, arithmetic and copies ran while one was open for 0% of the time, Pallas kernels for 16%

profile of v2, /device:TPU:0, one launch (start us, length us, event | category | flops | bytes accessed | tf_op | source)
XLA Modules:
  0.0 53.0 jit_solution(3807027887658563978)
XLA Ops:
  0.0 0.7 %fusion = (bf16[1,48,128]{2,1,0:T(8,128)(2,1)S(1)}, bf16[1,48,128]{2,1,0:T(8,128)(2,1)S(1)}) fusion(bf16[16,48,128]{2,1,0:T(8,128)(2,1)} %cot_hbm.1), kind=kLoop, calls=%fused_computation | loop fusion | bytes 49152 | tf_op jit(solution)/shard_map/slice | solution.py:343
  0.7 5.4 %collective-permute-start.1 = (bf16[1,48,128]{2,1,0:T(8,128)(2,1)S(1)}, bf16[1,48,128]{2,1,0:T(8,128)(2,1)S(1)}, u32[]{:S(2)}, u32[]{:S(2)}) collective-permute-start(bf16[1,48,128]{2,1,0:T(8,128)(2,1)S(1)} %get-tuple-element.21), channel_id=1, source_target_pairs={{1,0},{2,1},{3,2},{4,3},{5,4},{6,5},{7,6},{8,7},{9,8},{10,9},{11,1... | collective-permute-start | bytes 36872 | tf_op jit(solution)/shard_map/ppermute | solution.py:343
  6.8 0.0 copy-start
  6.8 2.2 %copy-done = bf16[128,128,128]{2,1,0:T(8,128)(2,1)S(1)} copy-done((bf16[128,128,128]{2,1,0:T(8,128)(2,1)S(1)}, bf16[128,128,128]{2,1,0:T(8,128)(2,1)}, u32[]{:S(2)}) %copy-start) | copy-done | bytes 4194328
  9.0 0.9 %copy-done.1 = bf16[16,48,128]{2,1,0:T(8,128)(2,1)S(1)} copy-done((bf16[16,48,128]{2,1,0:T(8,128)(2,1)S(1)}, bf16[16,48,128]{2,1,0:T(8,128)(2,1)}, u32[]{:S(2)}) %copy-start.1) | copy-done | bytes 196632
  9.9 0.7 %copy-done.2 = s32[1,128]{1,0:T(1,128)S(1)} copy-done((s32[1,128]{1,0:T(1,128)S(1)}, s32[1,128]{1,0:T(1,128)}, u32[]{:S(2)}) %copy-start.2) | copy-done | bytes 536
  10.6 0.7 %copy-done.3 = s32[1,128]{1,0:T(1,128)S(1)} copy-done((s32[1,128]{1,0:T(1,128)S(1)}, s32[1,128]{1,0:T(1,128)}, u32[]{:S(2)}) %copy-start.3) | copy-done | bytes 536
  11.3 0.7 %copy-done.4 = s32[1,128]{1,0:T(1,128)S(1)} copy-done((s32[1,128]{1,0:T(1,128)S(1)}, s32[1,128]{1,0:T(1,128)}, u32[]{:S(2)}) %copy-start.4) | copy-done | bytes 536
  11.9 7.1 %shard_map.82 = (f32[257,48,128]{2,1,0:T(8,128)S(1)}, bf16[128,128,128]{2,1,0:T(8,128)(2,1)S(1)}, s32[4,132]{1,0:T(4,128)S(1)}) custom-call(s32[1]{0:T(128)S(6)} %copy.11.count_ref, s32[1]{0:T(128)} %bitcast.me_ref, s32[1,128]{1,0:T(1,128)S(1)} %copy-done.2, s32[1,128]{1,0:T(1,128)S(1)} %copy-done.3, s32[1,128]{1,0:T(1,128)S(1)} %copy-done.4, ...), custom_call_target="tpu_custom_call" | custom-call | flops 201326592 | bytes 12582912 | tf_op jit(solution)/shard_map/pallas_call | solution.py:152
  19.0 2.0 %shard_map.83 = (f32[257,48,128]{2,1,0:T(8,128)S(1)}, s16[4,784,128]{2,1,0:T(8,128)(2,1)S(1)}) custom-call(s32[4,132]{1,0:T(4,128)S(1)} %get-tuple-element.13.ends, bf16[1,48,128]{2,1,0:T(8,128)(2,1)S(1)} %collective-permute-done.before, bf16[1,48,128]{2,1,0:T(8,128)(2,1)S(1)} %collective-permute-done.1.after, ...), custom_call_target="tpu_custom_call", output_to_operand_aliasing={{0}: (4, {})} | custom-call | flops 983040 | bytes 786432 | tf_op jit(solution)/shard_map/pallas_call | solution.py:217
  21.1 0.1 collective-permute-start.3
  21.2 0.4 shard_map.84
  21.5 0.6 %collective-permute-start.2 = (s16[4,784,128]{2,1,0:T(8,128)(2,1)S(1)}, s16[4,784,128]{2,1,0:T(8,128)(2,1)S(1)}, u32[]{:S(2)}, u32[]{:S(2)}) collective-permute-start(s16[4,784,128]{2,1,0:T(8,128)(2,1)S(1)} %shard_map.84), channel_id=1, source_target_pairs={{0,1},{1,0},{2,3},{3,2},{4,5},{5,4},{6,7},{7,6},{8,9},{9,8},{10,11... | collective-permute-start | bytes 2408456 | tf_op jit(solution)/shard_map/ppermute | solution.py:348
  22.1 1.4 %collective-permute-done.3.refs_0_ = s16[4,784,128]{2,1,0:T(8,128)(2,1)S(1)} collective-permute-done((s16[4,784,128]{2,1,0:T(8,128)(2,1)S(1)}, s16[4,784,128]{2,1,0:T(8,128)(2,1)S(1)}, u32[]{:S(2)}, u32[]{:S(2)}) %collective-permute-start.3) | collective-permute-done | bytes 802848 | tf_op jit(solution)/shard_map/ppermute | solution.py:348
  23.5 0.2 shard_map.87
  23.6 0.1 collective-permute-start.8
  23.7 0.4 shard_map.85
  24.1 2.1 %collective-permute-start.5 = (s16[1,784,128]{2,1,0:T(8,128)(2,1)S(1)}, s16[1,784,128]{2,1,0:T(8,128)(2,1)S(1)}, u32[]{:S(2)}, u32[]{:S(2)}) collective-permute-start(s16[1,784,128]{2,1,0:T(8,128)(2,1)S(1)} %get-tuple-element.19), channel_id=1, source_target_pairs={{0,2},{1,3},{2,0},{3,1},{4,6},{5,7},{6,4},{7,5},{8,10},{9,11},{10,... | collective-permute-start | bytes 602120 | tf_op jit(solution)/shard_map/ppermute | solution.py:348
  26.2 0.1 collective-permute-start.7
  26.3 5.2 %collective-permute-done.8.refs_1_ = s16[1,784,128]{2,1,0:T(8,128)(2,1)S(1)} collective-permute-done((s16[1,784,128]{2,1,0:T(8,128)(2,1)S(1)}, s16[1,784,128]{2,1,0:T(8,128)(2,1)S(1)}, u32[]{:S(2)}, u32[]{:S(2)}) %collective-permute-start.8) | collective-permute-done | bytes 200736 | tf_op jit(solution)/shard_map/ppermute | solution.py:348
  31.5 0.2 shard_map.88
  31.7 0.1 collective-permute-start.9
  31.8 0.1 collective-permute-start.4
  31.9 3.9 %collective-permute-done.5.refs_1_ = s16[1,784,128]{2,1,0:T(8,128)(2,1)S(1)} collective-permute-done((s16[1,784,128]{2,1,0:T(8,128)(2,1)S(1)}, s16[1,784,128]{2,1,0:T(8,128)(2,1)S(1)}, u32[]{:S(2)}, u32[]{:S(2)}) %collective-permute-start.5) | collective-permute-done | bytes 200736 | tf_op jit(solution)/shard_map/ppermute | solution.py:348
  35.8 0.2 shard_map.86
  36.0 0.1 collective-permute-start.6
  36.1 4.0 %collective-permute-done.7.refs_1_ = s16[1,784,128]{2,1,0:T(8,128)(2,1)S(1)} collective-permute-done((s16[1,784,128]{2,1,0:T(8,128)(2,1)S(1)}, s16[1,784,128]{2,1,0:T(8,128)(2,1)S(1)}, u32[]{:S(2)}, u32[]{:S(2)}) %collective-permute-start.7) | collective-permute-done | bytes 200736 | tf_op jit(solution)/shard_map/ppermute | solution.py:348
  40.1 0.3 shard_map.89
  40.4 0.1 collective-permute-start.10
  40.5 3.2 %collective-permute-done.4.refs_1_ = s16[1,784,128]{2,1,0:T(8,128)(2,1)S(1)} collective-permute-done((s16[1,784,128]{2,1,0:T(8,128)(2,1)S(1)}, s16[1,784,128]{2,1,0:T(8,128)(2,1)S(1)}, u32[]{:S(2)}, u32[]{:S(2)}) %collective-permute-start.4) | collective-permute-done | bytes 200736 | tf_op jit(solution)/shard_map/ppermute | solution.py:348
  43.6 7.4 %collective-permute-done.10.refs_3_ = s16[1,784,128]{2,1,0:T(8,128)(2,1)S(1)} collective-permute-done((s16[1,784,128]{2,1,0:T(8,128)(2,1)S(1)}, s16[1,784,128]{2,1,0:T(8,128)(2,1)S(1)}, u32[]{:S(2)}, u32[]{:S(2)}) %collective-permute-start.10) | collective-permute-done | bytes 200736 | tf_op jit(solution)/shard_map/ppermute | solution.py:348
  51.1 1.9 %shard_map.90 = f32[16,120,128]{2,1,0:T(8,128)} custom-call(s32[8]{0:T(128)S(1)} %copy-done.5, f32[8]{0:T(128)S(1)} %copy-done.6, f32[257,48,128]{2,1,0:T(8,128)S(1)} %get-tuple-element.16.acc, s16[4,784,128]{2,1,0:T(8,128)(2,1)S(1)} %collective-permute-done.2.refs_0_, s16[1,784,128]{2,1,0:T(8,128)(2,1)S(1)} %collective-permute-done.4.refs_1_, ...), custom_call_target="tpu_custom_call" | custom-call | flops 983040 | bytes 1572864 | tf_op jit(solution)/shard_map/pallas_call | solution.py:322
  (14 shorter events, 0.0 us)
Async XLA Ops:
  0.7 18.3 %collective-permute-start.1 = (bf16[1,48,128]{2,1,0:T(8,128)(2,1)S(1)}, bf16[1,48,128]{2,1,0:T(8,128)(2,1)S(1)}, u32[]{:S(2)}, u32[]{:S(2)}) collective-permute-start(bf16[1,48,128]{2,1,0:T(8,128)(2,1)S(1)} %get-tuple-element.21), channel_id=1, source_target_pairs={{1,0},{2,1},{3,2},{4,3},{5,4},{6,5},{7,6},{8,7},{9,8},{10,9},{11,1... | collective-permute-start | bytes 36872 | tf_op jit(solution)/shard_map/ppermute | solution.py:343
  6.2 12.9 %collective-permute-start = (bf16[1,48,128]{2,1,0:T(8,128)(2,1)S(1)}, bf16[1,48,128]{2,1,0:T(8,128)(2,1)S(1)}, u32[]{:S(2)}, u32[]{:S(2)}) collective-permute-start(bf16[1,48,128]{2,1,0:T(8,128)(2,1)S(1)} %get-tuple-element.22), channel_id=1, source_target_pairs={{0,1},{1,2},{2,3},{3,4},{4,5},{5,6},{6,7},{7,8},{8,9},{9,10},{10,1... | collective-permute-start | bytes 36872 | tf_op jit(solution)/shard_map/ppermute | solution.py:342
  6.8 2.2 %copy-start = (bf16[128,128,128]{2,1,0:T(8,128)(2,1)S(1)}, bf16[128,128,128]{2,1,0:T(8,128)(2,1)}, u32[]{:S(2)}) copy-start(bf16[128,128,128]{2,1,0:T(8,128)(2,1)} %w_hbm.1) | copy-start | bytes 12582916
  9.0 0.9 %copy-start.1 = (bf16[16,48,128]{2,1,0:T(8,128)(2,1)S(1)}, bf16[16,48,128]{2,1,0:T(8,128)(2,1)}, u32[]{:S(2)}) copy-start(bf16[16,48,128]{2,1,0:T(8,128)(2,1)} %cot_hbm.1) | copy-start | bytes 589828
  9.9 0.7 %copy-start.2 = (s32[1,128]{1,0:T(1,128)S(1)}, s32[1,128]{1,0:T(1,128)}, u32[]{:S(2)}) copy-start(s32[1,128]{1,0:T(1,128)} %tb_hbm.1) | copy-start | bytes 1540
  10.6 0.7 %copy-start.3 = (s32[1,128]{1,0:T(1,128)S(1)}, s32[1,128]{1,0:T(1,128)}, u32[]{:S(2)}) copy-start(s32[1,128]{1,0:T(1,128)} %dest_hbm.1) | copy-start | bytes 1540
  11.3 0.7 %copy-start.4 = (s32[1,128]{1,0:T(1,128)S(1)}, s32[1,128]{1,0:T(1,128)}, u32[]{:S(2)}) copy-start(s32[1,128]{1,0:T(1,128)} %src_hbm.1) | copy-start | bytes 1540
  21.1 2.4 %collective-permute-start.3 = (s16[4,784,128]{2,1,0:T(8,128)(2,1)S(1)}, s16[4,784,128]{2,1,0:T(8,128)(2,1)S(1)}, u32[]{:S(2)}, u32[]{:S(2)}) collective-permute-start(s16[4,784,128]{2,1,0:T(8,128)(2,1)S(1)} %get-tuple-element.17), channel_id=1, source_target_pairs={{0,1},{1,0},{2,3},{3,2},{4,5},{5,4},{6,7},{7,6},{8,9},{9,8},{10,11... | collective-permute-start | bytes 2408456 | tf_op jit(solution)/shard_map/ppermute | solution.py:348
  21.5 4.7 %collective-permute-start.2 = (s16[4,784,128]{2,1,0:T(8,128)(2,1)S(1)}, s16[4,784,128]{2,1,0:T(8,128)(2,1)S(1)}, u32[]{:S(2)}, u32[]{:S(2)}) collective-permute-start(s16[4,784,128]{2,1,0:T(8,128)(2,1)S(1)} %shard_map.84), channel_id=1, source_target_pairs={{0,1},{1,0},{2,3},{3,2},{4,5},{5,4},{6,7},{7,6},{8,9},{9,8},{10,11... | collective-permute-start | bytes 2408456 | tf_op jit(solution)/shard_map/ppermute | solution.py:348
  23.6 7.9 %collective-permute-start.8 = (s16[1,784,128]{2,1,0:T(8,128)(2,1)S(1)}, s16[1,784,128]{2,1,0:T(8,128)(2,1)S(1)}, u32[]{:S(2)}, u32[]{:S(2)}) collective-permute-start(s16[1,784,128]{2,1,0:T(8,128)(2,1)S(1)} %shard_map.87), channel_id=1, source_target_pairs={{0,2},{1,3},{2,0},{3,1},{4,6},{5,7},{6,4},{7,5},{8,10},{9,11},{10,... | collective-permute-start | bytes 602120 | tf_op jit(solution)/shard_map/ppermute | solution.py:348
  24.1 11.7 %collective-permute-start.5 = (s16[1,784,128]{2,1,0:T(8,128)(2,1)S(1)}, s16[1,784,128]{2,1,0:T(8,128)(2,1)S(1)}, u32[]{:S(2)}, u32[]{:S(2)}) collective-permute-start(s16[1,784,128]{2,1,0:T(8,128)(2,1)S(1)} %get-tuple-element.19), channel_id=1, source_target_pairs={{0,2},{1,3},{2,0},{3,1},{4,6},{5,7},{6,4},{7,5},{8,10},{9,11},{10,... | collective-permute-start | bytes 602120 | tf_op jit(solution)/shard_map/ppermute | solution.py:348
  26.2 13.9 %collective-permute-start.7 = (s16[1,784,128]{2,1,0:T(8,128)(2,1)S(1)}, s16[1,784,128]{2,1,0:T(8,128)(2,1)S(1)}, u32[]{:S(2)}, u32[]{:S(2)}) collective-permute-start(s16[1,784,128]{2,1,0:T(8,128)(2,1)S(1)} %get-tuple-element.20), channel_id=1, source_target_pairs={{0,2},{1,3},{2,0},{3,1},{4,6},{5,7},{6,4},{7,5},{8,10},{9,11},{10,... | collective-permute-start | bytes 602120 | tf_op jit(solution)/shard_map/ppermute | solution.py:348
  31.7 8.4 %collective-permute-start.9 = (s16[1,784,128]{2,1,0:T(8,128)(2,1)S(1)}, s16[1,784,128]{2,1,0:T(8,128)(2,1)S(1)}, u32[]{:S(2)}, u32[]{:S(2)}) collective-permute-start(s16[1,784,128]{2,1,0:T(8,128)(2,1)S(1)} %shard_map.88), channel_id=1, source_target_pairs={{0,4},{1,5},{2,6},{3,7},{4,0},{5,1},{6,2},{7,3},{8,12},{9,13},{10,... | collective-permute-start | bytes 602120 | tf_op jit(solution)/shard_map/ppermute | solution.py:348
  31.8 19.3 %copy-start.5 = (s32[8]{0:T(128)S(1)}, s32[8]{0:T(128)}, u32[]{:S(2)}) copy-start(s32[8]{0:T(128)} %index_ref.1) | copy-start | bytes 100
  31.8 19.2 %copy-start.6 = (f32[8]{0:T(128)S(1)}, f32[8]{0:T(128)}, u32[]{:S(2)}) copy-start(f32[8]{0:T(128)} %frac_ref.1) | copy-start | bytes 100
  31.8 11.8 %collective-permute-start.4 = (s16[1,784,128]{2,1,0:T(8,128)(2,1)S(1)}, s16[1,784,128]{2,1,0:T(8,128)(2,1)S(1)}, u32[]{:S(2)}, u32[]{:S(2)}) collective-permute-start(s16[1,784,128]{2,1,0:T(8,128)(2,1)S(1)} %get-tuple-element.18), channel_id=1, source_target_pairs={{0,2},{1,3},{2,0},{3,1},{4,6},{5,7},{6,4},{7,5},{8,10},{9,11},{10,... | collective-permute-start | bytes 602120 | tf_op jit(solution)/shard_map/ppermute | solution.py:348
  36.0 7.6 %collective-permute-start.6 = (s16[1,784,128]{2,1,0:T(8,128)(2,1)S(1)}, s16[1,784,128]{2,1,0:T(8,128)(2,1)S(1)}, u32[]{:S(2)}, u32[]{:S(2)}) collective-permute-start(s16[1,784,128]{2,1,0:T(8,128)(2,1)S(1)} %shard_map.86), channel_id=1, source_target_pairs={{0,4},{1,5},{2,6},{3,7},{4,0},{5,1},{6,2},{7,3},{8,12},{9,13},{10,... | collective-permute-start | bytes 602120 | tf_op jit(solution)/shard_map/ppermute | solution.py:348
  40.4 10.7 %collective-permute-start.10 = (s16[1,784,128]{2,1,0:T(8,128)(2,1)S(1)}, s16[1,784,128]{2,1,0:T(8,128)(2,1)S(1)}, u32[]{:S(2)}, u32[]{:S(2)}) collective-permute-start(s16[1,784,128]{2,1,0:T(8,128)(2,1)S(1)} %shard_map.89), channel_id=1, source_target_pairs={{0,8},{1,9},{2,10},{3,11},{4,12},{5,13},{6,14},{7,15},{8,0},{9,1},... | collective-permute-start | bytes 602120 | tf_op jit(solution)/shard_map/ppermute | solution.py:348

commit v3 on v2

--- a/solution.py
+++ b/solution.py
@@ -41,17 +41,43 @@
 TRASH = 16 * SB
 
 
-def add_products(first, entry_of, bin_of, left_of, w, acc, wide):
-    found = []
-    for i in range(wide):
-        e = entry_of(first + i)
-        found.append(jnp.dot(left_of(first + i), w[e], preferred_element_type=jnp.float32))
-    for i in range(wide):
-        at = bin_of(first + i)
-        acc[at] = acc[at] + found[i]
-
-
-def products_kernel(
+def add_products(entries, w, acc):
+    found = [jnp.dot(left, w[e], preferred_element_type=jnp.float32) for e, left, _ in entries]
+    for (_, _, at), value in zip(entries, found):
+        acc[at] = acc[at] + value
+
+
+def add_group(g, count, me, tables, cot, w, acc, ends):
+    blocks = cot.shape[0]
+
+    @pl.loop(0, GROUP // 8)
+    def _(part):
+        n = ends[3, 0]
+        entries = []
+        for i in range(8):
+            k = g * GROUP + part * 8 + i
+            block = tables[0, k]
+            rel = tables[1, k] ^ me
+            slot = (rel & 1) * 8 + ((rel >> 1) & 1) * 4 + (rel >> 2)
+            live = k < count
+            at = jnp.where(live, slot * SB + tables[2, k], TRASH)
+            outer = (block == 0) | (block == blocks + 1)
+            ends[0, n] = k
+            ends[1, n] = at
+            ends[2, n] = jnp.where(block == 0, 0, 1)
+            n = n + (outer & live).astype(jnp.int32)
+            left = cot[jnp.clip(block - 1, 0, blocks - 1)]
+            entries.append((k, left, jnp.where(outer, TRASH, at)))
+        ends[3, 0] = n
+        add_products(entries, w, acc)
+
+
+def first_half(count):
+    used = (count + GROUP - 1) // GROUP
+    return used, (used + 1) // 2
+
+
+def first_kernel(
     count_ref,
     me_ref,
     tb_hbm,
@@ -61,32 +87,25 @@
     w_hbm,
     acc,
     w,
+    cot,
+    low,
+    high,
+    tables,
     ends,
-    cot,
-    tb,
-    dest,
-    src,
-    bins,
     sems,
     w_sems,
 ):
-    entries, blocks = w.shape[0], cot.shape[0]
-    groups = entries // GROUP
+    groups = w.shape[0] // GROUP
     count = count_ref[0]
-    me = me_ref[0]
-    used = (count + GROUP - 1) // GROUP
+    used, half = first_half(count)
 
     def w_copy(g):
-        return pltpu.make_async_copy(
-            w_hbm.at[pl.ds(g * GROUP, GROUP)], w.at[pl.ds(g * GROUP, GROUP)], w_sems.at[g]
-        )
-
-    small = [
-        pltpu.make_async_copy(a, b, sems.at[i])
-        for i, (a, b) in enumerate(
-            ((tb_hbm, tb), (dest_hbm, dest), (src_hbm, src), (cot_hbm, cot))
-        )
-    ]
+        part = pl.ds(g * GROUP, GROUP)
+        return pltpu.make_async_copy(w_hbm.at[part], w.at[part], w_sems.at[g])
+
+    pairs = [(cot_hbm, cot)]
+    pairs += [(t, tables.at[pl.ds(i, 1)]) for i, t in enumerate((tb_hbm, dest_hbm, src_hbm))]
+    small = [pltpu.make_async_copy(a, b, sems.at[i]) for i, (a, b) in enumerate(pairs)]
     for copy in small:
         copy.start()
     for g in range(groups):
@@ -100,80 +119,99 @@
         acc[b] = jnp.zeros(acc.shape[1:], jnp.float32)
 
     acc[TRASH] = jnp.zeros(acc.shape[1:], jnp.float32)
+    ends[3, 0] = 0
 
     for copy in small:
         copy.wait()
-
-    @pl.loop(0, entries, init_carry=jnp.int32(0), unroll=4)
-    def listed(k, n):
-        rel = dest[0, k] ^ me
-        slot = (rel & 1) * 8 + ((rel >> 1) & 1) * 4 + (rel >> 2)
-        live = k < count
-        at = jnp.where(live, slot * SB + src[0, k], TRASH)
-        block = tb[0, k]
-        outer = (block == 0) | (block == blocks + 1)
-        bins[k] = jnp.where(outer, TRASH, at)
-        tb[0, k] = jnp.clip(block - 1, 0, blocks - 1)
-        ends[0, n] = k
-        ends[1, n] = at
-        ends[2, n] = jnp.where(block == 0, 0, 1)
-        return n + (outer & live).astype(jnp.int32)
-
+    low[0] = cot[0]
+    high[0] = cot[cot.shape[0] - 1]
+
+    for g in range(groups):
+
+        @pl.when(g < used)
+        def _():
+            w_copy(g).wait()
+
+        @pl.when(g < half)
+        def _():
+            add_group(g, count, me_ref[0], tables, cot, w, acc, ends)
+
+
+def in_hbm(x):
+    return pltpu.with_memory_space_constraint(x, pltpu.HBM)
+
+
+def products_first(tables, count, me, cotangent, weight):
+    entries, cells_in, cells = weight.shape
+    smem = pl.BlockSpec(memory_space=pltpu.SMEM)
+    vmem = pl.BlockSpec(memory_space=pltpu.VMEM)
+    hbm = pl.BlockSpec(memory_space=pltpu.HBM)
+    end = jax.ShapeDtypeStruct((1,) + cotangent.shape[1:], cotangent.dtype)
+    return pl.pallas_call(
+        first_kernel,
+        out_shape=(
+            jax.ShapeDtypeStruct((TRASH + 1, ROWS, cells), jnp.float32),
+            jax.ShapeDtypeStruct(weight.shape, weight.dtype),
+            jax.ShapeDtypeStruct(cotangent.shape, cotangent.dtype),
+            end,
+            end,
+            jax.ShapeDtypeStruct((3, entries), jnp.int32),
+            jax.ShapeDtypeStruct((4, entries + 4), jnp.int32),
+        ),
+        in_specs=[smem, smem] + [hbm] * 5,
+        out_specs=(vmem,) * 5 + (smem, smem),
+        scratch_shapes=[
+            pltpu.SemaphoreType.DMA((4,)),
+            pltpu.SemaphoreType.DMA((entries // GROUP,)),
+        ],
+        compiler_params=pltpu.CompilerParams(vmem_limit_bytes=24 * MIB),
+        cost_estimate=pl.CostEstimate(
+            flops=entries * ROWS * cells_in * cells, bytes_accessed=12 * MIB, transcendentals=0
+        ),
+    )(count, me, *[in_hbm(t) for t in tables], in_hbm(cotangent), in_hbm(weight))
+
+
+def second_kernel(count_ref, me_ref, tables, begun, cot, w, acc_in, acc, ends):
+    count = count_ref[0]
+    used, half = first_half(count)
+    listed = begun[3, 0]
+
+    @pl.loop(0, listed)
+    def _(n):
+        for i in range(3):
+            ends[i, n] = begun[i, n]
+
+    ends[3, 0] = listed
+
+    @pl.loop(half, used)
+    def _(g):
+        add_group(g, count, me_ref[0], tables, cot, w, acc, ends)
+
+    listed = ends[3, 0]
     for i in range(4):
         ends[0, listed + i] = 0
         ends[1, listed + i] = TRASH
         ends[2, listed + i] = 0
-    ends[3, 0] = listed
-
-    for g in range(groups):
-
-        @pl.when(g < used)
-        def _():
-            w_copy(g).wait()
-
-            @pl.loop(0, GROUP // 8)
-            def _(part):
-                add_products(
-                    g * GROUP + part * 8,
-                    lambda k: k,
-                    lambda k: bins[k],
-                    lambda k: cot[tb[0, k]],
-                    w,
-                    acc,
-                    8,
-                )
-
-
-def products(tables, count, me, cotangent, weight):
-    entries, cells_in, cells = weight.shape
+
+
+def products_second(tables, count, me, begun, cot, w, acc):
+    entries, cells_in, cells = w.shape
     smem = pl.BlockSpec(memory_space=pltpu.SMEM)
     vmem = pl.BlockSpec(memory_space=pltpu.VMEM)
-    hbm = pl.BlockSpec(memory_space=pltpu.HBM)
-    return pl.pallas_call(
-        products_kernel,
+    return pl.pallas_call(
+        second_kernel,
         out_shape=(
-            jax.ShapeDtypeStruct((TRASH + 1, ROWS, cells), jnp.float32),
-            jax.ShapeDtypeStruct(weight.shape, jnp.bfloat16),
-            jax.ShapeDtypeStruct((4, entries + 4), jnp.int32),
-        ),
-        in_specs=[smem, smem] + [hbm] * 5,
-        out_specs=(vmem, vmem, smem),
-        scratch_shapes=[
-            pltpu.VMEM(cotangent.shape, jnp.bfloat16),
-            pltpu.SMEM((1, entries), jnp.int32),
-            pltpu.SMEM((1, entries), jnp.int32),
-            pltpu.SMEM((1, entries), jnp.int32),
-            pltpu.SMEM((entries,), jnp.int32),
-            pltpu.SemaphoreType.DMA((4,)),
-            pltpu.SemaphoreType.DMA((entries // GROUP,)),
-        ],
-        compiler_params=pltpu.CompilerParams(vmem_limit_bytes=24 * MIB),
-        cost_estimate=pl.CostEstimate(
-            flops=2 * entries * ROWS * cells_in * cells,
-            bytes_accessed=12 * MIB,
-            transcendentals=0,
-        ),
-    )(count, me, *tables, cotangent, weight)
+            jax.ShapeDtypeStruct(acc.shape, acc.dtype),
+            jax.ShapeDtypeStruct(begun.shape, begun.dtype),
+        ),
+        in_specs=[smem] * 4 + [vmem] * 3,
+        out_specs=(vmem, smem),
+        input_output_aliases={6: 0},
+        compiler_params=pltpu.CompilerParams(vmem_limit_bytes=32 * MIB),
+        cost_estimate=pl.CostEstimate(
+            flops=entries * ROWS * cells_in * cells, bytes_accessed=12 * MIB, transcendentals=0
+        ),
+    )(count, me, tables, begun, cot, w, acc)
 
 
 def code_slot(acc, slot, coded, exps, out_ref, out_slot):
@@ -195,15 +233,8 @@
 
     @pl.loop(0, (ends[3, 0] + 3) // 4)
     def _(part):
-        add_products(
-            part * 4,
-            lambda k: ends[0, k],
-            lambda k: ends[1, k],
-            lambda k: sides[ends[2, k]],
-            w,
-            acc,
-            4,
-        )
+        at = [part * 4 + i for i in range(4)]
+        add_products([(ends[0, k], sides[ends[2, k]], ends[1, k]) for k in at], w, acc)
 
     @pl.loop(0, 4)
     def _(i):
@@ -234,22 +265,20 @@
     )(ends, before, after, w, acc)
 
 
-def code_kernel(slots, takes, acc, *refs):
-    arrays = refs[: len(refs) - len(slots) - 1]
-    outs, exps = refs[len(arrays) : -1], refs[-1]
-    for slot, pairs, out in zip(slots, takes, outs):
-        coded = [(arrays[a], i, scales(arrays[a], i)) for a, i in pairs]
-        code_slot(acc, slot, coded, exps, out, 0)
-
-
-def code(acc, slots, takes, arrays):
+def code_kernel(slot, takes, acc, *refs):
+    arrays, out, exps = refs[:-2], refs[-2], refs[-1]
+    coded = [(arrays[a], i, scales(arrays[a], i)) for a, i in takes]
+    code_slot(acc, slot, coded, exps, out, 0)
+
+
+def code(acc, slot, takes, arrays):
     cells = acc.shape[2]
     vmem = pl.BlockSpec(memory_space=pltpu.VMEM)
     return pl.pallas_call(
-        functools.partial(code_kernel, slots, takes),
-        out_shape=tuple(jax.ShapeDtypeStruct((1, CODED, cells), jnp.int16) for _ in slots),
+        functools.partial(code_kernel, slot, takes),
+        out_shape=jax.ShapeDtypeStruct((1, CODED, cells), jnp.int16),
         in_specs=[vmem] * (1 + len(arrays)),
-        out_specs=(vmem,) * len(slots),
+        out_specs=vmem,
         scratch_shapes=[pltpu.VMEM((SB, cells), jnp.float32)],
         compiler_params=pltpu.CompilerParams(vmem_limit_bytes=32 * MIB),
         cost_estimate=pl.CostEstimate(
@@ -335,13 +364,10 @@
     )(lev_index, lev_frac, acc, *arrays)
 
 
-def ring_ends(cotangent, peers):
+def ring_ends(low, high, peers):
     up = [(i, (i + 1) % peers) for i in range(peers)]
     down = [(j, i) for i, j in up]
-    return (
-        lax.ppermute(cotangent[-1:], "tile", up),
-        lax.ppermute(cotangent[:1], "tile", down),
-    )
+    return lax.ppermute(high, "tile", up), lax.ppermute(low, "tile", down)
 
 
 def swap(value, bits, peers):
@@ -351,21 +377,22 @@
 def staged(cotangent, weight, target_block, dest, source, count, lev_index, lev_frac):
     peers = 16
     me = lax.axis_index("tile").astype(jnp.int32).reshape(1)
-    before, after = ring_ends(cotangent, peers)
-    acc, w, ends = products((target_block, dest, source), count, me, cotangent, weight)
+    acc, w, cot, low, high, tables, ends = products_first(
+        (target_block, dest, source), count, me, cotangent, weight
+    )
+    before, after = ring_ends(low, high, peers)
+    acc, ends = products_second(tables, count, me, ends, cot, w, acc)
     acc, far = add_ends(ends, before, after, w, acc)
     far = swap(far, 1, peers)
     near = swap(code_near(acc), 1, peers)
-    (y3,) = code(acc, (7,), (((0, 3),),), (far,))
-    y3 = swap(y3, 2, peers)
-    y2, y1, y0 = code(acc, (6, 5, 4), (((0, 2),), ((0, 1),), ((0, 0),)), (far,))
-    y2, y1, y0 = (swap(v, 2, peers) for v in (y2, y1, y0))
-    (a3,) = code(acc, (3,), (((0, 3), (1, 0)),), (near, y3))
-    a3 = swap(a3, 4, peers)
-    (b2,) = code(acc, (2,), (((0, 2), (1, 0), (2, 0)),), (near, y2, a3))
-    b2 = swap(b2, 8, peers)
-    (a1,) = code(acc, (1,), (((0, 1), (1, 0)),), (near, y1))
-    a1 = swap(a1, 4, peers)
+    y3 = swap(code(acc, 7, ((0, 3),), (far,)), 2, peers)
+    o1 = swap(code(acc, 5, ((0, 1),), (far,)), 4, peers)
+    y2 = swap(code(acc, 6, ((0, 2),), (far, y3)), 2, peers)
+    a3 = swap(code(acc, 3, ((0, 3), (1, 0)), (near, y3)), 4, peers)
+    b2_own = code(acc, 2, ((0, 2), (1, 0), (2, 0)), (near, y2, a3))
+    b2 = swap(b2_own, 8, peers)
+    y0 = swap(code(acc, 4, ((0, 0), (1, 0)), (far, o1, y2)), 2, peers)
+    a1 = swap(code(acc, 1, ((0, 1),), (near, b2_own)), 4, peers)
     return finish(
         lev_index, lev_frac, acc, ((0, 0), (1, 0), (2, 0), (3, 0)), (near, y0, a1, b2)
     )
@@ -383,7 +410,7 @@
     entries, _, cells = weight.shape
     capacity = max(2, 2 * entries // peers)
     slots = peers * capacity
-    before, after = ring_ends(cotangent, peers)
+    before, after = ring_ends(cotangent[:1], cotangent[-1:], peers)
     window = jnp.concatenate([before, cotangent, after], axis=0)
     contrib = jnp.einsum(
         "ofp,ops->ofs", window[target_block[0]], weight, preferred_element_type=jnp.float32

time: 53.3 us -> 46.3 us (0.87)
  local copies, waits for them, and re-layouts: 5.81 us -> 0.01 us
  waiting for transfers between devices: 25.1 us -> 21.3 us
  starting transfers between devices: 8.59 us -> 11.3 us
    unnamed x14 -> x4, local copies, waits for them, and re-layouts: 5.09 us -> 0.01 us
    ppermute x9, waiting for transfers between devices: 25.1 us -> 21.3 us  [swap(): return lax.ppermute(value, 'tile', [(i, i ^ bits) for i in range(peers)])]
    ppermute x9, starting transfers between devices: 3.14 us -> 5.79 us  [swap(): return lax.ppermute(value, 'tile', [(i, i ^ bits) for i in range(peers)])]
    slice x1 -> x0, local copies, waits for them, and re-layouts: 0.73 us -> none  [ring_ends(): cotangent[:1]]
    pallas_call x6 -> x9, Pallas kernels: 8.36 us -> 8.6 us  [the longest x1 4.19 us: products_first(): pl.pallas_call(first_kernel, out_shape=(jax.ShapeDtypeStruct((TRASH + 1,...]
  transfers between devices with their start and end apart: 11 -> 11, of which waited for: 6 -> 6; matrix products, arithmetic and copies ran while one was open for 0% -> 0% of each run, Pallas kernels for 16% -> 10%
where the time goes in v3:
time: 46.3 us; the launch traced here: 46.1 us
  waiting for transfers between devices  21.3 us (46%)
  Pallas kernels  12.6 us (27%)
  starting transfers between devices  11.3 us (24%)
  between operations  0.79 us (2%)
    ppermute x9, waiting for transfers between devices, swap(): return lax.ppermute(value, 'tile', [(i, i ^ bits) for i in range(peers)])  21.3 us
    ppermute x9, starting transfers between devices, swap(): return lax.ppermute(value, 'tile', [(i, i ^ bits) for i in range(peers)])  5.79 us
    ppermute x2, starting transfers between devices, ring_ends(): return (lax.ppermute(high, 'tile', up), lax.ppermute(low, 'tile', down))  5.55 us
    pallas_call x1, Pallas kernels, products_first(): pl.pallas_call(first_kernel, out_shape=(jax.ShapeDtypeStruct((TRASH + 1,...  4.19 us
    pallas_call x1, Pallas kernels, products_second(): pl.pallas_call(second_kernel, out_shape=(jax.ShapeDtypeStruct(acc.shape,...  3.11 us
    pallas_call x1, Pallas kernels, finish(): pl.pallas_call(functools.partial(finish_kernel, takes), out_shape=result,...  1.91 us
    pallas_call x1, Pallas kernels, add_ends(): pl.pallas_call(ends_kernel, out_shape=(jax.ShapeDtypeStruct(acc.shape, jn...  1.69 us
    pallas_call x7, Pallas kernels, code(): pl.pallas_call(functools.partial(code_kernel, slot, takes), out_shape=jax...  1.29 us
  transfers between devices with their start and end apart: 11, of which 6 were waited for; matrix products, arithmetic and copies ran while one was open for 0% of the time, Pallas kernels for 10%

profile of v3, /device:TPU:0, one launch (start us, length us, event | category | flops | bytes accessed | tf_op | source)
XLA Modules:
  0.0 46.1 jit_solution(873232422629316242)
XLA Ops:
  0.7 4.2 %shard_map.82 = (f32[257,48,128]{2,1,0:T(8,128)S(1)}, bf16[128,128,128]{2,1,0:T(8,128)(2,1)S(1)}, bf16[16,48,128]{2,1,0:T(8,128)(2,1)S(1)}, bf16[1,48,128]{2,1,0...) custom-call(s32[1]{0:T(128)S(6)} %copy.13.count_ref, ...), custom_call_target="tpu_custom_call" | custom-call | flops 100663296 | bytes 12582912 | tf_op jit(solution)/shard_map/pallas_call | solution.py:150
  4.9 0.1 collective-permute-start
  4.9 5.5 %collective-permute-start.1 = (bf16[1,48,128]{2,1,0:T(8,128)(2,1)S(1)}, bf16[1,48,128]{2,1,0:T(8,128)(2,1)S(1)}, u32[]{:S(2)}, u32[]{:S(2)}) collective-permute-start(bf16[1,48,128]{2,1,0:T(8,128)(2,1)S(1)} %get-tuple-element.23), channel_id=1, source_target_pairs={{1,0},{2,1},{3,2},{4,3},{5,4},{6,5},{7,6},{8,7},{9,8},{10,9},{11,1... | collective-permute-start | bytes 36872 | tf_op jit(solution)/shard_map/ppermute | solution.py:370
  10.4 3.1 %shard_map.83 = (f32[257,48,128]{2,1,0:T(8,128)S(1)}, s32[4,132]{1,0:T(4,128)S(1)}) custom-call(s32[1]{0:T(128)S(6)} %copy.13.count_ref, s32[1]{0:T(128)} %bitcast.me_ref, s32[3,128]{1,0:T(4,128)S(1)} %get-tuple-element.16.tables, s32[4,132]{1,0:T(4,128)S(1)} %get-tuple-element.17.begun, ...), custom_call_target="tpu_custom_call", output_to_operand_aliasing={{0}: (6, {})} | custom-call | flops 100663296 | bytes 12582912 | tf_op jit(solution)/shard_map/pallas_call | solution.py:201
  13.5 0.0 collective-permute-done.1.after
  13.6 1.7 %shard_map.84 = (f32[257,48,128]{2,1,0:T(8,128)S(1)}, s16[4,784,128]{2,1,0:T(8,128)(2,1)S(1)}) custom-call(s32[4,132]{1,0:T(4,128)S(1)} %get-tuple-element.21.ends, bf16[1,48,128]{2,1,0:T(8,128)(2,1)S(1)} %collective-permute-done.before, bf16[1,48,128]{2,1,0:T(8,128)(2,1)S(1)} %collective-permute-done.1.after, ...), custom_call_target="tpu_custom_call", output_to_operand_aliasing={{0}: (4, {})} | custom-call | flops 983040 | bytes 786432 | tf_op jit(solution)/shard_map/pallas_call | solution.py:248
  15.3 0.1 collective-permute-start.3
  15.3 0.4 shard_map.85
  15.7 0.6 %collective-permute-start.2 = (s16[4,784,128]{2,1,0:T(8,128)(2,1)S(1)}, s16[4,784,128]{2,1,0:T(8,128)(2,1)S(1)}, u32[]{:S(2)}, u32[]{:S(2)}) collective-permute-start(s16[4,784,128]{2,1,0:T(8,128)(2,1)S(1)} %shard_map.85), channel_id=1, source_target_pairs={{0,1},{1,0},{2,3},{3,2},{4,5},{5,4},{6,7},{7,6},{8,9},{9,8},{10,11... | collective-permute-start | bytes 2408456 | tf_op jit(solution)/shard_map/ppermute | solution.py:374
  16.3 1.4 %collective-permute-done.3.refs_0_ = s16[4,784,128]{2,1,0:T(8,128)(2,1)S(1)} collective-permute-done((s16[4,784,128]{2,1,0:T(8,128)(2,1)S(1)}, s16[4,784,128]{2,1,0:T(8,128)(2,1)S(1)}, u32[]{:S(2)}, u32[]{:S(2)}) %collective-permute-start.3) | collective-permute-done | bytes 802848 | tf_op jit(solution)/shard_map/ppermute | solution.py:374
  17.6 0.2 shard_map.87
  17.8 0.1 collective-permute-start.5
  17.9 0.2 shard_map.86
  18.0 0.1 collective-permute-start.4
  18.1 6.8 %collective-permute-done.5.refs_1_ = s16[1,784,128]{2,1,0:T(8,128)(2,1)S(1)} collective-permute-done((s16[1,784,128]{2,1,0:T(8,128)(2,1)S(1)}, s16[1,784,128]{2,1,0:T(8,128)(2,1)S(1)}, u32[]{:S(2)}, u32[]{:S(2)}) %collective-permute-start.5) | collective-permute-done | bytes 200736 | tf_op jit(solution)/shard_map/ppermute | solution.py:374
  24.9 0.2 shard_map.88
  25.0 0.4 collective-permute-start.6
  25.4 0.2 shard_map.90
  25.6 0.1 collective-permute-start.8
  25.7 5.6 %collective-permute-done.6.refs_2_.refs_1_ = s16[1,784,128]{2,1,0:T(8,128)(2,1)S(1)} collective-permute-done((s16[1,784,128]{2,1,0:T(8,128)(2,1)S(1)}, s16[1,784,128]{2,1,0:T(8,128)(2,1)S(1)}, u32[]{:S(2)}, u32[]{:S(2)}) %collective-permute-start.6) | collective-permute-done | bytes 200736 | tf_op jit(solution)/shard_map/ppermute | solution.py:374
  31.3 0.2 shard_map.89
  31.5 0.0 copy-start
  31.5 0.0 copy-start.1
  31.5 0.7 %collective-permute-start.7 = (s16[1,784,128]{2,1,0:T(8,128)(2,1)S(1)}, s16[1,784,128]{2,1,0:T(8,128)(2,1)S(1)}, u32[]{:S(2)}, u32[]{:S(2)}) collective-permute-start(s16[1,784,128]{2,1,0:T(8,128)(2,1)S(1)} %shard_map.89), channel_id=1, source_target_pairs={{0,2},{1,3},{2,0},{3,1},{4,6},{5,7},{6,4},{7,5},{8,10},{9,11},{10,... | collective-permute-start | bytes 602120 | tf_op jit(solution)/shard_map/ppermute | solution.py:374
  32.2 0.3 shard_map.91.refs_1_
  32.5 0.2 shard_map.92
  32.6 0.1 collective-permute-start.9
  32.7 3.9 %collective-permute-start.10 = (s16[1,784,128]{2,1,0:T(8,128)(2,1)S(1)}, s16[1,784,128]{2,1,0:T(8,128)(2,1)S(1)}, u32[]{:S(2)}, u32[]{:S(2)}) collective-permute-start(s16[1,784,128]{2,1,0:T(8,128)(2,1)S(1)} %shard_map.91.refs_1_), channel_id=1, source_target_pairs={{0,8},{1,9},{2,10},{3,11},{4,12},{5,13},{6,14},{7,15},{8,0},{9,1},... | collective-permute-start | bytes 602120 | tf_op jit(solution)/shard_map/ppermute | solution.py:374
  36.6 0.7 %collective-permute-done.7.refs_1_ = s16[1,784,128]{2,1,0:T(8,128)(2,1)S(1)} collective-permute-done((s16[1,784,128]{2,1,0:T(8,128)(2,1)S(1)}, s16[1,784,128]{2,1,0:T(8,128)(2,1)S(1)}, u32[]{:S(2)}, u32[]{:S(2)}) %collective-permute-start.7) | collective-permute-done | bytes 200736 | tf_op jit(solution)/shard_map/ppermute | solution.py:374
  37.3 4.7 %collective-permute-done.9.refs_2_ = s16[1,784,128]{2,1,0:T(8,128)(2,1)S(1)} collective-permute-done((s16[1,784,128]{2,1,0:T(8,128)(2,1)S(1)}, s16[1,784,128]{2,1,0:T(8,128)(2,1)S(1)}, u32[]{:S(2)}, u32[]{:S(2)}) %collective-permute-start.9) | collective-permute-done | bytes 200736 | tf_op jit(solution)/shard_map/ppermute | solution.py:374
  42.0 2.1 %collective-permute-done.10.refs_3_ = s16[1,784,128]{2,1,0:T(8,128)(2,1)S(1)} collective-permute-done((s16[1,784,128]{2,1,0:T(8,128)(2,1)S(1)}, s16[1,784,128]{2,1,0:T(8,128)(2,1)S(1)}, u32[]{:S(2)}, u32[]{:S(2)}) %collective-permute-start.10) | collective-permute-done | bytes 200736 | tf_op jit(solution)/shard_map/ppermute | solution.py:374
  44.2 1.9 %shard_map.93 = f32[16,120,128]{2,1,0:T(8,128)} custom-call(s32[8]{0:T(128)S(1)} %copy-done, f32[8]{0:T(128)S(1)} %copy-done.1, f32[257,48,128]{2,1,0:T(8,128)S(1)} %get-tuple-element.25.acc, s16[4,784,128]{2,1,0:T(8,128)(2,1)S(1)} %collective-permute-done.2.refs_0_, s16[1,784,128]{2,1,0:T(8,128)(2,1)S(1)} %collective-permute-done.7.refs_1_, ...), custom_call_target="tpu_custom_call" | custom-call | flops 983040 | bytes 1572864 | tf_op jit(solution)/shard_map/pallas_call | solution.py:351
  (6 shorter events, 0.0 us)
Async XLA Ops:
  4.9 8.7 %collective-permute-start = (bf16[1,48,128]{2,1,0:T(8,128)(2,1)S(1)}, bf16[1,48,128]{2,1,0:T(8,128)(2,1)S(1)}, u32[]{:S(2)}, u32[]{:S(2)}) collective-permute-start(bf16[1,48,128]{2,1,0:T(8,128)(2,1)S(1)} %get-tuple-element.22), channel_id=1, source_target_pairs={{0,1},{1,2},{2,3},{3,4},{4,5},{5,6},{6,7},{7,8},{8,9},{9,10},{10,1... | collective-permute-start | bytes 36872 | tf_op jit(solution)/shard_map/ppermute | solution.py:370
  4.9 8.6 %collective-permute-start.1 = (bf16[1,48,128]{2,1,0:T(8,128)(2,1)S(1)}, bf16[1,48,128]{2,1,0:T(8,128)(2,1)S(1)}, u32[]{:S(2)}, u32[]{:S(2)}) collective-permute-start(bf16[1,48,128]{2,1,0:T(8,128)(2,1)S(1)} %get-tuple-element.23), channel_id=1, source_target_pairs={{1,0},{2,1},{3,2},{4,3},{5,4},{6,5},{7,6},{8,7},{9,8},{10,9},{11,1... | collective-permute-start | bytes 36872 | tf_op jit(solution)/shard_map/ppermute | solution.py:370
  15.3 2.4 %collective-permute-start.3 = (s16[4,784,128]{2,1,0:T(8,128)(2,1)S(1)}, s16[4,784,128]{2,1,0:T(8,128)(2,1)S(1)}, u32[]{:S(2)}, u32[]{:S(2)}) collective-permute-start(s16[4,784,128]{2,1,0:T(8,128)(2,1)S(1)} %get-tuple-element.26), channel_id=1, source_target_pairs={{0,1},{1,0},{2,3},{3,2},{4,5},{5,4},{6,7},{7,6},{8,9},{9,8},{10,11... | collective-permute-start | bytes 2408456 | tf_op jit(solution)/shard_map/ppermute | solution.py:374
  15.7 9.7 %collective-permute-start.2 = (s16[4,784,128]{2,1,0:T(8,128)(2,1)S(1)}, s16[4,784,128]{2,1,0:T(8,128)(2,1)S(1)}, u32[]{:S(2)}, u32[]{:S(2)}) collective-permute-start(s16[4,784,128]{2,1,0:T(8,128)(2,1)S(1)} %shard_map.85), channel_id=1, source_target_pairs={{0,1},{1,0},{2,3},{3,2},{4,5},{5,4},{6,7},{7,6},{8,9},{9,8},{10,11... | collective-permute-start | bytes 2408456 | tf_op jit(solution)/shard_map/ppermute | solution.py:374
  17.8 7.1 %collective-permute-start.5 = (s16[1,784,128]{2,1,0:T(8,128)(2,1)S(1)}, s16[1,784,128]{2,1,0:T(8,128)(2,1)S(1)}, u32[]{:S(2)}, u32[]{:S(2)}) collective-permute-start(s16[1,784,128]{2,1,0:T(8,128)(2,1)S(1)} %shard_map.87), channel_id=1, source_target_pairs={{0,2},{1,3},{2,0},{3,1},{4,6},{5,7},{6,4},{7,5},{8,10},{9,11},{10,... | collective-permute-start | bytes 602120 | tf_op jit(solution)/shard_map/ppermute | solution.py:374
  18.0 7.7 %collective-permute-start.4 = (s16[1,784,128]{2,1,0:T(8,128)(2,1)S(1)}, s16[1,784,128]{2,1,0:T(8,128)(2,1)S(1)}, u32[]{:S(2)}, u32[]{:S(2)}) collective-permute-start(s16[1,784,128]{2,1,0:T(8,128)(2,1)S(1)} %shard_map.86), channel_id=1, source_target_pairs={{0,4},{1,5},{2,6},{3,7},{4,0},{5,1},{6,2},{7,3},{8,12},{9,13},{10,... | collective-permute-start | bytes 602120 | tf_op jit(solution)/shard_map/ppermute | solution.py:374
  25.0 6.3 %collective-permute-start.6 = (s16[1,784,128]{2,1,0:T(8,128)(2,1)S(1)}, s16[1,784,128]{2,1,0:T(8,128)(2,1)S(1)}, u32[]{:S(2)}, u32[]{:S(2)}) collective-permute-start(s16[1,784,128]{2,1,0:T(8,128)(2,1)S(1)} %shard_map.88), channel_id=1, source_target_pairs={{0,2},{1,3},{2,0},{3,1},{4,6},{5,7},{6,4},{7,5},{8,10},{9,11},{10,... | collective-permute-start | bytes 602120 | tf_op jit(solution)/shard_map/ppermute | solution.py:374
  25.6 6.6 %collective-permute-start.8 = (s16[1,784,128]{2,1,0:T(8,128)(2,1)S(1)}, s16[1,784,128]{2,1,0:T(8,128)(2,1)S(1)}, u32[]{:S(2)}, u32[]{:S(2)}) collective-permute-start(s16[1,784,128]{2,1,0:T(8,128)(2,1)S(1)} %shard_map.90), channel_id=1, source_target_pairs={{0,4},{1,5},{2,6},{3,7},{4,0},{5,1},{6,2},{7,3},{8,12},{9,13},{10,... | collective-permute-start | bytes 602120 | tf_op jit(solution)/shard_map/ppermute | solution.py:374
  31.5 12.6 %copy-start = (s32[8]{0:T(128)S(1)}, s32[8]{0:T(128)}, u32[]{:S(2)}) copy-start(s32[8]{0:T(128)} %index_ref.1) | copy-start | bytes 100
  31.5 12.6 %copy-start.1 = (f32[8]{0:T(128)S(1)}, f32[8]{0:T(128)}, u32[]{:S(2)}) copy-start(f32[8]{0:T(128)} %frac_ref.1) | copy-start | bytes 100
  31.5 5.8 %collective-permute-start.7 = (s16[1,784,128]{2,1,0:T(8,128)(2,1)S(1)}, s16[1,784,128]{2,1,0:T(8,128)(2,1)S(1)}, u32[]{:S(2)}, u32[]{:S(2)}) collective-permute-start(s16[1,784,128]{2,1,0:T(8,128)(2,1)S(1)} %shard_map.89), channel_id=1, source_target_pairs={{0,2},{1,3},{2,0},{3,1},{4,6},{5,7},{6,4},{7,5},{8,10},{9,11},{10,... | collective-permute-start | bytes 602120 | tf_op jit(solution)/shard_map/ppermute | solution.py:374
  32.6 9.4 %collective-permute-start.9 = (s16[1,784,128]{2,1,0:T(8,128)(2,1)S(1)}, s16[1,784,128]{2,1,0:T(8,128)(2,1)S(1)}, u32[]{:S(2)}, u32[]{:S(2)}) collective-permute-start(s16[1,784,128]{2,1,0:T(8,128)(2,1)S(1)} %shard_map.92), channel_id=1, source_target_pairs={{0,4},{1,5},{2,6},{3,7},{4,0},{5,1},{6,2},{7,3},{8,12},{9,13},{10,... | collective-permute-start | bytes 602120 | tf_op jit(solution)/shard_map/ppermute | solution.py:374
  32.7 11.4 %collective-permute-start.10 = (s16[1,784,128]{2,1,0:T(8,128)(2,1)S(1)}, s16[1,784,128]{2,1,0:T(8,128)(2,1)S(1)}, u32[]{:S(2)}, u32[]{:S(2)}) collective-permute-start(s16[1,784,128]{2,1,0:T(8,128)(2,1)S(1)} %shard_map.91.refs_1_), channel_id=1, source_target_pairs={{0,8},{1,9},{2,10},{3,11},{4,12},{5,13},{6,14},{7,15},{8,0},{9,1},... | collective-permute-start | bytes 602120 | tf_op jit(solution)/shard_map/ppermute | solution.py:374

commit v4 on v3

--- a/solution.py
+++ b/solution.py
@@ -12,21 +12,23 @@
 LEVT = 8
 SB = 16
 ROWS = VARS * LEVT
-BODY = SB * ROWS
-CODED = BODY + SB
+HALF = SB // 2
+BODY = HALF * ROWS
+CODED = BODY + 16
 GROUP = 16
 MIB = 1 << 20
 
 
 def encode(read, write, exps):
-    for b in range(SB):
+    exps[HALF:, :] = jnp.zeros((16 - HALF, exps.shape[1]), jnp.float32)
+    for b in range(HALF):
         x = read(b)
         top = jnp.max(jnp.abs(x), axis=0, keepdims=True)
         e = jnp.ceil(jnp.log2(jnp.maximum(top, 1e-30)) + 0.001) - 15.0
         exps[b : b + 1, :] = e
         q = jnp.round(x * jnp.exp2(-e))
         write(b * ROWS, ROWS, q.astype(jnp.int32).astype(jnp.int16))
-    write(BODY, SB, exps[...].astype(jnp.int32).astype(jnp.int16))
+    write(BODY, 16, exps[...].astype(jnp.int32).astype(jnp.int16))
 
 
 def scales(ref, i):
@@ -214,15 +216,15 @@
     )(count, me, tables, begun, cot, w, acc)
 
 
-def code_slot(acc, slot, coded, exps, out_ref, out_slot):
+def code_half(acc, unit, coded, exps, out_ref, at):
     def read(b):
-        total = acc[slot * SB + b]
+        total = acc[unit * HALF + b]
         for r, i, s in coded:
             total = total + decode(r, i, s, b)
         return total
 
     def write(row, rows, value):
-        out_ref[out_slot, row : row + rows, :] = value
+        out_ref[at, row : row + rows, :] = value
 
     encode(read, write, exps)
 
@@ -236,9 +238,9 @@
         at = [part * 4 + i for i in range(4)]
         add_products([(ends[0, k], sides[ends[2, k]], ends[1, k]) for k in at], w, acc)
 
-    @pl.loop(0, 4)
+    @pl.loop(0, 8)
     def _(i):
-        code_slot(acc, 12 + i, [], exps, far_ref, i)
+        code_half(acc, 24 + i, [], exps, far_ref, i)
 
 
 def add_ends(ends, before, after, w, acc):
@@ -249,13 +251,13 @@
         ends_kernel,
         out_shape=(
             jax.ShapeDtypeStruct(acc.shape, jnp.float32),
-            jax.ShapeDtypeStruct((4, CODED, cells), jnp.int16),
+            jax.ShapeDtypeStruct((8, CODED, cells), jnp.int16),
         ),
         in_specs=[smem] + [vmem] * 4,
         out_specs=(vmem, vmem),
         scratch_shapes=[
             pltpu.VMEM((2,) + before.shape[1:], jnp.bfloat16),
-            pltpu.VMEM((SB, cells), jnp.float32),
+            pltpu.VMEM((16, cells), jnp.float32),
         ],
         input_output_aliases={4: 0},
         compiler_params=pltpu.CompilerParams(vmem_limit_bytes=32 * MIB),
@@ -265,52 +267,55 @@
     )(ends, before, after, w, acc)
 
 
-def code_kernel(slot, takes, acc, *refs):
-    arrays, out, exps = refs[:-2], refs[-2], refs[-1]
-    coded = [(arrays[a], i, scales(arrays[a], i)) for a, i in takes]
-    code_slot(acc, slot, coded, exps, out, 0)
-
-
-def code(acc, slot, takes, arrays):
+def code_kernel(jobs, acc, *refs):
+    arrays, outs, exps = refs[: -1 - len(jobs)], refs[-1 - len(jobs) : -1], refs[-1]
+    for parts, out in zip(jobs, outs):
+        for at, (unit, takes) in enumerate(parts):
+            coded = [(arrays[a], i, scales(arrays[a], i)) for a, i in takes]
+            code_half(acc, unit, coded, exps, out, at)
+
+
+def code(acc, jobs, arrays):
     cells = acc.shape[2]
     vmem = pl.BlockSpec(memory_space=pltpu.VMEM)
     return pl.pallas_call(
-        functools.partial(code_kernel, slot, takes),
-        out_shape=jax.ShapeDtypeStruct((1, CODED, cells), jnp.int16),
+        functools.partial(code_kernel, jobs),
+        out_shape=tuple(
+            jax.ShapeDtypeStruct((len(parts), CODED, cells), jnp.int16) for parts in jobs
+        ),
         in_specs=[vmem] * (1 + len(arrays)),
+        out_specs=(vmem,) * len(jobs),
+        scratch_shapes=[pltpu.VMEM((16, cells), jnp.float32)],
+        compiler_params=pltpu.CompilerParams(vmem_limit_bytes=32 * MIB),
+        cost_estimate=pl.CostEstimate(
+            flops=10 * BODY * cells, bytes_accessed=8 * BODY * cells, transcendentals=0
+        ),
+    )(acc, *arrays)
+
+
+def code_near_kernel(acc, after, near_ref, exps):
+    @pl.loop(0, 8)
+    def _(i):
+        code_half(acc, 16 + i, [], exps, near_ref, i)
+
+
+def code_near(acc, after):
+    cells = acc.shape[2]
+    vmem = pl.BlockSpec(memory_space=pltpu.VMEM)
+    return pl.pallas_call(
+        code_near_kernel,
+        out_shape=jax.ShapeDtypeStruct((8, CODED, cells), jnp.int16),
+        in_specs=[vmem, vmem],
         out_specs=vmem,
-        scratch_shapes=[pltpu.VMEM((SB, cells), jnp.float32)],
+        scratch_shapes=[pltpu.VMEM((16, cells), jnp.float32)],
         compiler_params=pltpu.CompilerParams(vmem_limit_bytes=32 * MIB),
         cost_estimate=pl.CostEstimate(
             flops=10 * BODY * cells, bytes_accessed=8 * BODY * cells, transcendentals=0
         ),
-    )(acc, *arrays)
-
-
-def code_near_kernel(acc, near_ref, exps):
-    @pl.loop(0, 4)
-    def _(i):
-        code_slot(acc, 8 + i, [], exps, near_ref, i)
-
-
-def code_near(acc):
-    cells = acc.shape[2]
-    vmem = pl.BlockSpec(memory_space=pltpu.VMEM)
-    return pl.pallas_call(
-        code_near_kernel,
-        out_shape=jax.ShapeDtypeStruct((4, CODED, cells), jnp.int16),
-        in_specs=[vmem],
-        out_specs=vmem,
-        scratch_shapes=[pltpu.VMEM((SB, cells), jnp.float32)],
-        compiler_params=pltpu.CompilerParams(vmem_limit_bytes=32 * MIB),
-        cost_estimate=pl.CostEstimate(
-            flops=10 * BODY * cells, bytes_accessed=8 * BODY * cells, transcendentals=0
-        ),
-    )(acc)
-
-
-def finish_kernel(takes, index_ref, frac_ref, acc, *refs):
-    arrays, out_hbm, out, sems = refs[:-3], refs[-3], refs[-2], refs[-1]
+    )(acc, after)
+
+
+def lift_kernel(index_ref, frac_ref, after, left):
     high = VARS * LEV
     row = lax.broadcasted_iota(jnp.int32, (high, ROWS), 0)
     col = lax.broadcasted_iota(jnp.int32, (high, ROWS), 1)
@@ -323,45 +328,64 @@
     lift = jnp.where(row // LEV == col // LEVT, lift, 0.0)
     high_part = lift.astype(jnp.bfloat16)
     low_part = (lift - high_part.astype(jnp.float32)).astype(jnp.bfloat16)
-    left = jnp.concatenate([high_part, high_part, low_part, low_part], axis=1)
+    left[...] = jnp.concatenate([high_part, high_part, low_part, low_part], axis=1)
+
+
+def lift_matrix(lev_index, lev_frac, after):
+    smem = pl.BlockSpec(memory_space=pltpu.SMEM)
+    vmem = pl.BlockSpec(memory_space=pltpu.VMEM)
+    return pl.pallas_call(
+        lift_kernel,
+        out_shape=jax.ShapeDtypeStruct((VARS * LEV, 4 * ROWS), jnp.bfloat16),
+        in_specs=[smem, smem, vmem],
+        out_specs=vmem,
+    )(lev_index, lev_frac, after)
+
+
+def finish_kernel(half, takes, left, acc, *refs):
+    arrays, out_hbm, out, sems = refs[:-3], refs[-3], refs[-2], refs[-1]
     coded = [(arrays[a], i, scales(arrays[a], i)) for a, i in takes]
     copies = []
-    for b in range(SB):
-        total = acc[b]
+    for b in range(HALF):
+        total = acc[half * HALF + b]
         for r, i, s in coded:
             total = total + decode(r, i, s, b)
         first = total.astype(jnp.bfloat16)
         second = (total - first.astype(jnp.float32)).astype(jnp.bfloat16)
         right = jnp.concatenate([first, second, first, second], axis=0)
-        out[b] = jnp.dot(left, right, preferred_element_type=jnp.float32)
+        out[b] = jnp.dot(left[...], right, preferred_element_type=jnp.float32)
         if b % 4 == 3:
-            part = pl.ds(b - 3, 4)
-            copy = pltpu.make_async_copy(out.at[part], out_hbm.at[part], sems.at[b // 4])
+            copy = pltpu.make_async_copy(
+                out.at[pl.ds(b - 3, 4)],
+                out_hbm.at[pl.ds(half * HALF + b - 3, 4)],
+                sems.at[b // 4],
+            )
             copy.start()
             copies.append(copy)
     for copy in copies:
         copy.wait()
 
 
-def finish(lev_index, lev_frac, acc, takes, arrays):
+def finish(half, left, acc, takes, arrays, begun=None):
     cells = acc.shape[2]
-    smem = pl.BlockSpec(memory_space=pltpu.SMEM)
-    vmem = pl.BlockSpec(memory_space=pltpu.VMEM)
-    result = jax.ShapeDtypeStruct((SB, VARS * LEV, cells), jnp.float32)
-    return pl.pallas_call(
-        functools.partial(finish_kernel, takes),
-        out_shape=result,
-        in_specs=[smem, smem] + [vmem] * (1 + len(arrays)),
-        out_specs=pl.BlockSpec(memory_space=pltpu.HBM),
+    vmem = pl.BlockSpec(memory_space=pltpu.VMEM)
+    hbm = pl.BlockSpec(memory_space=pltpu.HBM)
+    extra = () if begun is None else (begun,)
+    return pl.pallas_call(
+        functools.partial(finish_kernel, half, takes),
+        out_shape=jax.ShapeDtypeStruct((SB, VARS * LEV, cells), jnp.float32),
+        in_specs=[vmem] * (2 + len(arrays)) + [hbm] * len(extra),
+        out_specs=hbm,
         scratch_shapes=[
-            pltpu.VMEM(result.shape, jnp.float32),
-            pltpu.SemaphoreType.DMA((SB // 4,)),
+            pltpu.VMEM((HALF, VARS * LEV, cells), jnp.float32),
+            pltpu.SemaphoreType.DMA((HALF // 4,)),
         ],
+        input_output_aliases={2 + len(arrays): 0} if extra else {},
         compiler_params=pltpu.CompilerParams(vmem_limit_bytes=32 * MIB),
         cost_estimate=pl.CostEstimate(
             flops=10 * BODY * cells, bytes_accessed=16 * BODY * cells, transcendentals=0
         ),
-    )(lev_index, lev_frac, acc, *arrays)
+    )(left, acc, *arrays, *extra)
 
 
 def ring_ends(low, high, peers):
@@ -384,18 +408,27 @@
     acc, ends = products_second(tables, count, me, ends, cot, w, acc)
     acc, far = add_ends(ends, before, after, w, acc)
     far = swap(far, 1, peers)
-    near = swap(code_near(acc), 1, peers)
-    y3 = swap(code(acc, 7, ((0, 3),), (far,)), 2, peers)
-    o1 = swap(code(acc, 5, ((0, 1),), (far,)), 4, peers)
-    y2 = swap(code(acc, 6, ((0, 2),), (far, y3)), 2, peers)
-    a3 = swap(code(acc, 3, ((0, 3), (1, 0)), (near, y3)), 4, peers)
-    b2_own = code(acc, 2, ((0, 2), (1, 0), (2, 0)), (near, y2, a3))
-    b2 = swap(b2_own, 8, peers)
-    y0 = swap(code(acc, 4, ((0, 0), (1, 0)), (far, o1, y2)), 2, peers)
-    a1 = swap(code(acc, 1, ((0, 1),), (near, b2_own)), 4, peers)
-    return finish(
-        lev_index, lev_frac, acc, ((0, 0), (1, 0), (2, 0), (3, 0)), (near, y0, a1, b2)
-    )
+    y3 = code(acc, (((14, ((0, 6),)),), ((15, ((0, 7),)),)), (far,))
+    (o1_own,) = code(acc, (((10, ((0, 2),)), (11, ((0, 3),))),), (far, y3[0]))
+    y2 = code(acc, (((12, ((0, 4),)),), ((13, ((0, 5),)),)), (far, o1_own))
+    near = code_near(acc, y2[0])
+    y3 = [swap(v, 2, peers) for v in y3]
+    o1 = swap(o1_own, 4, peers)
+    y2 = [swap(v, 2, peers) for v in y2]
+    near = swap(near, 1, peers)
+    (a3_low,) = code(acc, (((6, ((0, 6), (1, 0))),),), (near, y3[0]))
+    (a3_high,) = code(acc, (((7, ((0, 7), (1, 0))),),), (near, y3[1], a3_low))
+    a3 = [swap(a3_low, 4, peers), swap(a3_high, 4, peers)]
+    (a1_own,) = code(acc, (((2, ((0, 2),)), (3, ((0, 3),))),), (near, a3_high))
+    a1 = swap(a1_own, 4, peers)
+    (y0_own,) = code(acc, (((8, ((0, 0), (1, 0))), (9, ((0, 1), (1, 1)))),), (far, o1, a1_own))
+    y0 = swap(y0_own, 2, peers)
+    (b2_low,) = code(acc, (((4, ((0, 4), (1, 0), (2, 0))),),), (near, y2[0], a3[0], y0_own))
+    (b2_high,) = code(acc, (((5, ((0, 5), (1, 0), (2, 0))),),), (near, y2[1], a3[1], b2_low))
+    b2 = [swap(b2_low, 8, peers), swap(b2_high, 8, peers)]
+    left = lift_matrix(lev_index, lev_frac, b2_high)
+    out = finish(0, left, acc, ((0, 0), (1, 0), (2, 0), (3, 0)), (near, y0, a1, b2[0]))
+    return finish(1, left, acc, ((0, 1), (1, 1), (2, 1), (3, 0)), (near, y0, a1, b2[1]), out)
 
 
 def vertical_matrix(lev_index, lev_frac, levels):

time: 46.3 us -> 45.6 us (0.985)
  waiting for transfers between devices: 21.3 us -> 6.18 us
  starting transfers between devices: 11.3 us -> 19.9 us
  local copies, waits for them, and re-layouts: 0.01 us -> 3.63 us
  Pallas kernels: 12.6 us -> 14.7 us
    ppermute x9 -> x13, waiting for transfers between devices: 21.3 us -> 6.18 us  [swap(): return lax.ppermute(value, 'tile', [(i, i ^ bits) for i in range(peers)])]
    ppermute x9 -> x13, starting transfers between devices: 5.79 us -> 14.3 us  [swap(): return lax.ppermute(value, 'tile', [(i, i ^ bits) for i in range(peers)])]
    unnamed x4 -> x8, local copies, waits for them, and re-layouts: 0.01 us -> 3.63 us
    pallas_call x9 -> x13, Pallas kernels: 3.58 us -> 5.6 us  [the longest x2 2.11 us: finish(): pl.pallas_call(functools.partial(finish_kernel, half, takes), out_shape=j...]
  transfers between devices with their start and end apart: 11 -> 15, of which waited for: 6 -> 3; matrix products, arithmetic and copies ran while one was open for 0% -> 0% of each run, Pallas kernels for 10% -> 15%
where the time goes in v4:
time: 45.6 us; the launch traced here: 45.2 us
  starting transfers between devices  19.9 us (44%)
  Pallas kernels  14.7 us (32%)
  waiting for transfers between devices  6.18 us (14%)
  local copies, waits for them, and re-layouts  3.63 us (8%)
  between operations  0.8 us (2%)
    ppermute x13, starting transfers between devices, swap(): return lax.ppermute(value, 'tile', [(i, i ^ bits) for i in range(peers)])  14.3 us
    ppermute x13, waiting for transfers between devices, swap(): return lax.ppermute(value, 'tile', [(i, i ^ bits) for i in range(peers)])  6.18 us
    ppermute x2, starting transfers between devices, ring_ends(): return (lax.ppermute(high, 'tile', up), lax.ppermute(low, 'tile', down))  5.56 us
    pallas_call x1, Pallas kernels, products_first(): pl.pallas_call(first_kernel, out_shape=(jax.ShapeDtypeStruct((TRASH + 1,...  4.19 us
    unnamed x8, local copies, waits for them, and re-layouts  3.63 us
    pallas_call x1, Pallas kernels, products_second(): pl.pallas_call(second_kernel, out_shape=(jax.ShapeDtypeStruct(acc.shape,...  3.13 us
    pallas_call x2, Pallas kernels, finish(): pl.pallas_call(functools.partial(finish_kernel, half, takes), out_shape=j...  2.11 us
    pallas_call x1, Pallas kernels, lift_matrix(): pl.pallas_call(lift_kernel, out_shape=jax.ShapeDtypeStruct((VARS * LEV, 4...  1.74 us
  transfers between devices with their start and end apart: 15, of which 3 were waited for; matrix products, arithmetic and copies ran while one was open for 0% of the time, Pallas kernels for 15%

profile of v4, /device:TPU:0, one launch (start us, length us, event | category | flops | bytes accessed | tf_op | source)
XLA Modules:
  0.0 45.2 jit_solution(18158038729533417345)
XLA Ops:
  0.7 4.2 %shard_map.82 = (f32[257,48,128]{2,1,0:T(8,128)S(1)}, bf16[128,128,128]{2,1,0:T(8,128)(2,1)S(1)}, bf16[16,48,128]{2,1,0:T(8,128)(2,1)S(1)}, bf16[1,48,128]{2,1,0...) custom-call(s32[1]{0:T(128)S(6)} %copy.15.count_ref, ...), custom_call_target="tpu_custom_call" | custom-call | flops 100663296 | bytes 12582912 | tf_op jit(solution)/shard_map/pallas_call | solution.py:152
  4.9 5.5 %collective-permute-start.1 = (bf16[1,48,128]{2,1,0:T(8,128)(2,1)S(1)}, bf16[1,48,128]{2,1,0:T(8,128)(2,1)S(1)}, u32[]{:S(2)}, u32[]{:S(2)}) collective-permute-start(bf16[1,48,128]{2,1,0:T(8,128)(2,1)S(1)} %get-tuple-element.27), channel_id=1, source_target_pairs={{1,0},{2,1},{3,2},{4,3},{5,4},{6,5},{7,6},{8,7},{9,8},{10,9},{11,1... | collective-permute-start | bytes 36872 | tf_op jit(solution)/shard_map/ppermute | solution.py:394
  10.4 3.1 %shard_map.83 = (f32[257,48,128]{2,1,0:T(8,128)S(1)}, s32[4,132]{1,0:T(4,128)S(1)}) custom-call(s32[1]{0:T(128)S(6)} %copy.15.count_ref, s32[1]{0:T(128)} %bitcast.me_ref, s32[3,128]{1,0:T(4,128)S(1)} %get-tuple-element.20.tables, s32[4,132]{1,0:T(4,128)S(1)} %get-tuple-element.21.begun, ...), custom_call_target="tpu_custom_call", output_to_operand_aliasing={{0}: (6, {})} | custom-call | flops 100663296 | bytes 12582912 | tf_op jit(solution)/shard_map/pallas_call | solution.py:203
  13.6 1.7 %shard_map.84 = (f32[257,48,128]{2,1,0:T(8,128)S(1)}, s16[8,400,128]{2,1,0:T(8,128)(2,1)S(1)}) custom-call(s32[4,132]{1,0:T(4,128)S(1)} %get-tuple-element.25.ends, bf16[1,48,128]{2,1,0:T(8,128)(2,1)S(1)} %collective-permute-done.before, bf16[1,48,128]{2,1,0:T(8,128)(2,1)S(1)} %collective-permute-done.1.after, ...), custom_call_target="tpu_custom_call", output_to_operand_aliasing={{0}: (4, {})} | custom-call | flops 491520 | bytes 393216 | tf_op jit(solution)/shard_map/pallas_call | solution.py:250
  15.4 2.3 %collective-permute-done.2.refs_0_ = s16[8,400,128]{2,1,0:T(8,128)(2,1)S(1)} collective-permute-done((s16[8,400,128]{2,1,0:T(8,128)(2,1)S(1)}, s16[8,400,128]{2,1,0:T(8,128)(2,1)S(1)}, u32[]{:S(2)}, u32[]{:S(2)}) %collective-permute-start.2) | collective-permute-done | bytes 819232 | tf_op jit(solution)/shard_map/ppermute | solution.py:398
  17.7 0.2 shard_map.85
  17.9 0.2 shard_map.86.refs_1_
  18.0 0.2 shard_map.87
  18.2 0.4 shard_map.88
  18.6 0.2 collective-permute-start.3
  18.8 0.2 collective-permute-start.6
  19.0 1.9 %collective-permute-start.5 = (s16[1,400,128]{2,1,0:T(8,128)(2,1)S(1)}, s16[1,400,128]{2,1,0:T(8,128)(2,1)S(1)}, u32[]{:S(2)}, u32[]{:S(2)}) collective-permute-start(s16[1,400,128]{2,1,0:T(8,128)(2,1)S(1)} %get-tuple-element.34), channel_id=1, source_target_pairs={{0,2},{1,3},{2,0},{3,1},{4,6},{5,7},{6,4},{7,5},{8,10},{9,11},{10,... | collective-permute-start | bytes 307208 | tf_op jit(solution)/shard_map/ppermute | solution.py:398
  20.9 0.2 collective-permute-start.8
  21.0 3.5 %collective-permute-done.6.refs_1_ = s16[1,400,128]{2,1,0:T(8,128)(2,1)S(1)} collective-permute-done((s16[1,400,128]{2,1,0:T(8,128)(2,1)S(1)}, s16[1,400,128]{2,1,0:T(8,128)(2,1)S(1)}, u32[]{:S(2)}, u32[]{:S(2)}) %collective-permute-start.6) | collective-permute-done | bytes 102432 | tf_op jit(solution)/shard_map/ppermute | solution.py:398
  24.6 0.1 collective-permute-start.4
  24.7 0.1 shard_map.89.refs_2_
  24.8 2.0 %collective-permute-start.9 = (s16[1,400,128]{2,1,0:T(8,128)(2,1)S(1)}, s16[1,400,128]{2,1,0:T(8,128)(2,1)S(1)}, u32[]{:S(2)}, u32[]{:S(2)}) collective-permute-start(s16[1,400,128]{2,1,0:T(8,128)(2,1)S(1)} %shard_map.89.refs_2_), channel_id=1, source_target_pairs={{0,4},{1,5},{2,6},{3,7},{4,0},{5,1},{6,2},{7,3},{8,12},{9,13},{10,... | collective-permute-start | bytes 307208 | tf_op jit(solution)/shard_map/ppermute | solution.py:398
  26.8 0.1 shard_map.90.refs_1_
  26.9 2.1 %collective-permute-start.7 = (s16[1,400,128]{2,1,0:T(8,128)(2,1)S(1)}, s16[1,400,128]{2,1,0:T(8,128)(2,1)S(1)}, u32[]{:S(2)}, u32[]{:S(2)}) collective-permute-start(s16[1,400,128]{2,1,0:T(8,128)(2,1)S(1)} %shard_map.90.refs_1_), channel_id=1, source_target_pairs={{0,4},{1,5},{2,6},{3,7},{4,0},{5,1},{6,2},{7,3},{8,12},{9,13},{10,... | collective-permute-start | bytes 307208 | tf_op jit(solution)/shard_map/ppermute | solution.py:398
  29.0 0.2 shard_map.91.refs_2_
  29.2 0.2 shard_map.92.refs_3_
  29.5 2.0 %collective-permute-start.12 = (s16[2,400,128]{2,1,0:T(8,128)(2,1)S(1)}, s16[2,400,128]{2,1,0:T(8,128)(2,1)S(1)}, u32[]{:S(2)}, u32[]{:S(2)}) collective-permute-start(s16[2,400,128]{2,1,0:T(8,128)(2,1)S(1)} %shard_map.91.refs_2_), channel_id=1, source_target_pairs={{0,4},{1,5},{2,6},{3,7},{4,0},{5,1},{6,2},{7,3},{8,12},{9,13},{10,... | collective-permute-start | bytes 614408 | tf_op jit(solution)/shard_map/ppermute | solution.py:398
  31.5 0.1 shard_map.93.refs_3_
  31.6 3.5 %collective-permute-start.14 = (s16[1,400,128]{2,1,0:T(8,128)(2,1)S(1)}, s16[1,400,128]{2,1,0:T(8,128)(2,1)S(1)}, u32[]{:S(2)}, u32[]{:S(2)}) collective-permute-start(s16[1,400,128]{2,1,0:T(8,128)(2,1)S(1)} %shard_map.93.refs_3_), channel_id=1, source_target_pairs={{0,8},{1,9},{2,10},{3,11},{4,12},{5,13},{6,14},{7,15},{8,0},{9,1},... | collective-permute-start | bytes 307208 | tf_op jit(solution)/shard_map/ppermute | solution.py:398
  35.2 0.1 shard_map.94.after
  35.3 2.0 %collective-permute-start.13 = (s16[1,400,128]{2,1,0:T(8,128)(2,1)S(1)}, s16[1,400,128]{2,1,0:T(8,128)(2,1)S(1)}, u32[]{:S(2)}, u32[]{:S(2)}) collective-permute-start(s16[1,400,128]{2,1,0:T(8,128)(2,1)S(1)} %shard_map.94.after), channel_id=1, source_target_pairs={{0,8},{1,9},{2,10},{3,11},{4,12},{5,13},{6,14},{7,15},{8,0},{9,1},... | collective-permute-start | bytes 307208 | tf_op jit(solution)/shard_map/ppermute | solution.py:398
  37.4 1.7 %shard_map.95.left = bf16[120,192]{1,0:T(8,128)(2,1)} custom-call(s32[8]{0:T(128)} %index_ref.1, f32[8]{0:T(128)} %frac_ref.1, s16[1,400,128]{2,1,0:T(8,128)(2,1)} %copy-done.3), custom_call_target="tpu_custom_call" | custom-call | tf_op jit(solution)/shard_map/pallas_call | solution.py:337
  39.1 0.3 collective-permute-done.12.refs_2_
  39.4 2.8 %copy-done.1 = f32[257,48,128]{2,1,0:T(8,128)S(1)} copy-done((f32[257,48,128]{2,1,0:T(8,128)S(1)}, f32[257,48,128]{2,1,0:T(8,128)}, u32[]{:S(2)}) %copy-start.1) | copy-done | bytes 6316056
  42.2 0.8 %copy-done.2 = bf16[120,192]{1,0:T(8,128)(2,1)S(1)} copy-done((bf16[120,192]{1,0:T(8,128)(2,1)S(1)}, bf16[120,192]{1,0:T(8,128)(2,1)}, u32[]{:S(2)}) %copy-start.2) | copy-done | bytes 46104
  43.0 1.0 %shard_map.96.refs_4_ = f32[16,120,128]{2,1,0:T(8,128)} custom-call(bf16[120,192]{1,0:T(8,128)(2,1)S(1)} %copy-done.2, f32[257,48,128]{2,1,0:T(8,128)S(1)} %copy-done.1, s16[8,400,128]{2,1,0:T(8,128)(2,1)S(1)} %collective-permute-done.3.refs_0_, s16[2,400,128]{2,1,0:T(8,128)(2,1)S(1)} %collective-permute-done.11.refs_1_, ...), custom_call_target="tpu_custom_call" | custom-call | flops 491520 | bytes 786432 | tf_op jit(solution)/shard_map/pallas_call | solution.py:374
  44.1 1.1 %shard_map.97 = f32[16,120,128]{2,1,0:T(8,128)} custom-call(bf16[120,192]{1,0:T(8,128)(2,1)S(1)} %copy-done.2, f32[257,48,128]{2,1,0:T(8,128)S(1)} %copy-done.1, s16[8,400,128]{2,1,0:T(8,128)(2,1)S(1)} %collective-permute-done.3.refs_0_, s16[2,400,128]{2,1,0:T(8,128)(2,1)S(1)} %collective-permute-done.11.refs_1_, ...), custom_call_target="tpu_custom_call", output_to_operand_aliasing={{}: (6, {})} | custom-call | flops 491520 | bytes 786432 | tf_op jit(solution)/shard_map/pallas_call | solution.py:374
  (22 shorter events, 0.3 us)
Async XLA Ops:
  4.9 8.7 %collective-permute-start = (bf16[1,48,128]{2,1,0:T(8,128)(2,1)S(1)}, bf16[1,48,128]{2,1,0:T(8,128)(2,1)S(1)}, u32[]{:S(2)}, u32[]{:S(2)}) collective-permute-start(bf16[1,48,128]{2,1,0:T(8,128)(2,1)S(1)} %get-tuple-element.26), channel_id=1, source_target_pairs={{0,1},{1,2},{2,3},{3,4},{4,5},{5,6},{6,7},{7,8},{8,9},{9,10},{10,1... | collective-permute-start | bytes 36872 | tf_op jit(solution)/shard_map/ppermute | solution.py:394
  4.9 8.7 %collective-permute-start.1 = (bf16[1,48,128]{2,1,0:T(8,128)(2,1)S(1)}, bf16[1,48,128]{2,1,0:T(8,128)(2,1)S(1)}, u32[]{:S(2)}, u32[]{:S(2)}) collective-permute-start(bf16[1,48,128]{2,1,0:T(8,128)(2,1)S(1)} %get-tuple-element.27), channel_id=1, source_target_pairs={{1,0},{2,1},{3,2},{4,3},{5,4},{6,5},{7,6},{8,7},{9,8},{10,9},{11,1... | collective-permute-start | bytes 36872 | tf_op jit(solution)/shard_map/ppermute | solution.py:394
  15.3 19.8 %copy-start = (f32[257,48,128]{2,1,0:T(8,128)}, f32[257,48,128]{2,1,0:T(8,128)S(1)}, u32[]{:S(2)}) copy-start(f32[257,48,128]{2,1,0:T(8,128)S(1)} %get-tuple-element.29.acc) | copy-start | bytes 18948100
  15.3 2.4 %collective-permute-start.2 = (s16[8,400,128]{2,1,0:T(8,128)(2,1)S(1)}, s16[8,400,128]{2,1,0:T(8,128)(2,1)S(1)}, u32[]{:S(2)}, u32[]{:S(2)}) collective-permute-start(s16[8,400,128]{2,1,0:T(8,128)(2,1)S(1)} %get-tuple-element.30), channel_id=1, source_target_pairs={{0,1},{1,0},{2,3},{3,2},{4,5},{5,4},{6,7},{7,6},{8,9},{9,8},{10,11... | collective-permute-start | bytes 2457608 | tf_op jit(solution)/shard_map/ppermute | solution.py:398
  18.6 6.1 %collective-permute-start.3 = (s16[8,400,128]{2,1,0:T(8,128)(2,1)S(1)}, s16[8,400,128]{2,1,0:T(8,128)(2,1)S(1)}, u32[]{:S(2)}, u32[]{:S(2)}) collective-permute-start(s16[8,400,128]{2,1,0:T(8,128)(2,1)S(1)} %shard_map.88), channel_id=1, source_target_pairs={{0,1},{1,0},{2,3},{3,2},{4,5},{5,4},{6,7},{7,6},{8,9},{9,8},{10,11... | collective-permute-start | bytes 2457608 | tf_op jit(solution)/shard_map/ppermute | solution.py:398
  18.8 10.3 %collective-permute-start.10 = (s16[2,400,128]{2,1,0:T(8,128)(2,1)S(1)}, s16[2,400,128]{2,1,0:T(8,128)(2,1)S(1)}, u32[]{:S(2)}, u32[]{:S(2)}) collective-permute-start(s16[2,400,128]{2,1,0:T(8,128)(2,1)S(1)} %shard_map.86.refs_1_), channel_id=1, source_target_pairs={{0,4},{1,5},{2,6},{3,7},{4,0},{5,1},{6,2},{7,3},{8,12},{9,13},{10,... | collective-permute-start | bytes 614408 | tf_op jit(solution)/shard_map/ppermute | solution.py:398
  18.8 5.7 %collective-permute-start.6 = (s16[1,400,128]{2,1,0:T(8,128)(2,1)S(1)}, s16[1,400,128]{2,1,0:T(8,128)(2,1)S(1)}, u32[]{:S(2)}, u32[]{:S(2)}) collective-permute-start(s16[1,400,128]{2,1,0:T(8,128)(2,1)S(1)} %get-tuple-element.31.refs_1_), channel_id=1, source_target_pairs={{0,2},{1,3},{2,0},{3,1},{4,6},{5,7},{6,4},{7,5},{8,10},{9,11},{10,... | collective-permute-start | bytes 307208 | tf_op jit(solution)/shard_map/ppermute | solution.py:398
  19.0 7.8 %collective-permute-start.5 = (s16[1,400,128]{2,1,0:T(8,128)(2,1)S(1)}, s16[1,400,128]{2,1,0:T(8,128)(2,1)S(1)}, u32[]{:S(2)}, u32[]{:S(2)}) collective-permute-start(s16[1,400,128]{2,1,0:T(8,128)(2,1)S(1)} %get-tuple-element.34), channel_id=1, source_target_pairs={{0,2},{1,3},{2,0},{3,1},{4,6},{5,7},{6,4},{7,5},{8,10},{9,11},{10,... | collective-permute-start | bytes 307208 | tf_op jit(solution)/shard_map/ppermute | solution.py:398
  20.9 8.6 %collective-permute-start.8 = (s16[1,400,128]{2,1,0:T(8,128)(2,1)S(1)}, s16[1,400,128]{2,1,0:T(8,128)(2,1)S(1)}, u32[]{:S(2)}, u32[]{:S(2)}) collective-permute-start(s16[1,400,128]{2,1,0:T(8,128)(2,1)S(1)} %get-tuple-element.32.after), channel_id=1, source_target_pairs={{0,2},{1,3},{2,0},{3,1},{4,6},{5,7},{6,4},{7,5},{8,10},{9,11},{10,... | collective-permute-start | bytes 307208 | tf_op jit(solution)/shard_map/ppermute | solution.py:398
  24.6 10.6 %collective-permute-start.4 = (s16[1,400,128]{2,1,0:T(8,128)(2,1)S(1)}, s16[1,400,128]{2,1,0:T(8,128)(2,1)S(1)}, u32[]{:S(2)}, u32[]{:S(2)}) collective-permute-start(s16[1,400,128]{2,1,0:T(8,128)(2,1)S(1)} %get-tuple-element.33), channel_id=1, source_target_pairs={{0,2},{1,3},{2,0},{3,1},{4,6},{5,7},{6,4},{7,5},{8,10},{9,11},{10,... | collective-permute-start | bytes 307208 | tf_op jit(solution)/shard_map/ppermute | solution.py:398
  24.8 6.7 %collective-permute-start.9 = (s16[1,400,128]{2,1,0:T(8,128)(2,1)S(1)}, s16[1,400,128]{2,1,0:T(8,128)(2,1)S(1)}, u32[]{:S(2)}, u32[]{:S(2)}) collective-permute-start(s16[1,400,128]{2,1,0:T(8,128)(2,1)S(1)} %shard_map.89.refs_2_), channel_id=1, source_target_pairs={{0,4},{1,5},{2,6},{3,7},{4,0},{5,1},{6,2},{7,3},{8,12},{9,13},{10,... | collective-permute-start | bytes 307208 | tf_op jit(solution)/shard_map/ppermute | solution.py:398
  26.9 8.2 %collective-permute-start.7 = (s16[1,400,128]{2,1,0:T(8,128)(2,1)S(1)}, s16[1,400,128]{2,1,0:T(8,128)(2,1)S(1)}, u32[]{:S(2)}, u32[]{:S(2)}) collective-permute-start(s16[1,400,128]{2,1,0:T(8,128)(2,1)S(1)} %shard_map.90.refs_1_), channel_id=1, source_target_pairs={{0,4},{1,5},{2,6},{3,7},{4,0},{5,1},{6,2},{7,3},{8,12},{9,13},{10,... | collective-permute-start | bytes 307208 | tf_op jit(solution)/shard_map/ppermute | solution.py:398
  29.4 9.7 %collective-permute-start.11 = (s16[2,400,128]{2,1,0:T(8,128)(2,1)S(1)}, s16[2,400,128]{2,1,0:T(8,128)(2,1)S(1)}, u32[]{:S(2)}, u32[]{:S(2)}) collective-permute-start(s16[2,400,128]{2,1,0:T(8,128)(2,1)S(1)} %shard_map.92.refs_3_), channel_id=1, source_target_pairs={{0,2},{1,3},{2,0},{3,1},{4,6},{5,7},{6,4},{7,5},{8,10},{9,11},{10,... | collective-permute-start | bytes 614408 | tf_op jit(solution)/shard_map/ppermute | solution.py:398
  29.5 10.0 %collective-permute-start.12 = (s16[2,400,128]{2,1,0:T(8,128)(2,1)S(1)}, s16[2,400,128]{2,1,0:T(8,128)(2,1)S(1)}, u32[]{:S(2)}, u32[]{:S(2)}) collective-permute-start(s16[2,400,128]{2,1,0:T(8,128)(2,1)S(1)} %shard_map.91.refs_2_), channel_id=1, source_target_pairs={{0,4},{1,5},{2,6},{3,7},{4,0},{5,1},{6,2},{7,3},{8,12},{9,13},{10,... | collective-permute-start | bytes 614408 | tf_op jit(solution)/shard_map/ppermute | solution.py:398
  31.6 7.5 %collective-permute-start.14 = (s16[1,400,128]{2,1,0:T(8,128)(2,1)S(1)}, s16[1,400,128]{2,1,0:T(8,128)(2,1)S(1)}, u32[]{:S(2)}, u32[]{:S(2)}) collective-permute-start(s16[1,400,128]{2,1,0:T(8,128)(2,1)S(1)} %shard_map.93.refs_3_), channel_id=1, source_target_pairs={{0,8},{1,9},{2,10},{3,11},{4,12},{5,13},{6,14},{7,15},{8,0},{9,1},... | collective-permute-start | bytes 307208 | tf_op jit(solution)/shard_map/ppermute | solution.py:398
  35.3 2.1 %copy-start.3 = (s16[1,400,128]{2,1,0:T(8,128)(2,1)}, s16[1,400,128]{2,1,0:T(8,128)(2,1)S(1)}, u32[]{:S(2)}) copy-start(s16[1,400,128]{2,1,0:T(8,128)(2,1)S(1)} %shard_map.94.after) | copy-start | bytes 307204
  35.3 8.8 %collective-permute-start.13 = (s16[1,400,128]{2,1,0:T(8,128)(2,1)S(1)}, s16[1,400,128]{2,1,0:T(8,128)(2,1)S(1)}, u32[]{:S(2)}, u32[]{:S(2)}) collective-permute-start(s16[1,400,128]{2,1,0:T(8,128)(2,1)S(1)} %shard_map.94.after), channel_id=1, source_target_pairs={{0,8},{1,9},{2,10},{3,11},{4,12},{5,13},{6,14},{7,15},{8,0},{9,1},... | collective-permute-start | bytes 307208 | tf_op jit(solution)/shard_map/ppermute | solution.py:398
  39.4 2.8 %copy-start.1 = (f32[257,48,128]{2,1,0:T(8,128)S(1)}, f32[257,48,128]{2,1,0:T(8,128)}, u32[]{:S(2)}) copy-start(f32[257,48,128]{2,1,0:T(8,128)} %copy-done) | copy-start | bytes 18948100
  42.2 0.8 %copy-start.2 = (bf16[120,192]{1,0:T(8,128)(2,1)S(1)}, bf16[120,192]{1,0:T(8,128)(2,1)}, u32[]{:S(2)}) copy-start(bf16[120,192]{1,0:T(8,128)(2,1)} %shard_map.95.left) | copy-start | bytes 138244

commit v5 on v4

--- a/solution.py
+++ b/solution.py
@@ -293,26 +293,26 @@
     )(acc, *arrays)
 
 
-def code_near_kernel(acc, after, near_ref, exps):
+def code_near_kernel(acc, near_ref, exps):
     @pl.loop(0, 8)
     def _(i):
         code_half(acc, 16 + i, [], exps, near_ref, i)
 
 
-def code_near(acc, after):
+def code_near(acc):
     cells = acc.shape[2]
     vmem = pl.BlockSpec(memory_space=pltpu.VMEM)
     return pl.pallas_call(
         code_near_kernel,
         out_shape=jax.ShapeDtypeStruct((8, CODED, cells), jnp.int16),
-        in_specs=[vmem, vmem],
+        in_specs=[vmem],
         out_specs=vmem,
         scratch_shapes=[pltpu.VMEM((16, cells), jnp.float32)],
         compiler_params=pltpu.CompilerParams(vmem_limit_bytes=32 * MIB),
         cost_estimate=pl.CostEstimate(
             flops=10 * BODY * cells, bytes_accessed=8 * BODY * cells, transcendentals=0
         ),
-    )(acc, after)
+    )(acc)
 
 
 def lift_kernel(index_ref, frac_ref, after, left):
@@ -339,6 +339,7 @@
         out_shape=jax.ShapeDtypeStruct((VARS * LEV, 4 * ROWS), jnp.bfloat16),
         in_specs=[smem, smem, vmem],
         out_specs=vmem,
+        compiler_params=pltpu.CompilerParams(vmem_limit_bytes=4 * MIB),
     )(lev_index, lev_frac, after)
 
 
@@ -408,25 +409,24 @@
     acc, ends = products_second(tables, count, me, ends, cot, w, acc)
     acc, far = add_ends(ends, before, after, w, acc)
     far = swap(far, 1, peers)
+    near = swap(code_near(acc), 1, peers)
     y3 = code(acc, (((14, ((0, 6),)),), ((15, ((0, 7),)),)), (far,))
-    (o1_own,) = code(acc, (((10, ((0, 2),)), (11, ((0, 3),))),), (far, y3[0]))
-    y2 = code(acc, (((12, ((0, 4),)),), ((13, ((0, 5),)),)), (far, o1_own))
-    near = code_near(acc, y2[0])
     y3 = [swap(v, 2, peers) for v in y3]
-    o1 = swap(o1_own, 4, peers)
-    y2 = [swap(v, 2, peers) for v in y2]
-    near = swap(near, 1, peers)
-    (a3_low,) = code(acc, (((6, ((0, 6), (1, 0))),),), (near, y3[0]))
+    (y2_own,) = code(acc, (((12, ((0, 4),)), (13, ((0, 5),))),), (far, y3[0]))
+    y2 = swap(y2_own, 2, peers)
+    (a3_low,) = code(acc, (((6, ((0, 6), (1, 0))),),), (near, y3[0], y2_own))
     (a3_high,) = code(acc, (((7, ((0, 7), (1, 0))),),), (near, y3[1], a3_low))
     a3 = [swap(a3_low, 4, peers), swap(a3_high, 4, peers)]
-    (a1_own,) = code(acc, (((2, ((0, 2),)), (3, ((0, 3),))),), (near, a3_high))
+    (y1_own,) = code(acc, (((10, ((0, 2),)), (11, ((0, 3),))),), (far, a3_high))
+    y1 = swap(y1_own, 2, peers)
+    (b2_low,) = code(acc, (((4, ((0, 4), (1, 0), (2, 0))),),), (near, y2, a3[0], y1_own))
+    (b2_high,) = code(acc, (((5, ((0, 5), (1, 1), (2, 0))),),), (near, y2, a3[1], b2_low))
+    b2 = [swap(b2_low, 8, peers), swap(b2_high, 8, peers)]
+    (y0_own,) = code(acc, (((8, ((0, 0),)), (9, ((0, 1),))),), (far, b2_high))
+    y0 = swap(y0_own, 2, peers)
+    (a1_own,) = code(acc, (((2, ((0, 2), (1, 0))), (3, ((0, 3), (1, 1)))),), (near, y1, y0_own))
     a1 = swap(a1_own, 4, peers)
-    (y0_own,) = code(acc, (((8, ((0, 0), (1, 0))), (9, ((0, 1), (1, 1)))),), (far, o1, a1_own))
-    y0 = swap(y0_own, 2, peers)
-    (b2_low,) = code(acc, (((4, ((0, 4), (1, 0), (2, 0))),),), (near, y2[0], a3[0], y0_own))
-    (b2_high,) = code(acc, (((5, ((0, 5), (1, 0), (2, 0))),),), (near, y2[1], a3[1], b2_low))
-    b2 = [swap(b2_low, 8, peers), swap(b2_high, 8, peers)]
-    left = lift_matrix(lev_index, lev_frac, b2_high)
+    left = lift_matrix(lev_index, lev_frac, a1_own)
     out = finish(0, left, acc, ((0, 0), (1, 0), (2, 0), (3, 0)), (near, y0, a1, b2[0]))
     return finish(1, left, acc, ((0, 1), (1, 1), (2, 1), (3, 0)), (near, y0, a1, b2[1]), out)
 

time: 45.6 us -> 47.8 us (1.048)
  waiting for transfers between devices: 6.18 us -> 17.3 us
  starting transfers between devices: 19.9 us -> 15.8 us
  local copies, waits for them, and re-layouts: 3.63 us -> 0.01 us
  Pallas kernels: 14.7 us -> 13.7 us
    ppermute x13 -> x12, waiting for transfers between devices: 6.18 us -> 17.3 us  [swap(): return lax.ppermute(value, 'tile', [(i, i ^ bits) for i in range(peers)])]
    ppermute x13 -> x12, starting transfers between devices: 14.3 us -> 10.3 us  [swap(): return lax.ppermute(value, 'tile', [(i, i ^ bits) for i in range(peers)])]
    unnamed x8 -> x4, local copies, waits for them, and re-layouts: 3.63 us -> 0.01 us
    pallas_call x1, Pallas kernels: 1.74 us -> 0.75 us  [lift_matrix(): pl.pallas_call(lift_kernel, out_shape=jax.ShapeDtypeStruct((VARS * LEV, 4...]
  transfers between devices with their start and end apart: 15 -> 14, of which waited for: 3 -> 8; matrix products, arithmetic and copies ran while one was open for 0% -> 0% of each run, Pallas kernels for 15% -> 14%
where the time goes in v5:
time: 47.8 us; the launch traced here: 47.7 us
  waiting for transfers between devices  17.3 us (36%)
  starting transfers between devices  15.8 us (33%)
  Pallas kernels  13.7 us (29%)
  between operations  0.82 us (2%)
    ppermute x12, waiting for transfers between devices, swap(): return lax.ppermute(value, 'tile', [(i, i ^ bits) for i in range(peers)])  17.3 us
    ppermute x12, starting transfers between devices, swap(): return lax.ppermute(value, 'tile', [(i, i ^ bits) for i in range(peers)])  10.3 us
    ppermute x2, starting transfers between devices, ring_ends(): return (lax.ppermute(high, 'tile', up), lax.ppermute(low, 'tile', down))  5.56 us
    pallas_call x1, Pallas kernels, products_first(): pl.pallas_call(first_kernel, out_shape=(jax.ShapeDtypeStruct((TRASH + 1,...  4.19 us
    pallas_call x1, Pallas kernels, products_second(): pl.pallas_call(second_kernel, out_shape=(jax.ShapeDtypeStruct(acc.shape,...  3.15 us
    pallas_call x2, Pallas kernels, finish(): pl.pallas_call(functools.partial(finish_kernel, half, takes), out_shape=j...  2.11 us
    pallas_call x1, Pallas kernels, add_ends(): pl.pallas_call(ends_kernel, out_shape=(jax.ShapeDtypeStruct(acc.shape, jn...  1.74 us
    pallas_call x9, Pallas kernels, code(): pl.pallas_call(functools.partial(code_kernel, jobs), out_shape=tuple((jax...  1.34 us
  transfers between devices with their start and end apart: 14, of which 8 were waited for; matrix products, arithmetic and copies ran while one was open for 0% of the time, Pallas kernels for 14%

profile of v5, /device:TPU:0, one launch (start us, length us, event | category | flops | bytes accessed | tf_op | source)
XLA Modules:
  0.0 47.7 jit_solution(5645275437202221638)
XLA Ops:
  0.7 4.2 %shard_map.82 = (f32[257,48,128]{2,1,0:T(8,128)S(1)}, bf16[128,128,128]{2,1,0:T(8,128)(2,1)S(1)}, bf16[16,48,128]{2,1,0:T(8,128)(2,1)S(1)}, bf16[1,48,128]{2,1,0...) custom-call(s32[1]{0:T(128)S(6)} %copy.15.count_ref, ...), custom_call_target="tpu_custom_call" | custom-call | flops 100663296 | bytes 12582912 | tf_op jit(solution)/shard_map/pallas_call | solution.py:152
  4.9 5.5 %collective-permute-start.1 = (bf16[1,48,128]{2,1,0:T(8,128)(2,1)S(1)}, bf16[1,48,128]{2,1,0:T(8,128)(2,1)S(1)}, u32[]{:S(2)}, u32[]{:S(2)}) collective-permute-start(bf16[1,48,128]{2,1,0:T(8,128)(2,1)S(1)} %get-tuple-element.25), channel_id=1, source_target_pairs={{1,0},{2,1},{3,2},{4,3},{5,4},{6,5},{7,6},{8,7},{9,8},{10,9},{11,1... | collective-permute-start | bytes 36872 | tf_op jit(solution)/shard_map/ppermute | solution.py:395
  10.4 3.1 %shard_map.83 = (f32[257,48,128]{2,1,0:T(8,128)S(1)}, s32[4,132]{1,0:T(4,128)S(1)}) custom-call(s32[1]{0:T(128)S(6)} %copy.15.count_ref, s32[1]{0:T(128)} %bitcast.me_ref, s32[3,128]{1,0:T(4,128)S(1)} %get-tuple-element.18.tables, s32[4,132]{1,0:T(4,128)S(1)} %get-tuple-element.19.begun, ...), custom_call_target="tpu_custom_call", output_to_operand_aliasing={{0}: (6, {})} | custom-call | flops 100663296 | bytes 12582912 | tf_op jit(solution)/shard_map/pallas_call | solution.py:203
  13.6 1.7 %shard_map.84 = (f32[257,48,128]{2,1,0:T(8,128)S(1)}, s16[8,400,128]{2,1,0:T(8,128)(2,1)S(1)}) custom-call(s32[4,132]{1,0:T(4,128)S(1)} %get-tuple-element.23.ends, bf16[1,48,128]{2,1,0:T(8,128)(2,1)S(1)} %collective-permute-done.before, bf16[1,48,128]{2,1,0:T(8,128)(2,1)S(1)} %collective-permute-done.1.after, ...), custom_call_target="tpu_custom_call", output_to_operand_aliasing={{0}: (4, {})} | custom-call | flops 491520 | bytes 393216 | tf_op jit(solution)/shard_map/pallas_call | solution.py:250
  15.4 0.4 shard_map.85
  15.8 0.6 %collective-permute-start.2 = (s16[8,400,128]{2,1,0:T(8,128)(2,1)S(1)}, s16[8,400,128]{2,1,0:T(8,128)(2,1)S(1)}, u32[]{:S(2)}, u32[]{:S(2)}) collective-permute-start(s16[8,400,128]{2,1,0:T(8,128)(2,1)S(1)} %shard_map.85), channel_id=1, source_target_pairs={{0,1},{1,0},{2,3},{3,2},{4,5},{5,4},{6,7},{7,6},{8,9},{9,8},{10,11... | collective-permute-start | bytes 2457608 | tf_op jit(solution)/shard_map/ppermute | solution.py:399
  16.4 1.3 %collective-permute-done.3.refs_0_ = s16[8,400,128]{2,1,0:T(8,128)(2,1)S(1)} collective-permute-done((s16[8,400,128]{2,1,0:T(8,128)(2,1)S(1)}, s16[8,400,128]{2,1,0:T(8,128)(2,1)S(1)}, u32[]{:S(2)}, u32[]{:S(2)}) %collective-permute-start.3) | collective-permute-done | bytes 819232 | tf_op jit(solution)/shard_map/ppermute | solution.py:399
  17.7 0.2 shard_map.86
  17.9 0.1 collective-permute-start.5
  18.0 2.0 %collective-permute-start.4 = (s16[1,400,128]{2,1,0:T(8,128)(2,1)S(1)}, s16[1,400,128]{2,1,0:T(8,128)(2,1)S(1)}, u32[]{:S(2)}, u32[]{:S(2)}) collective-permute-start(s16[1,400,128]{2,1,0:T(8,128)(2,1)S(1)} %get-tuple-element.29), channel_id=1, source_target_pairs={{0,2},{1,3},{2,0},{3,1},{4,6},{5,7},{6,4},{7,5},{8,10},{9,11},{10,... | collective-permute-start | bytes 307208 | tf_op jit(solution)/shard_map/ppermute | solution.py:399
  20.0 3.7 %collective-permute-done.5.refs_1_ = s16[1,400,128]{2,1,0:T(8,128)(2,1)S(1)} collective-permute-done((s16[1,400,128]{2,1,0:T(8,128)(2,1)S(1)}, s16[1,400,128]{2,1,0:T(8,128)(2,1)S(1)}, u32[]{:S(2)}, u32[]{:S(2)}) %collective-permute-start.5) | collective-permute-done | bytes 102432 | tf_op jit(solution)/shard_map/ppermute | solution.py:399
  23.7 0.2 shard_map.87.refs_2_
  23.9 0.1 shard_map.88.refs_2_
  24.0 1.0 %collective-permute-done.4.refs_1_ = s16[1,400,128]{2,1,0:T(8,128)(2,1)S(1)} collective-permute-done((s16[1,400,128]{2,1,0:T(8,128)(2,1)S(1)}, s16[1,400,128]{2,1,0:T(8,128)(2,1)S(1)}, u32[]{:S(2)}, u32[]{:S(2)}) %collective-permute-start.4) | collective-permute-done | bytes 102432 | tf_op jit(solution)/shard_map/ppermute | solution.py:399
  25.1 0.1 shard_map.89.refs_1_
  25.2 0.2 shard_map.90.refs_3_
  25.4 1.0 %collective-permute-start.6 = (s16[2,400,128]{2,1,0:T(8,128)(2,1)S(1)}, s16[2,400,128]{2,1,0:T(8,128)(2,1)S(1)}, u32[]{:S(2)}, u32[]{:S(2)}) collective-permute-start(s16[2,400,128]{2,1,0:T(8,128)(2,1)S(1)} %shard_map.90.refs_3_), channel_id=1, source_target_pairs={{0,2},{1,3},{2,0},{3,1},{4,6},{5,7},{6,4},{7,5},{8,10},{9,11},{10,... | collective-permute-start | bytes 614408 | tf_op jit(solution)/shard_map/ppermute | solution.py:399
  26.4 2.0 %collective-permute-start.8 = (s16[1,400,128]{2,1,0:T(8,128)(2,1)S(1)}, s16[1,400,128]{2,1,0:T(8,128)(2,1)S(1)}, u32[]{:S(2)}, u32[]{:S(2)}) collective-permute-start(s16[1,400,128]{2,1,0:T(8,128)(2,1)S(1)} %shard_map.89.refs_1_), channel_id=1, source_target_pairs={{0,4},{1,5},{2,6},{3,7},{4,0},{5,1},{6,2},{7,3},{8,12},{9,13},{10,... | collective-permute-start | bytes 307208 | tf_op jit(solution)/shard_map/ppermute | solution.py:399
  28.4 2.6 %collective-permute-done.9.refs_2_ = s16[1,400,128]{2,1,0:T(8,128)(2,1)S(1)} collective-permute-done((s16[1,400,128]{2,1,0:T(8,128)(2,1)S(1)}, s16[1,400,128]{2,1,0:T(8,128)(2,1)S(1)}, u32[]{:S(2)}, u32[]{:S(2)}) %collective-permute-start.9) | collective-permute-done | bytes 102432 | tf_op jit(solution)/shard_map/ppermute | solution.py:399
  31.1 0.6 %collective-permute-done.7.refs_1_ = s16[2,400,128]{2,1,0:T(8,128)(2,1)S(1)} collective-permute-done((s16[2,400,128]{2,1,0:T(8,128)(2,1)S(1)}, s16[2,400,128]{2,1,0:T(8,128)(2,1)S(1)}, u32[]{:S(2)}, u32[]{:S(2)}) %collective-permute-start.7) | collective-permute-done | bytes 204832 | tf_op jit(solution)/shard_map/ppermute | solution.py:399
  31.7 0.1 shard_map.91.refs_3_
  31.9 0.3 collective-permute-done.8.refs_2_
  32.2 0.1 shard_map.92.refs_1_
  32.3 0.2 shard_map.93.refs_2_
  32.5 1.4 %collective-permute-done.6.refs_1_ = s16[2,400,128]{2,1,0:T(8,128)(2,1)S(1)} collective-permute-done((s16[2,400,128]{2,1,0:T(8,128)(2,1)S(1)}, s16[2,400,128]{2,1,0:T(8,128)(2,1)S(1)}, u32[]{:S(2)}, u32[]{:S(2)}) %collective-permute-start.6) | collective-permute-done | bytes 204832 | tf_op jit(solution)/shard_map/ppermute | solution.py:399
  33.9 0.2 shard_map.94.after
  34.2 0.6 %collective-permute-start.10 = (s16[2,400,128]{2,1,0:T(8,128)(2,1)S(1)}, s16[2,400,128]{2,1,0:T(8,128)(2,1)S(1)}, u32[]{:S(2)}, u32[]{:S(2)}) collective-permute-start(s16[2,400,128]{2,1,0:T(8,128)(2,1)S(1)} %shard_map.93.refs_2_), channel_id=1, source_target_pairs={{0,2},{1,3},{2,0},{3,1},{4,6},{5,7},{6,4},{7,5},{8,10},{9,11},{10,... | collective-permute-start | bytes 614408 | tf_op jit(solution)/shard_map/ppermute | solution.py:399
  34.8 3.8 %collective-permute-start.13 = (s16[1,400,128]{2,1,0:T(8,128)(2,1)S(1)}, s16[1,400,128]{2,1,0:T(8,128)(2,1)S(1)}, u32[]{:S(2)}, u32[]{:S(2)}) collective-permute-start(s16[1,400,128]{2,1,0:T(8,128)(2,1)S(1)} %shard_map.91.refs_3_), channel_id=1, source_target_pairs={{0,8},{1,9},{2,10},{3,11},{4,12},{5,13},{6,14},{7,15},{8,0},{9,1},... | collective-permute-start | bytes 307208 | tf_op jit(solution)/shard_map/ppermute | solution.py:399
  38.6 0.7 %shard_map.95.left = bf16[120,192]{1,0:T(8,128)(2,1)S(1)} custom-call(s32[8]{0:T(128)S(1)} %copy-done, f32[8]{0:T(128)S(1)} %copy-done.1, s16[2,400,128]{2,1,0:T(8,128)(2,1)S(1)} %shard_map.94.after), custom_call_target="tpu_custom_call" | custom-call | tf_op jit(solution)/shard_map/pallas_call | solution.py:337
  39.3 6.2 %collective-permute-done.13.refs_3_ = s16[1,400,128]{2,1,0:T(8,128)(2,1)S(1)} collective-permute-done((s16[1,400,128]{2,1,0:T(8,128)(2,1)S(1)}, s16[1,400,128]{2,1,0:T(8,128)(2,1)S(1)}, u32[]{:S(2)}, u32[]{:S(2)}) %collective-permute-start.13) | collective-permute-done | bytes 102432 | tf_op jit(solution)/shard_map/ppermute | solution.py:399
  45.5 1.1 %shard_map.96.refs_4_ = f32[16,120,128]{2,1,0:T(8,128)} custom-call(bf16[120,192]{1,0:T(8,128)(2,1)S(1)} %shard_map.95.left, f32[257,48,128]{2,1,0:T(8,128)S(1)} %get-tuple-element.27.acc, s16[8,400,128]{2,1,0:T(8,128)(2,1)S(1)} %collective-permute-done.2.refs_0_, s16[2,400,128]{2,1,0:T(8,128)(2,1)S(1)} %collective-permute-done.10.refs_1_, ...), custom_call_target="tpu_custom_call" | custom-call | flops 491520 | bytes 786432 | tf_op jit(solution)/shard_map/pallas_call | solution.py:375
  46.6 1.1 %shard_map.97 = f32[16,120,128]{2,1,0:T(8,128)} custom-call(bf16[120,192]{1,0:T(8,128)(2,1)S(1)} %shard_map.95.left, f32[257,48,128]{2,1,0:T(8,128)S(1)} %get-tuple-element.27.acc, s16[8,400,128]{2,1,0:T(8,128)(2,1)S(1)} %collective-permute-done.2.refs_0_, s16[2,400,128]{2,1,0:T(8,128)(2,1)S(1)} %collective-permute-done.10.refs_1_, ...), custom_call_target="tpu_custom_call", output_to_operand_aliasing={{}: (6, {})} | custom-call | flops 491520 | bytes 786432 | tf_op jit(solution)/shard_map/pallas_call | solution.py:375
  (16 shorter events, 0.4 us)
Async XLA Ops:
  4.9 8.7 %collective-permute-start = (bf16[1,48,128]{2,1,0:T(8,128)(2,1)S(1)}, bf16[1,48,128]{2,1,0:T(8,128)(2,1)S(1)}, u32[]{:S(2)}, u32[]{:S(2)}) collective-permute-start(bf16[1,48,128]{2,1,0:T(8,128)(2,1)S(1)} %get-tuple-element.24), channel_id=1, source_target_pairs={{0,1},{1,2},{2,3},{3,4},{4,5},{5,6},{6,7},{7,8},{8,9},{9,10},{10,1... | collective-permute-start | bytes 36872 | tf_op jit(solution)/shard_map/ppermute | solution.py:395
  4.9 8.7 %collective-permute-start.1 = (bf16[1,48,128]{2,1,0:T(8,128)(2,1)S(1)}, bf16[1,48,128]{2,1,0:T(8,128)(2,1)S(1)}, u32[]{:S(2)}, u32[]{:S(2)}) collective-permute-start(bf16[1,48,128]{2,1,0:T(8,128)(2,1)S(1)} %get-tuple-element.25), channel_id=1, source_target_pairs={{1,0},{2,1},{3,2},{4,3},{5,4},{6,5},{7,6},{8,7},{9,8},{10,9},{11,1... | collective-permute-start | bytes 36872 | tf_op jit(solution)/shard_map/ppermute | solution.py:395
  15.3 2.4 %collective-permute-start.3 = (s16[8,400,128]{2,1,0:T(8,128)(2,1)S(1)}, s16[8,400,128]{2,1,0:T(8,128)(2,1)S(1)}, u32[]{:S(2)}, u32[]{:S(2)}) collective-permute-start(s16[8,400,128]{2,1,0:T(8,128)(2,1)S(1)} %get-tuple-element.28), channel_id=1, source_target_pairs={{0,1},{1,0},{2,3},{3,2},{4,5},{5,4},{6,7},{7,6},{8,9},{9,8},{10,11... | collective-permute-start | bytes 2457608 | tf_op jit(solution)/shard_map/ppermute | solution.py:399
  15.8 8.1 %collective-permute-start.2 = (s16[8,400,128]{2,1,0:T(8,128)(2,1)S(1)}, s16[8,400,128]{2,1,0:T(8,128)(2,1)S(1)}, u32[]{:S(2)}, u32[]{:S(2)}) collective-permute-start(s16[8,400,128]{2,1,0:T(8,128)(2,1)S(1)} %shard_map.85), channel_id=1, source_target_pairs={{0,1},{1,0},{2,3},{3,2},{4,5},{5,4},{6,7},{7,6},{8,9},{9,8},{10,11... | collective-permute-start | bytes 2457608 | tf_op jit(solution)/shard_map/ppermute | solution.py:399
  17.9 5.8 %collective-permute-start.5 = (s16[1,400,128]{2,1,0:T(8,128)(2,1)S(1)}, s16[1,400,128]{2,1,0:T(8,128)(2,1)S(1)}, u32[]{:S(2)}, u32[]{:S(2)}) collective-permute-start(s16[1,400,128]{2,1,0:T(8,128)(2,1)S(1)} %get-tuple-element.30), channel_id=1, source_target_pairs={{0,2},{1,3},{2,0},{3,1},{4,6},{5,7},{6,4},{7,5},{8,10},{9,11},{10,... | collective-permute-start | bytes 307208 | tf_op jit(solution)/shard_map/ppermute | solution.py:399
  18.0 7.1 %collective-permute-start.4 = (s16[1,400,128]{2,1,0:T(8,128)(2,1)S(1)}, s16[1,400,128]{2,1,0:T(8,128)(2,1)S(1)}, u32[]{:S(2)}, u32[]{:S(2)}) collective-permute-start(s16[1,400,128]{2,1,0:T(8,128)(2,1)S(1)} %get-tuple-element.29), channel_id=1, source_target_pairs={{0,2},{1,3},{2,0},{3,1},{4,6},{5,7},{6,4},{7,5},{8,10},{9,11},{10,... | collective-permute-start | bytes 307208 | tf_op jit(solution)/shard_map/ppermute | solution.py:399
  23.8 7.9 %collective-permute-start.7 = (s16[2,400,128]{2,1,0:T(8,128)(2,1)S(1)}, s16[2,400,128]{2,1,0:T(8,128)(2,1)S(1)}, u32[]{:S(2)}, u32[]{:S(2)}) collective-permute-start(s16[2,400,128]{2,1,0:T(8,128)(2,1)S(1)} %shard_map.87.refs_2_), channel_id=1, source_target_pairs={{0,2},{1,3},{2,0},{3,1},{4,6},{5,7},{6,4},{7,5},{8,10},{9,11},{10,... | collective-permute-start | bytes 614408 | tf_op jit(solution)/shard_map/ppermute | solution.py:399
  25.4 8.5 %collective-permute-start.6 = (s16[2,400,128]{2,1,0:T(8,128)(2,1)S(1)}, s16[2,400,128]{2,1,0:T(8,128)(2,1)S(1)}, u32[]{:S(2)}, u32[]{:S(2)}) collective-permute-start(s16[2,400,128]{2,1,0:T(8,128)(2,1)S(1)} %shard_map.90.refs_3_), channel_id=1, source_target_pairs={{0,2},{1,3},{2,0},{3,1},{4,6},{5,7},{6,4},{7,5},{8,10},{9,11},{10,... | collective-permute-start | bytes 614408 | tf_op jit(solution)/shard_map/ppermute | solution.py:399
  26.4 4.7 %collective-permute-start.9 = (s16[1,400,128]{2,1,0:T(8,128)(2,1)S(1)}, s16[1,400,128]{2,1,0:T(8,128)(2,1)S(1)}, u32[]{:S(2)}, u32[]{:S(2)}) collective-permute-start(s16[1,400,128]{2,1,0:T(8,128)(2,1)S(1)} %shard_map.88.refs_2_), channel_id=1, source_target_pairs={{0,4},{1,5},{2,6},{3,7},{4,0},{5,1},{6,2},{7,3},{8,12},{9,13},{10,... | collective-permute-start | bytes 307208 | tf_op jit(solution)/shard_map/ppermute | solution.py:399
  26.4 5.8 %collective-permute-start.8 = (s16[1,400,128]{2,1,0:T(8,128)(2,1)S(1)}, s16[1,400,128]{2,1,0:T(8,128)(2,1)S(1)}, u32[]{:S(2)}, u32[]{:S(2)}) collective-permute-start(s16[1,400,128]{2,1,0:T(8,128)(2,1)S(1)} %shard_map.89.refs_1_), channel_id=1, source_target_pairs={{0,4},{1,5},{2,6},{3,7},{4,0},{5,1},{6,2},{7,3},{8,12},{9,13},{10,... | collective-permute-start | bytes 307208 | tf_op jit(solution)/shard_map/ppermute | solution.py:399
  32.3 6.2 %copy-start = (s32[8]{0:T(128)S(1)}, s32[8]{0:T(128)}, u32[]{:S(2)}) copy-start(s32[8]{0:T(128)} %index_ref.1) | copy-start | bytes 100
  32.3 6.2 %copy-start.1 = (f32[8]{0:T(128)S(1)}, f32[8]{0:T(128)}, u32[]{:S(2)}) copy-start(f32[8]{0:T(128)} %frac_ref.1) | copy-start | bytes 100
  34.1 11.4 %collective-permute-start.11 = (s16[2,400,128]{2,1,0:T(8,128)(2,1)S(1)}, s16[2,400,128]{2,1,0:T(8,128)(2,1)S(1)}, u32[]{:S(2)}, u32[]{:S(2)}) collective-permute-start(s16[2,400,128]{2,1,0:T(8,128)(2,1)S(1)} %shard_map.94.after), channel_id=1, source_target_pairs={{0,4},{1,5},{2,6},{3,7},{4,0},{5,1},{6,2},{7,3},{8,12},{9,13},{10,... | collective-permute-start | bytes 614408 | tf_op jit(solution)/shard_map/ppermute | solution.py:399
  34.2 11.3 %collective-permute-start.10 = (s16[2,400,128]{2,1,0:T(8,128)(2,1)S(1)}, s16[2,400,128]{2,1,0:T(8,128)(2,1)S(1)}, u32[]{:S(2)}, u32[]{:S(2)}) collective-permute-start(s16[2,400,128]{2,1,0:T(8,128)(2,1)S(1)} %shard_map.93.refs_2_), channel_id=1, source_target_pairs={{0,2},{1,3},{2,0},{3,1},{4,6},{5,7},{6,4},{7,5},{8,10},{9,11},{10,... | collective-permute-start | bytes 614408 | tf_op jit(solution)/shard_map/ppermute | solution.py:399
  34.8 10.7 %collective-permute-start.13 = (s16[1,400,128]{2,1,0:T(8,128)(2,1)S(1)}, s16[1,400,128]{2,1,0:T(8,128)(2,1)S(1)}, u32[]{:S(2)}, u32[]{:S(2)}) collective-permute-start(s16[1,400,128]{2,1,0:T(8,128)(2,1)S(1)} %shard_map.91.refs_3_), channel_id=1, source_target_pairs={{0,8},{1,9},{2,10},{3,11},{4,12},{5,13},{6,14},{7,15},{8,0},{9,1},... | collective-permute-start | bytes 307208 | tf_op jit(solution)/shard_map/ppermute | solution.py:399
  38.5 8.1 %collective-permute-start.12 = (s16[1,400,128]{2,1,0:T(8,128)(2,1)S(1)}, s16[1,400,128]{2,1,0:T(8,128)(2,1)S(1)}, u32[]{:S(2)}, u32[]{:S(2)}) collective-permute-start(s16[1,400,128]{2,1,0:T(8,128)(2,1)S(1)} %shard_map.92.refs_1_), channel_id=1, source_target_pairs={{0,8},{1,9},{2,10},{3,11},{4,12},{5,13},{6,14},{7,15},{8,0},{9,1},... | collective-permute-start | bytes 307208 | tf_op jit(solution)/shard_map/ppermute | solution.py:399

commit v6 on v5

--- a/solution.py
+++ b/solution.py
@@ -17,6 +17,8 @@
 CODED = BODY + 16
 GROUP = 16
 MIB = 1 << 20
+LITTLE = pl.CostEstimate(flops=1, bytes_accessed=1, transcendentals=0)
+MUCH = pl.CostEstimate(flops=1 << 28, bytes_accessed=12 * MIB, transcendentals=0)
 
 
 def encode(read, write, exps):
@@ -74,43 +76,20 @@
         add_products(entries, w, acc)
 
 
-def first_half(count):
+def groups_of(count):
     used = (count + GROUP - 1) // GROUP
     return used, (used + 1) // 2
 
 
-def first_kernel(
-    count_ref,
-    me_ref,
-    tb_hbm,
-    dest_hbm,
-    src_hbm,
-    cot_hbm,
-    w_hbm,
-    acc,
-    w,
-    cot,
-    low,
-    high,
-    tables,
-    ends,
-    sems,
-    w_sems,
-):
-    groups = w.shape[0] // GROUP
-    count = count_ref[0]
-    used, half = first_half(count)
-
+def load(used, pairs, w_hbm, w, acc, sems, w_sems):
     def w_copy(g):
         part = pl.ds(g * GROUP, GROUP)
         return pltpu.make_async_copy(w_hbm.at[part], w.at[part], w_sems.at[g])
 
-    pairs = [(cot_hbm, cot)]
-    pairs += [(t, tables.at[pl.ds(i, 1)]) for i, t in enumerate((tb_hbm, dest_hbm, src_hbm))]
     small = [pltpu.make_async_copy(a, b, sems.at[i]) for i, (a, b) in enumerate(pairs)]
     for copy in small:
         copy.start()
-    for g in range(groups):
+    for g in range(w.shape[0] // GROUP):
 
         @pl.when(g < used)
         def _():
@@ -121,62 +100,56 @@
         acc[b] = jnp.zeros(acc.shape[1:], jnp.float32)
 
     acc[TRASH] = jnp.zeros(acc.shape[1:], jnp.float32)
-    ends[3, 0] = 0
-
     for copy in small:
         copy.wait()
-    low[0] = cot[0]
-    high[0] = cot[cot.shape[0] - 1]
-
-    for g in range(groups):
-
-        @pl.when(g < used)
-        def _():
-            w_copy(g).wait()
-
-        @pl.when(g < half)
-        def _():
-            add_group(g, count, me_ref[0], tables, cot, w, acc, ends)
-
-
-def in_hbm(x):
-    return pltpu.with_memory_space_constraint(x, pltpu.HBM)
-
-
-def products_first(tables, count, me, cotangent, weight):
-    entries, cells_in, cells = weight.shape
-    smem = pl.BlockSpec(memory_space=pltpu.SMEM)
-    vmem = pl.BlockSpec(memory_space=pltpu.VMEM)
-    hbm = pl.BlockSpec(memory_space=pltpu.HBM)
-    end = jax.ShapeDtypeStruct((1,) + cotangent.shape[1:], cotangent.dtype)
-    return pl.pallas_call(
-        first_kernel,
-        out_shape=(
-            jax.ShapeDtypeStruct((TRASH + 1, ROWS, cells), jnp.float32),
-            jax.ShapeDtypeStruct(weight.shape, weight.dtype),
-            jax.ShapeDtypeStruct(cotangent.shape, cotangent.dtype),
-            end,
-            end,
-            jax.ShapeDtypeStruct((3, entries), jnp.int32),
-            jax.ShapeDtypeStruct((4, entries + 4), jnp.int32),
-        ),
-        in_specs=[smem, smem] + [hbm] * 5,
-        out_specs=(vmem,) * 5 + (smem, smem),
-        scratch_shapes=[
-            pltpu.SemaphoreType.DMA((4,)),
-            pltpu.SemaphoreType.DMA((entries // GROUP,)),
-        ],
-        compiler_params=pltpu.CompilerParams(vmem_limit_bytes=24 * MIB),
-        cost_estimate=pl.CostEstimate(
-            flops=entries * ROWS * cells_in * cells, bytes_accessed=12 * MIB, transcendentals=0
-        ),
-    )(count, me, *[in_hbm(t) for t in tables], in_hbm(cotangent), in_hbm(weight))
-
-
-def second_kernel(count_ref, me_ref, tables, begun, cot, w, acc_in, acc, ends):
-    count = count_ref[0]
-    used, half = first_half(count)
-    listed = begun[3, 0]
+    return w_copy
+
+
+def ahead_kernel(
+    count_ref, me_ref, tb, dest, src, cot_hbm, w_hbm, low_in, acc, w, cot, low, ends, *scratch
+):
+    tables, sems, w_sems = scratch
+    used, half = groups_of(count_ref[0])
+    low[...] = low_in[...]
+
+    @pl.when(me_ref[0] == 0)
+    def _():
+        pairs = [(cot_hbm, cot)]
+        pairs += [(t, tables.at[pl.ds(i, 1)]) for i, t in enumerate((tb, dest, src))]
+        w_copy = load(used, pairs, w_hbm, w, acc, sems, w_sems)
+        ends[3, 0] = 0
+        for g in range(w.shape[0] // GROUP):
+
+            @pl.when(g < used)
+            def _():
+                w_copy(g).wait()
+
+            @pl.when(g < half)
+            def _():
+                add_group(g, count_ref[0], me_ref[0], tables, cot, w, acc, ends)
+
+
+def rest_kernel(
+    count_ref, me_ref, tb, dest, src, cot_hbm, w_hbm, begun, acc_in, w_in, cot_in, *refs
+):
+    acc, w, cot, ends, tables, sems, w_sems = refs
+    used, half = groups_of(count_ref[0])
+    early = me_ref[0] == 0
+    done = jnp.where(early, half, 0)
+    listed = jnp.where(early, begun[3, 0], 0)
+    three = [(t, tables.at[pl.ds(i, 1)]) for i, t in enumerate((tb, dest, src))]
+
+    @pl.when(early)
+    def _():
+        small = [pltpu.make_async_copy(a, b, sems.at[i]) for i, (a, b) in enumerate(three)]
+        for copy in small:
+            copy.start()
+        for copy in small:
+            copy.wait()
+
+    @pl.when(jnp.logical_not(early))
+    def _():
+        load(used, three + [(cot_hbm, cot)], w_hbm, w, acc, sems, w_sems)
 
     @pl.loop(0, listed)
     def _(n):
@@ -185,9 +158,16 @@
 
     ends[3, 0] = listed
 
-    @pl.loop(half, used)
-    def _(g):
-        add_group(g, count, me_ref[0], tables, cot, w, acc, ends)
+    for g in range(w.shape[0] // GROUP):
+
+        @pl.when(jnp.logical_not(early) & (g < used))
+        def _():
+            part = pl.ds(g * GROUP, GROUP)
+            pltpu.make_async_copy(w_hbm.at[part], w.at[part], w_sems.at[g]).wait()
+
+        @pl.when((g >= done) & (g < used))
+        def _():
+            add_group(g, count_ref[0], me_ref[0], tables, cot, w, acc, ends)
 
     listed = ends[3, 0]
     for i in range(4):
@@ -196,24 +176,39 @@
         ends[2, listed + i] = 0
 
 
-def products_second(tables, count, me, begun, cot, w, acc):
-    entries, cells_in, cells = w.shape
+def in_hbm(x):
+    return pltpu.with_memory_space_constraint(x, pltpu.HBM)
+
+
+def products_call(kernel, operands, given, low, cost):
+    cotangent, weight = operands[5], operands[6]
+    entries, _, cells = weight.shape
     smem = pl.BlockSpec(memory_space=pltpu.SMEM)
     vmem = pl.BlockSpec(memory_space=pltpu.VMEM)
-    return pl.pallas_call(
-        second_kernel,
-        out_shape=(
-            jax.ShapeDtypeStruct(acc.shape, acc.dtype),
-            jax.ShapeDtypeStruct(begun.shape, begun.dtype),
-        ),
-        in_specs=[smem] * 4 + [vmem] * 3,
-        out_specs=(vmem, smem),
-        input_output_aliases={6: 0},
-        compiler_params=pltpu.CompilerParams(vmem_limit_bytes=32 * MIB),
-        cost_estimate=pl.CostEstimate(
-            flops=entries * ROWS * cells_in * cells, bytes_accessed=12 * MIB, transcendentals=0
-        ),
-    )(count, me, tables, begun, cot, w, acc)
+    hbm = pl.BlockSpec(memory_space=pltpu.HBM)
+    results = [
+        jax.ShapeDtypeStruct((TRASH + 1, ROWS, cells), jnp.float32),
+        jax.ShapeDtypeStruct(weight.shape, weight.dtype),
+        jax.ShapeDtypeStruct(cotangent.shape, cotangent.dtype),
+    ]
+    listed = jax.ShapeDtypeStruct((4, entries + 4), jnp.int32)
+    first = not given
+    if first:
+        results.append(jax.ShapeDtypeStruct(low.shape, low.dtype))
+    return pl.pallas_call(
+        kernel,
+        out_shape=tuple(results + [listed]),
+        in_specs=[smem, smem] + [hbm] * 5 + ([vmem] if first else [smem] + [vmem] * 3),
+        out_specs=(vmem,) * len(results) + (smem,),
+        scratch_shapes=[
+            pltpu.SMEM((3, entries), jnp.int32),
+            pltpu.SemaphoreType.DMA((4,)),
+            pltpu.SemaphoreType.DMA((entries // GROUP,)),
+        ],
+        input_output_aliases={} if first else {8: 0, 9: 1, 10: 2},
+        compiler_params=pltpu.CompilerParams(vmem_limit_bytes=24 * MIB),
+        cost_estimate=cost,
+    )(*operands[:2], *[in_hbm(x) for x in operands[2:]], *([low] if first else given))
 
 
 def code_half(acc, unit, coded, exps, out_ref, at):
@@ -261,9 +256,7 @@
         ],
         input_output_aliases={4: 0},
         compiler_params=pltpu.CompilerParams(vmem_limit_bytes=32 * MIB),
-        cost_estimate=pl.CostEstimate(
-            flops=10 * BODY * cells, bytes_accessed=8 * BODY * cells, transcendentals=0
-        ),
+        cost_estimate=LITTLE,
     )(ends, before, after, w, acc)
 
 
@@ -287,9 +280,7 @@
         out_specs=(vmem,) * len(jobs),
         scratch_shapes=[pltpu.VMEM((16, cells), jnp.float32)],
         compiler_params=pltpu.CompilerParams(vmem_limit_bytes=32 * MIB),
-        cost_estimate=pl.CostEstimate(
-            flops=10 * BODY * cells, bytes_accessed=8 * BODY * cells, transcendentals=0
-        ),
+        cost_estimate=LITTLE,
     )(acc, *arrays)
 
 
@@ -309,9 +300,7 @@
         out_specs=vmem,
         scratch_shapes=[pltpu.VMEM((16, cells), jnp.float32)],
         compiler_params=pltpu.CompilerParams(vmem_limit_bytes=32 * MIB),
-        cost_estimate=pl.CostEstimate(
-            flops=10 * BODY * cells, bytes_accessed=8 * BODY * cells, transcendentals=0
-        ),
+        cost_estimate=LITTLE,
     )(acc)
 
 
@@ -340,6 +329,7 @@
         in_specs=[smem, smem, vmem],
         out_specs=vmem,
         compiler_params=pltpu.CompilerParams(vmem_limit_bytes=4 * MIB),
+        cost_estimate=LITTLE,
     )(lev_index, lev_frac, after)
 
 
@@ -383,16 +373,13 @@
         ],
         input_output_aliases={2 + len(arrays): 0} if extra else {},
         compiler_params=pltpu.CompilerParams(vmem_limit_bytes=32 * MIB),
-        cost_estimate=pl.CostEstimate(
-            flops=10 * BODY * cells, bytes_accessed=16 * BODY * cells, transcendentals=0
-        ),
+        cost_estimate=LITTLE,
     )(left, acc, *arrays, *extra)
 
 
-def ring_ends(low, high, peers):
+def ring(peers):
     up = [(i, (i + 1) % peers) for i in range(peers)]
-    down = [(j, i) for i, j in up]
-    return lax.ppermute(high, "tile", up), lax.ppermute(low, "tile", down)
+    return up, [(j, i) for i, j in up]
 
 
 def swap(value, bits, peers):
@@ -402,31 +389,34 @@
 def staged(cotangent, weight, target_block, dest, source, count, lev_index, lev_frac):
     peers = 16
     me = lax.axis_index("tile").astype(jnp.int32).reshape(1)
-    acc, w, cot, low, high, tables, ends = products_first(
-        (target_block, dest, source), count, me, cotangent, weight
-    )
-    before, after = ring_ends(low, high, peers)
-    acc, ends = products_second(tables, count, me, ends, cot, w, acc)
+    operands = (count, me, target_block, dest, source, cotangent, weight)
+    up, down = ring(peers)
+    before = lax.ppermute(cotangent[-1:], "tile", up)
+    acc, w, cot, low, ends = products_call(ahead_kernel, operands, (), cotangent[:1], MUCH)
+    after = lax.ppermute(low, "tile", down)
+    acc, w, cot, ends = products_call(rest_kernel, operands, (ends, acc, w, cot), None, LITTLE)
     acc, far = add_ends(ends, before, after, w, acc)
     far = swap(far, 1, peers)
     near = swap(code_near(acc), 1, peers)
     y3 = code(acc, (((14, ((0, 6),)),), ((15, ((0, 7),)),)), (far,))
+    y3_own = y3[0]
     y3 = [swap(v, 2, peers) for v in y3]
-    (y2_own,) = code(acc, (((12, ((0, 4),)), (13, ((0, 5),))),), (far, y3[0]))
-    y2 = swap(y2_own, 2, peers)
-    (a3_low,) = code(acc, (((6, ((0, 6), (1, 0))),),), (near, y3[0], y2_own))
+    y2 = code(acc, (((12, ((0, 4),)),), ((13, ((0, 5),)),)), (far, y3_own))
+    y2_own = y2[0]
+    y2 = [swap(v, 2, peers) for v in y2]
+    (a3_low,) = code(acc, (((6, ((0, 6), (1, 0))),),), (near, y3[0], far))
     (a3_high,) = code(acc, (((7, ((0, 7), (1, 0))),),), (near, y3[1], a3_low))
     a3 = [swap(a3_low, 4, peers), swap(a3_high, 4, peers)]
-    (y1_own,) = code(acc, (((10, ((0, 2),)), (11, ((0, 3),))),), (far, a3_high))
-    y1 = swap(y1_own, 2, peers)
-    (b2_low,) = code(acc, (((4, ((0, 4), (1, 0), (2, 0))),),), (near, y2, a3[0], y1_own))
-    (b2_high,) = code(acc, (((5, ((0, 5), (1, 1), (2, 0))),),), (near, y2, a3[1], b2_low))
+    (y1_own,) = code(acc, (((10, ((0, 2),)), (11, ((0, 3),))),), (far, y2_own))
+    o1 = swap(y1_own, 4, peers)
+    (b2_low,) = code(acc, (((4, ((0, 4), (1, 0), (2, 0))),),), (near, y2[0], a3[0], y1_own))
+    (b2_high,) = code(acc, (((5, ((0, 5), (1, 0), (2, 0))),),), (near, y2[1], a3[1], b2_low))
     b2 = [swap(b2_low, 8, peers), swap(b2_high, 8, peers)]
-    (y0_own,) = code(acc, (((8, ((0, 0),)), (9, ((0, 1),))),), (far, b2_high))
+    (y0_own,) = code(acc, (((8, ((0, 0), (1, 0))), (9, ((0, 1), (1, 1)))),), (far, o1, a3[0]))
     y0 = swap(y0_own, 2, peers)
-    (a1_own,) = code(acc, (((2, ((0, 2), (1, 0))), (3, ((0, 3), (1, 1)))),), (near, y1, y0_own))
+    (a1_own,) = code(acc, (((2, ((0, 2),)), (3, ((0, 3),))),), (near, y1_own))
     a1 = swap(a1_own, 4, peers)
-    left = lift_matrix(lev_index, lev_frac, a1_own)
+    left = lift_matrix(lev_index, lev_frac, b2_low)
     out = finish(0, left, acc, ((0, 0), (1, 0), (2, 0), (3, 0)), (near, y0, a1, b2[0]))
     return finish(1, left, acc, ((0, 1), (1, 1), (2, 1), (3, 0)), (near, y0, a1, b2[1]), out)
 
@@ -443,7 +433,9 @@
     entries, _, cells = weight.shape
     capacity = max(2, 2 * entries // peers)
     slots = peers * capacity
-    before, after = ring_ends(cotangent[:1], cotangent[-1:], peers)
+    up, down = ring(peers)
+    before = lax.ppermute(cotangent[-1:], "tile", up)
+    after = lax.ppermute(cotangent[:1], "tile", down)
     window = jnp.concatenate([before, cotangent, after], axis=0)
     contrib = jnp.einsum(
         "ofp,ops->ofs", window[target_block[0]], weight, preferred_element_type=jnp.float32

time: 47.8 us -> 42 us (0.88); the launches traced: 47.7 us -> 41.3 us
  waiting for transfers between devices: 17.3 us -> 8.17 us
  starting transfers between devices: 15.8 us -> 17.1 us
  Pallas kernels: 13.7 us -> 14.5 us
  local copies, waits for them, and re-layouts: 0.01 us -> 0.74 us
    ppermute x12 -> x13, waiting for transfers between devices: 17.3 us -> 8.16 us  [swap(): return lax.ppermute(value, 'tile', [(i, i ^ bits) for i in range(peers)])]
    ppermute x12 -> x13, starting transfers between devices: 10.3 us -> 15 us  [swap(): return lax.ppermute(value, 'tile', [(i, i ^ bits) for i in range(peers)])]
    ppermute x2, starting transfers between devices: 5.56 us -> 2.12 us  [the longest x1 1.67 us: staged(): after = lax.ppermute(low, 'tile', down)]
    pallas_call x2, Pallas kernels: 7.34 us -> 8.12 us  [products_call(): pl.pallas_call(kernel, out_shape=tuple(results + [listed]), in_specs=[sme...]
    slice x0 -> x1, local copies, waits for them, and re-layouts: none -> 0.73 us  [staged(): before = lax.ppermute(cotangent[-1:], 'tile', up)]
  transfers between devices with their start and end apart: 14 -> 15, of which waited for: 8 -> 5; matrix products, arithmetic and copies ran while one was open for 0% -> 0% of each run, Pallas kernels for 14% -> 28%
where the time goes in v6:
time: 42 us; the launch traced here: 41.3 us
  starting transfers between devices  17.1 us (41%)
  Pallas kernels  14.5 us (35%)
  waiting for transfers between devices  8.17 us (19%)
  between operations  0.83 us (2%)
  local copies, waits for them, and re-layouts  0.74 us (2%)
    ppermute x13, starting transfers between devices, swap(): return lax.ppermute(value, 'tile', [(i, i ^ bits) for i in range(peers)])  15 us
    ppermute x13, waiting for transfers between devices, swap(): return lax.ppermute(value, 'tile', [(i, i ^ bits) for i in range(peers)])  8.16 us
    pallas_call x2, Pallas kernels, products_call(): pl.pallas_call(kernel, out_shape=tuple(results + [listed]), in_specs=[sme...  8.12 us
    pallas_call x2, Pallas kernels, finish(): pl.pallas_call(functools.partial(finish_kernel, half, takes), out_shape=j...  2.11 us
    pallas_call x1, Pallas kernels, add_ends(): pl.pallas_call(ends_kernel, out_shape=(jax.ShapeDtypeStruct(acc.shape, jn...  1.74 us
    ppermute x1, starting transfers between devices, staged(): after = lax.ppermute(low, 'tile', down)  1.67 us
    pallas_call x9, Pallas kernels, code(): pl.pallas_call(functools.partial(code_kernel, jobs), out_shape=tuple((jax...  1.33 us
  transfers between devices with their start and end apart: 15, of which 5 were waited for; matrix products, arithmetic and copies ran while one was open for 0% of the time, Pallas kernels for 28%

profile of v6, /device:TPU:0, one launch (start us, length us, event | category | flops | bytes accessed | tf_op | source)
XLA Modules:
  0.0 41.3 jit_solution(1893341626077288777)
XLA Ops:
  0.0 0.7 %fusion = (bf16[1,48,128]{2,1,0:T(8,128)(2,1)S(1)}, bf16[1,48,128]{2,1,0:T(8,128)(2,1)S(1)}) fusion(bf16[16,48,128]{2,1,0:T(8,128)(2,1)} %cot_hbm.3), kind=kLoop, calls=%fused_computation | loop fusion | bytes 49152 | tf_op jit(solution)/shard_map/slice | solution.py:394
  0.7 0.5 %collective-permute-start = (bf16[1,48,128]{2,1,0:T(8,128)(2,1)S(1)}, bf16[1,48,128]{2,1,0:T(8,128)(2,1)S(1)}, u32[]{:S(2)}, u32[]{:S(2)}) collective-permute-start(bf16[1,48,128]{2,1,0:T(8,128)(2,1)S(1)} %get-tuple-element.33), channel_id=1, source_target_pairs={{0,1},{1,2},{2,3},{3,4},{4,5},{5,6},{6,7},{7,8},{8,9},{9,10},{10,1... | collective-permute-start | bytes 36872 | tf_op jit(solution)/shard_map/ppermute | solution.py:394
  1.8 4.2 %shard_map.82 = (f32[257,48,128]{2,1,0:T(8,128)S(1)}, bf16[128,128,128]{2,1,0:T(8,128)(2,1)S(1)}, bf16[16,48,128]{2,1,0:T(8,128)(2,1)S(1)}, bf16[1,48,128]{2,1,0:T(8,128)(2,1)S(1)}, s32[4,132]{1,0:T(4,128)S(1)}) custom-call(s32[1]{0:T(128)S(6)} %copy.19.count_ref, s32[1]{0:T(128)} %bitcast.me_ref, s32[1,128]{1,0:T(1,128)} %tb.3, s32[1,128]{1,0:T(1,128)} %dest.3, ...), custom_call_target="tpu_custom_call" | custom-call | flops 268435456 | bytes 12582912 | tf_op jit(solution)/shard_map/pallas_call | solution.py:198
  6.0 1.7 %collective-permute-start.1 = (bf16[1,48,128]{2,1,0:T(8,128)(2,1)S(1)}, bf16[1,48,128]{2,1,0:T(8,128)(2,1)S(1)}, u32[]{:S(2)}, u32[]{:S(2)}) collective-permute-start(bf16[1,48,128]{2,1,0:T(8,128)(2,1)S(1)} %get-tuple-element.24), channel_id=1, source_target_pairs={{1,0},{2,1},{3,2},{4,3},{5,4},{6,5},{7,6},{8,7},{9,8},{10,9},{11,1... | collective-permute-start | bytes 36872 | tf_op jit(solution)/shard_map/ppermute | solution.py:396
  7.7 4.0 %shard_map.83 = (f32[257,48,128]{2,1,0:T(8,128)S(1)}, bf16[128,128,128]{2,1,0:T(8,128)(2,1)S(1)}, bf16[16,48,128]{2,1,0:T(8,128)(2,1)S(1)}, s32[4,132]{1,0:T(4,128)S(1)}) custom-call(s32[1]{0:T(128)S(6)} %copy.19.count_ref, s32[1]{0:T(128)} %bitcast.me_ref, s32[1,128]{1,0:T(1,128)} %tb.3, ...), custom_call_target="tpu_custom_call", output_to_operand_aliasing={{0}: (8, {}), {1}: (9, {}), {2}: (10, {})} | custom-call | flops 1 | bytes 1 | tf_op jit(solution)/shard_map/pallas_call | solution.py:198
  11.7 1.7 %shard_map.84 = (f32[257,48,128]{2,1,0:T(8,128)S(1)}, s16[8,400,128]{2,1,0:T(8,128)(2,1)S(1)}) custom-call(s32[4,132]{1,0:T(4,128)S(1)} %get-tuple-element.23.ends, bf16[1,48,128]{2,1,0:T(8,128)(2,1)S(1)} %collective-permute-done.before, bf16[1,48,128]{2,1,0:T(8,128)(2,1)S(1)} %collective-permute-done.1.after, ...), custom_call_target="tpu_custom_call", output_to_operand_aliasing={{0}: (4, {})} | custom-call | flops 1 | bytes 1 | tf_op jit(solution)/shard_map/pallas_call | solution.py:245
  13.5 0.4 %shard_map.85 = s16[8,400,128]{2,1,0:T(8,128)(2,1)S(1)} custom-call(f32[257,48,128]{2,1,0:T(8,128)S(1)} %get-tuple-element.27.acc), custom_call_target="tpu_custom_call" | custom-call | flops 1 | bytes 1 | tf_op jit(solution)/shard_map/pallas_call | solution.py:296
  13.9 0.6 %collective-permute-start.2 = (s16[8,400,128]{2,1,0:T(8,128)(2,1)S(1)}, s16[8,400,128]{2,1,0:T(8,128)(2,1)S(1)}, u32[]{:S(2)}, u32[]{:S(2)}) collective-permute-start(s16[8,400,128]{2,1,0:T(8,128)(2,1)S(1)} %shard_map.85), channel_id=1, source_target_pairs={{0,1},{1,0},{2,3},{3,2},{4,5},{5,4},{6,7},{7,6},{8,9},{9,8},{10,11... | collective-permute-start | bytes 2457608 | tf_op jit(solution)/shard_map/ppermute | solution.py:386
  14.5 1.3 %collective-permute-done.3.refs_0_.refs_2_ = s16[8,400,128]{2,1,0:T(8,128)(2,1)S(1)} collective-permute-done((s16[8,400,128]{2,1,0:T(8,128)(2,1)S(1)}, s16[8,400,128]{2,1,0:T(8,128)(2,1)S(1)}, u32[]{:S(2)}, u32[]{:S(2)}) %collective-permute-start.3) | collective-permute-done | bytes 819232 | tf_op jit(solution)/shard_map/ppermute | solution.py:386
  15.8 0.2 shard_map.86
  16.0 0.2 shard_map.87
  16.2 0.2 shard_map.89.refs_3_.refs_1_
  16.3 1.5 %collective-permute-start.7 = (s16[2,400,128]{2,1,0:T(8,128)(2,1)S(1)}, s16[2,400,128]{2,1,0:T(8,128)(2,1)S(1)}, u32[]{:S(2)}, u32[]{:S(2)}) collective-permute-start(s16[2,400,128]{2,1,0:T(8,128)(2,1)S(1)} %shard_map.89.refs_3_.refs_1_), channel_id=1, source_target_pairs={{0,4},{1,5},{2,6},{3,7},{4,0},{5,1},{6,2},{7,3},{8,12},{9,13},{10,... | collective-permute-start | bytes 614408 | tf_op jit(solution)/shard_map/ppermute | solution.py:386
  17.9 0.6 %collective-permute-start.11 = (s16[1,400,128]{2,1,0:T(8,128)(2,1)S(1)}, s16[1,400,128]{2,1,0:T(8,128)(2,1)S(1)}, u32[]{:S(2)}, u32[]{:S(2)}) collective-permute-start(s16[1,400,128]{2,1,0:T(8,128)(2,1)S(1)} %get-tuple-element.32), channel_id=1, source_target_pairs={{0,2},{1,3},{2,0},{3,1},{4,6},{5,7},{6,4},{7,5},{8,10},{9,11},{10,... | collective-permute-start | bytes 307208 | tf_op jit(solution)/shard_map/ppermute | solution.py:386
  18.5 3.2 %collective-permute-done.5.refs_1_ = s16[1,400,128]{2,1,0:T(8,128)(2,1)S(1)} collective-permute-done((s16[1,400,128]{2,1,0:T(8,128)(2,1)S(1)}, s16[1,400,128]{2,1,0:T(8,128)(2,1)S(1)}, u32[]{:S(2)}, u32[]{:S(2)}) %collective-permute-start.5) | collective-permute-done | bytes 102432 | tf_op jit(solution)/shard_map/ppermute | solution.py:386
  21.7 0.1 shard_map.88.refs_2_
  21.9 0.7 %collective-permute-start.4 = (s16[1,400,128]{2,1,0:T(8,128)(2,1)S(1)}, s16[1,400,128]{2,1,0:T(8,128)(2,1)S(1)}, u32[]{:S(2)}, u32[]{:S(2)}) collective-permute-start(s16[1,400,128]{2,1,0:T(8,128)(2,1)S(1)} %get-tuple-element.30.refs_1_), channel_id=1, source_target_pairs={{0,2},{1,3},{2,0},{3,1},{4,6},{5,7},{6,4},{7,5},{8,10},{9,11},{10,... | collective-permute-start | bytes 307208 | tf_op jit(solution)/shard_map/ppermute | solution.py:386
  22.6 1.4 %collective-permute-start.10 = (s16[1,400,128]{2,1,0:T(8,128)(2,1)S(1)}, s16[1,400,128]{2,1,0:T(8,128)(2,1)S(1)}, u32[]{:S(2)}, u32[]{:S(2)}) collective-permute-start(s16[1,400,128]{2,1,0:T(8,128)(2,1)S(1)} %get-tuple-element.31), channel_id=1, source_target_pairs={{0,2},{1,3},{2,0},{3,1},{4,6},{5,7},{6,4},{7,5},{8,10},{9,11},{10,... | collective-permute-start | bytes 307208 | tf_op jit(solution)/shard_map/ppermute | solution.py:386
  24.0 0.2 shard_map.93
  24.2 2.0 %collective-permute-start.9 = (s16[2,400,128]{2,1,0:T(8,128)(2,1)S(1)}, s16[2,400,128]{2,1,0:T(8,128)(2,1)S(1)}, u32[]{:S(2)}, u32[]{:S(2)}) collective-permute-start(s16[2,400,128]{2,1,0:T(8,128)(2,1)S(1)} %shard_map.93), channel_id=1, source_target_pairs={{0,4},{1,5},{2,6},{3,7},{4,0},{5,1},{6,2},{7,3},{8,12},{9,13},{10,... | collective-permute-start | bytes 614408 | tf_op jit(solution)/shard_map/ppermute | solution.py:386
  26.3 1.3 %collective-permute-done.6.refs_2_ = s16[1,400,128]{2,1,0:T(8,128)(2,1)S(1)} collective-permute-done((s16[1,400,128]{2,1,0:T(8,128)(2,1)S(1)}, s16[1,400,128]{2,1,0:T(8,128)(2,1)S(1)}, u32[]{:S(2)}, u32[]{:S(2)}) %collective-permute-start.6) | collective-permute-done | bytes 102432 | tf_op jit(solution)/shard_map/ppermute | solution.py:386
  27.6 0.2 shard_map.92
  27.8 1.0 %collective-permute-start.8 = (s16[2,400,128]{2,1,0:T(8,128)(2,1)S(1)}, s16[2,400,128]{2,1,0:T(8,128)(2,1)S(1)}, u32[]{:S(2)}, u32[]{:S(2)}) collective-permute-start(s16[2,400,128]{2,1,0:T(8,128)(2,1)S(1)} %shard_map.92), channel_id=1, source_target_pairs={{0,2},{1,3},{2,0},{3,1},{4,6},{5,7},{6,4},{7,5},{8,10},{9,11},{10,... | collective-permute-start | bytes 614408 | tf_op jit(solution)/shard_map/ppermute | solution.py:386
  28.9 0.1 shard_map.90.after.refs_3_
  29.0 3.9 %collective-permute-start.14 = (s16[1,400,128]{2,1,0:T(8,128)(2,1)S(1)}, s16[1,400,128]{2,1,0:T(8,128)(2,1)S(1)}, u32[]{:S(2)}, u32[]{:S(2)}) collective-permute-start(s16[1,400,128]{2,1,0:T(8,128)(2,1)S(1)} %shard_map.90.after.refs_3_), channel_id=1, source_target_pairs={{0,8},{1,9},{2,10},{3,11},{4,12},{5,13},{6,14},{7,15},{8,0},{9,1},... | collective-permute-start | bytes 307208 | tf_op jit(solution)/shard_map/ppermute | solution.py:386
  33.0 0.9 %collective-permute-done.12.refs_2_ = s16[1,400,128]{2,1,0:T(8,128)(2,1)S(1)} collective-permute-done((s16[1,400,128]{2,1,0:T(8,128)(2,1)S(1)}, s16[1,400,128]{2,1,0:T(8,128)(2,1)S(1)}, u32[]{:S(2)}, u32[]{:S(2)}) %collective-permute-start.12) | collective-permute-done | bytes 102432 | tf_op jit(solution)/shard_map/ppermute | solution.py:386
  33.8 0.1 shard_map.95
  34.0 3.0 %collective-permute-start.13 = (s16[1,400,128]{2,1,0:T(8,128)(2,1)S(1)}, s16[1,400,128]{2,1,0:T(8,128)(2,1)S(1)}, u32[]{:S(2)}, u32[]{:S(2)}) collective-permute-start(s16[1,400,128]{2,1,0:T(8,128)(2,1)S(1)} %shard_map.95), channel_id=1, source_target_pairs={{0,8},{1,9},{2,10},{3,11},{4,12},{5,13},{6,14},{7,15},{8,0},{9,1},... | collective-permute-start | bytes 307208 | tf_op jit(solution)/shard_map/ppermute | solution.py:386
  37.0 0.7 %shard_map.91.left = bf16[120,192]{1,0:T(8,128)(2,1)S(1)} custom-call(s32[8]{0:T(128)S(1)} %copy-done, f32[8]{0:T(128)S(1)} %copy-done.1, s16[1,400,128]{2,1,0:T(8,128)(2,1)S(1)} %shard_map.90.after.refs_3_), custom_call_target="tpu_custom_call" | custom-call | flops 1 | bytes 1 | tf_op jit(solution)/shard_map/pallas_call | solution.py:326
  37.8 1.1 %shard_map.96.refs_4_ = f32[16,120,128]{2,1,0:T(8,128)} custom-call(bf16[120,192]{1,0:T(8,128)(2,1)S(1)} %shard_map.91.left, f32[257,48,128]{2,1,0:T(8,128)S(1)} %get-tuple-element.27.acc, s16[8,400,128]{2,1,0:T(8,128)(2,1)S(1)} %collective-permute-done.2.refs_0_, s16[2,400,128]{2,1,0:T(8,128)(2,1)S(1)} %collective-permute-done.8.refs_1_, ...), custom_call_target="tpu_custom_call" | custom-call | flops 1 | bytes 1 | tf_op jit(solution)/shard_map/pallas_call | solution.py:365
  38.8 1.4 %collective-permute-done.13.refs_3_ = s16[1,400,128]{2,1,0:T(8,128)(2,1)S(1)} collective-permute-done((s16[1,400,128]{2,1,0:T(8,128)(2,1)S(1)}, s16[1,400,128]{2,1,0:T(8,128)(2,1)S(1)}, u32[]{:S(2)}, u32[]{:S(2)}) %collective-permute-start.13) | collective-permute-done | bytes 102432 | tf_op jit(solution)/shard_map/ppermute | solution.py:386
  40.3 1.1 %shard_map.97 = f32[16,120,128]{2,1,0:T(8,128)} custom-call(bf16[120,192]{1,0:T(8,128)(2,1)S(1)} %shard_map.91.left, f32[257,48,128]{2,1,0:T(8,128)S(1)} %get-tuple-element.27.acc, s16[8,400,128]{2,1,0:T(8,128)(2,1)S(1)} %collective-permute-done.2.refs_0_, s16[2,400,128]{2,1,0:T(8,128)(2,1)S(1)} %collective-permute-done.8.refs_1_, ...), custom_call_target="tpu_custom_call", output_to_operand_aliasing={{}: (6, {})} | custom-call | flops 1 | bytes 1 | tf_op jit(solution)/shard_map/pallas_call | solution.py:365
  (19 shorter events, 0.4 us)
Async XLA Ops:
  0.7 10.9 %collective-permute-start = (bf16[1,48,128]{2,1,0:T(8,128)(2,1)S(1)}, bf16[1,48,128]{2,1,0:T(8,128)(2,1)S(1)}, u32[]{:S(2)}, u32[]{:S(2)}) collective-permute-start(bf16[1,48,128]{2,1,0:T(8,128)(2,1)S(1)} %get-tuple-element.33), channel_id=1, source_target_pairs={{0,1},{1,2},{2,3},{3,4},{4,5},{5,6},{6,7},{7,8},{8,9},{9,10},{10,1... | collective-permute-start | bytes 36872 | tf_op jit(solution)/shard_map/ppermute | solution.py:394
  6.0 5.6 %collective-permute-start.1 = (bf16[1,48,128]{2,1,0:T(8,128)(2,1)S(1)}, bf16[1,48,128]{2,1,0:T(8,128)(2,1)S(1)}, u32[]{:S(2)}, u32[]{:S(2)}) collective-permute-start(bf16[1,48,128]{2,1,0:T(8,128)(2,1)S(1)} %get-tuple-element.24), channel_id=1, source_target_pairs={{1,0},{2,1},{3,2},{4,3},{5,4},{6,5},{7,6},{8,7},{9,8},{10,9},{11,1... | collective-permute-start | bytes 36872 | tf_op jit(solution)/shard_map/ppermute | solution.py:396
  13.4 2.4 %collective-permute-start.3 = (s16[8,400,128]{2,1,0:T(8,128)(2,1)S(1)}, s16[8,400,128]{2,1,0:T(8,128)(2,1)S(1)}, u32[]{:S(2)}, u32[]{:S(2)}) collective-permute-start(s16[8,400,128]{2,1,0:T(8,128)(2,1)S(1)} %get-tuple-element.28), channel_id=1, source_target_pairs={{0,1},{1,0},{2,3},{3,2},{4,5},{5,4},{6,7},{7,6},{8,9},{9,8},{10,11... | collective-permute-start | bytes 2457608 | tf_op jit(solution)/shard_map/ppermute | solution.py:386
  13.9 4.6 %collective-permute-start.2 = (s16[8,400,128]{2,1,0:T(8,128)(2,1)S(1)}, s16[8,400,128]{2,1,0:T(8,128)(2,1)S(1)}, u32[]{:S(2)}, u32[]{:S(2)}) collective-permute-start(s16[8,400,128]{2,1,0:T(8,128)(2,1)S(1)} %shard_map.85), channel_id=1, source_target_pairs={{0,1},{1,0},{2,3},{3,2},{4,5},{5,4},{6,7},{7,6},{8,9},{9,8},{10,11... | collective-permute-start | bytes 2457608 | tf_op jit(solution)/shard_map/ppermute | solution.py:386
  16.0 5.8 %collective-permute-start.5 = (s16[1,400,128]{2,1,0:T(8,128)(2,1)S(1)}, s16[1,400,128]{2,1,0:T(8,128)(2,1)S(1)}, u32[]{:S(2)}, u32[]{:S(2)}) collective-permute-start(s16[1,400,128]{2,1,0:T(8,128)(2,1)S(1)} %get-tuple-element.29.refs_1_), channel_id=1, source_target_pairs={{0,2},{1,3},{2,0},{3,1},{4,6},{5,7},{6,4},{7,5},{8,10},{9,11},{10,... | collective-permute-start | bytes 307208 | tf_op jit(solution)/shard_map/ppermute | solution.py:386
  16.3 11.3 %collective-permute-start.7 = (s16[2,400,128]{2,1,0:T(8,128)(2,1)S(1)}, s16[2,400,128]{2,1,0:T(8,128)(2,1)S(1)}, u32[]{:S(2)}, u32[]{:S(2)}) collective-permute-start(s16[2,400,128]{2,1,0:T(8,128)(2,1)S(1)} %shard_map.89.refs_3_.refs_1_), channel_id=1, source_target_pairs={{0,4},{1,5},{2,6},{3,7},{4,0},{5,1},{6,2},{7,3},{8,12},{9,13},{10,... | collective-permute-start | bytes 614408 | tf_op jit(solution)/shard_map/ppermute | solution.py:386
  17.9 6.3 %collective-permute-start.11 = (s16[1,400,128]{2,1,0:T(8,128)(2,1)S(1)}, s16[1,400,128]{2,1,0:T(8,128)(2,1)S(1)}, u32[]{:S(2)}, u32[]{:S(2)}) collective-permute-start(s16[1,400,128]{2,1,0:T(8,128)(2,1)S(1)} %get-tuple-element.32), channel_id=1, source_target_pairs={{0,2},{1,3},{2,0},{3,1},{4,6},{5,7},{6,4},{7,5},{8,10},{9,11},{10,... | collective-permute-start | bytes 307208 | tf_op jit(solution)/shard_map/ppermute | solution.py:386
  21.9 5.7 %collective-permute-start.6 = (s16[1,400,128]{2,1,0:T(8,128)(2,1)S(1)}, s16[1,400,128]{2,1,0:T(8,128)(2,1)S(1)}, u32[]{:S(2)}, u32[]{:S(2)}) collective-permute-start(s16[1,400,128]{2,1,0:T(8,128)(2,1)S(1)} %shard_map.88.refs_2_), channel_id=1, source_target_pairs={{0,4},{1,5},{2,6},{3,7},{4,0},{5,1},{6,2},{7,3},{8,12},{9,13},{10,... | collective-permute-start | bytes 307208 | tf_op jit(solution)/shard_map/ppermute | solution.py:386
  21.9 6.9 %collective-permute-start.4 = (s16[1,400,128]{2,1,0:T(8,128)(2,1)S(1)}, s16[1,400,128]{2,1,0:T(8,128)(2,1)S(1)}, u32[]{:S(2)}, u32[]{:S(2)}) collective-permute-start(s16[1,400,128]{2,1,0:T(8,128)(2,1)S(1)} %get-tuple-element.30.refs_1_), channel_id=1, source_target_pairs={{0,2},{1,3},{2,0},{3,1},{4,6},{5,7},{6,4},{7,5},{8,10},{9,11},{10,... | collective-permute-start | bytes 307208 | tf_op jit(solution)/shard_map/ppermute | solution.py:386
  22.6 10.4 %collective-permute-start.10 = (s16[1,400,128]{2,1,0:T(8,128)(2,1)S(1)}, s16[1,400,128]{2,1,0:T(8,128)(2,1)S(1)}, u32[]{:S(2)}, u32[]{:S(2)}) collective-permute-start(s16[1,400,128]{2,1,0:T(8,128)(2,1)S(1)} %get-tuple-element.31), channel_id=1, source_target_pairs={{0,2},{1,3},{2,0},{3,1},{4,6},{5,7},{6,4},{7,5},{8,10},{9,11},{10,... | collective-permute-start | bytes 307208 | tf_op jit(solution)/shard_map/ppermute | solution.py:386
  24.2 13.5 %collective-permute-start.9 = (s16[2,400,128]{2,1,0:T(8,128)(2,1)S(1)}, s16[2,400,128]{2,1,0:T(8,128)(2,1)S(1)}, u32[]{:S(2)}, u32[]{:S(2)}) collective-permute-start(s16[2,400,128]{2,1,0:T(8,128)(2,1)S(1)} %shard_map.93), channel_id=1, source_target_pairs={{0,4},{1,5},{2,6},{3,7},{4,0},{5,1},{6,2},{7,3},{8,12},{9,13},{10,... | collective-permute-start | bytes 614408 | tf_op jit(solution)/shard_map/ppermute | solution.py:386
  27.6 6.2 %collective-permute-start.12 = (s16[1,400,128]{2,1,0:T(8,128)(2,1)S(1)}, s16[1,400,128]{2,1,0:T(8,128)(2,1)S(1)}, u32[]{:S(2)}, u32[]{:S(2)}) collective-permute-start(s16[1,400,128]{2,1,0:T(8,128)(2,1)S(1)} %shard_map.94), channel_id=1, source_target_pairs={{0,4},{1,5},{2,6},{3,7},{4,0},{5,1},{6,2},{7,3},{8,12},{9,13},{10,... | collective-permute-start | bytes 307208 | tf_op jit(solution)/shard_map/ppermute | solution.py:386
  27.8 9.2 %copy-start = (s32[8]{0:T(128)S(1)}, s32[8]{0:T(128)}, u32[]{:S(2)}) copy-start(s32[8]{0:T(128)} %index_ref.1) | copy-start | bytes 100
  27.8 9.2 %copy-start.1 = (f32[8]{0:T(128)S(1)}, f32[8]{0:T(128)}, u32[]{:S(2)}) copy-start(f32[8]{0:T(128)} %frac_ref.1) | copy-start | bytes 100
  27.8 9.9 %collective-permute-start.8 = (s16[2,400,128]{2,1,0:T(8,128)(2,1)S(1)}, s16[2,400,128]{2,1,0:T(8,128)(2,1)S(1)}, u32[]{:S(2)}, u32[]{:S(2)}) collective-permute-start(s16[2,400,128]{2,1,0:T(8,128)(2,1)S(1)} %shard_map.92), channel_id=1, source_target_pairs={{0,2},{1,3},{2,0},{3,1},{4,6},{5,7},{6,4},{7,5},{8,10},{9,11},{10,... | collective-permute-start | bytes 614408 | tf_op jit(solution)/shard_map/ppermute | solution.py:386
  29.0 8.7 %collective-permute-start.14 = (s16[1,400,128]{2,1,0:T(8,128)(2,1)S(1)}, s16[1,400,128]{2,1,0:T(8,128)(2,1)S(1)}, u32[]{:S(2)}, u32[]{:S(2)}) collective-permute-start(s16[1,400,128]{2,1,0:T(8,128)(2,1)S(1)} %shard_map.90.after.refs_3_), channel_id=1, source_target_pairs={{0,8},{1,9},{2,10},{3,11},{4,12},{5,13},{6,14},{7,15},{8,0},{9,1},... | collective-permute-start | bytes 307208 | tf_op jit(solution)/shard_map/ppermute | solution.py:386
  34.0 6.3 %collective-permute-start.13 = (s16[1,400,128]{2,1,0:T(8,128)(2,1)S(1)}, s16[1,400,128]{2,1,0:T(8,128)(2,1)S(1)}, u32[]{:S(2)}, u32[]{:S(2)}) collective-permute-start(s16[1,400,128]{2,1,0:T(8,128)(2,1)S(1)} %shard_map.95), channel_id=1, source_target_pairs={{0,8},{1,9},{2,10},{3,11},{4,12},{5,13},{6,14},{7,15},{8,0},{9,1},... | collective-permute-start | bytes 307208 | tf_op jit(solution)/shard_map/ppermute | solution.py:386

commit v7 on v6

--- a/solution.py
+++ b/solution.py
@@ -45,35 +45,28 @@
 TRASH = 16 * SB
 
 
-def add_products(entries, w, acc):
-    found = [jnp.dot(left, w[e], preferred_element_type=jnp.float32) for e, left, _ in entries]
-    for (_, _, at), value in zip(entries, found):
-        acc[at] = acc[at] + value
-
-
-def add_group(g, count, me, tables, cot, w, acc, ends):
+def add_group(g, count, me, tables, cot, w, acc, ends, add, listing):
     blocks = cot.shape[0]
-
-    @pl.loop(0, GROUP // 8)
-    def _(part):
-        n = ends[3, 0]
-        entries = []
-        for i in range(8):
-            k = g * GROUP + part * 8 + i
-            block = tables[0, k]
-            rel = tables[1, k] ^ me
-            slot = (rel & 1) * 8 + ((rel >> 1) & 1) * 4 + (rel >> 2)
-            live = k < count
-            at = jnp.where(live, slot * SB + tables[2, k], TRASH)
-            outer = (block == 0) | (block == blocks + 1)
+    n = ends[3, 0] if listing else None
+    for i in range(GROUP):
+        k = g * GROUP + i
+        block = tables[0, k]
+        rel = tables[1, k] ^ me
+        slot = (rel & 1) * 8 + ((rel >> 1) & 1) * 4 + (rel >> 2)
+        live = k < count
+        at = jnp.where(live, slot * SB + tables[2, k], TRASH)
+        outer = (block == 0) | (block == blocks + 1)
+        if listing:
             ends[0, n] = k
             ends[1, n] = at
             ends[2, n] = jnp.where(block == 0, 0, 1)
             n = n + (outer & live).astype(jnp.int32)
+        if add:
+            at = jnp.where(outer, TRASH, at)
             left = cot[jnp.clip(block - 1, 0, blocks - 1)]
-            entries.append((k, left, jnp.where(outer, TRASH, at)))
+            acc[at] = acc[at] + jnp.dot(left, w[k], preferred_element_type=jnp.float32)
+    if listing:
         ends[3, 0] = n
-        add_products(entries, w, acc)
 
 
 def groups_of(count):
@@ -106,7 +99,7 @@
 
 
 def ahead_kernel(
-    count_ref, me_ref, tb, dest, src, cot_hbm, w_hbm, low_in, acc, w, cot, low, ends, *scratch
+    count_ref, me_ref, tb, dest, src, cot_hbm, w_hbm, low_in, acc, w, cot, low, *scratch
 ):
     tables, sems, w_sems = scratch
     used, half = groups_of(count_ref[0])
@@ -117,7 +110,6 @@
         pairs = [(cot_hbm, cot)]
         pairs += [(t, tables.at[pl.ds(i, 1)]) for i, t in enumerate((tb, dest, src))]
         w_copy = load(used, pairs, w_hbm, w, acc, sems, w_sems)
-        ends[3, 0] = 0
         for g in range(w.shape[0] // GROUP):
 
             @pl.when(g < used)
@@ -126,17 +118,15 @@
 
             @pl.when(g < half)
             def _():
-                add_group(g, count_ref[0], me_ref[0], tables, cot, w, acc, ends)
-
-
-def rest_kernel(
-    count_ref, me_ref, tb, dest, src, cot_hbm, w_hbm, begun, acc_in, w_in, cot_in, *refs
-):
+                add_group(g, count_ref[0], me_ref[0], tables, cot, w, acc, None, True, False)
+
+
+def rest_kernel(count_ref, me_ref, tb, dest, src, cot_hbm, w_hbm, acc_in, w_in, cot_in, *refs):
     acc, w, cot, ends, tables, sems, w_sems = refs
     used, half = groups_of(count_ref[0])
     early = me_ref[0] == 0
     done = jnp.where(early, half, 0)
-    listed = jnp.where(early, begun[3, 0], 0)
+    ends[3, 0] = 0
     three = [(t, tables.at[pl.ds(i, 1)]) for i, t in enumerate((tb, dest, src))]
 
     @pl.when(early)
@@ -151,12 +141,9 @@
     def _():
         load(used, three + [(cot_hbm, cot)], w_hbm, w, acc, sems, w_sems)
 
-    @pl.loop(0, listed)
-    def _(n):
-        for i in range(3):
-            ends[i, n] = begun[i, n]
-
-    ends[3, 0] = listed
+    @pl.loop(0, done)
+    def _(g):
+        add_group(g, count_ref[0], me_ref[0], tables, cot, w, acc, ends, False, True)
 
     for g in range(w.shape[0] // GROUP):
 
@@ -167,10 +154,10 @@
 
         @pl.when((g >= done) & (g < used))
         def _():
-            add_group(g, count_ref[0], me_ref[0], tables, cot, w, acc, ends)
+            add_group(g, count_ref[0], me_ref[0], tables, cot, w, acc, ends, True, True)
 
     listed = ends[3, 0]
-    for i in range(4):
+    for i in range(8):
         ends[0, listed + i] = 0
         ends[1, listed + i] = TRASH
         ends[2, listed + i] = 0
@@ -191,21 +178,20 @@
         jax.ShapeDtypeStruct(weight.shape, weight.dtype),
         jax.ShapeDtypeStruct(cotangent.shape, cotangent.dtype),
     ]
-    listed = jax.ShapeDtypeStruct((4, entries + 4), jnp.int32)
     first = not given
-    if first:
-        results.append(jax.ShapeDtypeStruct(low.shape, low.dtype))
+    last = low if first else jax.ShapeDtypeStruct((4, entries + 8), jnp.int32)
+    results.append(jax.ShapeDtypeStruct(last.shape, last.dtype))
     return pl.pallas_call(
         kernel,
-        out_shape=tuple(results + [listed]),
-        in_specs=[smem, smem] + [hbm] * 5 + ([vmem] if first else [smem] + [vmem] * 3),
-        out_specs=(vmem,) * len(results) + (smem,),
+        out_shape=tuple(results),
+        in_specs=[smem, smem] + [hbm] * 5 + [vmem] * (1 if first else 3),
+        out_specs=(vmem,) * 3 + (vmem if first else smem,),
         scratch_shapes=[
             pltpu.SMEM((3, entries), jnp.int32),
             pltpu.SemaphoreType.DMA((4,)),
             pltpu.SemaphoreType.DMA((entries // GROUP,)),
         ],
-        input_output_aliases={} if first else {8: 0, 9: 1, 10: 2},
+        input_output_aliases={} if first else {7: 0, 8: 1, 9: 2},
         compiler_params=pltpu.CompilerParams(vmem_limit_bytes=24 * MIB),
         cost_estimate=cost,
     )(*operands[:2], *[in_hbm(x) for x in operands[2:]], *([low] if first else given))
@@ -228,10 +214,13 @@
     sides[0] = before[0]
     sides[1] = after[0]
 
-    @pl.loop(0, (ends[3, 0] + 3) // 4)
+    @pl.loop(0, (ends[3, 0] + 7) // 8)
     def _(part):
-        at = [part * 4 + i for i in range(4)]
-        add_products([(ends[0, k], sides[ends[2, k]], ends[1, k]) for k in at], w, acc)
+        for i in range(8):
+            k = part * 8 + i
+            at = ends[1, k]
+            left = sides[ends[2, k]]
+            acc[at] = acc[at] + jnp.dot(left, w[ends[0, k]], preferred_element_type=jnp.float32)
 
     @pl.loop(0, 8)
     def _(i):
@@ -373,7 +362,7 @@
         ],
         input_output_aliases={2 + len(arrays): 0} if extra else {},
         compiler_params=pltpu.CompilerParams(vmem_limit_bytes=32 * MIB),
-        cost_estimate=LITTLE,
+        cost_estimate=pl.CostEstimate(flops=1, bytes_accessed=4194304, transcendentals=0),
     )(left, acc, *arrays, *extra)
 
 
@@ -392,9 +381,9 @@
     operands = (count, me, target_block, dest, source, cotangent, weight)
     up, down = ring(peers)
     before = lax.ppermute(cotangent[-1:], "tile", up)
-    acc, w, cot, low, ends = products_call(ahead_kernel, operands, (), cotangent[:1], MUCH)
+    acc, w, cot, low = products_call(ahead_kernel, operands, (), cotangent[:1], MUCH)
     after = lax.ppermute(low, "tile", down)
-    acc, w, cot, ends = products_call(rest_kernel, operands, (ends, acc, w, cot), None, LITTLE)
+    acc, w, cot, ends = products_call(rest_kernel, operands, (acc, w, cot), None, LITTLE)
     acc, far = add_ends(ends, before, after, w, acc)
     far = swap(far, 1, peers)
     near = swap(code_near(acc), 1, peers)
@@ -409,16 +398,17 @@
     a3 = [swap(a3_low, 4, peers), swap(a3_high, 4, peers)]
     (y1_own,) = code(acc, (((10, ((0, 2),)), (11, ((0, 3),))),), (far, y2_own))
     o1 = swap(y1_own, 4, peers)
-    (b2_low,) = code(acc, (((4, ((0, 4), (1, 0), (2, 0))),),), (near, y2[0], a3[0], y1_own))
+    (b2_low,) = code(acc, (((4, ((0, 4), (1, 0), (2, 0))),),), (near, y2[0], a3[0], far))
     (b2_high,) = code(acc, (((5, ((0, 5), (1, 0), (2, 0))),),), (near, y2[1], a3[1], b2_low))
     b2 = [swap(b2_low, 8, peers), swap(b2_high, 8, peers)]
-    (y0_own,) = code(acc, (((8, ((0, 0), (1, 0))), (9, ((0, 1), (1, 1)))),), (far, o1, a3[0]))
-    y0 = swap(y0_own, 2, peers)
-    (a1_own,) = code(acc, (((2, ((0, 2),)), (3, ((0, 3),))),), (near, y1_own))
+    y0_own = code(acc, (((8, ((0, 0), (1, 0))),), ((9, ((0, 1), (1, 1))),)), (far, o1, b2_low))
+    y0 = [swap(v, 2, peers) for v in y0_own]
+    y0_own = y0_own[0]
+    (a1_own,) = code(acc, (((2, ((0, 2),)), (3, ((0, 3),))),), (near, a3_high))
     a1 = swap(a1_own, 4, peers)
-    left = lift_matrix(lev_index, lev_frac, b2_low)
-    out = finish(0, left, acc, ((0, 0), (1, 0), (2, 0), (3, 0)), (near, y0, a1, b2[0]))
-    return finish(1, left, acc, ((0, 1), (1, 1), (2, 1), (3, 0)), (near, y0, a1, b2[1]), out)
+    left = lift_matrix(lev_index, lev_frac, b2_high)
+    out = finish(0, left, acc, ((0, 0), (1, 0), (2, 0), (3, 0)), (near, y0[0], a1, b2[0]))
+    return finish(1, left, acc, ((0, 1), (1, 0), (2, 1), (3, 0)), (near, y0[1], a1, b2[1]), out)
 
 
 def vertical_matrix(lev_index, lev_frac, levels):

time: 42 us -> 39.5 us (0.940); the launches traced: 41.3 us -> 39.2 us
  waiting for transfers between devices: 8.17 us -> 13.2 us
  starting transfers between devices: 17.1 us -> 12.1 us
  Pallas kernels: 14.5 us -> 12.4 us
    ppermute x13 -> x14, starting transfers between devices: 15 us -> 9.33 us  [swap(): return lax.ppermute(value, 'tile', [(i, i ^ bits) for i in range(peers)])]
    ppermute x13 -> x14, waiting for transfers between devices: 8.16 us -> 13.2 us  [swap(): return lax.ppermute(value, 'tile', [(i, i ^ bits) for i in range(peers)])]
    pallas_call x2, Pallas kernels: 8.12 us -> 6.38 us  [products_call(): pl.pallas_call(kernel, out_shape=tuple(results), in_specs=[smem, smem] +...]
    ppermute x1, starting transfers between devices: 1.67 us -> 2.27 us  [staged(): after = lax.ppermute(low, 'tile', down)]
  transfers between devices with their start and end apart: 15 -> 16, of which waited for: 5 -> 7; matrix products, arithmetic and copies ran while one was open for 0% -> 0% of each run, Pallas kernels for 28% -> 25%
where the time goes in v7:
time: 39.5 us; the launch traced here: 39.2 us
  waiting for transfers between devices  13.2 us (33%)
  Pallas kernels  12.4 us (31%)
  starting transfers between devices  12.1 us (31%)
  between operations  0.8 us (2%)
  local copies, waits for them, and re-layouts  0.74 us (2%)
    ppermute x14, waiting for transfers between devices, swap(): return lax.ppermute(value, 'tile', [(i, i ^ bits) for i in range(peers)])  13.2 us
    ppermute x14, starting transfers between devices, swap(): return lax.ppermute(value, 'tile', [(i, i ^ bits) for i in range(peers)])  9.33 us
    pallas_call x2, Pallas kernels, products_call(): pl.pallas_call(kernel, out_shape=tuple(results), in_specs=[smem, smem] +...  6.38 us
    ppermute x1, starting transfers between devices, staged(): after = lax.ppermute(low, 'tile', down)  2.27 us
    pallas_call x2, Pallas kernels, finish(): pl.pallas_call(functools.partial(finish_kernel, half, takes), out_shape=j...  2.1 us
    pallas_call x1, Pallas kernels, add_ends(): pl.pallas_call(ends_kernel, out_shape=(jax.ShapeDtypeStruct(acc.shape, jn...  1.48 us
    pallas_call x9, Pallas kernels, code(): pl.pallas_call(functools.partial(code_kernel, jobs), out_shape=tuple((jax...  1.32 us
  transfers between devices with their start and end apart: 16, of which 7 were waited for; matrix products, arithmetic and copies ran while one was open for 0% of the time, Pallas kernels for 25%

profile of v7, /device:TPU:0, one launch (start us, length us, event | category | flops | bytes accessed | tf_op | source)
XLA Modules:
  0.0 39.2 jit_solution(14875917146880545649)
XLA Ops:
  0.0 0.7 %fusion = (bf16[1,48,128]{2,1,0:T(8,128)(2,1)S(1)}, bf16[1,48,128]{2,1,0:T(8,128)(2,1)S(1)}) fusion(bf16[16,48,128]{2,1,0:T(8,128)(2,1)} %cot_hbm.3), kind=kLoop, calls=%fused_computation | loop fusion | bytes 49152 | tf_op jit(solution)/shard_map/slice | solution.py:383
  0.7 0.5 %collective-permute-start = (bf16[1,48,128]{2,1,0:T(8,128)(2,1)S(1)}, bf16[1,48,128]{2,1,0:T(8,128)(2,1)S(1)}, u32[]{:S(2)}, u32[]{:S(2)}) collective-permute-start(bf16[1,48,128]{2,1,0:T(8,128)(2,1)S(1)} %get-tuple-element.35), channel_id=1, source_target_pairs={{0,1},{1,2},{2,3},{3,4},{4,5},{5,6},{6,7},{7,8},{8,9},{9,10},{10,1... | collective-permute-start | bytes 36872 | tf_op jit(solution)/shard_map/ppermute | solution.py:383
  1.8 2.9 %shard_map.82 = (f32[257,48,128]{2,1,0:T(8,128)S(1)}, bf16[128,128,128]{2,1,0:T(8,128)(2,1)S(1)}, bf16[16,48,128]{2,1,0:T(8,128)(2,1)S(1)}, bf16[1,48,128]{2,1,0:T(8,128)(2,1)S(1)}) custom-call(s32[1]{0:T(128)S(6)} %copy.19.count_ref, s32[1]{0:T(128)} %bitcast.me_ref, s32[1,128]{1,0:T(1,128)} %tb.3, s32[1,128]{1,0:T(1,128)} %dest.3, s32[1,128]{1,0:T(1,128)} %src.3, ...), custom_call_target="tpu_custom_call" | custom-call | flops 268435456 | bytes 12582912 | tf_op jit(solution)/shard_map/pallas_call | solution.py:184
  4.7 2.3 %collective-permute-start.1 = (bf16[1,48,128]{2,1,0:T(8,128)(2,1)S(1)}, bf16[1,48,128]{2,1,0:T(8,128)(2,1)S(1)}, u32[]{:S(2)}, u32[]{:S(2)}) collective-permute-start(bf16[1,48,128]{2,1,0:T(8,128)(2,1)S(1)} %get-tuple-element.24), channel_id=1, source_target_pairs={{1,0},{2,1},{3,2},{4,3},{5,4},{6,5},{7,6},{8,7},{9,8},{10,9},{11,1... | collective-permute-start | bytes 36872 | tf_op jit(solution)/shard_map/ppermute | solution.py:385
  7.0 3.5 %shard_map.83 = (f32[257,48,128]{2,1,0:T(8,128)S(1)}, bf16[128,128,128]{2,1,0:T(8,128)(2,1)S(1)}, bf16[16,48,128]{2,1,0:T(8,128)(2,1)S(1)}, s32[4,136]{1,0:T(4,128)S(1)}) custom-call(s32[1]{0:T(128)S(6)} %copy.19.count_ref, s32[1]{0:T(128)} %bitcast.me_ref, s32[1,128]{1,0:T(1,128)} %tb.3, ...), custom_call_target="tpu_custom_call", output_to_operand_aliasing={{0}: (7, {}), {1}: (8, {}), {2}: (9, {})} | custom-call | flops 1 | bytes 1 | tf_op jit(solution)/shard_map/pallas_call | solution.py:184
  10.5 1.5 %shard_map.84 = (f32[257,48,128]{2,1,0:T(8,128)S(1)}, s16[8,400,128]{2,1,0:T(8,128)(2,1)S(1)}) custom-call(s32[4,136]{1,0:T(4,128)S(1)} %get-tuple-element.23.ends, bf16[1,48,128]{2,1,0:T(8,128)(2,1)S(1)} %collective-permute-done.before, bf16[1,48,128]{2,1,0:T(8,128)(2,1)S(1)} %collective-permute-done.1.after, ...), custom_call_target="tpu_custom_call", output_to_operand_aliasing={{0}: (4, {})} | custom-call | flops 1 | bytes 1 | tf_op jit(solution)/shard_map/pallas_call | solution.py:234
  12.1 0.4 %shard_map.85 = s16[8,400,128]{2,1,0:T(8,128)(2,1)S(1)} custom-call(f32[257,48,128]{2,1,0:T(8,128)S(1)} %get-tuple-element.27.acc), custom_call_target="tpu_custom_call" | custom-call | flops 1 | bytes 1 | tf_op jit(solution)/shard_map/pallas_call | solution.py:285
  12.5 0.6 %collective-permute-start.2 = (s16[8,400,128]{2,1,0:T(8,128)(2,1)S(1)}, s16[8,400,128]{2,1,0:T(8,128)(2,1)S(1)}, u32[]{:S(2)}, u32[]{:S(2)}) collective-permute-start(s16[8,400,128]{2,1,0:T(8,128)(2,1)S(1)} %shard_map.85), channel_id=1, source_target_pairs={{0,1},{1,0},{2,3},{3,2},{4,5},{5,4},{6,7},{7,6},{8,9},{9,8},{10,11... | collective-permute-start | bytes 2457608 | tf_op jit(solution)/shard_map/ppermute | solution.py:375
  13.1 1.3 %collective-permute-done.3.refs_0_.refs_2_.refs_3_ = s16[8,400,128]{2,1,0:T(8,128)(2,1)S(1)} collective-permute-done((s16[8,400,128]{2,1,0:T(8,128)(2,1)S(1)}, s16[8,400,128]{2,1,0:T(8,128)(2,1)S(1)}, u32[]{:S(2)}, u32[]{:S(2)}) %collective-permute-start.3) | collective-permute-done | bytes 819232 | tf_op jit(solution)/shard_map/ppermute | solution.py:375
  14.4 0.1 shard_map.86
  14.6 0.2 shard_map.87
  14.8 0.2 shard_map.93
  14.9 0.8 %collective-permute-start.10 = (s16[2,400,128]{2,1,0:T(8,128)(2,1)S(1)}, s16[2,400,128]{2,1,0:T(8,128)(2,1)S(1)}, u32[]{:S(2)}, u32[]{:S(2)}) collective-permute-start(s16[2,400,128]{2,1,0:T(8,128)(2,1)S(1)} %shard_map.93), channel_id=1, source_target_pairs={{0,4},{1,5},{2,6},{3,7},{4,0},{5,1},{6,2},{7,3},{8,12},{9,13},{10,... | collective-permute-start | bytes 614408 | tf_op jit(solution)/shard_map/ppermute | solution.py:375
  15.7 1.4 %collective-permute-start.5 = (s16[1,400,128]{2,1,0:T(8,128)(2,1)S(1)}, s16[1,400,128]{2,1,0:T(8,128)(2,1)S(1)}, u32[]{:S(2)}, u32[]{:S(2)}) collective-permute-start(s16[1,400,128]{2,1,0:T(8,128)(2,1)S(1)} %get-tuple-element.31), channel_id=1, source_target_pairs={{0,2},{1,3},{2,0},{3,1},{4,6},{5,7},{6,4},{7,5},{8,10},{9,11},{10,... | collective-permute-start | bytes 307208 | tf_op jit(solution)/shard_map/ppermute | solution.py:375
  17.1 0.6 %collective-permute-start.8 = (s16[1,400,128]{2,1,0:T(8,128)(2,1)S(1)}, s16[1,400,128]{2,1,0:T(8,128)(2,1)S(1)}, u32[]{:S(2)}, u32[]{:S(2)}) collective-permute-start(s16[1,400,128]{2,1,0:T(8,128)(2,1)S(1)} %get-tuple-element.32.refs_1_), channel_id=1, source_target_pairs={{0,2},{1,3},{2,0},{3,1},{4,6},{5,7},{6,4},{7,5},{8,10},{9,11},{10,... | collective-permute-start | bytes 307208 | tf_op jit(solution)/shard_map/ppermute | solution.py:375
  17.7 2.6 %collective-permute-done.6.refs_1_ = s16[1,400,128]{2,1,0:T(8,128)(2,1)S(1)} collective-permute-done((s16[1,400,128]{2,1,0:T(8,128)(2,1)S(1)}, s16[1,400,128]{2,1,0:T(8,128)(2,1)S(1)}, u32[]{:S(2)}, u32[]{:S(2)}) %collective-permute-start.6) | collective-permute-done | bytes 102432 | tf_op jit(solution)/shard_map/ppermute | solution.py:375
  20.5 0.7 %collective-permute-start.4 = (s16[1,400,128]{2,1,0:T(8,128)(2,1)S(1)}, s16[1,400,128]{2,1,0:T(8,128)(2,1)S(1)}, u32[]{:S(2)}, u32[]{:S(2)}) collective-permute-start(s16[1,400,128]{2,1,0:T(8,128)(2,1)S(1)} %get-tuple-element.30), channel_id=1, source_target_pairs={{0,2},{1,3},{2,0},{3,1},{4,6},{5,7},{6,4},{7,5},{8,10},{9,11},{10,... | collective-permute-start | bytes 307208 | tf_op jit(solution)/shard_map/ppermute | solution.py:375
  21.3 1.3 %collective-permute-done.5.refs_1_ = s16[1,400,128]{2,1,0:T(8,128)(2,1)S(1)} collective-permute-done((s16[1,400,128]{2,1,0:T(8,128)(2,1)S(1)}, s16[1,400,128]{2,1,0:T(8,128)(2,1)S(1)}, u32[]{:S(2)}, u32[]{:S(2)}) %collective-permute-start.5) | collective-permute-done | bytes 102432 | tf_op jit(solution)/shard_map/ppermute | solution.py:375
  22.6 0.3 collective-permute-start.7
  23.1 1.7 %collective-permute-done.8.refs_1_ = s16[1,400,128]{2,1,0:T(8,128)(2,1)S(1)} collective-permute-done((s16[1,400,128]{2,1,0:T(8,128)(2,1)S(1)}, s16[1,400,128]{2,1,0:T(8,128)(2,1)S(1)}, u32[]{:S(2)}, u32[]{:S(2)}) %collective-permute-start.8) | collective-permute-done | bytes 102432 | tf_op jit(solution)/shard_map/ppermute | solution.py:375
  24.7 0.2 collective-permute-start.12
  25.0 1.1 %collective-permute-done.9.refs_2_ = s16[1,400,128]{2,1,0:T(8,128)(2,1)S(1)} collective-permute-done((s16[1,400,128]{2,1,0:T(8,128)(2,1)S(1)}, s16[1,400,128]{2,1,0:T(8,128)(2,1)S(1)}, u32[]{:S(2)}, u32[]{:S(2)}) %collective-permute-start.9) | collective-permute-done | bytes 102432 | tf_op jit(solution)/shard_map/ppermute | solution.py:375
  26.3 0.9 %collective-permute-start.15 = (s16[1,400,128]{2,1,0:T(8,128)(2,1)S(1)}, s16[1,400,128]{2,1,0:T(8,128)(2,1)S(1)}, u32[]{:S(2)}, u32[]{:S(2)}) collective-permute-start(s16[1,400,128]{2,1,0:T(8,128)(2,1)S(1)} %shard_map.90.refs_3_.refs_2_), channel_id=1, source_target_pairs={{0,8},{1,9},{2,10},{3,11},{4,12},{5,13},{6,14},{7,15},{8,0},{9,1},... | collective-permute-start | bytes 307208 | tf_op jit(solution)/shard_map/ppermute | solution.py:375
  27.2 0.2 shard_map.94
  27.4 1.6 %collective-permute-start.14 = (s16[1,400,128]{2,1,0:T(8,128)(2,1)S(1)}, s16[1,400,128]{2,1,0:T(8,128)(2,1)S(1)}, u32[]{:S(2)}, u32[]{:S(2)}) collective-permute-start(s16[1,400,128]{2,1,0:T(8,128)(2,1)S(1)} %get-tuple-element.34), channel_id=1, source_target_pairs={{0,2},{1,3},{2,0},{3,1},{4,6},{5,7},{6,4},{7,5},{8,10},{9,11},{10,... | collective-permute-start | bytes 307208 | tf_op jit(solution)/shard_map/ppermute | solution.py:375
  29.0 0.6 %collective-permute-done.7.refs_2_ = s16[1,400,128]{2,1,0:T(8,128)(2,1)S(1)} collective-permute-done((s16[1,400,128]{2,1,0:T(8,128)(2,1)S(1)}, s16[1,400,128]{2,1,0:T(8,128)(2,1)S(1)}, u32[]{:S(2)}, u32[]{:S(2)}) %collective-permute-start.7) | collective-permute-done | bytes 102432 | tf_op jit(solution)/shard_map/ppermute | solution.py:375
  29.7 1.1 %collective-permute-start.13 = (s16[1,400,128]{2,1,0:T(8,128)(2,1)S(1)}, s16[1,400,128]{2,1,0:T(8,128)(2,1)S(1)}, u32[]{:S(2)}, u32[]{:S(2)}) collective-permute-start(s16[1,400,128]{2,1,0:T(8,128)(2,1)S(1)} %shard_map.91.after), channel_id=1, source_target_pairs={{0,8},{1,9},{2,10},{3,11},{4,12},{5,13},{6,14},{7,15},{8,0},{9,1},... | collective-permute-start | bytes 307208 | tf_op jit(solution)/shard_map/ppermute | solution.py:375
  30.8 1.0 %collective-permute-start.11 = (s16[1,400,128]{2,1,0:T(8,128)(2,1)S(1)}, s16[1,400,128]{2,1,0:T(8,128)(2,1)S(1)}, u32[]{:S(2)}, u32[]{:S(2)}) collective-permute-start(s16[1,400,128]{2,1,0:T(8,128)(2,1)S(1)} %get-tuple-element.33), channel_id=1, source_target_pairs={{0,2},{1,3},{2,0},{3,1},{4,6},{5,7},{6,4},{7,5},{8,10},{9,11},{10,... | collective-permute-start | bytes 307208 | tf_op jit(solution)/shard_map/ppermute | solution.py:375
  31.8 0.7 %shard_map.92.left = bf16[120,192]{1,0:T(8,128)(2,1)S(1)} custom-call(s32[8]{0:T(128)S(1)} %copy-done, f32[8]{0:T(128)S(1)} %copy-done.1, s16[1,400,128]{2,1,0:T(8,128)(2,1)S(1)} %shard_map.91.after), custom_call_target="tpu_custom_call" | custom-call | flops 1 | bytes 1 | tf_op jit(solution)/shard_map/pallas_call | solution.py:315
  32.6 4.5 %collective-permute-done.15.refs_3_ = s16[1,400,128]{2,1,0:T(8,128)(2,1)S(1)} collective-permute-done((s16[1,400,128]{2,1,0:T(8,128)(2,1)S(1)}, s16[1,400,128]{2,1,0:T(8,128)(2,1)S(1)}, u32[]{:S(2)}, u32[]{:S(2)}) %collective-permute-start.15) | collective-permute-done | bytes 102432 | tf_op jit(solution)/shard_map/ppermute | solution.py:375
  37.1 1.1 %shard_map.96.refs_4_ = f32[16,120,128]{2,1,0:T(8,128)} custom-call(bf16[120,192]{1,0:T(8,128)(2,1)S(1)} %shard_map.92.left, f32[257,48,128]{2,1,0:T(8,128)S(1)} %get-tuple-element.27.acc, s16[8,400,128]{2,1,0:T(8,128)(2,1)S(1)} %collective-permute-done.2.refs_0_, s16[1,400,128]{2,1,0:T(8,128)(2,1)S(1)} %collective-permute-done.14.refs_1_, ...), custom_call_target="tpu_custom_call" | custom-call | flops 1 | bytes 4194304 | tf_op jit(solution)/shard_map/pallas_call | solution.py:354
  38.2 1.1 %shard_map.97 = f32[16,120,128]{2,1,0:T(8,128)} custom-call(bf16[120,192]{1,0:T(8,128)(2,1)S(1)} %shard_map.92.left, f32[257,48,128]{2,1,0:T(8,128)S(1)} %get-tuple-element.27.acc, s16[8,400,128]{2,1,0:T(8,128)(2,1)S(1)} %collective-permute-done.2.refs_0_, s16[1,400,128]{2,1,0:T(8,128)(2,1)S(1)} %collective-permute-done.11.refs_1_, ...), custom_call_target="tpu_custom_call", output_to_operand_aliasing={{}: (6, {})} | custom-call | flops 1 | bytes 4194304 | tf_op jit(solution)/shard_map/pallas_call | solution.py:354
  (21 shorter events, 1.0 us)
Async XLA Ops:
  0.7 9.8 %collective-permute-start = (bf16[1,48,128]{2,1,0:T(8,128)(2,1)S(1)}, bf16[1,48,128]{2,1,0:T(8,128)(2,1)S(1)}, u32[]{:S(2)}, u32[]{:S(2)}) collective-permute-start(bf16[1,48,128]{2,1,0:T(8,128)(2,1)S(1)} %get-tuple-element.35), channel_id=1, source_target_pairs={{0,1},{1,2},{2,3},{3,4},{4,5},{5,6},{6,7},{7,8},{8,9},{9,10},{10,1... | collective-permute-start | bytes 36872 | tf_op jit(solution)/shard_map/ppermute | solution.py:383
  4.7 5.8 %collective-permute-start.1 = (bf16[1,48,128]{2,1,0:T(8,128)(2,1)S(1)}, bf16[1,48,128]{2,1,0:T(8,128)(2,1)S(1)}, u32[]{:S(2)}, u32[]{:S(2)}) collective-permute-start(bf16[1,48,128]{2,1,0:T(8,128)(2,1)S(1)} %get-tuple-element.24), channel_id=1, source_target_pairs={{1,0},{2,1},{3,2},{4,3},{5,4},{6,5},{7,6},{8,7},{9,8},{10,9},{11,1... | collective-permute-start | bytes 36872 | tf_op jit(solution)/shard_map/ppermute | solution.py:385
  12.0 2.4 %collective-permute-start.3 = (s16[8,400,128]{2,1,0:T(8,128)(2,1)S(1)}, s16[8,400,128]{2,1,0:T(8,128)(2,1)S(1)}, u32[]{:S(2)}, u32[]{:S(2)}) collective-permute-start(s16[8,400,128]{2,1,0:T(8,128)(2,1)S(1)} %get-tuple-element.28), channel_id=1, source_target_pairs={{0,1},{1,0},{2,3},{3,2},{4,5},{5,4},{6,7},{7,6},{8,9},{9,8},{10,11... | collective-permute-start | bytes 2457608 | tf_op jit(solution)/shard_map/ppermute | solution.py:375
  12.5 5.2 %collective-permute-start.2 = (s16[8,400,128]{2,1,0:T(8,128)(2,1)S(1)}, s16[8,400,128]{2,1,0:T(8,128)(2,1)S(1)}, u32[]{:S(2)}, u32[]{:S(2)}) collective-permute-start(s16[8,400,128]{2,1,0:T(8,128)(2,1)S(1)} %shard_map.85), channel_id=1, source_target_pairs={{0,1},{1,0},{2,3},{3,2},{4,5},{5,4},{6,7},{7,6},{8,9},{9,8},{10,11... | collective-permute-start | bytes 2457608 | tf_op jit(solution)/shard_map/ppermute | solution.py:375
  14.5 5.8 %collective-permute-start.6 = (s16[1,400,128]{2,1,0:T(8,128)(2,1)S(1)}, s16[1,400,128]{2,1,0:T(8,128)(2,1)S(1)}, u32[]{:S(2)}, u32[]{:S(2)}) collective-permute-start(s16[1,400,128]{2,1,0:T(8,128)(2,1)S(1)} %get-tuple-element.29.refs_1_), channel_id=1, source_target_pairs={{0,2},{1,3},{2,0},{3,1},{4,6},{5,7},{6,4},{7,5},{8,10},{9,11},{10,... | collective-permute-start | bytes 307208 | tf_op jit(solution)/shard_map/ppermute | solution.py:375
  14.9 12.3 %collective-permute-start.10 = (s16[2,400,128]{2,1,0:T(8,128)(2,1)S(1)}, s16[2,400,128]{2,1,0:T(8,128)(2,1)S(1)}, u32[]{:S(2)}, u32[]{:S(2)}) collective-permute-start(s16[2,400,128]{2,1,0:T(8,128)(2,1)S(1)} %shard_map.93), channel_id=1, source_target_pairs={{0,4},{1,5},{2,6},{3,7},{4,0},{5,1},{6,2},{7,3},{8,12},{9,13},{10,... | collective-permute-start | bytes 614408 | tf_op jit(solution)/shard_map/ppermute | solution.py:375
  15.7 6.8 %collective-permute-start.5 = (s16[1,400,128]{2,1,0:T(8,128)(2,1)S(1)}, s16[1,400,128]{2,1,0:T(8,128)(2,1)S(1)}, u32[]{:S(2)}, u32[]{:S(2)}) collective-permute-start(s16[1,400,128]{2,1,0:T(8,128)(2,1)S(1)} %get-tuple-element.31), channel_id=1, source_target_pairs={{0,2},{1,3},{2,0},{3,1},{4,6},{5,7},{6,4},{7,5},{8,10},{9,11},{10,... | collective-permute-start | bytes 307208 | tf_op jit(solution)/shard_map/ppermute | solution.py:375
  17.1 7.6 %collective-permute-start.8 = (s16[1,400,128]{2,1,0:T(8,128)(2,1)S(1)}, s16[1,400,128]{2,1,0:T(8,128)(2,1)S(1)}, u32[]{:S(2)}, u32[]{:S(2)}) collective-permute-start(s16[1,400,128]{2,1,0:T(8,128)(2,1)S(1)} %get-tuple-element.32.refs_1_), channel_id=1, source_target_pairs={{0,2},{1,3},{2,0},{3,1},{4,6},{5,7},{6,4},{7,5},{8,10},{9,11},{10,... | collective-permute-start | bytes 307208 | tf_op jit(solution)/shard_map/ppermute | solution.py:375
  20.5 5.7 %collective-permute-start.9 = (s16[1,400,128]{2,1,0:T(8,128)(2,1)S(1)}, s16[1,400,128]{2,1,0:T(8,128)(2,1)S(1)}, u32[]{:S(2)}, u32[]{:S(2)}) collective-permute-start(s16[1,400,128]{2,1,0:T(8,128)(2,1)S(1)} %shard_map.88.refs_2_), channel_id=1, source_target_pairs={{0,4},{1,5},{2,6},{3,7},{4,0},{5,1},{6,2},{7,3},{8,12},{9,13},{10,... | collective-permute-start | bytes 307208 | tf_op jit(solution)/shard_map/ppermute | solution.py:375
  20.5 8.4 %collective-permute-start.4 = (s16[1,400,128]{2,1,0:T(8,128)(2,1)S(1)}, s16[1,400,128]{2,1,0:T(8,128)(2,1)S(1)}, u32[]{:S(2)}, u32[]{:S(2)}) collective-permute-start(s16[1,400,128]{2,1,0:T(8,128)(2,1)S(1)} %get-tuple-element.30), channel_id=1, source_target_pairs={{0,2},{1,3},{2,0},{3,1},{4,6},{5,7},{6,4},{7,5},{8,10},{9,11},{10,... | collective-permute-start | bytes 307208 | tf_op jit(solution)/shard_map/ppermute | solution.py:375
  22.6 6.9 %collective-permute-start.7 = (s16[1,400,128]{2,1,0:T(8,128)(2,1)S(1)}, s16[1,400,128]{2,1,0:T(8,128)(2,1)S(1)}, u32[]{:S(2)}, u32[]{:S(2)}) collective-permute-start(s16[1,400,128]{2,1,0:T(8,128)(2,1)S(1)} %shard_map.89.refs_1_), channel_id=1, source_target_pairs={{0,4},{1,5},{2,6},{3,7},{4,0},{5,1},{6,2},{7,3},{8,12},{9,13},{10,... | collective-permute-start | bytes 307208 | tf_op jit(solution)/shard_map/ppermute | solution.py:375
  24.7 12.4 %collective-permute-start.12 = (s16[2,400,128]{2,1,0:T(8,128)(2,1)S(1)}, s16[2,400,128]{2,1,0:T(8,128)(2,1)S(1)}, u32[]{:S(2)}, u32[]{:S(2)}) collective-permute-start(s16[2,400,128]{2,1,0:T(8,128)(2,1)S(1)} %shard_map.95), channel_id=1, source_target_pairs={{0,4},{1,5},{2,6},{3,7},{4,0},{5,1},{6,2},{7,3},{8,12},{9,13},{10,... | collective-permute-start | bytes 614408 | tf_op jit(solution)/shard_map/ppermute | solution.py:375
  26.3 5.5 %copy-start = (s32[8]{0:T(128)S(1)}, s32[8]{0:T(128)}, u32[]{:S(2)}) copy-start(s32[8]{0:T(128)} %index_ref.1) | copy-start | bytes 100
  26.3 5.5 %copy-start.1 = (f32[8]{0:T(128)S(1)}, f32[8]{0:T(128)}, u32[]{:S(2)}) copy-start(f32[8]{0:T(128)} %frac_ref.1) | copy-start | bytes 100
  26.3 10.8 %collective-permute-start.15 = (s16[1,400,128]{2,1,0:T(8,128)(2,1)S(1)}, s16[1,400,128]{2,1,0:T(8,128)(2,1)S(1)}, u32[]{:S(2)}, u32[]{:S(2)}) collective-permute-start(s16[1,400,128]{2,1,0:T(8,128)(2,1)S(1)} %shard_map.90.refs_3_.refs_2_), channel_id=1, source_target_pairs={{0,8},{1,9},{2,10},{3,11},{4,12},{5,13},{6,14},{7,15},{8,0},{9,1},... | collective-permute-start | bytes 307208 | tf_op jit(solution)/shard_map/ppermute | solution.py:375
  27.4 9.7 %collective-permute-start.14 = (s16[1,400,128]{2,1,0:T(8,128)(2,1)S(1)}, s16[1,400,128]{2,1,0:T(8,128)(2,1)S(1)}, u32[]{:S(2)}, u32[]{:S(2)}) collective-permute-start(s16[1,400,128]{2,1,0:T(8,128)(2,1)S(1)} %get-tuple-element.34), channel_id=1, source_target_pairs={{0,2},{1,3},{2,0},{3,1},{4,6},{5,7},{6,4},{7,5},{8,10},{9,11},{10,... | collective-permute-start | bytes 307208 | tf_op jit(solution)/shard_map/ppermute | solution.py:375
  29.7 8.5 %collective-permute-start.13 = (s16[1,400,128]{2,1,0:T(8,128)(2,1)S(1)}, s16[1,400,128]{2,1,0:T(8,128)(2,1)S(1)}, u32[]{:S(2)}, u32[]{:S(2)}) collective-permute-start(s16[1,400,128]{2,1,0:T(8,128)(2,1)S(1)} %shard_map.91.after), channel_id=1, source_target_pairs={{0,8},{1,9},{2,10},{3,11},{4,12},{5,13},{6,14},{7,15},{8,0},{9,1},... | collective-permute-start | bytes 307208 | tf_op jit(solution)/shard_map/ppermute | solution.py:375
  30.8 7.4 %collective-permute-start.11 = (s16[1,400,128]{2,1,0:T(8,128)(2,1)S(1)}, s16[1,400,128]{2,1,0:T(8,128)(2,1)S(1)}, u32[]{:S(2)}, u32[]{:S(2)}) collective-permute-start(s16[1,400,128]{2,1,0:T(8,128)(2,1)S(1)} %get-tuple-element.33), channel_id=1, source_target_pairs={{0,2},{1,3},{2,0},{3,1},{4,6},{5,7},{6,4},{7,5},{8,10},{9,11},{10,... | collective-permute-start | bytes 307208 | tf_op jit(solution)/shard_map/ppermute | solution.py:375

commit v8 on v7

--- a/solution.py
+++ b/solution.py
@@ -249,28 +249,36 @@
     )(ends, before, after, w, acc)
 
 
-def code_kernel(jobs, acc, *refs):
+def taken(takes, arrays, me):
+    for a, i, *pair in takes:
+        if pair:
+            i = i + pair[0] * jnp.where(me & pair[1], 0, 1)
+        yield arrays[a], i, scales(arrays[a], i)
+
+
+def code_kernel(jobs, me, acc, *refs):
     arrays, outs, exps = refs[: -1 - len(jobs)], refs[-1 - len(jobs) : -1], refs[-1]
     for parts, out in zip(jobs, outs):
         for at, (unit, takes) in enumerate(parts):
-            coded = [(arrays[a], i, scales(arrays[a], i)) for a, i in takes]
+            coded = list(taken(takes, arrays, me[0]))
             code_half(acc, unit, coded, exps, out, at)
 
 
-def code(acc, jobs, arrays):
+def code(me, acc, jobs, arrays):
     cells = acc.shape[2]
+    smem = pl.BlockSpec(memory_space=pltpu.SMEM)
     vmem = pl.BlockSpec(memory_space=pltpu.VMEM)
     return pl.pallas_call(
         functools.partial(code_kernel, jobs),
         out_shape=tuple(
             jax.ShapeDtypeStruct((len(parts), CODED, cells), jnp.int16) for parts in jobs
         ),
-        in_specs=[vmem] * (1 + len(arrays)),
+        in_specs=[smem] + [vmem] * (1 + len(arrays)),
         out_specs=(vmem,) * len(jobs),
         scratch_shapes=[pltpu.VMEM((16, cells), jnp.float32)],
         compiler_params=pltpu.CompilerParams(vmem_limit_bytes=32 * MIB),
         cost_estimate=LITTLE,
-    )(acc, *arrays)
+    )(me, acc, *arrays)
 
 
 def code_near_kernel(acc, near_ref, exps):
@@ -322,9 +330,9 @@
     )(lev_index, lev_frac, after)
 
 
-def finish_kernel(half, takes, left, acc, *refs):
+def finish_kernel(half, takes, me, left, acc, *refs):
     arrays, out_hbm, out, sems = refs[:-3], refs[-3], refs[-2], refs[-1]
-    coded = [(arrays[a], i, scales(arrays[a], i)) for a, i in takes]
+    coded = list(taken(takes, arrays, me[0]))
     copies = []
     for b in range(HALF):
         total = acc[half * HALF + b]
@@ -346,29 +354,35 @@
         copy.wait()
 
 
-def finish(half, left, acc, takes, arrays, begun=None):
+def finish(half, me, left, acc, takes, arrays, begun=None):
     cells = acc.shape[2]
+    smem = pl.BlockSpec(memory_space=pltpu.SMEM)
     vmem = pl.BlockSpec(memory_space=pltpu.VMEM)
     hbm = pl.BlockSpec(memory_space=pltpu.HBM)
     extra = () if begun is None else (begun,)
     return pl.pallas_call(
         functools.partial(finish_kernel, half, takes),
         out_shape=jax.ShapeDtypeStruct((SB, VARS * LEV, cells), jnp.float32),
-        in_specs=[vmem] * (2 + len(arrays)) + [hbm] * len(extra),
+        in_specs=[smem] + [vmem] * (2 + len(arrays)) + [hbm] * len(extra),
         out_specs=hbm,
         scratch_shapes=[
             pltpu.VMEM((HALF, VARS * LEV, cells), jnp.float32),
             pltpu.SemaphoreType.DMA((HALF // 4,)),
         ],
-        input_output_aliases={2 + len(arrays): 0} if extra else {},
+        input_output_aliases={3 + len(arrays): 0} if extra else {},
         compiler_params=pltpu.CompilerParams(vmem_limit_bytes=32 * MIB),
-        cost_estimate=pl.CostEstimate(flops=1, bytes_accessed=4194304, transcendentals=0),
-    )(left, acc, *arrays, *extra)
+        cost_estimate=LITTLE,
+    )(me, left, acc, *arrays, *extra)
 
 
 def ring(peers):
     up = [(i, (i + 1) % peers) for i in range(peers)]
     return up, [(j, i) for i, j in up]
+
+
+def both(value, bits, peers):
+    pairs = [[i, i ^ bits] for i in range(peers) if not i & bits]
+    return lax.all_gather(value, "tile", axis_index_groups=pairs, tiled=True)
 
 
 def swap(value, bits, peers):
@@ -387,28 +401,30 @@
     acc, far = add_ends(ends, before, after, w, acc)
     far = swap(far, 1, peers)
     near = swap(code_near(acc), 1, peers)
-    y3 = code(acc, (((14, ((0, 6),)),), ((15, ((0, 7),)),)), (far,))
+    add = functools.partial(code, me, acc)
+    y3 = add((((14, ((0, 6),)),), ((15, ((0, 7),)),)), (far,))
     y3_own = y3[0]
     y3 = [swap(v, 2, peers) for v in y3]
-    y2 = code(acc, (((12, ((0, 4),)),), ((13, ((0, 5),)),)), (far, y3_own))
+    (o1_own,) = add((((10, ((0, 2),)), (11, ((0, 3),))),), (far, y3_own))
+    o1 = both(o1_own, 4, peers)
+    y2 = add((((12, ((0, 4),)),), ((13, ((0, 5),)),)), (far, o1_own))
     y2_own = y2[0]
     y2 = [swap(v, 2, peers) for v in y2]
-    (a3_low,) = code(acc, (((6, ((0, 6), (1, 0))),),), (near, y3[0], far))
-    (a3_high,) = code(acc, (((7, ((0, 7), (1, 0))),),), (near, y3[1], a3_low))
+    (a3_low,) = add((((6, ((0, 6), (1, 0))),),), (near, y3[0], y2_own))
+    (a3_high,) = add((((7, ((0, 7), (1, 0))),),), (near, y3[1], a3_low))
     a3 = [swap(a3_low, 4, peers), swap(a3_high, 4, peers)]
-    (y1_own,) = code(acc, (((10, ((0, 2),)), (11, ((0, 3),))),), (far, y2_own))
-    o1 = swap(y1_own, 4, peers)
-    (b2_low,) = code(acc, (((4, ((0, 4), (1, 0), (2, 0))),),), (near, y2[0], a3[0], far))
-    (b2_high,) = code(acc, (((5, ((0, 5), (1, 0), (2, 0))),),), (near, y2[1], a3[1], b2_low))
+    (a1_own,) = add((((2, ((0, 2),)), (3, ((0, 3),))),), (near,))
+    a1 = both(a1_own, 4, peers)
+    (y0_own,) = add((((8, ((0, 0), (1, 0, 2, 4))), (9, ((0, 1), (1, 1, 2, 4)))),), (far, o1))
+    y0 = both(y0_own, 2, peers)
+    (b2_low,) = add((((4, ((0, 4), (1, 0), (2, 0))),),), (near, y2[0], a3[0]))
+    (b2_high,) = add((((5, ((0, 5), (1, 0), (2, 0))),),), (near, y2[1], a3[1], b2_low))
     b2 = [swap(b2_low, 8, peers), swap(b2_high, 8, peers)]
-    y0_own = code(acc, (((8, ((0, 0), (1, 0))),), ((9, ((0, 1), (1, 1))),)), (far, o1, b2_low))
-    y0 = [swap(v, 2, peers) for v in y0_own]
-    y0_own = y0_own[0]
-    (a1_own,) = code(acc, (((2, ((0, 2),)), (3, ((0, 3),))),), (near, a3_high))
-    a1 = swap(a1_own, 4, peers)
-    left = lift_matrix(lev_index, lev_frac, b2_high)
-    out = finish(0, left, acc, ((0, 0), (1, 0), (2, 0), (3, 0)), (near, y0[0], a1, b2[0]))
-    return finish(1, left, acc, ((0, 1), (1, 0), (2, 1), (3, 0)), (near, y0[1], a1, b2[1]), out)
+    left = lift_matrix(lev_index, lev_frac, b2_low)
+    sums = ((0, 0), (1, 0, 2, 2), (2, 0, 2, 4), (3, 0))
+    out = finish(0, me, left, acc, sums, (near, y0, a1, b2[0]))
+    sums = ((0, 1), (1, 1, 2, 2), (2, 1, 2, 4), (3, 0))
+    return finish(1, me, left, acc, sums, (near, y0, a1, b2[1]), out)
 
 
 def vertical_matrix(lev_index, lev_frac, levels):

time: 39.5 us -> 49.2 us (1.25)
  blocking collectives: 0 us -> 20.4 us
  waiting for transfers between devices: 13.2 us -> 1.37 us
  starting transfers between devices: 12.1 us -> 12.8 us
    all_gather x0 -> x3, blocking collectives: none -> 20.4 us  [both(): return lax.all_gather(value, 'tile', axis_index_groups=pairs, tiled=True)]
    ppermute x14 -> x10, waiting for transfers between devices: 13.2 us -> 1.36 us  [swap(): return lax.ppermute(value, 'tile', [(i, i ^ bits) for i in range(peers)])]
    ppermute x14 -> x10, starting transfers between devices: 9.33 us -> 10.1 us  [swap(): return lax.ppermute(value, 'tile', [(i, i ^ bits) for i in range(peers)])]
  transfers between devices with their start and end apart: 16 -> 12, of which waited for: 7 -> 1; matrix products, arithmetic and copies ran while one was open for 0% -> 0% of each run, Pallas kernels for 25% -> 20%
where the time goes in v8:
time: 49.2 us; the launch traced here: 48.8 us
  blocking collectives  20.4 us (41%)
  starting transfers between devices  12.8 us (26%)
  Pallas kernels  12.7 us (26%)
  waiting for transfers between devices  1.37 us (3%)
  between operations  0.8 us (2%)
  local copies, waits for them, and re-layouts  0.73 us (1%)
    all_gather x3, blocking collectives, both(): return lax.all_gather(value, 'tile', axis_index_groups=pairs, tiled=True)  20.4 us
    ppermute x10, starting transfers between devices, swap(): return lax.ppermute(value, 'tile', [(i, i ^ bits) for i in range(peers)])  10.1 us
    pallas_call x2, Pallas kernels, products_call(): pl.pallas_call(kernel, out_shape=tuple(results), in_specs=[smem, smem] +...  6.38 us
    ppermute x1, starting transfers between devices, staged(): after = lax.ppermute(low, 'tile', down)  2.27 us
    pallas_call x2, Pallas kernels, finish(): pl.pallas_call(functools.partial(finish_kernel, half, takes), out_shape=j...  2.11 us
    pallas_call x1, Pallas kernels, add_ends(): pl.pallas_call(ends_kernel, out_shape=(jax.ShapeDtypeStruct(acc.shape, jn...  1.69 us
    ppermute x10, waiting for transfers between devices, swap(): return lax.ppermute(value, 'tile', [(i, i ^ bits) for i in range(peers)])  1.36 us
    pallas_call x9, Pallas kernels, code(): pl.pallas_call(functools.partial(code_kernel, jobs), out_shape=tuple((jax...  1.34 us
  transfers between devices with their start and end apart: 12, of which 1 were waited for; matrix products, arithmetic and copies ran while one was open for 0% of the time, Pallas kernels for 20%

profile of v8, /device:TPU:0, one launch (start us, length us, event | category | flops | bytes accessed | tf_op | source)
XLA Modules:
  0.0 48.8 jit_solution(12309757222390532095)
XLA Ops:
  0.0 0.7 %fusion = (bf16[1,48,128]{2,1,0:T(8,128)(2,1)S(1)}, bf16[1,48,128]{2,1,0:T(8,128)(2,1)S(1)}) fusion(bf16[16,48,128]{2,1,0:T(8,128)(2,1)} %cot_hbm.3), kind=kLoop, calls=%fused_computation | loop fusion | bytes 49152 | tf_op jit(solution)/shard_map/slice | solution.py:397
  0.7 0.5 collective-permute-start
  1.8 2.9 %shard_map.82 = (f32[257,48,128]{2,1,0:T(8,128)S(1)}, bf16[128,128,128]{2,1,0:T(8,128)(2,1)S(1)}, bf16[16,48,128]{2,1,0:T(8,128)(2,1)S(1)}, bf16[1,48,128]{2,1,0:T(8,128)(2,1)S(1)}) custom-call(s32[1]{0:T(128)S(6)} %copy.19.count_ref, s32[1]{0:T(128)} %bitcast.me_ref.me, s32[1,128]{1,0:T(1,128)} %tb.3, s32[1,128]{1,0:T(1,128)} %dest.3, s32[1,128]{1,0:T(1,128)} %src.3, ...), custom_call_target="tpu_custom_call" | custom-call | flops 268435456 | bytes 12582912 | tf_op jit(solution)/shard_map/pallas_call | solution.py:184
  4.7 2.3 %collective-permute-start.1 = (bf16[1,48,128]{2,1,0:T(8,128)(2,1)S(1)}, bf16[1,48,128]{2,1,0:T(8,128)(2,1)S(1)}, u32[]{:S(2)}, u32[]{:S(2)}) collective-permute-start(bf16[1,48,128]{2,1,0:T(8,128)(2,1)S(1)} %get-tuple-element.22), channel_id=1, source_target_pairs={{1,0},{2,1},{3,2},{4,3},{5,4},{6,5},{7,6},{8,7},{9,8},{10,9},{11,1... | collective-permute-start | bytes 36872 | tf_op jit(solution)/shard_map/ppermute | solution.py:399
  7.0 3.5 %shard_map.83 = (f32[257,48,128]{2,1,0:T(8,128)S(1)}, bf16[128,128,128]{2,1,0:T(8,128)(2,1)S(1)}, bf16[16,48,128]{2,1,0:T(8,128)(2,1)S(1)}, s32[4,136]{1,0:T(4,128)S(1)}) custom-call(s32[1]{0:T(128)S(6)} %copy.19.count_ref, s32[1]{0:T(128)} %bitcast.me_ref.me, s32[1,128]{1,0:T(1,128)} %tb.3, ...), custom_call_target="tpu_custom_call", output_to_operand_aliasing={{0}: (7, {}), {1}: (8, {}), {2}: (9, {})} | custom-call | flops 1 | bytes 1 | tf_op jit(solution)/shard_map/pallas_call | solution.py:184
  10.5 1.7 %shard_map.84 = (f32[257,48,128]{2,1,0:T(8,128)S(1)}, s16[8,400,128]{2,1,0:T(8,128)(2,1)S(1)}) custom-call(s32[4,136]{1,0:T(4,128)S(1)} %get-tuple-element.21.ends, bf16[1,48,128]{2,1,0:T(8,128)(2,1)S(1)} %collective-permute-done.before, bf16[1,48,128]{2,1,0:T(8,128)(2,1)S(1)} %collective-permute-done.1.after, ...), custom_call_target="tpu_custom_call", output_to_operand_aliasing={{0}: (4, {})} | custom-call | flops 1 | bytes 1 | tf_op jit(solution)/shard_map/pallas_call | solution.py:234
  12.2 0.1 collective-permute-start.3
  12.3 0.4 shard_map.85
  12.7 0.6 %collective-permute-start.2 = (s16[8,400,128]{2,1,0:T(8,128)(2,1)S(1)}, s16[8,400,128]{2,1,0:T(8,128)(2,1)S(1)}, u32[]{:S(2)}, u32[]{:S(2)}) collective-permute-start(s16[8,400,128]{2,1,0:T(8,128)(2,1)S(1)} %shard_map.85), channel_id=1, source_target_pairs={{0,1},{1,0},{2,3},{3,2},{4,5},{5,4},{6,7},{7,6},{8,9},{9,8},{10,11... | collective-permute-start | bytes 2457608 | tf_op jit(solution)/shard_map/ppermute | solution.py:389
  13.3 1.3 %collective-permute-done.3.refs_0_ = s16[8,400,128]{2,1,0:T(8,128)(2,1)S(1)} collective-permute-done((s16[8,400,128]{2,1,0:T(8,128)(2,1)S(1)}, s16[8,400,128]{2,1,0:T(8,128)(2,1)S(1)}, u32[]{:S(2)}, u32[]{:S(2)}) %collective-permute-start.3) | collective-permute-done | bytes 819232 | tf_op jit(solution)/shard_map/ppermute | solution.py:389
  14.6 0.2 shard_map.86
  14.8 0.2 shard_map.87.refs_1_
  15.0 2.1 %collective-permute-start.8 = (s16[1,400,128]{2,1,0:T(8,128)(2,1)S(1)}, s16[1,400,128]{2,1,0:T(8,128)(2,1)S(1)}, u32[]{:S(2)}, u32[]{:S(2)}) collective-permute-start(s16[1,400,128]{2,1,0:T(8,128)(2,1)S(1)} %get-tuple-element.30), channel_id=1, source_target_pairs={{0,2},{1,3},{2,0},{3,1},{4,6},{5,7},{6,4},{7,5},{8,10},{9,11},{10,... | collective-permute-start | bytes 307208 | tf_op jit(solution)/shard_map/ppermute | solution.py:389
  17.1 0.2 shard_map.88
  17.2 0.1 collective-permute-start.7
  17.3 2.0 %collective-permute-start.4 = (s16[1,400,128]{2,1,0:T(8,128)(2,1)S(1)}, s16[1,400,128]{2,1,0:T(8,128)(2,1)S(1)}, u32[]{:S(2)}, u32[]{:S(2)}) collective-permute-start(s16[1,400,128]{2,1,0:T(8,128)(2,1)S(1)} %get-tuple-element.28.refs_2_), channel_id=1, source_target_pairs={{0,2},{1,3},{2,0},{3,1},{4,6},{5,7},{6,4},{7,5},{8,10},{9,11},{10,... | collective-permute-start | bytes 307208 | tf_op jit(solution)/shard_map/ppermute | solution.py:389
  19.3 6.6 %all_gather.9.refs_1_ = s16[4,400,128]{2,1,0:T(8,128)(2,1)S(1)} all-gather(s16[2,400,128]{2,1,0:T(8,128)(2,1)S(1)} %shard_map.87.refs_1_), channel_id=1, replica_groups={{0,4},{1,5},{2,6},{3,7},{8,12},{9,13},{10,14},{11,15},{16,20},{17,21},{..., dimensions={0}, use_global_device_ids=true | all-gather | bytes 614400 | tf_op jit(solution)/shard_map/all_gather | solution.py:385
  26.0 0.2 shard_map.93
  26.2 0.2 shard_map.92
  26.4 0.1 shard_map.89.refs_2_
  26.5 0.3 collective-permute-start.6
  26.8 0.1 shard_map.94
  26.9 1.8 %collective-permute-start.9 = (s16[1,400,128]{2,1,0:T(8,128)(2,1)S(1)}, s16[1,400,128]{2,1,0:T(8,128)(2,1)S(1)}, u32[]{:S(2)}, u32[]{:S(2)}) collective-permute-start(s16[1,400,128]{2,1,0:T(8,128)(2,1)S(1)} %shard_map.94), channel_id=1, source_target_pairs={{0,4},{1,5},{2,6},{3,7},{4,0},{5,1},{6,2},{7,3},{8,12},{9,13},{10,... | collective-permute-start | bytes 307208 | tf_op jit(solution)/shard_map/ppermute | solution.py:389
  28.8 7.3 %all_gather.11.refs_2_ = s16[4,400,128]{2,1,0:T(8,128)(2,1)S(1)} all-gather(s16[2,400,128]{2,1,0:T(8,128)(2,1)S(1)} %shard_map.93), channel_id=1, replica_groups={{0,4},{1,5},{2,6},{3,7},{8,12},{9,13},{10,14},{11,15},{16,20},{17,21},{..., dimensions={0}, use_global_device_ids=true | all-gather | bytes 614400 | tf_op jit(solution)/shard_map/all_gather | solution.py:385
  36.1 0.1 shard_map.90.after.refs_3_
  36.3 1.2 %collective-permute-start.11 = (s16[1,400,128]{2,1,0:T(8,128)(2,1)S(1)}, s16[1,400,128]{2,1,0:T(8,128)(2,1)S(1)}, u32[]{:S(2)}, u32[]{:S(2)}) collective-permute-start(s16[1,400,128]{2,1,0:T(8,128)(2,1)S(1)} %shard_map.90.after.refs_3_), channel_id=1, source_target_pairs={{0,8},{1,9},{2,10},{3,11},{4,12},{5,13},{6,14},{7,15},{8,0},{9,1},... | collective-permute-start | bytes 307208 | tf_op jit(solution)/shard_map/ppermute | solution.py:389
  37.5 0.1 shard_map.95
  37.6 1.9 %collective-permute-start.10 = (s16[1,400,128]{2,1,0:T(8,128)(2,1)S(1)}, s16[1,400,128]{2,1,0:T(8,128)(2,1)S(1)}, u32[]{:S(2)}, u32[]{:S(2)}) collective-permute-start(s16[1,400,128]{2,1,0:T(8,128)(2,1)S(1)} %shard_map.95), channel_id=1, source_target_pairs={{0,8},{1,9},{2,10},{3,11},{4,12},{5,13},{6,14},{7,15},{8,0},{9,1},... | collective-permute-start | bytes 307208 | tf_op jit(solution)/shard_map/ppermute | solution.py:389
  39.5 6.4 %all_gather.10.refs_1_ = s16[4,400,128]{2,1,0:T(8,128)(2,1)S(1)} all-gather(s16[2,400,128]{2,1,0:T(8,128)(2,1)S(1)} %shard_map.92), channel_id=1, replica_groups={{0,2},{1,3},{4,6},{5,7},{8,10},{9,11},{12,14},{13,15},{16,18},{17,19},{..., dimensions={0}, use_global_device_ids=true | all-gather | bytes 614400 | tf_op jit(solution)/shard_map/all_gather | solution.py:385
  45.9 0.7 %shard_map.91.left = bf16[120,192]{1,0:T(8,128)(2,1)S(1)} custom-call(s32[8]{0:T(128)S(1)} %copy-done, f32[8]{0:T(128)S(1)} %copy-done.1, s16[1,400,128]{2,1,0:T(8,128)(2,1)S(1)} %shard_map.90.after.refs_3_), custom_call_target="tpu_custom_call" | custom-call | flops 1 | bytes 1 | tf_op jit(solution)/shard_map/pallas_call | solution.py:323
  46.7 1.1 %shard_map.96.refs_4_ = f32[16,120,128]{2,1,0:T(8,128)} custom-call(s32[1]{0:T(128)} %bitcast.me_ref.me, bf16[120,192]{1,0:T(8,128)(2,1)S(1)} %shard_map.91.left, f32[257,48,128]{2,1,0:T(8,128)S(1)} %get-tuple-element.25.acc, s16[8,400,128]{2,1,0:T(8,128)(2,1)S(1)} %collective-permute-done.2.refs_0_, s16[4,400,128]{2,1,0:T(8,128)(2,1)S(1)} %all_gather.10.refs_1_, ...), custom_call_target="tpu_custom_call" | custom-call | flops 1 | bytes 1 | tf_op jit(solution)/shard_map/pallas_call | solution.py:363
  47.8 1.1 %shard_map.97 = f32[16,120,128]{2,1,0:T(8,128)} custom-call(s32[1]{0:T(128)} %bitcast.me_ref.me, bf16[120,192]{1,0:T(8,128)(2,1)S(1)} %shard_map.91.left, f32[257,48,128]{2,1,0:T(8,128)S(1)} %get-tuple-element.25.acc, s16[8,400,128]{2,1,0:T(8,128)(2,1)S(1)} %collective-permute-done.2.refs_0_, ...), custom_call_target="tpu_custom_call", output_to_operand_aliasing={{}: (7, {})} | custom-call | flops 1 | bytes 1 | tf_op jit(solution)/shard_map/pallas_call | solution.py:363
  (16 shorter events, 0.1 us)
Async XLA Ops:
  0.7 9.8 %collective-permute-start = (bf16[1,48,128]{2,1,0:T(8,128)(2,1)S(1)}, bf16[1,48,128]{2,1,0:T(8,128)(2,1)S(1)}, u32[]{:S(2)}, u32[]{:S(2)}) collective-permute-start(bf16[1,48,128]{2,1,0:T(8,128)(2,1)S(1)} %get-tuple-element.31), channel_id=1, source_target_pairs={{0,1},{1,2},{2,3},{3,4},{4,5},{5,6},{6,7},{7,8},{8,9},{9,10},{10,1... | collective-permute-start | bytes 36872 | tf_op jit(solution)/shard_map/ppermute | solution.py:397
  4.7 5.8 %collective-permute-start.1 = (bf16[1,48,128]{2,1,0:T(8,128)(2,1)S(1)}, bf16[1,48,128]{2,1,0:T(8,128)(2,1)S(1)}, u32[]{:S(2)}, u32[]{:S(2)}) collective-permute-start(bf16[1,48,128]{2,1,0:T(8,128)(2,1)S(1)} %get-tuple-element.22), channel_id=1, source_target_pairs={{1,0},{2,1},{3,2},{4,3},{5,4},{6,5},{7,6},{8,7},{9,8},{10,9},{11,1... | collective-permute-start | bytes 36872 | tf_op jit(solution)/shard_map/ppermute | solution.py:399
  12.2 2.4 %collective-permute-start.3 = (s16[8,400,128]{2,1,0:T(8,128)(2,1)S(1)}, s16[8,400,128]{2,1,0:T(8,128)(2,1)S(1)}, u32[]{:S(2)}, u32[]{:S(2)}) collective-permute-start(s16[8,400,128]{2,1,0:T(8,128)(2,1)S(1)} %get-tuple-element.26), channel_id=1, source_target_pairs={{0,1},{1,0},{2,3},{3,2},{4,5},{5,4},{6,7},{7,6},{8,9},{9,8},{10,11... | collective-permute-start | bytes 2457608 | tf_op jit(solution)/shard_map/ppermute | solution.py:389
  12.7 13.3 %collective-permute-start.2 = (s16[8,400,128]{2,1,0:T(8,128)(2,1)S(1)}, s16[8,400,128]{2,1,0:T(8,128)(2,1)S(1)}, u32[]{:S(2)}, u32[]{:S(2)}) collective-permute-start(s16[8,400,128]{2,1,0:T(8,128)(2,1)S(1)} %shard_map.85), channel_id=1, source_target_pairs={{0,1},{1,0},{2,3},{3,2},{4,5},{5,4},{6,7},{7,6},{8,9},{9,8},{10,11... | collective-permute-start | bytes 2457608 | tf_op jit(solution)/shard_map/ppermute | solution.py:389
  14.8 11.6 %collective-permute-start.5 = (s16[1,400,128]{2,1,0:T(8,128)(2,1)S(1)}, s16[1,400,128]{2,1,0:T(8,128)(2,1)S(1)}, u32[]{:S(2)}, u32[]{:S(2)}) collective-permute-start(s16[1,400,128]{2,1,0:T(8,128)(2,1)S(1)} %get-tuple-element.27.refs_1_), channel_id=1, source_target_pairs={{0,2},{1,3},{2,0},{3,1},{4,6},{5,7},{6,4},{7,5},{8,10},{9,11},{10,... | collective-permute-start | bytes 307208 | tf_op jit(solution)/shard_map/ppermute | solution.py:389
  15.0 11.8 %collective-permute-start.8 = (s16[1,400,128]{2,1,0:T(8,128)(2,1)S(1)}, s16[1,400,128]{2,1,0:T(8,128)(2,1)S(1)}, u32[]{:S(2)}, u32[]{:S(2)}) collective-permute-start(s16[1,400,128]{2,1,0:T(8,128)(2,1)S(1)} %get-tuple-element.30), channel_id=1, source_target_pairs={{0,2},{1,3},{2,0},{3,1},{4,6},{5,7},{6,4},{7,5},{8,10},{9,11},{10,... | collective-permute-start | bytes 307208 | tf_op jit(solution)/shard_map/ppermute | solution.py:389
  17.2 20.2 %collective-permute-start.7 = (s16[1,400,128]{2,1,0:T(8,128)(2,1)S(1)}, s16[1,400,128]{2,1,0:T(8,128)(2,1)S(1)}, u32[]{:S(2)}, u32[]{:S(2)}) collective-permute-start(s16[1,400,128]{2,1,0:T(8,128)(2,1)S(1)} %get-tuple-element.29), channel_id=1, source_target_pairs={{0,2},{1,3},{2,0},{3,1},{4,6},{5,7},{6,4},{7,5},{8,10},{9,11},{10,... | collective-permute-start | bytes 307208 | tf_op jit(solution)/shard_map/ppermute | solution.py:389
  17.3 18.8 %collective-permute-start.4 = (s16[1,400,128]{2,1,0:T(8,128)(2,1)S(1)}, s16[1,400,128]{2,1,0:T(8,128)(2,1)S(1)}, u32[]{:S(2)}, u32[]{:S(2)}) collective-permute-start(s16[1,400,128]{2,1,0:T(8,128)(2,1)S(1)} %get-tuple-element.28.refs_2_), channel_id=1, source_target_pairs={{0,2},{1,3},{2,0},{3,1},{4,6},{5,7},{6,4},{7,5},{8,10},{9,11},{10,... | collective-permute-start | bytes 307208 | tf_op jit(solution)/shard_map/ppermute | solution.py:389
  26.5 9.6 %collective-permute-start.6 = (s16[1,400,128]{2,1,0:T(8,128)(2,1)S(1)}, s16[1,400,128]{2,1,0:T(8,128)(2,1)S(1)}, u32[]{:S(2)}, u32[]{:S(2)}) collective-permute-start(s16[1,400,128]{2,1,0:T(8,128)(2,1)S(1)} %shard_map.89.refs_2_), channel_id=1, source_target_pairs={{0,4},{1,5},{2,6},{3,7},{4,0},{5,1},{6,2},{7,3},{8,12},{9,13},{10,... | collective-permute-start | bytes 307208 | tf_op jit(solution)/shard_map/ppermute | solution.py:389
  26.9 10.5 %collective-permute-start.9 = (s16[1,400,128]{2,1,0:T(8,128)(2,1)S(1)}, s16[1,400,128]{2,1,0:T(8,128)(2,1)S(1)}, u32[]{:S(2)}, u32[]{:S(2)}) collective-permute-start(s16[1,400,128]{2,1,0:T(8,128)(2,1)S(1)} %shard_map.94), channel_id=1, source_target_pairs={{0,4},{1,5},{2,6},{3,7},{4,0},{5,1},{6,2},{7,3},{8,12},{9,13},{10,... | collective-permute-start | bytes 307208 | tf_op jit(solution)/shard_map/ppermute | solution.py:389
  36.1 9.8 %copy-start = (s32[8]{0:T(128)S(1)}, s32[8]{0:T(128)}, u32[]{:S(2)}) copy-start(s32[8]{0:T(128)} %index_ref.1) | copy-start | bytes 100
  36.1 9.8 %copy-start.1 = (f32[8]{0:T(128)S(1)}, f32[8]{0:T(128)}, u32[]{:S(2)}) copy-start(f32[8]{0:T(128)} %frac_ref.1) | copy-start | bytes 100
  36.3 10.4 %collective-permute-start.11 = (s16[1,400,128]{2,1,0:T(8,128)(2,1)S(1)}, s16[1,400,128]{2,1,0:T(8,128)(2,1)S(1)}, u32[]{:S(2)}, u32[]{:S(2)}) collective-permute-start(s16[1,400,128]{2,1,0:T(8,128)(2,1)S(1)} %shard_map.90.after.refs_3_), channel_id=1, source_target_pairs={{0,8},{1,9},{2,10},{3,11},{4,12},{5,13},{6,14},{7,15},{8,0},{9,1},... | collective-permute-start | bytes 307208 | tf_op jit(solution)/shard_map/ppermute | solution.py:389
  37.6 10.1 %collective-permute-start.10 = (s16[1,400,128]{2,1,0:T(8,128)(2,1)S(1)}, s16[1,400,128]{2,1,0:T(8,128)(2,1)S(1)}, u32[]{:S(2)}, u32[]{:S(2)}) collective-permute-start(s16[1,400,128]{2,1,0:T(8,128)(2,1)S(1)} %shard_map.95), channel_id=1, source_target_pairs={{0,8},{1,9},{2,10},{3,11},{4,12},{5,13},{6,14},{7,15},{8,0},{9,1},... | collective-permute-start | bytes 307208 | tf_op jit(solution)/shard_map/ppermute | solution.py:389

commit v9 on v7

--- a/solution.py
+++ b/solution.py
@@ -222,9 +222,8 @@
             left = sides[ends[2, k]]
             acc[at] = acc[at] + jnp.dot(left, w[ends[0, k]], preferred_element_type=jnp.float32)
 
-    @pl.loop(0, 8)
-    def _(i):
-        code_half(acc, 24 + i, [], exps, far_ref, i)
+    for i in range(2):
+        code_half(acc, 30 + i, [], exps, far_ref, i)
 
 
 def add_ends(ends, before, after, w, acc):
@@ -235,7 +234,7 @@
         ends_kernel,
         out_shape=(
             jax.ShapeDtypeStruct(acc.shape, jnp.float32),
-            jax.ShapeDtypeStruct((8, CODED, cells), jnp.int16),
+            jax.ShapeDtypeStruct((2, CODED, cells), jnp.int16),
         ),
         in_specs=[smem] + [vmem] * 4,
         out_specs=(vmem, vmem),
@@ -273,24 +272,26 @@
     )(acc, *arrays)
 
 
-def code_near_kernel(acc, near_ref, exps):
-    @pl.loop(0, 8)
+def code_range_kernel(first, acc, *refs):
+    out, exps = refs[-2:]
+
+    @pl.loop(0, out.shape[0])
     def _(i):
-        code_half(acc, 16 + i, [], exps, near_ref, i)
-
-
-def code_near(acc):
+        code_half(acc, first + i, [], exps, out, i)
+
+
+def code_range(acc, first, number, after=()):
     cells = acc.shape[2]
     vmem = pl.BlockSpec(memory_space=pltpu.VMEM)
     return pl.pallas_call(
-        code_near_kernel,
-        out_shape=jax.ShapeDtypeStruct((8, CODED, cells), jnp.int16),
-        in_specs=[vmem],
+        functools.partial(code_range_kernel, first),
+        out_shape=jax.ShapeDtypeStruct((number, CODED, cells), jnp.int16),
+        in_specs=[vmem] * (1 + len(after)),
         out_specs=vmem,
         scratch_shapes=[pltpu.VMEM((16, cells), jnp.float32)],
         compiler_params=pltpu.CompilerParams(vmem_limit_bytes=32 * MIB),
         cost_estimate=LITTLE,
-    )(acc)
+    )(acc, *after)
 
 
 def lift_kernel(index_ref, frac_ref, after, left):
@@ -384,29 +385,30 @@
     acc, w, cot, low = products_call(ahead_kernel, operands, (), cotangent[:1], MUCH)
     after = lax.ppermute(low, "tile", down)
     acc, w, cot, ends = products_call(rest_kernel, operands, (acc, w, cot), None, LITTLE)
-    acc, far = add_ends(ends, before, after, w, acc)
-    far = swap(far, 1, peers)
-    near = swap(code_near(acc), 1, peers)
-    y3 = code(acc, (((14, ((0, 6),)),), ((15, ((0, 7),)),)), (far,))
+    acc, far3 = add_ends(ends, before, after, w, acc)
+    far3 = swap(far3, 1, peers)
+    near = swap(code_range(acc, 16, 8), 1, peers)
+    y3 = code(acc, (((14, ((0, 0),)),), ((15, ((0, 1),)),)), (far3,))
     y3_own = y3[0]
+    far = swap(code_range(acc, 24, 6, (y3_own,)), 1, peers)
     y3 = [swap(v, 2, peers) for v in y3]
     y2 = code(acc, (((12, ((0, 4),)),), ((13, ((0, 5),)),)), (far, y3_own))
     y2_own = y2[0]
     y2 = [swap(v, 2, peers) for v in y2]
-    (a3_low,) = code(acc, (((6, ((0, 6), (1, 0))),),), (near, y3[0], far))
+    (a3_low,) = code(acc, (((6, ((0, 6), (1, 0))),),), (near, y3[0], y2_own))
     (a3_high,) = code(acc, (((7, ((0, 7), (1, 0))),),), (near, y3[1], a3_low))
     a3 = [swap(a3_low, 4, peers), swap(a3_high, 4, peers)]
-    (y1_own,) = code(acc, (((10, ((0, 2),)), (11, ((0, 3),))),), (far, y2_own))
+    (y1_own,) = code(acc, (((10, ((0, 2),)), (11, ((0, 3),))),), (far, y3_own))
     o1 = swap(y1_own, 4, peers)
-    (b2_low,) = code(acc, (((4, ((0, 4), (1, 0), (2, 0))),),), (near, y2[0], a3[0], far))
+    (b2_low,) = code(acc, (((4, ((0, 4), (1, 0), (2, 0))),),), (near, y2[0], a3[0], y1_own))
     (b2_high,) = code(acc, (((5, ((0, 5), (1, 0), (2, 0))),),), (near, y2[1], a3[1], b2_low))
     b2 = [swap(b2_low, 8, peers), swap(b2_high, 8, peers)]
-    y0_own = code(acc, (((8, ((0, 0), (1, 0))),), ((9, ((0, 1), (1, 1))),)), (far, o1, b2_low))
+    y0_own = code(acc, (((8, ((0, 0), (1, 0))),), ((9, ((0, 1), (1, 1))),)), (far, o1, a3[0]))
     y0 = [swap(v, 2, peers) for v in y0_own]
     y0_own = y0_own[0]
     (a1_own,) = code(acc, (((2, ((0, 2),)), (3, ((0, 3),))),), (near, a3_high))
     a1 = swap(a1_own, 4, peers)
-    left = lift_matrix(lev_index, lev_frac, b2_high)
+    left = lift_matrix(lev_index, lev_frac, b2_low)
     out = finish(0, left, acc, ((0, 0), (1, 0), (2, 0), (3, 0)), (near, y0[0], a1, b2[0]))
     return finish(1, left, acc, ((0, 1), (1, 0), (2, 1), (3, 0)), (near, y0[1], a1, b2[1]), out)
 

time: 39.5 us -> 39.8 us (level)
  waiting for transfers between devices: 13.2 us -> 14.3 us
  starting transfers between devices: 12.1 us -> 11.1 us
    ppermute x14 -> x15, waiting for transfers between devices: 13.2 us -> 14.3 us  [swap(): return lax.ppermute(value, 'tile', [(i, i ^ bits) for i in range(peers)])]
    ppermute x14 -> x15, starting transfers between devices: 9.33 us -> 8.4 us  [swap(): return lax.ppermute(value, 'tile', [(i, i ^ bits) for i in range(peers)])]
  transfers between devices with their start and end apart: 16 -> 17, of which waited for: 7 -> 7; matrix products, arithmetic and copies ran while one was open for 0% -> 0% of each run, Pallas kernels for 25% -> 26%
where the time goes in v9:
time: 39.8 us; the launch traced here: 39.4 us
  waiting for transfers between devices  14.3 us (36%)
  Pallas kernels  12.4 us (31%)
  starting transfers between devices  11.1 us (28%)
  between operations  0.82 us (2%)
  local copies, waits for them, and re-layouts  0.74 us (2%)
    ppermute x15, waiting for transfers between devices, swap(): return lax.ppermute(value, 'tile', [(i, i ^ bits) for i in range(peers)])  14.3 us
    ppermute x15, starting transfers between devices, swap(): return lax.ppermute(value, 'tile', [(i, i ^ bits) for i in range(peers)])  8.4 us
    pallas_call x2, Pallas kernels, products_call(): pl.pallas_call(kernel, out_shape=tuple(results), in_specs=[smem, smem] +...  6.38 us
    ppermute x1, starting transfers between devices, staged(): after = lax.ppermute(low, 'tile', down)  2.27 us
    pallas_call x2, Pallas kernels, finish(): pl.pallas_call(functools.partial(finish_kernel, half, takes), out_shape=j...  2.11 us
    pallas_call x9, Pallas kernels, code(): pl.pallas_call(functools.partial(code_kernel, jobs), out_shape=tuple((jax...  1.32 us
    pallas_call x1, Pallas kernels, add_ends(): pl.pallas_call(ends_kernel, out_shape=(jax.ShapeDtypeStruct(acc.shape, jn...  1.15 us
  transfers between devices with their start and end apart: 17, of which 7 were waited for; matrix products, arithmetic and copies ran while one was open for 0% of the time, Pallas kernels for 26%

profile of v9, /device:TPU:0, one launch (start us, length us, event | category | flops | bytes accessed | tf_op | source)
XLA Modules:
  0.0 39.4 jit_solution(8079149692492800044)
XLA Ops:
  0.0 0.7 %fusion = (bf16[1,48,128]{2,1,0:T(8,128)(2,1)S(1)}, bf16[1,48,128]{2,1,0:T(8,128)(2,1)S(1)}) fusion(bf16[16,48,128]{2,1,0:T(8,128)(2,1)} %cot_hbm.3), kind=kLoop, calls=%fused_computation | loop fusion | bytes 49152 | tf_op jit(solution)/shard_map/slice | solution.py:384
  0.7 0.5 %collective-permute-start = (bf16[1,48,128]{2,1,0:T(8,128)(2,1)S(1)}, bf16[1,48,128]{2,1,0:T(8,128)(2,1)S(1)}, u32[]{:S(2)}, u32[]{:S(2)}) collective-permute-start(bf16[1,48,128]{2,1,0:T(8,128)(2,1)S(1)} %get-tuple-element.35), channel_id=1, source_target_pairs={{0,1},{1,2},{2,3},{3,4},{4,5},{5,6},{6,7},{7,8},{8,9},{9,10},{10,1... | collective-permute-start | bytes 36872 | tf_op jit(solution)/shard_map/ppermute | solution.py:384
  1.8 2.9 %shard_map.82 = (f32[257,48,128]{2,1,0:T(8,128)S(1)}, bf16[128,128,128]{2,1,0:T(8,128)(2,1)S(1)}, bf16[16,48,128]{2,1,0:T(8,128)(2,1)S(1)}, bf16[1,48,128]{2,1,0:T(8,128)(2,1)S(1)}) custom-call(s32[1]{0:T(128)S(6)} %copy.19.count_ref, s32[1]{0:T(128)} %bitcast.me_ref, s32[1,128]{1,0:T(1,128)} %tb.3, s32[1,128]{1,0:T(1,128)} %dest.3, s32[1,128]{1,0:T(1,128)} %src.3, ...), custom_call_target="tpu_custom_call" | custom-call | flops 268435456 | bytes 12582912 | tf_op jit(solution)/shard_map/pallas_call | solution.py:184
  4.7 2.3 %collective-permute-start.1 = (bf16[1,48,128]{2,1,0:T(8,128)(2,1)S(1)}, bf16[1,48,128]{2,1,0:T(8,128)(2,1)S(1)}, u32[]{:S(2)}, u32[]{:S(2)}) collective-permute-start(bf16[1,48,128]{2,1,0:T(8,128)(2,1)S(1)} %get-tuple-element.24), channel_id=1, source_target_pairs={{1,0},{2,1},{3,2},{4,3},{5,4},{6,5},{7,6},{8,7},{9,8},{10,9},{11,1... | collective-permute-start | bytes 36872 | tf_op jit(solution)/shard_map/ppermute | solution.py:386
  7.0 3.5 %shard_map.83 = (f32[257,48,128]{2,1,0:T(8,128)S(1)}, bf16[128,128,128]{2,1,0:T(8,128)(2,1)S(1)}, bf16[16,48,128]{2,1,0:T(8,128)(2,1)S(1)}, s32[4,136]{1,0:T(4,128)S(1)}) custom-call(s32[1]{0:T(128)S(6)} %copy.19.count_ref, s32[1]{0:T(128)} %bitcast.me_ref, s32[1,128]{1,0:T(1,128)} %tb.3, ...), custom_call_target="tpu_custom_call", output_to_operand_aliasing={{0}: (7, {}), {1}: (8, {}), {2}: (9, {})} | custom-call | flops 1 | bytes 1 | tf_op jit(solution)/shard_map/pallas_call | solution.py:184
  10.5 1.1 %shard_map.84 = (f32[257,48,128]{2,1,0:T(8,128)S(1)}, s16[2,400,128]{2,1,0:T(8,128)(2,1)S(1)}) custom-call(s32[4,136]{1,0:T(4,128)S(1)} %get-tuple-element.23.ends, bf16[1,48,128]{2,1,0:T(8,128)(2,1)S(1)} %collective-permute-done.before, bf16[1,48,128]{2,1,0:T(8,128)(2,1)S(1)} %collective-permute-done.1.after, ...), custom_call_target="tpu_custom_call", output_to_operand_aliasing={{0}: (4, {})} | custom-call | flops 1 | bytes 1 | tf_op jit(solution)/shard_map/pallas_call | solution.py:233
  11.7 0.4 %shard_map.85 = s16[8,400,128]{2,1,0:T(8,128)(2,1)S(1)} custom-call(f32[257,48,128]{2,1,0:T(8,128)S(1)} %get-tuple-element.27.acc), custom_call_target="tpu_custom_call" | custom-call | flops 1 | bytes 1 | tf_op jit(solution)/shard_map/pallas_call | solution.py:286
  12.2 0.6 %collective-permute-start.2 = (s16[8,400,128]{2,1,0:T(8,128)(2,1)S(1)}, s16[8,400,128]{2,1,0:T(8,128)(2,1)S(1)}, u32[]{:S(2)}, u32[]{:S(2)}) collective-permute-start(s16[8,400,128]{2,1,0:T(8,128)(2,1)S(1)} %shard_map.85), channel_id=1, source_target_pairs={{0,1},{1,0},{2,3},{3,2},{4,5},{5,4},{6,7},{7,6},{8,9},{9,8},{10,11... | collective-permute-start | bytes 2457608 | tf_op jit(solution)/shard_map/ppermute | solution.py:376
  12.7 0.5 %collective-permute-done.3.refs_0_ = s16[2,400,128]{2,1,0:T(8,128)(2,1)S(1)} collective-permute-done((s16[2,400,128]{2,1,0:T(8,128)(2,1)S(1)}, s16[2,400,128]{2,1,0:T(8,128)(2,1)S(1)}, u32[]{:S(2)}, u32[]{:S(2)}) %collective-permute-start.3) | collective-permute-done | bytes 204832 | tf_op jit(solution)/shard_map/ppermute | solution.py:376
  13.2 0.2 shard_map.86
  13.3 0.3 shard_map.87
  13.7 0.2 collective-permute-start.4
  13.9 2.1 %collective-permute-start.10 = (s16[1,400,128]{2,1,0:T(8,128)(2,1)S(1)}, s16[1,400,128]{2,1,0:T(8,128)(2,1)S(1)}, u32[]{:S(2)}, u32[]{:S(2)}) collective-permute-start(s16[1,400,128]{2,1,0:T(8,128)(2,1)S(1)} %get-tuple-element.32), channel_id=1, source_target_pairs={{0,2},{1,3},{2,0},{3,1},{4,6},{5,7},{6,4},{7,5},{8,10},{9,11},{10,... | collective-permute-start | bytes 307208 | tf_op jit(solution)/shard_map/ppermute | solution.py:376
  15.9 0.1 shard_map.90.refs_3_
  16.2 0.2 shard_map.88
  16.3 0.9 %collective-permute-start.5 = (s16[1,400,128]{2,1,0:T(8,128)(2,1)S(1)}, s16[1,400,128]{2,1,0:T(8,128)(2,1)S(1)}, u32[]{:S(2)}, u32[]{:S(2)}) collective-permute-start(s16[1,400,128]{2,1,0:T(8,128)(2,1)S(1)} %get-tuple-element.30.refs_2_), channel_id=1, source_target_pairs={{0,2},{1,3},{2,0},{3,1},{4,6},{5,7},{6,4},{7,5},{8,10},{9,11},{10,... | collective-permute-start | bytes 307208 | tf_op jit(solution)/shard_map/ppermute | solution.py:376
  17.2 2.4 %collective-permute-done.6.refs_1_ = s16[1,400,128]{2,1,0:T(8,128)(2,1)S(1)} collective-permute-done((s16[1,400,128]{2,1,0:T(8,128)(2,1)S(1)}, s16[1,400,128]{2,1,0:T(8,128)(2,1)S(1)}, u32[]{:S(2)}, u32[]{:S(2)}) %collective-permute-start.6) | collective-permute-done | bytes 102432 | tf_op jit(solution)/shard_map/ppermute | solution.py:376
  19.8 0.9 %collective-permute-start.12 = (s16[1,400,128]{2,1,0:T(8,128)(2,1)S(1)}, s16[1,400,128]{2,1,0:T(8,128)(2,1)S(1)}, u32[]{:S(2)}, u32[]{:S(2)}) collective-permute-start(s16[1,400,128]{2,1,0:T(8,128)(2,1)S(1)} %get-tuple-element.33), channel_id=1, source_target_pairs={{0,2},{1,3},{2,0},{3,1},{4,6},{5,7},{6,4},{7,5},{8,10},{9,11},{10,... | collective-permute-start | bytes 307208 | tf_op jit(solution)/shard_map/ppermute | solution.py:376
  20.7 1.1 %collective-permute-done.10.refs_1_ = s16[1,400,128]{2,1,0:T(8,128)(2,1)S(1)} collective-permute-done((s16[1,400,128]{2,1,0:T(8,128)(2,1)S(1)}, s16[1,400,128]{2,1,0:T(8,128)(2,1)S(1)}, u32[]{:S(2)}, u32[]{:S(2)}) %collective-permute-start.10) | collective-permute-done | bytes 102432 | tf_op jit(solution)/shard_map/ppermute | solution.py:376
  22.0 0.1 shard_map.95
  22.2 1.8 %collective-permute-done.5.refs_1_ = s16[1,400,128]{2,1,0:T(8,128)(2,1)S(1)} collective-permute-done((s16[1,400,128]{2,1,0:T(8,128)(2,1)S(1)}, s16[1,400,128]{2,1,0:T(8,128)(2,1)S(1)}, u32[]{:S(2)}, u32[]{:S(2)}) %collective-permute-start.5) | collective-permute-done | bytes 102432 | tf_op jit(solution)/shard_map/ppermute | solution.py:376
  24.0 0.2 collective-permute-start.11
  24.2 2.1 %collective-permute-done.7.refs_2_ = s16[1,400,128]{2,1,0:T(8,128)(2,1)S(1)} collective-permute-done((s16[1,400,128]{2,1,0:T(8,128)(2,1)S(1)}, s16[1,400,128]{2,1,0:T(8,128)(2,1)S(1)}, u32[]{:S(2)}, u32[]{:S(2)}) %collective-permute-start.7) | collective-permute-done | bytes 102432 | tf_op jit(solution)/shard_map/ppermute | solution.py:376
  26.5 1.2 %collective-permute-start.16 = (s16[1,400,128]{2,1,0:T(8,128)(2,1)S(1)}, s16[1,400,128]{2,1,0:T(8,128)(2,1)S(1)}, u32[]{:S(2)}, u32[]{:S(2)}) collective-permute-start(s16[1,400,128]{2,1,0:T(8,128)(2,1)S(1)} %shard_map.91.after.refs_3_), channel_id=1, source_target_pairs={{0,8},{1,9},{2,10},{3,11},{4,12},{5,13},{6,14},{7,15},{8,0},{9,1},... | collective-permute-start | bytes 307208 | tf_op jit(solution)/shard_map/ppermute | solution.py:376
  27.6 2.0 %collective-permute-done.13.refs_2_ = s16[1,400,128]{2,1,0:T(8,128)(2,1)S(1)} collective-permute-done((s16[1,400,128]{2,1,0:T(8,128)(2,1)S(1)}, s16[1,400,128]{2,1,0:T(8,128)(2,1)S(1)}, u32[]{:S(2)}, u32[]{:S(2)}) %collective-permute-start.13) | collective-permute-done | bytes 102432 | tf_op jit(solution)/shard_map/ppermute | solution.py:376
  29.7 0.2 shard_map.93
  30.0 1.1 %collective-permute-start.14 = (s16[1,400,128]{2,1,0:T(8,128)(2,1)S(1)}, s16[1,400,128]{2,1,0:T(8,128)(2,1)S(1)}, u32[]{:S(2)}, u32[]{:S(2)}) collective-permute-start(s16[1,400,128]{2,1,0:T(8,128)(2,1)S(1)} %shard_map.96), channel_id=1, source_target_pairs={{0,8},{1,9},{2,10},{3,11},{4,12},{5,13},{6,14},{7,15},{8,0},{9,1},... | collective-permute-start | bytes 307208 | tf_op jit(solution)/shard_map/ppermute | solution.py:376
  31.2 0.9 %collective-permute-start.9 = (s16[1,400,128]{2,1,0:T(8,128)(2,1)S(1)}, s16[1,400,128]{2,1,0:T(8,128)(2,1)S(1)}, u32[]{:S(2)}, u32[]{:S(2)}) collective-permute-start(s16[1,400,128]{2,1,0:T(8,128)(2,1)S(1)} %get-tuple-element.31), channel_id=1, source_target_pairs={{0,2},{1,3},{2,0},{3,1},{4,6},{5,7},{6,4},{7,5},{8,10},{9,11},{10,... | collective-permute-start | bytes 307208 | tf_op jit(solution)/shard_map/ppermute | solution.py:376
  32.0 0.7 %shard_map.92.left = bf16[120,192]{1,0:T(8,128)(2,1)S(1)} custom-call(s32[8]{0:T(128)S(1)} %copy-done, f32[8]{0:T(128)S(1)} %copy-done.1, s16[1,400,128]{2,1,0:T(8,128)(2,1)S(1)} %shard_map.91.after.refs_3_), custom_call_target="tpu_custom_call" | custom-call | flops 1 | bytes 1 | tf_op jit(solution)/shard_map/pallas_call | solution.py:316
  32.8 4.5 %collective-permute-done.16.refs_3_ = s16[1,400,128]{2,1,0:T(8,128)(2,1)S(1)} collective-permute-done((s16[1,400,128]{2,1,0:T(8,128)(2,1)S(1)}, s16[1,400,128]{2,1,0:T(8,128)(2,1)S(1)}, u32[]{:S(2)}, u32[]{:S(2)}) %collective-permute-start.16) | collective-permute-done | bytes 102432 | tf_op jit(solution)/shard_map/ppermute | solution.py:376
  37.3 1.1 %shard_map.97.refs_4_ = f32[16,120,128]{2,1,0:T(8,128)} custom-call(bf16[120,192]{1,0:T(8,128)(2,1)S(1)} %shard_map.92.left, f32[257,48,128]{2,1,0:T(8,128)S(1)} %get-tuple-element.27.acc, s16[8,400,128]{2,1,0:T(8,128)(2,1)S(1)} %collective-permute-done.2.refs_0_, s16[1,400,128]{2,1,0:T(8,128)(2,1)S(1)} %collective-permute-done.15.refs_1_, ...), custom_call_target="tpu_custom_call" | custom-call | flops 1 | bytes 4194304 | tf_op jit(solution)/shard_map/pallas_call | solution.py:355
  38.4 1.1 %shard_map.98 = f32[16,120,128]{2,1,0:T(8,128)} custom-call(bf16[120,192]{1,0:T(8,128)(2,1)S(1)} %shard_map.92.left, f32[257,48,128]{2,1,0:T(8,128)S(1)} %get-tuple-element.27.acc, s16[8,400,128]{2,1,0:T(8,128)(2,1)S(1)} %collective-permute-done.2.refs_0_, s16[1,400,128]{2,1,0:T(8,128)(2,1)S(1)} %collective-permute-done.9.refs_1_, ...), custom_call_target="tpu_custom_call", output_to_operand_aliasing={{}: (6, {})} | custom-call | flops 1 | bytes 4194304 | tf_op jit(solution)/shard_map/pallas_call | solution.py:355
  (24 shorter events, 1.0 us)
Async XLA Ops:
  0.7 9.8 %collective-permute-start = (bf16[1,48,128]{2,1,0:T(8,128)(2,1)S(1)}, bf16[1,48,128]{2,1,0:T(8,128)(2,1)S(1)}, u32[]{:S(2)}, u32[]{:S(2)}) collective-permute-start(bf16[1,48,128]{2,1,0:T(8,128)(2,1)S(1)} %get-tuple-element.35), channel_id=1, source_target_pairs={{0,1},{1,2},{2,3},{3,4},{4,5},{5,6},{6,7},{7,8},{8,9},{9,10},{10,1... | collective-permute-start | bytes 36872 | tf_op jit(solution)/shard_map/ppermute | solution.py:384
  4.7 5.8 %collective-permute-start.1 = (bf16[1,48,128]{2,1,0:T(8,128)(2,1)S(1)}, bf16[1,48,128]{2,1,0:T(8,128)(2,1)S(1)}, u32[]{:S(2)}, u32[]{:S(2)}) collective-permute-start(bf16[1,48,128]{2,1,0:T(8,128)(2,1)S(1)} %get-tuple-element.24), channel_id=1, source_target_pairs={{1,0},{2,1},{3,2},{4,3},{5,4},{6,5},{7,6},{8,7},{9,8},{10,9},{11,1... | collective-permute-start | bytes 36872 | tf_op jit(solution)/shard_map/ppermute | solution.py:386
  11.7 1.5 %collective-permute-start.3 = (s16[2,400,128]{2,1,0:T(8,128)(2,1)S(1)}, s16[2,400,128]{2,1,0:T(8,128)(2,1)S(1)}, u32[]{:S(2)}, u32[]{:S(2)}) collective-permute-start(s16[2,400,128]{2,1,0:T(8,128)(2,1)S(1)} %get-tuple-element.28), channel_id=1, source_target_pairs={{0,1},{1,0},{2,3},{3,2},{4,5},{5,4},{6,7},{7,6},{8,9},{9,8},{10,11... | collective-permute-start | bytes 614408 | tf_op jit(solution)/shard_map/ppermute | solution.py:376
  12.2 7.4 %collective-permute-start.2 = (s16[8,400,128]{2,1,0:T(8,128)(2,1)S(1)}, s16[8,400,128]{2,1,0:T(8,128)(2,1)S(1)}, u32[]{:S(2)}, u32[]{:S(2)}) collective-permute-start(s16[8,400,128]{2,1,0:T(8,128)(2,1)S(1)} %shard_map.85), channel_id=1, source_target_pairs={{0,1},{1,0},{2,3},{3,2},{4,5},{5,4},{6,7},{7,6},{8,9},{9,8},{10,11... | collective-permute-start | bytes 2457608 | tf_op jit(solution)/shard_map/ppermute | solution.py:376
  13.7 2.3 %collective-permute-start.4 = (s16[6,400,128]{2,1,0:T(8,128)(2,1)S(1)}, s16[6,400,128]{2,1,0:T(8,128)(2,1)S(1)}, u32[]{:S(2)}, u32[]{:S(2)}) collective-permute-start(s16[6,400,128]{2,1,0:T(8,128)(2,1)S(1)} %shard_map.87), channel_id=1, source_target_pairs={{0,1},{1,0},{2,3},{3,2},{4,5},{5,4},{6,7},{7,6},{8,9},{9,8},{10,11... | collective-permute-start | bytes 1843208 | tf_op jit(solution)/shard_map/ppermute | solution.py:376
  13.9 5.7 %collective-permute-start.6 = (s16[1,400,128]{2,1,0:T(8,128)(2,1)S(1)}, s16[1,400,128]{2,1,0:T(8,128)(2,1)S(1)}, u32[]{:S(2)}, u32[]{:S(2)}) collective-permute-start(s16[1,400,128]{2,1,0:T(8,128)(2,1)S(1)} %get-tuple-element.29.refs_0_.refs_1_), channel_id=1, source_target_pairs={{0,2},{1,3},{2,0},{3,1},{4,6},{5,7},{6,4},{7,5},{8,10},{9,11},{10,... | collective-permute-start | bytes 307208 | tf_op jit(solution)/shard_map/ppermute | solution.py:376
  13.9 7.9 %collective-permute-start.10 = (s16[1,400,128]{2,1,0:T(8,128)(2,1)S(1)}, s16[1,400,128]{2,1,0:T(8,128)(2,1)S(1)}, u32[]{:S(2)}, u32[]{:S(2)}) collective-permute-start(s16[1,400,128]{2,1,0:T(8,128)(2,1)S(1)} %get-tuple-element.32), channel_id=1, source_target_pairs={{0,2},{1,3},{2,0},{3,1},{4,6},{5,7},{6,4},{7,5},{8,10},{9,11},{10,... | collective-permute-start | bytes 307208 | tf_op jit(solution)/shard_map/ppermute | solution.py:376
  16.1 13.6 %collective-permute-start.8 = (s16[2,400,128]{2,1,0:T(8,128)(2,1)S(1)}, s16[2,400,128]{2,1,0:T(8,128)(2,1)S(1)}, u32[]{:S(2)}, u32[]{:S(2)}) collective-permute-start(s16[2,400,128]{2,1,0:T(8,128)(2,1)S(1)} %shard_map.90.refs_3_), channel_id=1, source_target_pairs={{0,4},{1,5},{2,6},{3,7},{4,0},{5,1},{6,2},{7,3},{8,12},{9,13},{10,... | collective-permute-start | bytes 614408 | tf_op jit(solution)/shard_map/ppermute | solution.py:376
  16.3 7.7 %collective-permute-start.5 = (s16[1,400,128]{2,1,0:T(8,128)(2,1)S(1)}, s16[1,400,128]{2,1,0:T(8,128)(2,1)S(1)}, u32[]{:S(2)}, u32[]{:S(2)}) collective-permute-start(s16[1,400,128]{2,1,0:T(8,128)(2,1)S(1)} %get-tuple-element.30.refs_2_), channel_id=1, source_target_pairs={{0,2},{1,3},{2,0},{3,1},{4,6},{5,7},{6,4},{7,5},{8,10},{9,11},{10,... | collective-permute-start | bytes 307208 | tf_op jit(solution)/shard_map/ppermute | solution.py:376
  19.7 6.6 %collective-permute-start.7 = (s16[1,400,128]{2,1,0:T(8,128)(2,1)S(1)}, s16[1,400,128]{2,1,0:T(8,128)(2,1)S(1)}, u32[]{:S(2)}, u32[]{:S(2)}) collective-permute-start(s16[1,400,128]{2,1,0:T(8,128)(2,1)S(1)} %shard_map.89.refs_2_), channel_id=1, source_target_pairs={{0,4},{1,5},{2,6},{3,7},{4,0},{5,1},{6,2},{7,3},{8,12},{9,13},{10,... | collective-permute-start | bytes 307208 | tf_op jit(solution)/shard_map/ppermute | solution.py:376
  19.8 7.8 %collective-permute-start.12 = (s16[1,400,128]{2,1,0:T(8,128)(2,1)S(1)}, s16[1,400,128]{2,1,0:T(8,128)(2,1)S(1)}, u32[]{:S(2)}, u32[]{:S(2)}) collective-permute-start(s16[1,400,128]{2,1,0:T(8,128)(2,1)S(1)} %get-tuple-element.33), channel_id=1, source_target_pairs={{0,2},{1,3},{2,0},{3,1},{4,6},{5,7},{6,4},{7,5},{8,10},{9,11},{10,... | collective-permute-start | bytes 307208 | tf_op jit(solution)/shard_map/ppermute | solution.py:376
  21.9 7.7 %collective-permute-start.13 = (s16[1,400,128]{2,1,0:T(8,128)(2,1)S(1)}, s16[1,400,128]{2,1,0:T(8,128)(2,1)S(1)}, u32[]{:S(2)}, u32[]{:S(2)}) collective-permute-start(s16[1,400,128]{2,1,0:T(8,128)(2,1)S(1)} %shard_map.94.refs_1_), channel_id=1, source_target_pairs={{0,4},{1,5},{2,6},{3,7},{4,0},{5,1},{6,2},{7,3},{8,12},{9,13},{10,... | collective-permute-start | bytes 307208 | tf_op jit(solution)/shard_map/ppermute | solution.py:376
  24.0 13.3 %collective-permute-start.11 = (s16[2,400,128]{2,1,0:T(8,128)(2,1)S(1)}, s16[2,400,128]{2,1,0:T(8,128)(2,1)S(1)}, u32[]{:S(2)}, u32[]{:S(2)}) collective-permute-start(s16[2,400,128]{2,1,0:T(8,128)(2,1)S(1)} %shard_map.95), channel_id=1, source_target_pairs={{0,4},{1,5},{2,6},{3,7},{4,0},{5,1},{6,2},{7,3},{8,12},{9,13},{10,... | collective-permute-start | bytes 614408 | tf_op jit(solution)/shard_map/ppermute | solution.py:376
  26.4 5.6 %copy-start = (s32[8]{0:T(128)S(1)}, s32[8]{0:T(128)}, u32[]{:S(2)}) copy-start(s32[8]{0:T(128)} %index_ref.1) | copy-start | bytes 100
  26.4 5.6 %copy-start.1 = (f32[8]{0:T(128)S(1)}, f32[8]{0:T(128)}, u32[]{:S(2)}) copy-start(f32[8]{0:T(128)} %frac_ref.1) | copy-start | bytes 100
  26.5 10.8 %collective-permute-start.16 = (s16[1,400,128]{2,1,0:T(8,128)(2,1)S(1)}, s16[1,400,128]{2,1,0:T(8,128)(2,1)S(1)}, u32[]{:S(2)}, u32[]{:S(2)}) collective-permute-start(s16[1,400,128]{2,1,0:T(8,128)(2,1)S(1)} %shard_map.91.after.refs_3_), channel_id=1, source_target_pairs={{0,8},{1,9},{2,10},{3,11},{4,12},{5,13},{6,14},{7,15},{8,0},{9,1},... | collective-permute-start | bytes 307208 | tf_op jit(solution)/shard_map/ppermute | solution.py:376
  29.9 7.4 %collective-permute-start.15 = (s16[1,400,128]{2,1,0:T(8,128)(2,1)S(1)}, s16[1,400,128]{2,1,0:T(8,128)(2,1)S(1)}, u32[]{:S(2)}, u32[]{:S(2)}) collective-permute-start(s16[1,400,128]{2,1,0:T(8,128)(2,1)S(1)} %get-tuple-element.34), channel_id=1, source_target_pairs={{0,2},{1,3},{2,0},{3,1},{4,6},{5,7},{6,4},{7,5},{8,10},{9,11},{10,... | collective-permute-start | bytes 307208 | tf_op jit(solution)/shard_map/ppermute | solution.py:376
  30.0 8.4 %collective-permute-start.14 = (s16[1,400,128]{2,1,0:T(8,128)(2,1)S(1)}, s16[1,400,128]{2,1,0:T(8,128)(2,1)S(1)}, u32[]{:S(2)}, u32[]{:S(2)}) collective-permute-start(s16[1,400,128]{2,1,0:T(8,128)(2,1)S(1)} %shard_map.96), channel_id=1, source_target_pairs={{0,8},{1,9},{2,10},{3,11},{4,12},{5,13},{6,14},{7,15},{8,0},{9,1},... | collective-permute-start | bytes 307208 | tf_op jit(solution)/shard_map/ppermute | solution.py:376
  31.2 7.2 %collective-permute-start.9 = (s16[1,400,128]{2,1,0:T(8,128)(2,1)S(1)}, s16[1,400,128]{2,1,0:T(8,128)(2,1)S(1)}, u32[]{:S(2)}, u32[]{:S(2)}) collective-permute-start(s16[1,400,128]{2,1,0:T(8,128)(2,1)S(1)} %get-tuple-element.31), channel_id=1, source_target_pairs={{0,2},{1,3},{2,0},{3,1},{4,6},{5,7},{6,4},{7,5},{8,10},{9,11},{10,... | collective-permute-start | bytes 307208 | tf_op jit(solution)/shard_map/ppermute | solution.py:376

commit v10 on v7

--- a/solution.py
+++ b/solution.py
@@ -222,7 +222,7 @@
             left = sides[ends[2, k]]
             acc[at] = acc[at] + jnp.dot(left, w[ends[0, k]], preferred_element_type=jnp.float32)
 
-    @pl.loop(0, 8)
+    @pl.loop(0, 8, unroll=4)
     def _(i):
         code_half(acc, 24 + i, [], exps, far_ref, i)
 
@@ -274,7 +274,7 @@
 
 
 def code_near_kernel(acc, near_ref, exps):
-    @pl.loop(0, 8)
+    @pl.loop(0, 8, unroll=4)
     def _(i):
         code_half(acc, 16 + i, [], exps, near_ref, i)
 
@@ -334,11 +334,11 @@
         second = (total - first.astype(jnp.float32)).astype(jnp.bfloat16)
         right = jnp.concatenate([first, second, first, second], axis=0)
         out[b] = jnp.dot(left[...], right, preferred_element_type=jnp.float32)
-        if b % 4 == 3:
+        if b % 2:
             copy = pltpu.make_async_copy(
-                out.at[pl.ds(b - 3, 4)],
-                out_hbm.at[pl.ds(half * HALF + b - 3, 4)],
-                sems.at[b // 4],
+                out.at[pl.ds(b - 1, 2)],
+                out_hbm.at[pl.ds(half * HALF + b - 1, 2)],
+                sems.at[b // 2],
             )
             copy.start()
             copies.append(copy)
@@ -358,7 +358,7 @@
         out_specs=hbm,
         scratch_shapes=[
             pltpu.VMEM((HALF, VARS * LEV, cells), jnp.float32),
-            pltpu.SemaphoreType.DMA((HALF // 4,)),
+            pltpu.SemaphoreType.DMA((HALF // 2,)),
         ],
         input_output_aliases={2 + len(arrays): 0} if extra else {},
         compiler_params=pltpu.CompilerParams(vmem_limit_bytes=32 * MIB),

time: 39.5 us -> 39.5 us (level)
  transfers between devices with their start and end apart: 16 -> 16, of which waited for: 7 -> 8; matrix products, arithmetic and copies ran while one was open for 0% -> 0% of each run, Pallas kernels for 25% -> 25%
where the time goes in v10:
time: 39.5 us; the launch traced here: 39.2 us
  waiting for transfers between devices  13.3 us (34%)
  Pallas kernels  12.3 us (31%)
  starting transfers between devices  12.1 us (31%)
  between operations  0.8 us (2%)
  local copies, waits for them, and re-layouts  0.74 us (2%)
    ppermute x14, waiting for transfers between devices, swap(): return lax.ppermute(value, 'tile', [(i, i ^ bits) for i in range(peers)])  13.2 us
    ppermute x14, starting transfers between devices, swap(): return lax.ppermute(value, 'tile', [(i, i ^ bits) for i in range(peers)])  9.38 us
    pallas_call x2, Pallas kernels, products_call(): pl.pallas_call(kernel, out_shape=tuple(results), in_specs=[smem, smem] +...  6.38 us
    ppermute x1, starting transfers between devices, staged(): after = lax.ppermute(low, 'tile', down)  2.26 us
    pallas_call x2, Pallas kernels, finish(): pl.pallas_call(functools.partial(finish_kernel, half, takes), out_shape=j...  2.06 us
    pallas_call x1, Pallas kernels, add_ends(): pl.pallas_call(ends_kernel, out_shape=(jax.ShapeDtypeStruct(acc.shape, jn...  1.41 us
    pallas_call x9, Pallas kernels, code(): pl.pallas_call(functools.partial(code_kernel, jobs), out_shape=tuple((jax...  1.32 us
  transfers between devices with their start and end apart: 16, of which 8 were waited for; matrix products, arithmetic and copies ran while one was open for 0% of the time, Pallas kernels for 25%

profile of v10, /device:TPU:0, one launch (start us, length us, event | category | flops | bytes accessed | tf_op | source)
XLA Modules:
  0.0 39.2 jit_solution(13993944005184361502)
XLA Ops:
  0.0 0.7 %fusion = (bf16[1,48,128]{2,1,0:T(8,128)(2,1)S(1)}, bf16[1,48,128]{2,1,0:T(8,128)(2,1)S(1)}) fusion(bf16[16,48,128]{2,1,0:T(8,128)(2,1)} %cot_hbm.3), kind=kLoop, calls=%fused_computation | loop fusion | bytes 49152 | tf_op jit(solution)/shard_map/slice | solution.py:383
  0.7 0.5 %collective-permute-start = (bf16[1,48,128]{2,1,0:T(8,128)(2,1)S(1)}, bf16[1,48,128]{2,1,0:T(8,128)(2,1)S(1)}, u32[]{:S(2)}, u32[]{:S(2)}) collective-permute-start(bf16[1,48,128]{2,1,0:T(8,128)(2,1)S(1)} %get-tuple-element.35), channel_id=1, source_target_pairs={{0,1},{1,2},{2,3},{3,4},{4,5},{5,6},{6,7},{7,8},{8,9},{9,10},{10,1... | collective-permute-start | bytes 36872 | tf_op jit(solution)/shard_map/ppermute | solution.py:383
  1.8 2.9 %shard_map.82 = (f32[257,48,128]{2,1,0:T(8,128)S(1)}, bf16[128,128,128]{2,1,0:T(8,128)(2,1)S(1)}, bf16[16,48,128]{2,1,0:T(8,128)(2,1)S(1)}, bf16[1,48,128]{2,1,0:T(8,128)(2,1)S(1)}) custom-call(s32[1]{0:T(128)S(6)} %copy.19.count_ref, s32[1]{0:T(128)} %bitcast.me_ref, s32[1,128]{1,0:T(1,128)} %tb.3, s32[1,128]{1,0:T(1,128)} %dest.3, s32[1,128]{1,0:T(1,128)} %src.3, ...), custom_call_target="tpu_custom_call" | custom-call | flops 268435456 | bytes 12582912 | tf_op jit(solution)/shard_map/pallas_call | solution.py:184
  4.8 2.3 %collective-permute-start.1 = (bf16[1,48,128]{2,1,0:T(8,128)(2,1)S(1)}, bf16[1,48,128]{2,1,0:T(8,128)(2,1)S(1)}, u32[]{:S(2)}, u32[]{:S(2)}) collective-permute-start(bf16[1,48,128]{2,1,0:T(8,128)(2,1)S(1)} %get-tuple-element.24), channel_id=1, source_target_pairs={{1,0},{2,1},{3,2},{4,3},{5,4},{6,5},{7,6},{8,7},{9,8},{10,9},{11,1... | collective-permute-start | bytes 36872 | tf_op jit(solution)/shard_map/ppermute | solution.py:385
  7.0 3.5 %shard_map.83 = (f32[257,48,128]{2,1,0:T(8,128)S(1)}, bf16[128,128,128]{2,1,0:T(8,128)(2,1)S(1)}, bf16[16,48,128]{2,1,0:T(8,128)(2,1)S(1)}, s32[4,136]{1,0:T(4,128)S(1)}) custom-call(s32[1]{0:T(128)S(6)} %copy.19.count_ref, s32[1]{0:T(128)} %bitcast.me_ref, s32[1,128]{1,0:T(1,128)} %tb.3, ...), custom_call_target="tpu_custom_call", output_to_operand_aliasing={{0}: (7, {}), {1}: (8, {}), {2}: (9, {})} | custom-call | flops 1 | bytes 1 | tf_op jit(solution)/shard_map/pallas_call | solution.py:184
  10.5 1.4 %shard_map.84 = (f32[257,48,128]{2,1,0:T(8,128)S(1)}, s16[8,400,128]{2,1,0:T(8,128)(2,1)S(1)}) custom-call(s32[4,136]{1,0:T(4,128)S(1)} %get-tuple-element.23.ends, bf16[1,48,128]{2,1,0:T(8,128)(2,1)S(1)} %collective-permute-done.before, bf16[1,48,128]{2,1,0:T(8,128)(2,1)S(1)} %collective-permute-done.1.after, ...), custom_call_target="tpu_custom_call", output_to_operand_aliasing={{0}: (4, {})} | custom-call | flops 1 | bytes 1 | tf_op jit(solution)/shard_map/pallas_call | solution.py:234
  12.0 0.4 shard_map.85
  12.4 0.6 %collective-permute-start.2 = (s16[8,400,128]{2,1,0:T(8,128)(2,1)S(1)}, s16[8,400,128]{2,1,0:T(8,128)(2,1)S(1)}, u32[]{:S(2)}, u32[]{:S(2)}) collective-permute-start(s16[8,400,128]{2,1,0:T(8,128)(2,1)S(1)} %shard_map.85), channel_id=1, source_target_pairs={{0,1},{1,0},{2,3},{3,2},{4,5},{5,4},{6,7},{7,6},{8,9},{9,8},{10,11... | collective-permute-start | bytes 2457608 | tf_op jit(solution)/shard_map/ppermute | solution.py:375
  12.9 1.4 %collective-permute-done.3.refs_0_.refs_2_.refs_3_ = s16[8,400,128]{2,1,0:T(8,128)(2,1)S(1)} collective-permute-done((s16[8,400,128]{2,1,0:T(8,128)(2,1)S(1)}, s16[8,400,128]{2,1,0:T(8,128)(2,1)S(1)}, u32[]{:S(2)}, u32[]{:S(2)}) %collective-permute-start.3) | collective-permute-done | bytes 819232 | tf_op jit(solution)/shard_map/ppermute | solution.py:375
  14.3 0.1 shard_map.86
  14.6 0.2 shard_map.87
  14.7 0.2 shard_map.93
  14.9 1.0 %collective-permute-start.10 = (s16[2,400,128]{2,1,0:T(8,128)(2,1)S(1)}, s16[2,400,128]{2,1,0:T(8,128)(2,1)S(1)}, u32[]{:S(2)}, u32[]{:S(2)}) collective-permute-start(s16[2,400,128]{2,1,0:T(8,128)(2,1)S(1)} %shard_map.93), channel_id=1, source_target_pairs={{0,4},{1,5},{2,6},{3,7},{4,0},{5,1},{6,2},{7,3},{8,12},{9,13},{10,... | collective-permute-start | bytes 614408 | tf_op jit(solution)/shard_map/ppermute | solution.py:375
  15.9 1.2 %collective-permute-start.5 = (s16[1,400,128]{2,1,0:T(8,128)(2,1)S(1)}, s16[1,400,128]{2,1,0:T(8,128)(2,1)S(1)}, u32[]{:S(2)}, u32[]{:S(2)}) collective-permute-start(s16[1,400,128]{2,1,0:T(8,128)(2,1)S(1)} %get-tuple-element.31), channel_id=1, source_target_pairs={{0,2},{1,3},{2,0},{3,1},{4,6},{5,7},{6,4},{7,5},{8,10},{9,11},{10,... | collective-permute-start | bytes 307208 | tf_op jit(solution)/shard_map/ppermute | solution.py:375
  17.0 0.9 %collective-permute-start.8 = (s16[1,400,128]{2,1,0:T(8,128)(2,1)S(1)}, s16[1,400,128]{2,1,0:T(8,128)(2,1)S(1)}, u32[]{:S(2)}, u32[]{:S(2)}) collective-permute-start(s16[1,400,128]{2,1,0:T(8,128)(2,1)S(1)} %get-tuple-element.32.refs_1_), channel_id=1, source_target_pairs={{0,2},{1,3},{2,0},{3,1},{4,6},{5,7},{6,4},{7,5},{8,10},{9,11},{10,... | collective-permute-start | bytes 307208 | tf_op jit(solution)/shard_map/ppermute | solution.py:375
  17.9 2.4 %collective-permute-done.6.refs_1_ = s16[1,400,128]{2,1,0:T(8,128)(2,1)S(1)} collective-permute-done((s16[1,400,128]{2,1,0:T(8,128)(2,1)S(1)}, s16[1,400,128]{2,1,0:T(8,128)(2,1)S(1)}, u32[]{:S(2)}, u32[]{:S(2)}) %collective-permute-start.6) | collective-permute-done | bytes 102432 | tf_op jit(solution)/shard_map/ppermute | solution.py:375
  20.5 0.7 %collective-permute-start.4 = (s16[1,400,128]{2,1,0:T(8,128)(2,1)S(1)}, s16[1,400,128]{2,1,0:T(8,128)(2,1)S(1)}, u32[]{:S(2)}, u32[]{:S(2)}) collective-permute-start(s16[1,400,128]{2,1,0:T(8,128)(2,1)S(1)} %get-tuple-element.30), channel_id=1, source_target_pairs={{0,2},{1,3},{2,0},{3,1},{4,6},{5,7},{6,4},{7,5},{8,10},{9,11},{10,... | collective-permute-start | bytes 307208 | tf_op jit(solution)/shard_map/ppermute | solution.py:375
  21.2 1.3 %collective-permute-done.5.refs_1_ = s16[1,400,128]{2,1,0:T(8,128)(2,1)S(1)} collective-permute-done((s16[1,400,128]{2,1,0:T(8,128)(2,1)S(1)}, s16[1,400,128]{2,1,0:T(8,128)(2,1)S(1)}, u32[]{:S(2)}, u32[]{:S(2)}) %collective-permute-start.5) | collective-permute-done | bytes 102432 | tf_op jit(solution)/shard_map/ppermute | solution.py:375
  22.7 0.1 shard_map.95
  22.8 1.8 %collective-permute-done.8.refs_1_ = s16[1,400,128]{2,1,0:T(8,128)(2,1)S(1)} collective-permute-done((s16[1,400,128]{2,1,0:T(8,128)(2,1)S(1)}, s16[1,400,128]{2,1,0:T(8,128)(2,1)S(1)}, u32[]{:S(2)}, u32[]{:S(2)}) %collective-permute-start.8) | collective-permute-done | bytes 102432 | tf_op jit(solution)/shard_map/ppermute | solution.py:375
  24.7 0.2 collective-permute-start.12
  24.9 1.1 %collective-permute-done.9.refs_2_ = s16[1,400,128]{2,1,0:T(8,128)(2,1)S(1)} collective-permute-done((s16[1,400,128]{2,1,0:T(8,128)(2,1)S(1)}, s16[1,400,128]{2,1,0:T(8,128)(2,1)S(1)}, u32[]{:S(2)}, u32[]{:S(2)}) %collective-permute-start.9) | collective-permute-done | bytes 102432 | tf_op jit(solution)/shard_map/ppermute | solution.py:375
  26.2 1.6 %collective-permute-start.15 = (s16[1,400,128]{2,1,0:T(8,128)(2,1)S(1)}, s16[1,400,128]{2,1,0:T(8,128)(2,1)S(1)}, u32[]{:S(2)}, u32[]{:S(2)}) collective-permute-start(s16[1,400,128]{2,1,0:T(8,128)(2,1)S(1)} %shard_map.90.refs_3_.refs_2_), channel_id=1, source_target_pairs={{0,8},{1,9},{2,10},{3,11},{4,12},{5,13},{6,14},{7,15},{8,0},{9,1},... | collective-permute-start | bytes 307208 | tf_op jit(solution)/shard_map/ppermute | solution.py:375
  27.8 0.2 shard_map.94
  28.0 0.9 %collective-permute-start.14 = (s16[1,400,128]{2,1,0:T(8,128)(2,1)S(1)}, s16[1,400,128]{2,1,0:T(8,128)(2,1)S(1)}, u32[]{:S(2)}, u32[]{:S(2)}) collective-permute-start(s16[1,400,128]{2,1,0:T(8,128)(2,1)S(1)} %get-tuple-element.34), channel_id=1, source_target_pairs={{0,2},{1,3},{2,0},{3,1},{4,6},{5,7},{6,4},{7,5},{8,10},{9,11},{10,... | collective-permute-start | bytes 307208 | tf_op jit(solution)/shard_map/ppermute | solution.py:375
  28.9 0.6 %collective-permute-done.7.refs_2_ = s16[1,400,128]{2,1,0:T(8,128)(2,1)S(1)} collective-permute-done((s16[1,400,128]{2,1,0:T(8,128)(2,1)S(1)}, s16[1,400,128]{2,1,0:T(8,128)(2,1)S(1)}, u32[]{:S(2)}, u32[]{:S(2)}) %collective-permute-start.7) | collective-permute-done | bytes 102432 | tf_op jit(solution)/shard_map/ppermute | solution.py:375
  29.6 1.1 %collective-permute-start.13 = (s16[1,400,128]{2,1,0:T(8,128)(2,1)S(1)}, s16[1,400,128]{2,1,0:T(8,128)(2,1)S(1)}, u32[]{:S(2)}, u32[]{:S(2)}) collective-permute-start(s16[1,400,128]{2,1,0:T(8,128)(2,1)S(1)} %shard_map.91.after), channel_id=1, source_target_pairs={{0,8},{1,9},{2,10},{3,11},{4,12},{5,13},{6,14},{7,15},{8,0},{9,1},... | collective-permute-start | bytes 307208 | tf_op jit(solution)/shard_map/ppermute | solution.py:375
  30.8 1.0 %collective-permute-start.11 = (s16[1,400,128]{2,1,0:T(8,128)(2,1)S(1)}, s16[1,400,128]{2,1,0:T(8,128)(2,1)S(1)}, u32[]{:S(2)}, u32[]{:S(2)}) collective-permute-start(s16[1,400,128]{2,1,0:T(8,128)(2,1)S(1)} %get-tuple-element.33), channel_id=1, source_target_pairs={{0,2},{1,3},{2,0},{3,1},{4,6},{5,7},{6,4},{7,5},{8,10},{9,11},{10,... | collective-permute-start | bytes 307208 | tf_op jit(solution)/shard_map/ppermute | solution.py:375
  31.7 0.7 %shard_map.92.left = bf16[120,192]{1,0:T(8,128)(2,1)S(1)} custom-call(s32[8]{0:T(128)S(1)} %copy-done, f32[8]{0:T(128)S(1)} %copy-done.1, s16[1,400,128]{2,1,0:T(8,128)(2,1)S(1)} %shard_map.91.after), custom_call_target="tpu_custom_call" | custom-call | flops 1 | bytes 1 | tf_op jit(solution)/shard_map/pallas_call | solution.py:315
  32.5 4.5 %collective-permute-done.15.refs_3_ = s16[1,400,128]{2,1,0:T(8,128)(2,1)S(1)} collective-permute-done((s16[1,400,128]{2,1,0:T(8,128)(2,1)S(1)}, s16[1,400,128]{2,1,0:T(8,128)(2,1)S(1)}, u32[]{:S(2)}, u32[]{:S(2)}) %collective-permute-start.15) | collective-permute-done | bytes 102432 | tf_op jit(solution)/shard_map/ppermute | solution.py:375
  37.0 1.0 %shard_map.96.refs_4_ = f32[16,120,128]{2,1,0:T(8,128)} custom-call(bf16[120,192]{1,0:T(8,128)(2,1)S(1)} %shard_map.92.left, f32[257,48,128]{2,1,0:T(8,128)S(1)} %get-tuple-element.27.acc, s16[8,400,128]{2,1,0:T(8,128)(2,1)S(1)} %collective-permute-done.2.refs_0_, s16[1,400,128]{2,1,0:T(8,128)(2,1)S(1)} %collective-permute-done.14.refs_1_, ...), custom_call_target="tpu_custom_call" | custom-call | flops 1 | bytes 4194304 | tf_op jit(solution)/shard_map/pallas_call | solution.py:354
  38.1 1.0 %shard_map.97 = f32[16,120,128]{2,1,0:T(8,128)} custom-call(bf16[120,192]{1,0:T(8,128)(2,1)S(1)} %shard_map.92.left, f32[257,48,128]{2,1,0:T(8,128)S(1)} %get-tuple-element.27.acc, s16[8,400,128]{2,1,0:T(8,128)(2,1)S(1)} %collective-permute-done.2.refs_0_, s16[1,400,128]{2,1,0:T(8,128)(2,1)S(1)} %collective-permute-done.11.refs_1_, ...), custom_call_target="tpu_custom_call", output_to_operand_aliasing={{}: (6, {})} | custom-call | flops 1 | bytes 4194304 | tf_op jit(solution)/shard_map/pallas_call | solution.py:354
  (21 shorter events, 0.9 us)
Async XLA Ops:
  0.7 9.8 %collective-permute-start = (bf16[1,48,128]{2,1,0:T(8,128)(2,1)S(1)}, bf16[1,48,128]{2,1,0:T(8,128)(2,1)S(1)}, u32[]{:S(2)}, u32[]{:S(2)}) collective-permute-start(bf16[1,48,128]{2,1,0:T(8,128)(2,1)S(1)} %get-tuple-element.35), channel_id=1, source_target_pairs={{0,1},{1,2},{2,3},{3,4},{4,5},{5,6},{6,7},{7,8},{8,9},{9,10},{10,1... | collective-permute-start | bytes 36872 | tf_op jit(solution)/shard_map/ppermute | solution.py:383
  4.8 5.8 %collective-permute-start.1 = (bf16[1,48,128]{2,1,0:T(8,128)(2,1)S(1)}, bf16[1,48,128]{2,1,0:T(8,128)(2,1)S(1)}, u32[]{:S(2)}, u32[]{:S(2)}) collective-permute-start(bf16[1,48,128]{2,1,0:T(8,128)(2,1)S(1)} %get-tuple-element.24), channel_id=1, source_target_pairs={{1,0},{2,1},{3,2},{4,3},{5,4},{6,5},{7,6},{8,7},{9,8},{10,9},{11,1... | collective-permute-start | bytes 36872 | tf_op jit(solution)/shard_map/ppermute | solution.py:385
  11.9 2.4 %collective-permute-start.3 = (s16[8,400,128]{2,1,0:T(8,128)(2,1)S(1)}, s16[8,400,128]{2,1,0:T(8,128)(2,1)S(1)}, u32[]{:S(2)}, u32[]{:S(2)}) collective-permute-start(s16[8,400,128]{2,1,0:T(8,128)(2,1)S(1)} %get-tuple-element.28), channel_id=1, source_target_pairs={{0,1},{1,0},{2,3},{3,2},{4,5},{5,4},{6,7},{7,6},{8,9},{9,8},{10,11... | collective-permute-start | bytes 2457608 | tf_op jit(solution)/shard_map/ppermute | solution.py:375
  12.4 5.5 %collective-permute-start.2 = (s16[8,400,128]{2,1,0:T(8,128)(2,1)S(1)}, s16[8,400,128]{2,1,0:T(8,128)(2,1)S(1)}, u32[]{:S(2)}, u32[]{:S(2)}) collective-permute-start(s16[8,400,128]{2,1,0:T(8,128)(2,1)S(1)} %shard_map.85), channel_id=1, source_target_pairs={{0,1},{1,0},{2,3},{3,2},{4,5},{5,4},{6,7},{7,6},{8,9},{9,8},{10,11... | collective-permute-start | bytes 2457608 | tf_op jit(solution)/shard_map/ppermute | solution.py:375
  14.5 5.8 %collective-permute-start.6 = (s16[1,400,128]{2,1,0:T(8,128)(2,1)S(1)}, s16[1,400,128]{2,1,0:T(8,128)(2,1)S(1)}, u32[]{:S(2)}, u32[]{:S(2)}) collective-permute-start(s16[1,400,128]{2,1,0:T(8,128)(2,1)S(1)} %get-tuple-element.29.refs_1_), channel_id=1, source_target_pairs={{0,2},{1,3},{2,0},{3,1},{4,6},{5,7},{6,4},{7,5},{8,10},{9,11},{10,... | collective-permute-start | bytes 307208 | tf_op jit(solution)/shard_map/ppermute | solution.py:375
  14.9 12.9 %collective-permute-start.10 = (s16[2,400,128]{2,1,0:T(8,128)(2,1)S(1)}, s16[2,400,128]{2,1,0:T(8,128)(2,1)S(1)}, u32[]{:S(2)}, u32[]{:S(2)}) collective-permute-start(s16[2,400,128]{2,1,0:T(8,128)(2,1)S(1)} %shard_map.93), channel_id=1, source_target_pairs={{0,4},{1,5},{2,6},{3,7},{4,0},{5,1},{6,2},{7,3},{8,12},{9,13},{10,... | collective-permute-start | bytes 614408 | tf_op jit(solution)/shard_map/ppermute | solution.py:375
  15.9 6.6 %collective-permute-start.5 = (s16[1,400,128]{2,1,0:T(8,128)(2,1)S(1)}, s16[1,400,128]{2,1,0:T(8,128)(2,1)S(1)}, u32[]{:S(2)}, u32[]{:S(2)}) collective-permute-start(s16[1,400,128]{2,1,0:T(8,128)(2,1)S(1)} %get-tuple-element.31), channel_id=1, source_target_pairs={{0,2},{1,3},{2,0},{3,1},{4,6},{5,7},{6,4},{7,5},{8,10},{9,11},{10,... | collective-permute-start | bytes 307208 | tf_op jit(solution)/shard_map/ppermute | solution.py:375
  17.0 7.6 %collective-permute-start.8 = (s16[1,400,128]{2,1,0:T(8,128)(2,1)S(1)}, s16[1,400,128]{2,1,0:T(8,128)(2,1)S(1)}, u32[]{:S(2)}, u32[]{:S(2)}) collective-permute-start(s16[1,400,128]{2,1,0:T(8,128)(2,1)S(1)} %get-tuple-element.32.refs_1_), channel_id=1, source_target_pairs={{0,2},{1,3},{2,0},{3,1},{4,6},{5,7},{6,4},{7,5},{8,10},{9,11},{10,... | collective-permute-start | bytes 307208 | tf_op jit(solution)/shard_map/ppermute | solution.py:375
  20.4 5.7 %collective-permute-start.9 = (s16[1,400,128]{2,1,0:T(8,128)(2,1)S(1)}, s16[1,400,128]{2,1,0:T(8,128)(2,1)S(1)}, u32[]{:S(2)}, u32[]{:S(2)}) collective-permute-start(s16[1,400,128]{2,1,0:T(8,128)(2,1)S(1)} %shard_map.88.refs_2_), channel_id=1, source_target_pairs={{0,4},{1,5},{2,6},{3,7},{4,0},{5,1},{6,2},{7,3},{8,12},{9,13},{10,... | collective-permute-start | bytes 307208 | tf_op jit(solution)/shard_map/ppermute | solution.py:375
  20.5 8.4 %collective-permute-start.4 = (s16[1,400,128]{2,1,0:T(8,128)(2,1)S(1)}, s16[1,400,128]{2,1,0:T(8,128)(2,1)S(1)}, u32[]{:S(2)}, u32[]{:S(2)}) collective-permute-start(s16[1,400,128]{2,1,0:T(8,128)(2,1)S(1)} %get-tuple-element.30), channel_id=1, source_target_pairs={{0,2},{1,3},{2,0},{3,1},{4,6},{5,7},{6,4},{7,5},{8,10},{9,11},{10,... | collective-permute-start | bytes 307208 | tf_op jit(solution)/shard_map/ppermute | solution.py:375
  22.6 6.9 %collective-permute-start.7 = (s16[1,400,128]{2,1,0:T(8,128)(2,1)S(1)}, s16[1,400,128]{2,1,0:T(8,128)(2,1)S(1)}, u32[]{:S(2)}, u32[]{:S(2)}) collective-permute-start(s16[1,400,128]{2,1,0:T(8,128)(2,1)S(1)} %shard_map.89.refs_1_), channel_id=1, source_target_pairs={{0,4},{1,5},{2,6},{3,7},{4,0},{5,1},{6,2},{7,3},{8,12},{9,13},{10,... | collective-permute-start | bytes 307208 | tf_op jit(solution)/shard_map/ppermute | solution.py:375
  24.7 12.4 %collective-permute-start.12 = (s16[2,400,128]{2,1,0:T(8,128)(2,1)S(1)}, s16[2,400,128]{2,1,0:T(8,128)(2,1)S(1)}, u32[]{:S(2)}, u32[]{:S(2)}) collective-permute-start(s16[2,400,128]{2,1,0:T(8,128)(2,1)S(1)} %shard_map.95), channel_id=1, source_target_pairs={{0,4},{1,5},{2,6},{3,7},{4,0},{5,1},{6,2},{7,3},{8,12},{9,13},{10,... | collective-permute-start | bytes 614408 | tf_op jit(solution)/shard_map/ppermute | solution.py:375
  26.2 5.5 %copy-start = (s32[8]{0:T(128)S(1)}, s32[8]{0:T(128)}, u32[]{:S(2)}) copy-start(s32[8]{0:T(128)} %index_ref.1) | copy-start | bytes 100
  26.2 5.5 %copy-start.1 = (f32[8]{0:T(128)S(1)}, f32[8]{0:T(128)}, u32[]{:S(2)}) copy-start(f32[8]{0:T(128)} %frac_ref.1) | copy-start | bytes 100
  26.2 10.8 %collective-permute-start.15 = (s16[1,400,128]{2,1,0:T(8,128)(2,1)S(1)}, s16[1,400,128]{2,1,0:T(8,128)(2,1)S(1)}, u32[]{:S(2)}, u32[]{:S(2)}) collective-permute-start(s16[1,400,128]{2,1,0:T(8,128)(2,1)S(1)} %shard_map.90.refs_3_.refs_2_), channel_id=1, source_target_pairs={{0,8},{1,9},{2,10},{3,11},{4,12},{5,13},{6,14},{7,15},{8,0},{9,1},... | collective-permute-start | bytes 307208 | tf_op jit(solution)/shard_map/ppermute | solution.py:375
  28.0 9.0 %collective-permute-start.14 = (s16[1,400,128]{2,1,0:T(8,128)(2,1)S(1)}, s16[1,400,128]{2,1,0:T(8,128)(2,1)S(1)}, u32[]{:S(2)}, u32[]{:S(2)}) collective-permute-start(s16[1,400,128]{2,1,0:T(8,128)(2,1)S(1)} %get-tuple-element.34), channel_id=1, source_target_pairs={{0,2},{1,3},{2,0},{3,1},{4,6},{5,7},{6,4},{7,5},{8,10},{9,11},{10,... | collective-permute-start | bytes 307208 | tf_op jit(solution)/shard_map/ppermute | solution.py:375
  29.6 8.5 %collective-permute-start.13 = (s16[1,400,128]{2,1,0:T(8,128)(2,1)S(1)}, s16[1,400,128]{2,1,0:T(8,128)(2,1)S(1)}, u32[]{:S(2)}, u32[]{:S(2)}) collective-permute-start(s16[1,400,128]{2,1,0:T(8,128)(2,1)S(1)} %shard_map.91.after), channel_id=1, source_target_pairs={{0,8},{1,9},{2,10},{3,11},{4,12},{5,13},{6,14},{7,15},{8,0},{9,1},... | collective-permute-start | bytes 307208 | tf_op jit(solution)/shard_map/ppermute | solution.py:375
  30.8 7.4 %collective-permute-start.11 = (s16[1,400,128]{2,1,0:T(8,128)(2,1)S(1)}, s16[1,400,128]{2,1,0:T(8,128)(2,1)S(1)}, u32[]{:S(2)}, u32[]{:S(2)}) collective-permute-start(s16[1,400,128]{2,1,0:T(8,128)(2,1)S(1)} %get-tuple-element.33), channel_id=1, source_target_pairs={{0,2},{1,3},{2,0},{3,1},{4,6},{5,7},{6,4},{7,5},{8,10},{9,11},{10,... | collective-permute-start | bytes 307208 | tf_op jit(solution)/shard_map/ppermute | solution.py:375

commit v11 on v7

--- a/solution.py
+++ b/solution.py
@@ -71,7 +71,7 @@
 
 def groups_of(count):
     used = (count + GROUP - 1) // GROUP
-    return used, (used + 1) // 2
+    return used, (3 * used + 3) // 4
 
 
 def load(used, pairs, w_hbm, w, acc, sems, w_sems):
@@ -362,7 +362,7 @@
         ],
         input_output_aliases={2 + len(arrays): 0} if extra else {},
         compiler_params=pltpu.CompilerParams(vmem_limit_bytes=32 * MIB),
-        cost_estimate=pl.CostEstimate(flops=1, bytes_accessed=4194304, transcendentals=0),
+        cost_estimate=LITTLE,
     )(left, acc, *arrays, *extra)
 
 
@@ -396,12 +396,12 @@
     (a3_low,) = code(acc, (((6, ((0, 6), (1, 0))),),), (near, y3[0], far))
     (a3_high,) = code(acc, (((7, ((0, 7), (1, 0))),),), (near, y3[1], a3_low))
     a3 = [swap(a3_low, 4, peers), swap(a3_high, 4, peers)]
-    (y1_own,) = code(acc, (((10, ((0, 2),)), (11, ((0, 3),))),), (far, y2_own))
+    (y1_own,) = code(acc, (((10, ((0, 2),)), (11, ((0, 3),))),), (far, y3_own))
     o1 = swap(y1_own, 4, peers)
-    (b2_low,) = code(acc, (((4, ((0, 4), (1, 0), (2, 0))),),), (near, y2[0], a3[0], far))
+    (b2_low,) = code(acc, (((4, ((0, 4), (1, 0), (2, 0))),),), (near, y2[0], a3[0], a3_high))
     (b2_high,) = code(acc, (((5, ((0, 5), (1, 0), (2, 0))),),), (near, y2[1], a3[1], b2_low))
     b2 = [swap(b2_low, 8, peers), swap(b2_high, 8, peers)]
-    y0_own = code(acc, (((8, ((0, 0), (1, 0))),), ((9, ((0, 1), (1, 1))),)), (far, o1, b2_low))
+    y0_own = code(acc, (((8, ((0, 0), (1, 0))),), ((9, ((0, 1), (1, 1))),)), (far, o1, a3_high))
     y0 = [swap(v, 2, peers) for v in y0_own]
     y0_own = y0_own[0]
     (a1_own,) = code(acc, (((2, ((0, 2),)), (3, ((0, 3),))),), (near, a3_high))

time: 39.5 us -> 39.4 us (level)
  starting transfers between devices: 12.1 us -> 11.5 us
where the time goes in v11:
time: 39.4 us; the launch traced here: 39.1 us
  waiting for transfers between devices  13.4 us (34%)
  Pallas kernels  12.6 us (32%)
  starting transfers between devices  11.5 us (29%)
  between operations  0.8 us (2%)
  local copies, waits for them, and re-layouts  0.74 us (2%)
    ppermute x14, waiting for transfers between devices, swap(): return lax.ppermute(value, 'tile', [(i, i ^ bits) for i in range(peers)])  13.4 us
    ppermute x14, starting transfers between devices, swap(): return lax.ppermute(value, 'tile', [(i, i ^ bits) for i in range(peers)])  8.96 us
    pallas_call x2, Pallas kernels, products_call(): pl.pallas_call(kernel, out_shape=tuple(results), in_specs=[smem, smem] +...  6.35 us
    ppermute x1, starting transfers between devices, staged(): after = lax.ppermute(low, 'tile', down)  2.12 us
    pallas_call x2, Pallas kernels, finish(): pl.pallas_call(functools.partial(finish_kernel, half, takes), out_shape=j...  2.11 us
    pallas_call x1, Pallas kernels, add_ends(): pl.pallas_call(ends_kernel, out_shape=(jax.ShapeDtypeStruct(acc.shape, jn...  1.69 us
    pallas_call x9, Pallas kernels, code(): pl.pallas_call(functools.partial(code_kernel, jobs), out_shape=tuple((jax...  1.33 us
  transfers between devices with their start and end apart: 16, of which 7 were waited for; matrix products, arithmetic and copies ran while one was open for 0% of the time, Pallas kernels for 25%

profile of v11, /device:TPU:0, one launch (start us, length us, event | category | flops | bytes accessed | tf_op | source)
XLA Modules:
  0.0 39.1 jit_solution(15340332375860438015)
XLA Ops:
  0.0 0.7 %fusion = (bf16[1,48,128]{2,1,0:T(8,128)(2,1)S(1)}, bf16[1,48,128]{2,1,0:T(8,128)(2,1)S(1)}) fusion(bf16[16,48,128]{2,1,0:T(8,128)(2,1)} %cot_hbm.3), kind=kLoop, calls=%fused_computation | loop fusion | bytes 49152 | tf_op jit(solution)/shard_map/slice | solution.py:383
  0.7 0.5 %collective-permute-start = (bf16[1,48,128]{2,1,0:T(8,128)(2,1)S(1)}, bf16[1,48,128]{2,1,0:T(8,128)(2,1)S(1)}, u32[]{:S(2)}, u32[]{:S(2)}) collective-permute-start(bf16[1,48,128]{2,1,0:T(8,128)(2,1)S(1)} %get-tuple-element.35), channel_id=1, source_target_pairs={{0,1},{1,2},{2,3},{3,4},{4,5},{5,6},{6,7},{7,8},{8,9},{9,10},{10,1... | collective-permute-start | bytes 36872 | tf_op jit(solution)/shard_map/ppermute | solution.py:383
  1.8 3.1 %shard_map.82 = (f32[257,48,128]{2,1,0:T(8,128)S(1)}, bf16[128,128,128]{2,1,0:T(8,128)(2,1)S(1)}, bf16[16,48,128]{2,1,0:T(8,128)(2,1)S(1)}, bf16[1,48,128]{2,1,0:T(8,128)(2,1)S(1)}) custom-call(s32[1]{0:T(128)S(6)} %copy.19.count_ref, s32[1]{0:T(128)} %bitcast.me_ref, s32[1,128]{1,0:T(1,128)} %tb.3, s32[1,128]{1,0:T(1,128)} %dest.3, s32[1,128]{1,0:T(1,128)} %src.3, ...), custom_call_target="tpu_custom_call" | custom-call | flops 268435456 | bytes 12582912 | tf_op jit(solution)/shard_map/pallas_call | solution.py:184
  4.9 2.1 %collective-permute-start.1 = (bf16[1,48,128]{2,1,0:T(8,128)(2,1)S(1)}, bf16[1,48,128]{2,1,0:T(8,128)(2,1)S(1)}, u32[]{:S(2)}, u32[]{:S(2)}) collective-permute-start(bf16[1,48,128]{2,1,0:T(8,128)(2,1)S(1)} %get-tuple-element.24), channel_id=1, source_target_pairs={{1,0},{2,1},{3,2},{4,3},{5,4},{6,5},{7,6},{8,7},{9,8},{10,9},{11,1... | collective-permute-start | bytes 36872 | tf_op jit(solution)/shard_map/ppermute | solution.py:385
  7.0 3.3 %shard_map.83 = (f32[257,48,128]{2,1,0:T(8,128)S(1)}, bf16[128,128,128]{2,1,0:T(8,128)(2,1)S(1)}, bf16[16,48,128]{2,1,0:T(8,128)(2,1)S(1)}, s32[4,136]{1,0:T(4,128)S(1)}) custom-call(s32[1]{0:T(128)S(6)} %copy.19.count_ref, s32[1]{0:T(128)} %bitcast.me_ref, s32[1,128]{1,0:T(1,128)} %tb.3, ...), custom_call_target="tpu_custom_call", output_to_operand_aliasing={{0}: (7, {}), {1}: (8, {}), {2}: (9, {})} | custom-call | flops 1 | bytes 1 | tf_op jit(solution)/shard_map/pallas_call | solution.py:184
  10.3 1.7 %shard_map.84 = (f32[257,48,128]{2,1,0:T(8,128)S(1)}, s16[8,400,128]{2,1,0:T(8,128)(2,1)S(1)}) custom-call(s32[4,136]{1,0:T(4,128)S(1)} %get-tuple-element.23.ends, bf16[1,48,128]{2,1,0:T(8,128)(2,1)S(1)} %collective-permute-done.before, bf16[1,48,128]{2,1,0:T(8,128)(2,1)S(1)} %collective-permute-done.1.after, ...), custom_call_target="tpu_custom_call", output_to_operand_aliasing={{0}: (4, {})} | custom-call | flops 1 | bytes 1 | tf_op jit(solution)/shard_map/pallas_call | solution.py:234
  12.1 0.4 %shard_map.85 = s16[8,400,128]{2,1,0:T(8,128)(2,1)S(1)} custom-call(f32[257,48,128]{2,1,0:T(8,128)S(1)} %get-tuple-element.27.acc), custom_call_target="tpu_custom_call" | custom-call | flops 1 | bytes 1 | tf_op jit(solution)/shard_map/pallas_call | solution.py:285
  12.5 0.6 %collective-permute-start.2 = (s16[8,400,128]{2,1,0:T(8,128)(2,1)S(1)}, s16[8,400,128]{2,1,0:T(8,128)(2,1)S(1)}, u32[]{:S(2)}, u32[]{:S(2)}) collective-permute-start(s16[8,400,128]{2,1,0:T(8,128)(2,1)S(1)} %shard_map.85), channel_id=1, source_target_pairs={{0,1},{1,0},{2,3},{3,2},{4,5},{5,4},{6,7},{7,6},{8,9},{9,8},{10,11... | collective-permute-start | bytes 2457608 | tf_op jit(solution)/shard_map/ppermute | solution.py:375
  13.1 1.3 %collective-permute-done.3.refs_0_.refs_2_ = s16[8,400,128]{2,1,0:T(8,128)(2,1)S(1)} collective-permute-done((s16[8,400,128]{2,1,0:T(8,128)(2,1)S(1)}, s16[8,400,128]{2,1,0:T(8,128)(2,1)S(1)}, u32[]{:S(2)}, u32[]{:S(2)}) %collective-permute-start.3) | collective-permute-done | bytes 819232 | tf_op jit(solution)/shard_map/ppermute | solution.py:375
  14.4 0.2 shard_map.86
  14.7 0.2 shard_map.93
  14.8 0.7 %collective-permute-start.10 = (s16[2,400,128]{2,1,0:T(8,128)(2,1)S(1)}, s16[2,400,128]{2,1,0:T(8,128)(2,1)S(1)}, u32[]{:S(2)}, u32[]{:S(2)}) collective-permute-start(s16[2,400,128]{2,1,0:T(8,128)(2,1)S(1)} %shard_map.93), channel_id=1, source_target_pairs={{0,4},{1,5},{2,6},{3,7},{4,0},{5,1},{6,2},{7,3},{8,12},{9,13},{10,... | collective-permute-start | bytes 614408 | tf_op jit(solution)/shard_map/ppermute | solution.py:375
  15.5 1.5 %collective-permute-start.5 = (s16[1,400,128]{2,1,0:T(8,128)(2,1)S(1)}, s16[1,400,128]{2,1,0:T(8,128)(2,1)S(1)}, u32[]{:S(2)}, u32[]{:S(2)}) collective-permute-start(s16[1,400,128]{2,1,0:T(8,128)(2,1)S(1)} %get-tuple-element.31), channel_id=1, source_target_pairs={{0,2},{1,3},{2,0},{3,1},{4,6},{5,7},{6,4},{7,5},{8,10},{9,11},{10,... | collective-permute-start | bytes 307208 | tf_op jit(solution)/shard_map/ppermute | solution.py:375
  17.0 0.2 shard_map.87
  17.1 0.6 %collective-permute-start.8 = (s16[1,400,128]{2,1,0:T(8,128)(2,1)S(1)}, s16[1,400,128]{2,1,0:T(8,128)(2,1)S(1)}, u32[]{:S(2)}, u32[]{:S(2)}) collective-permute-start(s16[1,400,128]{2,1,0:T(8,128)(2,1)S(1)} %get-tuple-element.32), channel_id=1, source_target_pairs={{0,2},{1,3},{2,0},{3,1},{4,6},{5,7},{6,4},{7,5},{8,10},{9,11},{10,... | collective-permute-start | bytes 307208 | tf_op jit(solution)/shard_map/ppermute | solution.py:375
  17.8 2.6 %collective-permute-done.6.refs_1_ = s16[1,400,128]{2,1,0:T(8,128)(2,1)S(1)} collective-permute-done((s16[1,400,128]{2,1,0:T(8,128)(2,1)S(1)}, s16[1,400,128]{2,1,0:T(8,128)(2,1)S(1)}, u32[]{:S(2)}, u32[]{:S(2)}) %collective-permute-start.6) | collective-permute-done | bytes 102432 | tf_op jit(solution)/shard_map/ppermute | solution.py:375
  20.6 0.8 %collective-permute-start.4 = (s16[1,400,128]{2,1,0:T(8,128)(2,1)S(1)}, s16[1,400,128]{2,1,0:T(8,128)(2,1)S(1)}, u32[]{:S(2)}, u32[]{:S(2)}) collective-permute-start(s16[1,400,128]{2,1,0:T(8,128)(2,1)S(1)} %get-tuple-element.30), channel_id=1, source_target_pairs={{0,2},{1,3},{2,0},{3,1},{4,6},{5,7},{6,4},{7,5},{8,10},{9,11},{10,... | collective-permute-start | bytes 307208 | tf_op jit(solution)/shard_map/ppermute | solution.py:375
  21.4 1.2 %collective-permute-done.5.refs_1_ = s16[1,400,128]{2,1,0:T(8,128)(2,1)S(1)} collective-permute-done((s16[1,400,128]{2,1,0:T(8,128)(2,1)S(1)}, s16[1,400,128]{2,1,0:T(8,128)(2,1)S(1)}, u32[]{:S(2)}, u32[]{:S(2)}) %collective-permute-start.5) | collective-permute-done | bytes 102432 | tf_op jit(solution)/shard_map/ppermute | solution.py:375
  22.8 0.2 shard_map.95
  22.9 1.8 %collective-permute-done.8.refs_1_ = s16[1,400,128]{2,1,0:T(8,128)(2,1)S(1)} collective-permute-done((s16[1,400,128]{2,1,0:T(8,128)(2,1)S(1)}, s16[1,400,128]{2,1,0:T(8,128)(2,1)S(1)}, u32[]{:S(2)}, u32[]{:S(2)}) %collective-permute-start.8) | collective-permute-done | bytes 102432 | tf_op jit(solution)/shard_map/ppermute | solution.py:375
  24.8 0.2 collective-permute-start.12
  25.0 1.1 %collective-permute-done.9.refs_2_ = s16[1,400,128]{2,1,0:T(8,128)(2,1)S(1)} collective-permute-done((s16[1,400,128]{2,1,0:T(8,128)(2,1)S(1)}, s16[1,400,128]{2,1,0:T(8,128)(2,1)S(1)}, u32[]{:S(2)}, u32[]{:S(2)}) %collective-permute-start.9) | collective-permute-done | bytes 102432 | tf_op jit(solution)/shard_map/ppermute | solution.py:375
  26.3 0.7 %collective-permute-start.15 = (s16[1,400,128]{2,1,0:T(8,128)(2,1)S(1)}, s16[1,400,128]{2,1,0:T(8,128)(2,1)S(1)}, u32[]{:S(2)}, u32[]{:S(2)}) collective-permute-start(s16[1,400,128]{2,1,0:T(8,128)(2,1)S(1)} %shard_map.90.refs_3_), channel_id=1, source_target_pairs={{0,8},{1,9},{2,10},{3,11},{4,12},{5,13},{6,14},{7,15},{8,0},{9,1},... | collective-permute-start | bytes 307208 | tf_op jit(solution)/shard_map/ppermute | solution.py:375
  27.1 0.2 shard_map.94
  27.3 1.5 %collective-permute-start.14 = (s16[1,400,128]{2,1,0:T(8,128)(2,1)S(1)}, s16[1,400,128]{2,1,0:T(8,128)(2,1)S(1)}, u32[]{:S(2)}, u32[]{:S(2)}) collective-permute-start(s16[1,400,128]{2,1,0:T(8,128)(2,1)S(1)} %get-tuple-element.34), channel_id=1, source_target_pairs={{0,2},{1,3},{2,0},{3,1},{4,6},{5,7},{6,4},{7,5},{8,10},{9,11},{10,... | collective-permute-start | bytes 307208 | tf_op jit(solution)/shard_map/ppermute | solution.py:375
  28.8 0.8 %collective-permute-done.7.refs_2_ = s16[1,400,128]{2,1,0:T(8,128)(2,1)S(1)} collective-permute-done((s16[1,400,128]{2,1,0:T(8,128)(2,1)S(1)}, s16[1,400,128]{2,1,0:T(8,128)(2,1)S(1)}, u32[]{:S(2)}, u32[]{:S(2)}) %collective-permute-start.7) | collective-permute-done | bytes 102432 | tf_op jit(solution)/shard_map/ppermute | solution.py:375
  29.8 1.0 %collective-permute-start.13 = (s16[1,400,128]{2,1,0:T(8,128)(2,1)S(1)}, s16[1,400,128]{2,1,0:T(8,128)(2,1)S(1)}, u32[]{:S(2)}, u32[]{:S(2)}) collective-permute-start(s16[1,400,128]{2,1,0:T(8,128)(2,1)S(1)} %shard_map.91.after), channel_id=1, source_target_pairs={{0,8},{1,9},{2,10},{3,11},{4,12},{5,13},{6,14},{7,15},{8,0},{9,1},... | collective-permute-start | bytes 307208 | tf_op jit(solution)/shard_map/ppermute | solution.py:375
  30.7 1.1 %collective-permute-start.11 = (s16[1,400,128]{2,1,0:T(8,128)(2,1)S(1)}, s16[1,400,128]{2,1,0:T(8,128)(2,1)S(1)}, u32[]{:S(2)}, u32[]{:S(2)}) collective-permute-start(s16[1,400,128]{2,1,0:T(8,128)(2,1)S(1)} %get-tuple-element.33), channel_id=1, source_target_pairs={{0,2},{1,3},{2,0},{3,1},{4,6},{5,7},{6,4},{7,5},{8,10},{9,11},{10,... | collective-permute-start | bytes 307208 | tf_op jit(solution)/shard_map/ppermute | solution.py:375
  31.9 0.7 %shard_map.92.left = bf16[120,192]{1,0:T(8,128)(2,1)S(1)} custom-call(s32[8]{0:T(128)S(1)} %copy-done, f32[8]{0:T(128)S(1)} %copy-done.1, s16[1,400,128]{2,1,0:T(8,128)(2,1)S(1)} %shard_map.91.after), custom_call_target="tpu_custom_call" | custom-call | flops 1 | bytes 1 | tf_op jit(solution)/shard_map/pallas_call | solution.py:315
  32.6 4.3 %collective-permute-done.15.refs_3_ = s16[1,400,128]{2,1,0:T(8,128)(2,1)S(1)} collective-permute-done((s16[1,400,128]{2,1,0:T(8,128)(2,1)S(1)}, s16[1,400,128]{2,1,0:T(8,128)(2,1)S(1)}, u32[]{:S(2)}, u32[]{:S(2)}) %collective-permute-start.15) | collective-permute-done | bytes 102432 | tf_op jit(solution)/shard_map/ppermute | solution.py:375
  36.9 1.1 %shard_map.96.refs_4_ = f32[16,120,128]{2,1,0:T(8,128)} custom-call(bf16[120,192]{1,0:T(8,128)(2,1)S(1)} %shard_map.92.left, f32[257,48,128]{2,1,0:T(8,128)S(1)} %get-tuple-element.27.acc, s16[8,400,128]{2,1,0:T(8,128)(2,1)S(1)} %collective-permute-done.2.refs_0_, s16[1,400,128]{2,1,0:T(8,128)(2,1)S(1)} %collective-permute-done.14.refs_1_, ...), custom_call_target="tpu_custom_call" | custom-call | flops 1 | bytes 1 | tf_op jit(solution)/shard_map/pallas_call | solution.py:354
  38.0 1.1 %shard_map.97 = f32[16,120,128]{2,1,0:T(8,128)} custom-call(bf16[120,192]{1,0:T(8,128)(2,1)S(1)} %shard_map.92.left, f32[257,48,128]{2,1,0:T(8,128)S(1)} %get-tuple-element.27.acc, s16[8,400,128]{2,1,0:T(8,128)(2,1)S(1)} %collective-permute-done.2.refs_0_, s16[1,400,128]{2,1,0:T(8,128)(2,1)S(1)} %collective-permute-done.11.refs_1_, ...), custom_call_target="tpu_custom_call", output_to_operand_aliasing={{}: (6, {})} | custom-call | flops 1 | bytes 1 | tf_op jit(solution)/shard_map/pallas_call | solution.py:354
  (21 shorter events, 0.9 us)
Async XLA Ops:
  0.7 9.6 %collective-permute-start = (bf16[1,48,128]{2,1,0:T(8,128)(2,1)S(1)}, bf16[1,48,128]{2,1,0:T(8,128)(2,1)S(1)}, u32[]{:S(2)}, u32[]{:S(2)}) collective-permute-start(bf16[1,48,128]{2,1,0:T(8,128)(2,1)S(1)} %get-tuple-element.35), channel_id=1, source_target_pairs={{0,1},{1,2},{2,3},{3,4},{4,5},{5,6},{6,7},{7,8},{8,9},{9,10},{10,1... | collective-permute-start | bytes 36872 | tf_op jit(solution)/shard_map/ppermute | solution.py:383
  4.9 5.4 %collective-permute-start.1 = (bf16[1,48,128]{2,1,0:T(8,128)(2,1)S(1)}, bf16[1,48,128]{2,1,0:T(8,128)(2,1)S(1)}, u32[]{:S(2)}, u32[]{:S(2)}) collective-permute-start(bf16[1,48,128]{2,1,0:T(8,128)(2,1)S(1)} %get-tuple-element.24), channel_id=1, source_target_pairs={{1,0},{2,1},{3,2},{4,3},{5,4},{6,5},{7,6},{8,7},{9,8},{10,9},{11,1... | collective-permute-start | bytes 36872 | tf_op jit(solution)/shard_map/ppermute | solution.py:385
  12.0 2.4 %collective-permute-start.3 = (s16[8,400,128]{2,1,0:T(8,128)(2,1)S(1)}, s16[8,400,128]{2,1,0:T(8,128)(2,1)S(1)}, u32[]{:S(2)}, u32[]{:S(2)}) collective-permute-start(s16[8,400,128]{2,1,0:T(8,128)(2,1)S(1)} %get-tuple-element.28), channel_id=1, source_target_pairs={{0,1},{1,0},{2,3},{3,2},{4,5},{5,4},{6,7},{7,6},{8,9},{9,8},{10,11... | collective-permute-start | bytes 2457608 | tf_op jit(solution)/shard_map/ppermute | solution.py:375
  12.5 5.2 %collective-permute-start.2 = (s16[8,400,128]{2,1,0:T(8,128)(2,1)S(1)}, s16[8,400,128]{2,1,0:T(8,128)(2,1)S(1)}, u32[]{:S(2)}, u32[]{:S(2)}) collective-permute-start(s16[8,400,128]{2,1,0:T(8,128)(2,1)S(1)} %shard_map.85), channel_id=1, source_target_pairs={{0,1},{1,0},{2,3},{3,2},{4,5},{5,4},{6,7},{7,6},{8,9},{9,8},{10,11... | collective-permute-start | bytes 2457608 | tf_op jit(solution)/shard_map/ppermute | solution.py:375
  14.6 5.8 %collective-permute-start.6 = (s16[1,400,128]{2,1,0:T(8,128)(2,1)S(1)}, s16[1,400,128]{2,1,0:T(8,128)(2,1)S(1)}, u32[]{:S(2)}, u32[]{:S(2)}) collective-permute-start(s16[1,400,128]{2,1,0:T(8,128)(2,1)S(1)} %get-tuple-element.29.refs_1_), channel_id=1, source_target_pairs={{0,2},{1,3},{2,0},{3,1},{4,6},{5,7},{6,4},{7,5},{8,10},{9,11},{10,... | collective-permute-start | bytes 307208 | tf_op jit(solution)/shard_map/ppermute | solution.py:375
  14.8 12.3 %collective-permute-start.10 = (s16[2,400,128]{2,1,0:T(8,128)(2,1)S(1)}, s16[2,400,128]{2,1,0:T(8,128)(2,1)S(1)}, u32[]{:S(2)}, u32[]{:S(2)}) collective-permute-start(s16[2,400,128]{2,1,0:T(8,128)(2,1)S(1)} %shard_map.93), channel_id=1, source_target_pairs={{0,4},{1,5},{2,6},{3,7},{4,0},{5,1},{6,2},{7,3},{8,12},{9,13},{10,... | collective-permute-start | bytes 614408 | tf_op jit(solution)/shard_map/ppermute | solution.py:375
  15.5 7.1 %collective-permute-start.5 = (s16[1,400,128]{2,1,0:T(8,128)(2,1)S(1)}, s16[1,400,128]{2,1,0:T(8,128)(2,1)S(1)}, u32[]{:S(2)}, u32[]{:S(2)}) collective-permute-start(s16[1,400,128]{2,1,0:T(8,128)(2,1)S(1)} %get-tuple-element.31), channel_id=1, source_target_pairs={{0,2},{1,3},{2,0},{3,1},{4,6},{5,7},{6,4},{7,5},{8,10},{9,11},{10,... | collective-permute-start | bytes 307208 | tf_op jit(solution)/shard_map/ppermute | solution.py:375
  17.1 7.6 %collective-permute-start.8 = (s16[1,400,128]{2,1,0:T(8,128)(2,1)S(1)}, s16[1,400,128]{2,1,0:T(8,128)(2,1)S(1)}, u32[]{:S(2)}, u32[]{:S(2)}) collective-permute-start(s16[1,400,128]{2,1,0:T(8,128)(2,1)S(1)} %get-tuple-element.32), channel_id=1, source_target_pairs={{0,2},{1,3},{2,0},{3,1},{4,6},{5,7},{6,4},{7,5},{8,10},{9,11},{10,... | collective-permute-start | bytes 307208 | tf_op jit(solution)/shard_map/ppermute | solution.py:375
  20.5 5.7 %collective-permute-start.9 = (s16[1,400,128]{2,1,0:T(8,128)(2,1)S(1)}, s16[1,400,128]{2,1,0:T(8,128)(2,1)S(1)}, u32[]{:S(2)}, u32[]{:S(2)}) collective-permute-start(s16[1,400,128]{2,1,0:T(8,128)(2,1)S(1)} %shard_map.88.refs_2_), channel_id=1, source_target_pairs={{0,4},{1,5},{2,6},{3,7},{4,0},{5,1},{6,2},{7,3},{8,12},{9,13},{10,... | collective-permute-start | bytes 307208 | tf_op jit(solution)/shard_map/ppermute | solution.py:375
  20.6 8.2 %collective-permute-start.4 = (s16[1,400,128]{2,1,0:T(8,128)(2,1)S(1)}, s16[1,400,128]{2,1,0:T(8,128)(2,1)S(1)}, u32[]{:S(2)}, u32[]{:S(2)}) collective-permute-start(s16[1,400,128]{2,1,0:T(8,128)(2,1)S(1)} %get-tuple-element.30), channel_id=1, source_target_pairs={{0,2},{1,3},{2,0},{3,1},{4,6},{5,7},{6,4},{7,5},{8,10},{9,11},{10,... | collective-permute-start | bytes 307208 | tf_op jit(solution)/shard_map/ppermute | solution.py:375
  22.7 6.9 %collective-permute-start.7 = (s16[1,400,128]{2,1,0:T(8,128)(2,1)S(1)}, s16[1,400,128]{2,1,0:T(8,128)(2,1)S(1)}, u32[]{:S(2)}, u32[]{:S(2)}) collective-permute-start(s16[1,400,128]{2,1,0:T(8,128)(2,1)S(1)} %shard_map.89.refs_3_.refs_2_.refs_1_), channel_id=1, source_target_pairs={{0,4},{1,5},{2,6},{3,7},{4,0},{5,1},{6,2},{7,3},{8,12},{9,13},{10,... | collective-permute-start | bytes 307208 | tf_op jit(solution)/shard_map/ppermute | solution.py:375
  24.8 12.2 %collective-permute-start.12 = (s16[2,400,128]{2,1,0:T(8,128)(2,1)S(1)}, s16[2,400,128]{2,1,0:T(8,128)(2,1)S(1)}, u32[]{:S(2)}, u32[]{:S(2)}) collective-permute-start(s16[2,400,128]{2,1,0:T(8,128)(2,1)S(1)} %shard_map.95), channel_id=1, source_target_pairs={{0,4},{1,5},{2,6},{3,7},{4,0},{5,1},{6,2},{7,3},{8,12},{9,13},{10,... | collective-permute-start | bytes 614408 | tf_op jit(solution)/shard_map/ppermute | solution.py:375
  26.3 5.5 %copy-start = (s32[8]{0:T(128)S(1)}, s32[8]{0:T(128)}, u32[]{:S(2)}) copy-start(s32[8]{0:T(128)} %index_ref.1) | copy-start | bytes 100
  26.3 5.5 %copy-start.1 = (f32[8]{0:T(128)S(1)}, f32[8]{0:T(128)}, u32[]{:S(2)}) copy-start(f32[8]{0:T(128)} %frac_ref.1) | copy-start | bytes 100
  26.3 10.6 %collective-permute-start.15 = (s16[1,400,128]{2,1,0:T(8,128)(2,1)S(1)}, s16[1,400,128]{2,1,0:T(8,128)(2,1)S(1)}, u32[]{:S(2)}, u32[]{:S(2)}) collective-permute-start(s16[1,400,128]{2,1,0:T(8,128)(2,1)S(1)} %shard_map.90.refs_3_), channel_id=1, source_target_pairs={{0,8},{1,9},{2,10},{3,11},{4,12},{5,13},{6,14},{7,15},{8,0},{9,1},... | collective-permute-start | bytes 307208 | tf_op jit(solution)/shard_map/ppermute | solution.py:375
  27.3 9.6 %collective-permute-start.14 = (s16[1,400,128]{2,1,0:T(8,128)(2,1)S(1)}, s16[1,400,128]{2,1,0:T(8,128)(2,1)S(1)}, u32[]{:S(2)}, u32[]{:S(2)}) collective-permute-start(s16[1,400,128]{2,1,0:T(8,128)(2,1)S(1)} %get-tuple-element.34), channel_id=1, source_target_pairs={{0,2},{1,3},{2,0},{3,1},{4,6},{5,7},{6,4},{7,5},{8,10},{9,11},{10,... | collective-permute-start | bytes 307208 | tf_op jit(solution)/shard_map/ppermute | solution.py:375
  29.8 8.3 %collective-permute-start.13 = (s16[1,400,128]{2,1,0:T(8,128)(2,1)S(1)}, s16[1,400,128]{2,1,0:T(8,128)(2,1)S(1)}, u32[]{:S(2)}, u32[]{:S(2)}) collective-permute-start(s16[1,400,128]{2,1,0:T(8,128)(2,1)S(1)} %shard_map.91.after), channel_id=1, source_target_pairs={{0,8},{1,9},{2,10},{3,11},{4,12},{5,13},{6,14},{7,15},{8,0},{9,1},... | collective-permute-start | bytes 307208 | tf_op jit(solution)/shard_map/ppermute | solution.py:375
  30.7 7.3 %collective-permute-start.11 = (s16[1,400,128]{2,1,0:T(8,128)(2,1)S(1)}, s16[1,400,128]{2,1,0:T(8,128)(2,1)S(1)}, u32[]{:S(2)}, u32[]{:S(2)}) collective-permute-start(s16[1,400,128]{2,1,0:T(8,128)(2,1)S(1)} %get-tuple-element.33), channel_id=1, source_target_pairs={{0,2},{1,3},{2,0},{3,1},{4,6},{5,7},{6,4},{7,5},{8,10},{9,11},{10,... | collective-permute-start | bytes 307208 | tf_op jit(solution)/shard_map/ppermute | solution.py:375
